TPU v7x, 32 devices: a whole 2x2x4 slice. The times are simulated.
32 devices in a mesh: section: 2 (over core), dp: 16 (over z, y, x).
Axes of the slice: x: 2, y: 2, z: 4, core: 2. Of those that a mesh axis runs over, the one named last changes fastest.
Arguments:
- global_ends: bfloat16 [2, 32, 197, 384], P('section', 'dp'), may hold values from -6 to 6
- local_ends: bfloat16 [2, 160, 37, 384], P('section', 'dp'), may hold values from -6 to 6
- global_live: int32 [32], P('dp'), may hold values from 0 to 1, as said below
- local_live: int32 [160], P('dp'), may hold values from 0 to 1, as said below
- ln1_gain: bfloat16 [2, 384], P('section'), may hold values from 0.25 to 1.75
- ln1_bias: bfloat16 [2, 384], P('section'), may hold values from -3 to 3
- qkv_weight: bfloat16 [2, 384, 1152], P('section'), may hold values from -0.3125 to 0.3125
- query_bias: bfloat16 [2, 384], P('section'), may hold values from -3 to 3
- value_bias: bfloat16 [2, 384], P('section'), may hold values from -3 to 3
- proj_weight: bfloat16 [2, 384, 384], P('section'), may hold values from -1.25 to 1.25
- proj_bias: bfloat16 [2, 384], P('section'), may hold values from -3 to 3
- ln2_gain: bfloat16 [2, 384], P('section'), may hold values from 0.25 to 1.75
- ln2_bias: bfloat16 [2, 384], P('section'), may hold values from -3 to 3
- fc1_weight: bfloat16 [2, 384, 1536], P('section'), may hold values from -0.3125 to 0.3125
- fc1_bias: bfloat16 [2, 1536], P('section'), may hold values from -3 to 3
- fc2_weight: bfloat16 [2, 1536, 384], P('section'), may hold values from -0.15625 to 0.15625
- fc2_bias: bfloat16 [2, 384], P('section'), may hold values from -3 to 3
Outputs:
- global_result: bfloat16 [2, 32, 197, 384], P('section', 'dp')
- local_result: bfloat16 [2, 160, 37, 384], P('section', 'dp')
- grad_ln1_gain: float32 [2, 384], P('section')
- grad_ln1_bias: float32 [2, 384], P('section')
- grad_qkv_weight: float32 [2, 384, 1152], P('section')
- grad_query_bias: float32 [2, 384], P('section')
- grad_value_bias: float32 [2, 384], P('section')
- grad_proj_weight: float32 [2, 384, 384], P('section')
- grad_proj_bias: float32 [2, 384], P('section')
- grad_ln2_gain: float32 [2, 384], P('section')
- grad_ln2_bias: float32 [2, 384], P('section')
- grad_fc1_weight: float32 [2, 384, 1536], P('section')
- grad_fc1_bias: float32 [2, 1536], P('section')
- grad_fc2_weight: float32 [2, 1536, 384], P('section')
- grad_fc2_bias: float32 [2, 384], P('section')
Inputs may be any that keep to these rules, and one draw needn't show every extreme that they name: `global_live`: device d of dp holds slots d * 2 to (d + 1) * 2 - 1; on some device every global and every local slot is live. `local_live`: device d of dp holds slots d * 10 to (d + 1) * 10 - 1; on some device every global and every local slot is live.
All inputs are finite; a program needn't handle non-finite values.
Results may differ from a plain program's by a relative error of at most 0.015.
Values may be sent and summed in bfloat16 or wider, within the bound.
No kernel may reach another device: no remote copies, remote signals or barrier semaphores. Data moves between devices by JAX's collectives and lax.ppermute only.
A program may use at most 128 MiB of HBM per device.

v0:
```python
import jax
import jax.numpy as jnp
from jax import lax
from jax.sharding import PartitionSpec as P

HEAD = 64
GT = 197
LT = 37
MICRO = 2


EPSILON = 1e-06


def from_behind(x, axis, by):
    length = lax.axis_size(axis)
    pairs = [(i, i + by) for i in range(length) if 0 <= i + by < length]
    return lax.ppermute(x, axis, pairs)


def layer_norm(values_in, gain_vector, shift_vector):
    centred = values_in - jnp.mean(values_in, axis=-1, keepdims=True)
    spread = jnp.mean(centred * centred, axis=-1, keepdims=True)
    return centred * lax.rsqrt(spread + EPSILON) * gain_vector + shift_vector


def exact_gelu(values_in):
    return jax.nn.gelu(values_in, approximate=False)


def product(left, right):
    return jnp.dot(left, right, preferred_element_type=jnp.float32)


def outer_sum(left, right):
    return jnp.einsum("ti,to->io", left, right, preferred_element_type=jnp.float32)


def back_product(grad_rows, matrix):
    return jnp.einsum("to,io->ti", grad_rows, matrix, preferred_element_type=jnp.float32)


def weight_products(factors):
    return tuple((outer_sum(left, right) for left, right in factors))


def assemble(small_grads, large_grads):
    (
        grad_ln1_gain,
        grad_ln1_bias,
        grad_query_bias,
        grad_value_bias,
        grad_proj_bias,
        grad_ln2_gain,
        grad_ln2_bias,
        grad_fc1_bias,
        grad_fc2_bias,
    ) = small_grads
    grad_qkv, grad_proj, grad_fc1, grad_fc2 = large_grads
    return (
        grad_ln1_gain,
        grad_ln1_bias,
        grad_qkv,
        grad_query_bias,
        grad_value_bias,
        grad_proj,
        grad_proj_bias,
        grad_ln2_gain,
        grad_ln2_bias,
        grad_fc1,
        grad_fc1_bias,
        grad_fc2,
        grad_fc2_bias,
    )


def attend(queries, key_rows, value_rows, crop_count, crop_length):
    features = queries.shape[-1]
    split_shape = (crop_count, crop_length, features // HEAD, HEAD)
    query_heads = queries.reshape(split_shape)
    key_heads = key_rows.reshape(split_shape)
    value_heads = value_rows.reshape(split_shape)
    scores = jnp.einsum(
        "cqhe,ckhe->chqk", query_heads, key_heads, preferred_element_type=jnp.float32
    ) * HEAD ** (-0.5)
    highest = jnp.max(scores, axis=-1, keepdims=True)
    raised = jnp.exp(scores - highest)
    soft_weights = raised / jnp.sum(raised, axis=-1, keepdims=True)
    soft_low = soft_weights.astype(jnp.bfloat16)
    mixed = jnp.einsum("chqk,ckhe->cqhe", soft_low, value_heads, preferred_element_type=jnp.float32)
    return (
        mixed.reshape(crop_count * crop_length, features),
        (query_heads, key_heads, value_heads, soft_weights, soft_low),
    )


def attend_back(saved_parts, grad_mixed, crop_count, crop_length):
    query_heads, key_heads, value_heads, soft_weights, soft_low = saved_parts
    features = grad_mixed.shape[-1]
    total_rows = crop_count * crop_length
    grad_split = grad_mixed.reshape(query_heads.shape)
    grad_values = jnp.einsum(
        "chqk,cqhe->ckhe", soft_low, grad_split, preferred_element_type=jnp.float32
    )
    grad_soft = jnp.einsum(
        "cqhe,ckhe->chqk", grad_split, value_heads, preferred_element_type=jnp.float32
    )
    grad_scores = (
        soft_weights * (grad_soft - jnp.sum(grad_soft * soft_weights, axis=-1, keepdims=True))
    ).astype(jnp.bfloat16)
    grad_queries = jnp.einsum(
        "chqk,ckhe->cqhe", grad_scores, key_heads, preferred_element_type=jnp.float32
    ) * HEAD ** (-0.5)
    grad_keys = jnp.einsum(
        "chqk,cqhe->ckhe", grad_scores, query_heads, preferred_element_type=jnp.float32
    ) * HEAD ** (-0.5)
    return (
        grad_queries.reshape(total_rows, features),
        grad_keys.reshape(total_rows, features),
        grad_values.reshape(total_rows, features),
    )


def layer_parts(packed, params, global_count, local_count):
    (
        ln1_gain,
        ln1_bias,
        qkv_weight,
        query_bias,
        value_bias,
        proj_weight,
        proj_bias,
        ln2_gain,
        ln2_bias,
        fc1_weight,
        fc1_bias,
        fc2_weight,
        fc2_bias,
    ) = params
    features = packed.shape[-1]
    boundary = global_count * GT
    residual = packed.astype(jnp.float32)
    normed, norm_first = jax.vjp(
        layer_norm, residual, ln1_gain.astype(jnp.float32), ln1_bias.astype(jnp.float32)
    )
    normed_low = normed.astype(jnp.bfloat16)
    triple = product(normed_low, qkv_weight)
    queries = (triple[:, :features] + query_bias).astype(jnp.bfloat16)
    key_rows = triple[:, features : 2 * features].astype(jnp.bfloat16)
    value_rows = (triple[:, 2 * features :] + value_bias).astype(jnp.bfloat16)
    mixed_global, saved_global = attend(
        queries[:boundary], key_rows[:boundary], value_rows[:boundary], global_count, GT
    )
    mixed_local, saved_local = attend(
        queries[boundary:], key_rows[boundary:], value_rows[boundary:], local_count, LT
    )
    mixed_low = jnp.concatenate([mixed_global, mixed_local], axis=0).astype(jnp.bfloat16)
    middle = residual + (product(mixed_low, proj_weight) + proj_bias)
    second_normed, norm_second = jax.vjp(
        layer_norm, middle, ln2_gain.astype(jnp.float32), ln2_bias.astype(jnp.float32)
    )
    second_low = second_normed.astype(jnp.bfloat16)
    hidden = product(second_low, fc1_weight) + fc1_bias
    active, gelu_back = jax.vjp(exact_gelu, hidden)
    active_low = active.astype(jnp.bfloat16)
    result = middle + (product(active_low, fc2_weight) + fc2_bias)
    saved_parts = (
        norm_first,
        normed_low,
        saved_global,
        saved_local,
        mixed_low,
        norm_second,
        second_low,
        gelu_back,
        active_low,
    )
    return (result, saved_parts)


def layer_back(packed, params, grad_rows, global_count, local_count):
    (
        ln1_gain,
        ln1_bias,
        qkv_weight,
        query_bias,
        value_bias,
        proj_weight,
        proj_bias,
        ln2_gain,
        ln2_bias,
        fc1_weight,
        fc1_bias,
        fc2_weight,
        fc2_bias,
    ) = params
    unused, saved_parts = layer_parts(packed, params, global_count, local_count)
    (
        norm_first,
        normed_low,
        saved_global,
        saved_local,
        mixed_low,
        norm_second,
        second_low,
        gelu_back,
        active_low,
    ) = saved_parts
    features = packed.shape[-1]
    boundary = global_count * GT
    grad_fc2_bias = jnp.sum(grad_rows, axis=0, dtype=jnp.float32)
    grad_active = back_product(grad_rows, fc2_weight)
    grad_hidden = gelu_back(grad_active)[0].astype(jnp.bfloat16)
    grad_fc1_bias = jnp.sum(grad_hidden, axis=0, dtype=jnp.float32)
    grad_second = back_product(grad_hidden, fc1_weight)
    back_middle, grad_ln2_gain, grad_ln2_bias = norm_second(grad_second)
    grad_middle = grad_rows.astype(jnp.float32) + back_middle
    grad_branch = grad_middle.astype(jnp.bfloat16)
    grad_proj_bias = jnp.sum(grad_branch, axis=0, dtype=jnp.float32)
    grad_mixed = back_product(grad_branch, proj_weight).astype(jnp.bfloat16)
    global_grads = attend_back(saved_global, grad_mixed[:boundary], global_count, GT)
    local_grads = attend_back(saved_local, grad_mixed[boundary:], local_count, LT)
    grad_triple = jnp.concatenate(
        [
            jnp.concatenate([global_grads[0], local_grads[0]], axis=0),
            jnp.concatenate([global_grads[1], local_grads[1]], axis=0),
            jnp.concatenate([global_grads[2], local_grads[2]], axis=0),
        ],
        axis=1,
    ).astype(jnp.bfloat16)
    grad_query_bias = jnp.sum(grad_triple[:, :features], axis=0, dtype=jnp.float32)
    grad_value_bias = jnp.sum(grad_triple[:, 2 * features :], axis=0, dtype=jnp.float32)
    grad_first = back_product(grad_triple, qkv_weight)
    back_input, grad_ln1_gain, grad_ln1_bias = norm_first(grad_first)
    grad_input = grad_middle + back_input
    small_grads = (
        grad_ln1_gain,
        grad_ln1_bias,
        grad_query_bias,
        grad_value_bias,
        grad_proj_bias,
        grad_ln2_gain,
        grad_ln2_bias,
        grad_fc1_bias,
        grad_fc2_bias,
    )
    factors = (
        (normed_low, grad_triple),
        (mixed_low, grad_branch),
        (second_low, grad_hidden),
        (active_low, grad_rows),
    )
    return (grad_input, small_grads, factors)


def on_device(
    global_ends,
    local_ends,
    global_live,
    local_live,
    ln1_gain,
    ln1_bias,
    qkv_weight,
    query_bias,
    value_bias,
    proj_weight,
    proj_bias,
    ln2_gain,
    ln2_bias,
    fc1_weight,
    fc1_bias,
    fc2_weight,
    fc2_bias,
):
    params = tuple(
        (
            weight[0]
            for weight in (
                ln1_gain,
                ln1_bias,
                qkv_weight,
                query_bias,
                value_bias,
                proj_weight,
                proj_bias,
                ln2_gain,
                ln2_bias,
                fc1_weight,
                fc1_bias,
                fc2_weight,
                fc2_bias,
            )
        )
    )
    leading = lax.axis_index("section") == 0
    own_global = global_ends[0]
    own_local = local_ends[0]
    features = own_global.shape[-1]
    global_count = own_global.shape[0] // MICRO
    local_count = own_local.shape[0] // MICRO
    global_rows = global_count * GT
    blank_rows = jnp.zeros((global_rows + local_count * LT, features), jnp.bfloat16)
    global_mask = global_live.astype(jnp.bfloat16)
    local_mask = local_live.astype(jnp.bfloat16)

    def packed_part(position):
        global_piece = own_global[position * global_count : (position + 1) * global_count].reshape(
            -1, features
        )
        local_piece = own_local[position * local_count : (position + 1) * local_count].reshape(
            -1, features
        )
        return jnp.concatenate([global_piece, local_piece], axis=0)

    def live_rows(position):
        global_flags = jnp.repeat(
            global_mask[position * global_count : (position + 1) * global_count], GT
        )
        local_flags = jnp.repeat(
            local_mask[position * local_count : (position + 1) * local_count], LT
        )
        return jnp.concatenate([global_flags, local_flags])[:, None]

    arrived = blank_rows
    inputs_kept = []
    outputs_made = []
    for instant in range(MICRO + 1):
        own_part = packed_part(instant) if instant < MICRO else blank_rows
        start = jnp.where(leading, own_part, arrived)
        inputs_kept.append(start)
        produced, unused = layer_parts(start, params, global_count, local_count)
        if instant >= 1:
            outputs_made.append((produced * live_rows(instant - 1)).astype(jnp.bfloat16))
        if instant < MICRO:
            arrived = from_behind(produced.astype(jnp.bfloat16), "section", 1)
    arrived = blank_rows
    pending = tuple((jnp.zeros(weight.shape, jnp.float32) for weight in params))
    input_grads = []
    for instant in range(MICRO + 1):
        cotangent_part = (
            packed_part(instant) * live_rows(instant) if instant < MICRO else blank_rows
        )
        incoming = jnp.where(leading, arrived, cotangent_part)
        source = jnp.where(
            leading, inputs_kept[max(instant - 1, 0)], inputs_kept[min(instant + 1, MICRO)]
        )
        grad_input, small_grads, factors = layer_back(
            source, params, incoming, global_count, local_count
        )
        if instant >= 1:
            input_grads.append(grad_input.astype(jnp.bfloat16))
        if instant < MICRO:
            arrived = from_behind(grad_input.astype(jnp.bfloat16), "section", -1)
        gradients = assemble(small_grads, weight_products(factors))
        pending = tuple((left + right for left, right in zip(pending, gradients)))
    summed = lax.psum(
        (
            pending[0],
            pending[1],
            pending[2],
            pending[3],
            pending[4],
            pending[5],
            pending[6],
            pending[7],
            pending[8],
            pending[9],
            pending[10],
            pending[11],
            pending[12],
        ),
        "dp",
    )
    pieces = [
        jnp.where(leading, input_grads[position], outputs_made[position])
        for position in range(MICRO)
    ]
    global_out = jnp.concatenate(
        [segment[:global_rows].reshape(global_count, GT, features) for segment in pieces], axis=0
    )[None]
    local_out = jnp.concatenate(
        [segment[global_rows:].reshape(local_count, LT, features) for segment in pieces], axis=0
    )[None]
    return (global_out, local_out) + tuple((accumulated[None] for accumulated in summed))


def solution(mesh):
    return jax.shard_map(
        on_device,
        mesh=mesh,
        in_specs=(
            P("section", "dp", None, None),
            P("section", "dp", None, None),
            P("dp"),
            P("dp"),
            P("section", None),
            P("section", None),
            P("section", None, None),
            P("section", None),
            P("section", None),
            P("section", None, None),
            P("section", None),
            P("section", None),
            P("section", None),
            P("section", None, None),
            P("section", None),
            P("section", None, None),
            P("section", None),
        ),
        out_specs=(
            P("section", "dp", None, None),
            P("section", "dp", None, None),
            P("section", None),
            P("section", None),
            P("section", None, None),
            P("section", None),
            P("section", None),
            P("section", None, None),
            P("section", None),
            P("section", None),
            P("section", None),
            P("section", None, None),
            P("section", None),
            P("section", None, None),
            P("section", None),
        ),
        check_vma=False,
    )
```

profile of v0, /device:TPU:0, one launch (start us, length us, event | category | flops | bytes accessed | tf_op | source)
XLA Modules:
  0.0 608.9 jit_solution(5913483529059739543)
XLA Ops:
  35.8 2.5 convolution_convert_fusion.20
  40.2 8.4 %fusion.105 = bf16[382,384]{1,0:T(8,128)(2,1)} fusion(f32[382,384]{1,0:T(8,128)S(1)} %get-tuple-element.142, bf16[1,1536,384]{2,1,0:T(8,128)(2,1)} %param.32, bf16[1,384,1536]{2,1,0:T(8,128)(2,1)S(1)} %copy-done, f32[1536]{0:T(1024)S(1)} %convert_reduce_fusion.21, f32[384]{0:T(512)S(1)} %convert_reduce_fusion.22, f32[384]{0:T(512)S(1)} %convert_reduce_fusion.23, ...), kind=kOutput, calls=%fused_computation.227 | convolution fusion | flops 941150208 | bytes 3253232 | tf_op jit(solution)/shard_map/dot_general | solution.py:32
  83.3 2.5 fusion.107
  90.6 2.7 fusion.642
  93.3 2.6 convolution_convert_fusion.19
  97.8 5.5 fusion.18
  103.4 3.1 convert_reduce_fusion.2
  106.5 2.5 fusion.121
  114.2 2.5 fusion.109
  122.3 2.6 convolution_convert_fusion.17
  127.5 9.0 %fusion.633 = (bf16[382,384]{1,0:T(8,128)(2,1)}, f32[382,384]{1,0:T(8,128)}) fusion(f32[382,384]{1,0:T(8,128)} %copy-done.111, f32[384]{0:T(512)S(1)} %copy-done.231, bf16[1,1536,384]{2,1,0:T(8,128)(2,1)} %param.32, bf16[1,384,1536]{2,1,0:T(8,128)(2,1)S(1)} %copy-done, f32[1536]{0:T(1024)S(1)} %copy-done.221, f32[382]{0:T(512)S(1)} %add_rsqrt_fusion.2, ...), kind=kOutput, calls=%fused_computation.799 | convolution fusion | flops 941150208 | bytes 3839984 | tf_op jit(solution)/shard_map/dot_general | solution.py:32
  138.8 3.0 multiply_reduce_fusion.8
  155.3 2.5 convolution_convert_fusion.18
  177.9 3.1 fusion.605
  228.9 2.5 fusion.110
  236.8 2.5 convolution_convert_fusion.14
  241.9 3.2 fusion.658
  245.1 2.6 convolution_convert_fusion.16
  249.6 6.5 %fusion.22 = (f32[382,1536]{1,0:T(8,128)S(1)}, f32[382,1536]{1,0:T(8,128)S(1)}) fusion(f32[1536]{0:T(1024)} %copy-done.219, bf16[1,384,1536]{2,1,0:T(8,128)(2,1)S(1)} %copy-done, f32[382,384]{1,0:T(8,128)S(1)} %get-tuple-element.182, f32[382]{0:T(512)S(1)} %fusion.374, f32[382]{0:T(512)S(1)} %broadcast_multiply_fusion.4, f32[384]{0:T(512)S(1)} %copy-done.149, ...), kind=kOutput, calls=%fused_computation.40 | convolution fusion | flops 488324352 | bytes 6472688 | tf_op jit(solution)/shard_map/dot_general | solution.py:32
  256.2 6.9 %fusion.23 = (f32[382,1536]{1,0:T(8,128)}, f32[382,1536]{1,0:T(8,128)}) fusion(f32[1536]{0:T(1024)S(1)} %copy-done.222, bf16[1,384,1536]{2,1,0:T(8,128)(2,1)S(1)} %copy-done, f32[382,384]{1,0:T(8,128)S(1)} %get-tuple-element.172, f32[382]{0:T(512)S(1)} %copy-done.182, f32[382]{0:T(512)S(1)} %broadcast_multiply_fusion.2, f32[384]{0:T(512)S(1)} %copy-done.149, ...), kind=kOutput, calls=%fused_computation.41 | convolution fusion | flops 488324352 | bytes 6472688 | tf_op jit(solution)/shard_map/dot_general | solution.py:32
  285.1 2.5 convolution_convert_fusion.15
  292.3 2.5 convolution_add_fusion.3
  311.8 3.3 fusion.604
  338.3 2.6 convolution_convert_fusion.13
  354.1 4.2 fusion.12
  369.0 2.8 fusion.114
  379.5 2.6 convolution_convert_fusion.12
  391.3 2.6 fusion.606
  394.8 8.3 %fusion.267 = bf16[382,384]{1,0:T(8,128)(2,1)S(1)} fusion(f32[382,384]{1,0:T(8,128)S(1)} %copy-done.38, f32[382]{0:T(512)S(1)} %copy-done.237, f32[382,384]{1,0:T(8,128)} %copy-done.109, bf16[1,1536,384]{2,1,0:T(8,128)(2,1)} %param.32, bf16[1,384,1536]{2,1,0:T(8,128)(2,1)S(1)} %copy-done, f32[1536]{0:T(1024)S(1)} %copy-done.223, ...), kind=kOutput, calls=%fused_computation.482 | convolution fusion | flops 943497216 | bytes 5024193 | tf_op jit(solution)/shard_map/dot_general | solution.py:32
  404.3 79.9 %all-reduce.2 = (f32[1,384]{1,0:T(1,128)}, f32[1,384]{1,0:T(1,128)}, f32[1,384]{1,0:T(1,128)}, f32[1,384]{1,0:T(1,128)}, f32[1,384]{1,0:T(1,128)}, /*index=5*/f3...) all-reduce(f32[1,384]{1,0:T(1,128)S(1)} %broadcast_in_dim.77, ...), channel_id=1, replica_groups=mesh['section'=2,'dp'=16] {'dp'}, use_global_device_ids=true, to_apply=%region_69.70 | all-reduce | flops 4608 | bytes 36864 | tf_op jit(solution)/shard_map/psum | solution.py:356
  485.0 109.0 %all-reduce.6.cloned.1.call-done = (f32[1,384,1152]{2,1,0:T(8,128)}, f32[1,384,384]{2,1,0:T(8,128)}, f32[1,384,1536]{2,1,0:T(8,128)}, f32[1,1536,384]{2,1,0:T(8,128)}) async-done(((f32[1,384,1152]{2,1,0:T(8,128)}, f32[1,384,384]{2,1,0:T(8,128)}, f32[1,384,1536]{2,1,0:T(8,128)}, f32[1,1536,384]{2,1,0:T(8,128)}), (f32[1,384,1152]{2,1,0:T(8,128)}, f32[1,384,384]{2,1,0:T(8,128)}, f32[1,384,1536]{2,1,0:T(8,128)}, ...) | async-done | bytes 7077904 | tf_op jit(solution)/shard_map/psum | solution.py:356
  594.0 2.9 copy.456
  (846 shorter events, 291.1 us)
Async XLA Ops:
  7.2 33.0 %copy-start = (bf16[1,384,1536]{2,1,0:T(8,128)(2,1)S(1)}, bf16[1,384,1536]{2,1,0:T(8,128)(2,1)}, u32[]{:S(2)}) copy-start(bf16[1,384,1536]{2,1,0:T(8,128)(2,1)} %param.30) | copy-start | bytes 3538948
  7.2 586.8 %all-reduce.6.cloned.1.call-start = ((), (), s32[]{:S(2)}) async-start(), calls=%async_computation | async-start | bytes 14155776 | tf_op jit(solution)/shard_map/psum | solution.py:356
  10.1 45.0 %copy-start.117 = (f32[384]{0:T(512)}, f32[384]{0:T(512)S(1)}, u32[]{:S(2)}) copy-start(f32[384]{0:T(512)S(1)} %convert_reduce_fusion.29) | copy-start | bytes 4612
  10.8 44.3 %copy-start.135 = (f32[384]{0:T(512)}, f32[384]{0:T(512)S(1)}, u32[]{:S(2)}) copy-start(f32[384]{0:T(512)S(1)} %convert_reduce_fusion.28) | copy-start | bytes 4612
  25.5 14.7 %copy-start.132 = (f32[384]{0:T(512)}, f32[384]{0:T(512)S(1)}, u32[]{:S(2)}) copy-start(f32[384]{0:T(512)S(1)} %convert_reduce_fusion.24) | copy-start | bytes 4612
  25.6 14.6 %copy-start.146 = (f32[384]{0:T(512)}, f32[384]{0:T(512)S(1)}, u32[]{:S(2)}) copy-start(f32[384]{0:T(512)S(1)} %convert_reduce_fusion.23) | copy-start | bytes 4612
  25.6 12.7 %copy-start.233 = (f32[384]{0:T(512)}, f32[384]{0:T(512)S(1)}, u32[]{:S(2)}) copy-start(f32[384]{0:T(512)S(1)} %convert_reduce_fusion.25) | copy-start | bytes 4612
  25.7 14.5 %copy-start.230 = (f32[384]{0:T(512)}, f32[384]{0:T(512)S(1)}, u32[]{:S(2)}) copy-start(f32[384]{0:T(512)S(1)} %convert_reduce_fusion.22) | copy-start | bytes 4612
  25.7 14.5 %copy-start.219 = (f32[1536]{0:T(1024)}, f32[1536]{0:T(1024)S(1)}, u32[]{:S(2)}) copy-start(f32[1536]{0:T(1024)S(1)} %convert_reduce_fusion.21) | copy-start | bytes 18436
  48.6 5.0 collective-permute-start
  67.6 12.5 %copy-start.114 = (bf16[185,384]{1,0:T(8,128)(2,1)S(1)}, bf16[185,384]{1,0:T(8,128)(2,1)}, u32[]{:S(2)}) copy-start(bf16[185,384]{1,0:T(8,128)(2,1)} %slice.325) | copy-start | bytes 426244
  136.4 8.2 %collective-permute-start.2 = (bf16[382,384]{1,0:T(8,128)(2,1)}, bf16[382,384]{1,0:T(8,128)(2,1)S(1)}, u32[]{:S(2)}, u32[]{:S(2)}) collective-permute-start(bf16[382,384]{1,0:T(8,128)(2,1)} %get-tuple-element.147), channel_id=1, source_target_pairs={{0,16},{1,17},{2,18},{3,19},{4,20},{5,21},{6,22},{7,23},{8,24},{9,... | collective-permute-start | bytes 880136 | tf_op jit(solution)/shard_map/ppermute | solution.py:18
  144.6 41.6 %copy-start.19 = (bf16[382,384]{1,0:T(8,128)(2,1)}, bf16[382,384]{1,0:T(8,128)(2,1)S(1)}, u32[]{:S(2)}) copy-start(bf16[382,384]{1,0:T(8,128)(2,1)S(1)} %collective-permute-done.2) | copy-start | bytes 880132
  162.6 15.2 %copy-start.118 = (f32[384]{0:T(512)S(1)}, f32[384]{0:T(512)}, u32[]{:S(2)}) copy-start(f32[384]{0:T(512)} %copy-done.117) | copy-start | bytes 4612
  162.6 15.2 %copy-start.141 = (f32[382]{0:T(512)S(1)}, f32[382]{0:T(512)}, u32[]{:S(2)}) copy-start(f32[382]{0:T(512)} %copy-done.140) | copy-start | bytes 4588
  166.9 14.0 %copy-start.83 = (bf16[185,384]{0,1:T(8,128)(2,1)}, bf16[185,384]{0,1:T(8,128)(2,1)S(1)}, u32[]{:S(2)}) copy-start(bf16[185,384]{0,1:T(8,128)(2,1)S(1)} %copy.154) | copy-start | bytes 426244
  188.0 14.1 %copy-start.66 = (bf16[382,384]{1,0:T(8,128)(2,1)}, bf16[382,384]{1,0:T(8,128)(2,1)S(1)}, u32[]{:S(2)}) copy-start(bf16[382,384]{1,0:T(8,128)(2,1)S(1)} %get-tuple-element.128) | copy-start | bytes 880132
  188.0 11.1 %copy-start.113 = (bf16[185,384]{1,0:T(8,128)(2,1)S(1)}, bf16[185,384]{1,0:T(8,128)(2,1)}, u32[]{:S(2)}) copy-start(bf16[185,384]{1,0:T(8,128)(2,1)} %slice.345) | copy-start | bytes 426244
  194.4 73.5 %collective-permute-start.1 = (bf16[382,384]{1,0:T(8,128)(2,1)}, bf16[382,384]{1,0:T(8,128)(2,1)}, u32[]{:S(2)}, u32[]{:S(2)}) collective-permute-start(bf16[382,384]{1,0:T(8,128)(2,1)} %get-tuple-element.120), channel_id=1, source_target_pairs={{16,0},{17,1},{18,2},{19,3},{20,4},{21,5},{22,6},{23,7},{24,8},{25... | collective-permute-start | bytes 880136 | tf_op jit(solution)/shard_map/ppermute | solution.py:18
  200.3 36.4 %copy-start.95 = (bf16[197,384]{0,1:T(8,128)(2,1)}, bf16[197,384]{0,1:T(8,128)(2,1)S(1)}, u32[]{:S(2)}) copy-start(bf16[197,384]{0,1:T(8,128)(2,1)S(1)} %copy.200) | copy-start | bytes 453892
  207.4 27.8 %copy-start.97 = (bf16[197,384]{0,1:T(8,128)(2,1)}, bf16[197,384]{0,1:T(8,128)(2,1)S(1)}, u32[]{:S(2)}) copy-start(bf16[197,384]{0,1:T(8,128)(2,1)S(1)} %copy.201) | copy-start | bytes 453892
  208.6 11.9 %copy-start.48 = (bf16[5,37,6,64]{3,2,1,0:T(8,128)(2,1)}, bf16[5,37,6,64]{3,2,1,0:T(8,128)(2,1)S(1)}, u32[]{:S(2)}) copy-start(bf16[5,37,6,64]{3,2,1,0:T(8,128)(2,1)S(1)} %reshape.924) | copy-start | bytes 426244
  241.0 15.1 %copy-start.153 = (f32[382]{0:T(512)}, f32[382]{0:T(512)S(1)}, u32[]{:S(2)}) copy-start(f32[382]{0:T(512)S(1)} %broadcast_multiply_fusion.2) | copy-start | bytes 4588
  249.3 23.9 %copy-start.6 = (f32[382,384]{1,0:T(8,128)}, f32[382,384]{1,0:T(8,128)S(1)}, u32[]{:S(2)}) copy-start(f32[382,384]{1,0:T(8,128)S(1)} %get-tuple-element.182) | copy-start | bytes 1760260
  249.3 23.9 %copy-start.155 = (f32[382]{0:T(512)}, f32[382]{0:T(512)S(1)}, u32[]{:S(2)}) copy-start(f32[382]{0:T(512)S(1)} %broadcast_multiply_fusion.4) | copy-start | bytes 4588
  249.6 23.6 %copy-start.184 = (f32[382]{0:T(512)}, f32[382]{0:T(512)S(1)}, u32[]{:S(2)}) copy-start(f32[382]{0:T(512)S(1)} %fusion.374) | copy-start | bytes 4588
  256.1 13.5 %copy-start.39 = (f32[382,1536]{1,0:T(8,128)}, f32[382,1536]{1,0:T(8,128)S(1)}, u32[]{:S(2)}) copy-start(f32[382,1536]{1,0:T(8,128)S(1)} %get-tuple-element.183) | copy-start | bytes 7041028
  256.1 13.5 %copy-start.41 = (f32[382,1536]{1,0:T(8,128)}, f32[382,1536]{1,0:T(8,128)S(1)}, u32[]{:S(2)}) copy-start(f32[382,1536]{1,0:T(8,128)S(1)} %get-tuple-element.184) | copy-start | bytes 7041028
  297.2 14.6 %copy-start.145 = (f32[382]{0:T(512)S(1)}, f32[382]{0:T(512)}, u32[]{:S(2)}) copy-start(f32[382]{0:T(512)} %copy-done.144) | copy-start | bytes 4588
  300.9 17.9 %copy-start.88 = (bf16[185,384]{0,1:T(8,128)(2,1)}, bf16[185,384]{0,1:T(8,128)(2,1)S(1)}, u32[]{:S(2)}) copy-start(bf16[185,384]{0,1:T(8,128)(2,1)S(1)} %copy.190) | copy-start | bytes 426244
  317.3 5.1 collective-permute-start.3
  394.8 89.4 %copy-start.106 = (bf16[5,37,384]{2,1,0:T(8,128)(2,1)S(1)}, bf16[5,37,384]{2,1,0:T(8,128)(2,1)}, u32[]{:S(2)}) copy-start(bf16[5,37,384]{2,1,0:T(8,128)(2,1)} %reshape.943) | copy-start | bytes 426244
  (230 other events, 820.7 us)
Sparse Core Ops, SparseCore 0:
  360.9 232.9 all-reduce.5
where the time goes:
time: 621 us; the launch traced here: 609 us
  matrix products  204 us (33%)
  local copies, waits for them, and re-layouts  158 us (25%)
  waiting for transfers between devices  109 us (18%)
  blocking collectives  79.9 us (13%)
  other arithmetic  32.6 us (5%)
  between operations  17.7 us (3%)
  starting transfers between devices  7.6 us (1%)
    psum x1, waiting for transfers between devices, on_device(): lax.psum((pending[0], pending[1], pending[2], pending[3], pending[4], pen...  109 us
    psum x1, blocking collectives, on_device(): lax.psum((pending[0], pending[1], pending[2], pending[3], pending[4], pen...  79.9 us
    dot_general x18, matrix products, product(): return jnp.dot(left, right, preferred_element_type=jnp.float32)  59.4 us
    dot_general x12, matrix products, attend(): jnp.einsum('chqk,ckhe->cqhe', soft_low, value_heads, preferred_element_ty...  29.9 us
    dot_general x12, matrix products, outer_sum(): jnp.einsum('ti,to->io', left, right, preferred_element_type=jnp.float32)  26.8 us
    dot_general x12, matrix products, back_product(): jnp.einsum('to,io->ti', grad_rows, matrix, preferred_element_type=jnp.flo...  23.2 us
    sub x12, matrix products, attend(): raised = jnp.exp(scores - highest)  22.2 us
    unnamed x515, local copies, waits for them, and re-layouts  18.5 us
  transfers between devices with their start and end apart: 5, of which 1 were waited for; matrix products, arithmetic and copies ran while one was open for 20% of the time, Pallas kernels for 0%

commit v1 on v0

v1 whole, which is shorter than its diff:
```python
import functools

import jax
import jax.numpy as jnp
from jax import lax
from jax.experimental import pallas as pl
from jax.experimental.pallas import tpu as pltpu
from jax.sharding import PartitionSpec as P

HEAD = 64
GT = 197
LT = 37
WIDTH = 384
FF = 1536
SEQ = 208
ROWS = 2 * SEQ
SLOT = 40
LOCALS = 5
VECS = 16
BLOCKS = 12
HALF_ROWS = BLOCKS // 2 * WIDTH
EPSILON = 1e-06
MASKED = -1e30
LN1G, LN1B, QB, VB, PB, LN2G, LN2B, F2B, F1B = range(9)
VMEM_LIMIT = 56 * 1024 * 1024
BF16 = jnp.bfloat16
F32 = jnp.float32
ANY = pl.BlockSpec(memory_space=pl.ANY)
VMEM = pl.BlockSpec(memory_space=pltpu.VMEM)
SMEM = pl.BlockSpec(memory_space=pltpu.SMEM)


def mm(left, right):
    return jnp.dot(left, right, preferred_element_type=F32)


def mm_right_t(left, right):
    return lax.dot_general(left, right, (((1,), (1,)), ((), ())), preferred_element_type=F32)


def mm_left_t(left, right):
    return lax.dot_general(left, right, (((0,), (0,)), ((), ())), preferred_element_type=F32)


def normalise(values_in):
    centred = values_in - jnp.mean(values_in, axis=-1, keepdims=True)
    scale = lax.rsqrt(jnp.mean(centred * centred, axis=-1, keepdims=True) + EPSILON)
    return centred * scale, scale


def normalise_back(unit, scale, grad_rows, gain):
    e = grad_rows * gain
    return scale * (
        e
        - jnp.mean(e, axis=-1, keepdims=True)
        - unit * jnp.mean(e * unit, axis=-1, keepdims=True)
    )


def seq_rows(seq):
    return pl.ds(pl.multiple_of(seq * SEQ, 16), SEQ)


def column(block):
    return slice(block * WIDTH, (block + 1) * WIDTH)


def row_sum(values_in):
    return jnp.sum(values_in, axis=0, keepdims=True)


def pack_kernel(glive, llive, g, l, *refs):
    vecs, (keep, send, rows, tail) = refs[:9], refs[9:]
    core = lax.axis_index("section")
    tail[...] = jnp.zeros_like(tail)
    for i, vec in enumerate(vecs[:8]):
        tail[i : i + 1, :] = vec[...].astype(F32)
    for i in range(FF // WIDTH):
        tail[F1B + i : F1B + i + 1, :] = vecs[8][:, column(i)].astype(F32)
    tail_low = tail[...].astype(BF16)
    rows[...] = jnp.zeros_like(rows)
    for out, half in ((keep, core), (send, 1 - core)):
        live = jnp.where(core == 1, glive[half], 1).astype(F32)
        rows[:GT, :] = g[half].astype(F32) * live
        for j in range(LOCALS):
            live = jnp.where(core == 1, llive[half * LOCALS + j], 1).astype(F32)
            rows[SEQ + j * SLOT : SEQ + j * SLOT + LT, :] = l[half * LOCALS + j].astype(F32) * live
        out[:ROWS, :] = rows[...].astype(BF16)
        out[ROWS:, :] = tail_low


def fill_masks(masks):
    row = lax.broadcasted_iota(jnp.int32, (SEQ, SEQ), 0)
    col = lax.broadcasted_iota(jnp.int32, (SEQ, SEQ), 1)
    masks[0] = jnp.where(col < GT, 0.0, MASKED)
    inside = jnp.zeros((SEQ, SEQ), jnp.bool_)
    for j in range(LOCALS):
        inside = inside | (
            (row >= j * SLOT)
            & (row < (j + 1) * SLOT)
            & (col >= j * SLOT)
            & (col < j * SLOT + LT)
        )
    masks[1] = jnp.where(inside, 0.0, MASKED)


def head_lanes():
    lane = lax.broadcasted_iota(jnp.int32, (SEQ, 2 * HEAD), 1)
    return (lane < HEAD, lane >= HEAD)


def only(mask, values_in):
    return jnp.where(mask, values_in, jnp.zeros_like(values_in))


def attention_forward(x, vec, masks, qkv_w, proj_w, n1, qkv, probs, mixed, middle):
    def body(seq, carry):
        rows = seq_rows(seq)
        x_rows = x[rows, :].astype(F32)
        unit, _ = normalise(x_rows)
        normed = (unit * vec[LN1G : LN1G + 1, :] + vec[LN1B : LN1B + 1, :]).astype(BF16)
        n1[rows, :] = normed
        for part in range(3):
            value = mm(normed, qkv_w[:, column(part)])
            if part == 0:
                value = (value + vec[QB : QB + 1, :]).astype(BF16) * BF16(HEAD**-0.5)
            if part == 2:
                value = value + vec[VB : VB + 1, :]
            qkv[rows, column(part)] = value.astype(BF16)
        lanes = head_lanes()
        mask = masks[seq]
        for pair in range(3):
            q = qkv[rows, pair * 128 : pair * 128 + 128]
            k = qkv[rows, WIDTH + pair * 128 : WIDTH + pair * 128 + 128]
            v = qkv[rows, 2 * WIDTH + pair * 128 : 2 * WIDTH + pair * 128 + 128]
            total = None
            for a in range(2):
                s = mm_right_t(only(lanes[a], q), k) + mask
                e = jnp.exp(s - jnp.max(s, axis=-1, keepdims=True))
                p = (e * (1.0 / jnp.sum(e, axis=-1, keepdims=True))).astype(BF16)
                probs[seq * 6 + pair * 2 + a] = p
                part = mm(p, only(lanes[a], v))
                total = part if total is None else total + part
            mixed[rows, pair * 128 : pair * 128 + 128] = total.astype(BF16)
        middle[rows, :] = x_rows + (mm(mixed[rows, :], proj_w[...]) + vec[PB : PB + 1, :])
        return carry

    lax.fori_loop(0, 2, body, 0)


def mlp_forward(vec, fc1_w, fc2_w, middle, n2, slope, active, result):
    def body(seq, carry):
        rows = seq_rows(seq)
        unit, _ = normalise(middle[rows, :])
        normed = (unit * vec[LN2G : LN2G + 1, :] + vec[LN2B : LN2B + 1, :]).astype(BF16)
        n2[rows, :] = normed
        for part in range(FF // WIDTH):
            hidden = mm(normed, fc1_w[:, column(part)]) + vec[F1B + part : F1B + part + 1, :]
            cdf = 0.5 + 0.5 * lax.erf(hidden * (0.5**0.5))
            active[rows, column(part)] = (hidden * cdf).astype(BF16)
            density = jnp.exp(hidden * hidden * -0.5) * 0.3989422804014327
            slope[rows, column(part)] = (cdf + hidden * density).astype(BF16)
        y = middle[rows, :] + (mm(active[rows, :], fc2_w[...]) + vec[F2B : F2B + 1, :])
        result[rows, :] = y.astype(BF16)
        return carry

    lax.fori_loop(0, 2, body, 0)


def mlp_backward(vec, fc1_w, fc2_w, middle, n2, slope, active, dy, dh, dmid, da, sums, emit):
    def body(seq, carry):
        rows = seq_rows(seq)
        dy_rows = dy[rows, :]
        for part in range(FF // WIDTH):
            dactive = mm_right_t(dy_rows, fc2_w[column(part), :])
            low = (slope[rows, column(part)].astype(F32) * dactive).astype(BF16)
            dh[rows, column(part)] = low
            sums[F1B + part : F1B + part + 1, :] += row_sum(low.astype(F32))
        dn2 = mm_right_t(dh[rows, :], fc1_w[...])
        unit, scale = normalise(middle[rows, :])
        dy_wide = dy_rows.astype(F32)
        grad = dy_wide + normalise_back(unit, scale, dn2, vec[LN2G : LN2G + 1, :])
        dmid[rows, :] = grad
        low = grad.astype(BF16)
        da[rows, :] = low
        sums[LN2G : LN2G + 1, :] += row_sum(dn2 * unit)
        sums[LN2B : LN2B + 1, :] += row_sum(dn2)
        sums[F2B : F2B + 1, :] += row_sum(dy_wide)
        sums[PB : PB + 1, :] += row_sum(low.astype(F32))
        return carry

    lax.fori_loop(0, 2, body, 0)
    for part in range(FF // WIDTH):
        emit(part, mm_left_t(active[:, column(part)], dy[:ROWS, :]))
    for part in range(FF // WIDTH):
        emit(4 + part, mm_left_t(n2[...], dh[:, column(part)]))


def attention_backward(
    x, vec, qkv_w, proj_w, n1, qkv, probs, mixed, dmid, da, dt, sums, emit, result
):
    def body(seq, carry):
        rows = seq_rows(seq)
        dmixed = mm_right_t(da[rows, :], proj_w[...]).astype(BF16)
        lanes = head_lanes()
        for pair in range(3):
            q = qkv[rows, pair * 128 : pair * 128 + 128]
            k = qkv[rows, WIDTH + pair * 128 : WIDTH + pair * 128 + 128]
            v = qkv[rows, 2 * WIDTH + pair * 128 : 2 * WIDTH + pair * 128 + 128]
            dm = dmixed[:, pair * 128 : pair * 128 + 128]
            dq = dk = dv = None
            for a in range(2):
                dm_a = only(lanes[a], dm)
                p = probs[seq * 6 + pair * 2 + a]
                dp = mm_right_t(dm_a, v)
                p_wide = p.astype(F32)
                ds = p_wide * (dp - jnp.sum(dp * p_wide, axis=-1, keepdims=True))
                ds = ds.astype(BF16)
                parts = (
                    mm(ds, only(lanes[a], k)),
                    mm_left_t(ds, only(lanes[a], q)),
                    mm_left_t(p, dm_a),
                )
                if a == 0:
                    dq, dk, dv = parts
                else:
                    dq, dk, dv = dq + parts[0], dk + parts[1], dv + parts[2]
            dq = (dq * HEAD**-0.5).astype(BF16)
            dv = dv.astype(BF16)
            here = slice(pair * 128, pair * 128 + 128)
            dt[rows, pair * 128 : pair * 128 + 128] = dq
            dt[rows, WIDTH + pair * 128 : WIDTH + pair * 128 + 128] = dk.astype(BF16)
            dt[rows, 2 * WIDTH + pair * 128 : 2 * WIDTH + pair * 128 + 128] = dv
            sums[QB : QB + 1, here] += row_sum(dq.astype(F32))
            sums[VB : VB + 1, here] += row_sum(dv.astype(F32))
        dn1 = mm_right_t(dt[rows, :], qkv_w[...])
        unit, scale = normalise(x[rows, :].astype(F32))
        grad = dmid[rows, :] + normalise_back(unit, scale, dn1, vec[LN1G : LN1G + 1, :])
        result[rows, :] = grad.astype(BF16)
        sums[LN1G : LN1G + 1, :] += row_sum(dn1 * unit)
        sums[LN1B : LN1B + 1, :] += row_sum(dn1)
        return carry

    lax.fori_loop(0, 2, body, 0)
    emit(8, mm_left_t(mixed[...], da[...]))
    for part in range(3):
        emit(9 + part, mm_left_t(n1[...], dt[:, column(part)]))


def make_emit(grads, core):
    def emit(block, value):
        half = block % 2
        place = block // 2
        grads[half ^ core, place * WIDTH : (place + 1) * WIDTH, :] = value.astype(BF16)

    return emit


def start_all(copies):
    for copy in copies:
        copy.start()


def wait_all(copies):
    for copy in copies:
        copy.wait()


def forward_kernel(*refs):
    (
        keep, recv, qkv_own, proj_own, fc1_own, fc2_own,
        qkv_got, proj_got, fc1_got, fc2_got,
        n1_out, qkv_out, probs_out, mixed_out, middle_out, n2_out, slope_out, active_out,
        result_out, dx_out, keep_out, send_out,
        pack, qkv_w, proj_w, fc1_w, fc2_w, vec, masks, between,
        n1, qkv, probs, mixed, middle, n2, slope, active,
        result, dh, dmid, da, dt, dx, sums, grads, in_sem, out_sem,
    ) = refs
    core = lax.axis_index("section")
    other = 1 - core
    own = (keep, qkv_own, proj_own, fc1_own, fc2_own)
    got = (recv, qkv_got, proj_got, fc1_got, fc2_got)
    held = (pack, qkv_w, proj_w, fc1_w, fc2_w)

    def loads(sources, layer):
        return [
            pltpu.make_async_copy(source, place.at[layer], in_sem.at[layer, i])
            for i, (source, place) in enumerate(zip(sources, held))
        ]

    start_all(loads(own, core))
    start_all(loads(got, other))
    fill_masks(masks)
    sums[...] = jnp.zeros_like(sums)
    wait_all(loads(own, 0))
    for layer in range(2):
        if layer == 1:
            wait_all(loads(own, 1)[:1])
        vec[layer] = pack[layer, ROWS:, :].astype(F32)
    saves = []
    for layer in range(2):
        if layer == 1:
            wait_all(loads(own, 1)[1:])
        x = pack.at[0] if layer == 0 else between
        attention_forward(
            x, vec.at[layer], masks, qkv_w.at[layer], proj_w.at[layer],
            n1.at[layer], qkv.at[layer], probs.at[layer], mixed.at[layer], middle.at[layer],
        )
        mlp_forward(
            vec.at[layer], fc1_w.at[layer], fc2_w.at[layer], middle.at[layer], n2.at[layer],
            slope.at[layer], active.at[layer], between if layer == 0 else result,
        )
        if layer == 0:
            pairs = (
                (n1, n1_out), (qkv, qkv_out), (probs, probs_out), (mixed, mixed_out),
                (middle, middle_out), (n2, n2_out), (slope, slope_out), (active, active_out),
            )
            saves = [
                pltpu.make_async_copy(source.at[0], place, out_sem.at[i])
                for i, (source, place) in enumerate(pairs)
            ]
            start_all(saves)
    result_copy = pltpu.make_async_copy(result, result_out, out_sem.at[8])
    result_copy.start()
    emit = make_emit(grads, core)
    mlp_backward(
        vec.at[1], fc1_w.at[1], fc2_w.at[1], middle.at[1], n2.at[1], slope.at[1], active.at[1],
        pack.at[1], dh, dmid, da, sums, emit,
    )
    attention_backward(
        between, vec.at[1], qkv_w.at[1], proj_w.at[1], n1.at[1], qkv.at[1], probs.at[1],
        mixed.at[1], dmid, da, dt, sums, emit, dx,
    )
    for place in range(2):
        grads[place, HALF_ROWS:, :] = sums[...].astype(BF16)
    last = [
        pltpu.make_async_copy(dx, dx_out, out_sem.at[9]),
        pltpu.make_async_copy(grads.at[0], keep_out, out_sem.at[10]),
        pltpu.make_async_copy(grads.at[1], send_out, out_sem.at[11]),
    ]
    start_all(last)
    wait_all(saves + [result_copy] + last)


def backward_kernel(*refs):
    (
        keep, recv, qkv_own, proj_own, fc1_own, fc2_own,
        qkv_got, proj_got, fc1_got, fc2_got,
        n1_in, qkv_in, probs_in, mixed_in, middle_in, n2_in, slope_in, active_in, dx_in, out_in,
        rows_keep, rows_send, keep_out, send_out,
        pack, qkv_w, proj_w, fc1_w, fc2_w, vec,
        n1, qkv, probs, mixed, middle, n2, slope, active, dy,
        dh, dmid, da, dt, dx, sums, grads, in_sem, out_sem,
    ) = refs
    core = lax.axis_index("section")
    own = (keep, qkv_own, proj_own, fc1_own, fc2_own)
    got = (recv, qkv_got, proj_got, fc1_got, fc2_got)
    held = (pack, qkv_w, proj_w, fc1_w, fc2_w)

    def loads(sources):
        return [
            pltpu.make_async_copy(source, place, in_sem.at[i])
            for i, (source, place) in enumerate(zip(sources, held))
        ]

    saved = (
        (middle_in, middle), (slope_in, slope), (active_in, active), (n2_in, n2), (dx_in, dy),
        (n1_in, n1), (qkv_in, qkv), (probs_in, probs), (mixed_in, mixed),
    )
    saved = [
        pltpu.make_async_copy(source, place, in_sem.at[5 + i])
        for i, (source, place) in enumerate(saved)
    ]

    @pl.when(core == 0)
    def _():
        start_all(loads(own))
        pltpu.make_async_copy(out_in, rows_send, out_sem.at[0]).start()

    @pl.when(core == 1)
    def _():
        start_all(loads(got))
        pltpu.make_async_copy(out_in, rows_keep, out_sem.at[0]).start()

    start_all(saved)
    sums[...] = jnp.zeros_like(sums)
    wait_all(loads(own))
    wait_all(saved[:5])
    vec[...] = pack[ROWS:, :].astype(F32)
    emit = make_emit(grads, core)
    mlp_backward(
        vec, fc1_w, fc2_w, middle, n2, slope, active, dy, dh, dmid, da, sums, emit
    )
    wait_all(saved[5:])
    attention_backward(
        pack, vec, qkv_w, proj_w, n1, qkv, probs, mixed, dmid, da, dt, sums, emit, dx
    )
    for place in range(2):
        grads[place, HALF_ROWS:, :] = sums[...].astype(BF16)
    last = [
        pltpu.make_async_copy(grads.at[0], keep_out, out_sem.at[2]),
        pltpu.make_async_copy(grads.at[1], send_out, out_sem.at[3]),
    ]
    start_all(last)

    @pl.when(core == 0)
    def _():
        pltpu.make_async_copy(dx, rows_keep, out_sem.at[1]).start()

    @pl.when(core == 1)
    def _():
        pltpu.make_async_copy(dx, rows_send, out_sem.at[1]).start()

    wait_all(last)
    pltpu.make_async_copy(dx, rows_keep, out_sem.at[1]).wait()
    pltpu.make_async_copy(out_in, rows_send, out_sem.at[0]).wait()


def rows_kernel(glive, llive, keep, recv, g_out, l_out, wide):
    core = lax.axis_index("section")
    for source, half in ((keep, core), (recv, 1 - core)):
        wide[...] = source[...].astype(F32)
        live = jnp.where(core == 1, glive[half], 1).astype(F32)
        g_out[half] = (wide[:GT, :] * live).astype(BF16)
        for j in range(LOCALS):
            live = jnp.where(core == 1, llive[half * LOCALS + j], 1).astype(F32)
            piece = wide[SEQ + j * SLOT : SEQ + j * SLOT + LT, :]
            l_out[half * LOCALS + j] = (piece * live).astype(BF16)


def grads_kernel(*refs):
    (
        half_a, half_b, got_a, got_b, sums_a, sums_b,
        ln1g, ln1b, qkv, qb, vb, proj, pb, ln2g, ln2b, fc1, fc1b, fc2, fc2b,
        halves, sums, sem,
    ) = refs
    core = lax.axis_index("section")

    def copies(own, got, vectors, first):
        return [
            pltpu.make_async_copy(own, halves.at[first], sem.at[0]),
            pltpu.make_async_copy(got, halves.at[1 - first], sem.at[1]),
            pltpu.make_async_copy(vectors, sums, sem.at[2]),
        ]

    @pl.when(core == 0)
    def _():
        start_all(copies(half_a, got_a, sums_a, 0))

    @pl.when(core == 1)
    def _():
        start_all(copies(half_b, got_b, sums_b, 1))

    wait_all(copies(half_a, got_a, sums_a, 0))

    def block(index):
        place = index // 2
        return halves[index % 2, place * WIDTH : (place + 1) * WIDTH, :].astype(F32)

    for part in range(4):
        fc2[0, column(part), :] = block(part)
        fc1[0, :, column(part)] = block(4 + part)
    proj[0] = block(8)
    for part in range(3):
        qkv[0, :, column(part)] = block(9 + part)
    for out, row in (
        (ln1g, LN1G), (ln1b, LN1B), (qb, QB), (vb, VB), (pb, PB), (ln2g, LN2G), (ln2b, LN2B),
        (fc2b, F2B),
    ):
        out[...] = sums[row : row + 1, :]
    for part in range(4):
        fc1b[:, column(part)] = sums[F1B + part : F1B + part + 1, :]


def shape(*dims, dtype=BF16):
    return jax.ShapeDtypeStruct(dims, dtype)


def call(kernel, outs, in_specs, out_specs, scratch=(), flops=0, moved=0):
    return pl.pallas_call(
        kernel,
        out_shape=outs,
        in_specs=in_specs,
        out_specs=out_specs,
        scratch_shapes=list(scratch),
        compiler_params=pltpu.CompilerParams(vmem_limit_bytes=VMEM_LIMIT),
        cost_estimate=pl.CostEstimate(flops=flops, bytes_accessed=moved, transcendentals=0),
    )


CHUNK = 48


def add_rows(out, start_out, left, right, start, count):
    def step(i, carry):
        here = pl.ds(pl.multiple_of(start + i * CHUNK, 16), CHUNK)
        there = pl.ds(pl.multiple_of(start_out + i * CHUNK, 16), CHUNK)
        out[there, :] = (left[here, :].astype(F32) + right[here, :].astype(F32)).astype(BF16)
        return carry

    lax.fori_loop(0, count // CHUNK, step, 0, unroll=2)


def add_tail(outs, start_out, left, right, start):
    here = slice(start, start + VECS)
    tail = (left[here, :].astype(F32) + right[here, :].astype(F32)).astype(BF16)
    for out in outs:
        out[start_out : start_out + VECS, :] = tail


def position():
    dp = lax.axis_index("dp")
    return dp % 2, dp // 2 % 2, dp // 4


def bit_of(step):
    x, y, _ = position()
    core = lax.axis_index("section")
    return jnp.where(core == step, x, y)


def halve_kernel(step, count, keep, recv, keep_out, send_out):
    bit = bit_of(step)
    half = count // 2
    add_rows(send_out, 0, keep, recv, (1 - bit) * half, half)
    add_rows(keep_out, 0, keep, recv, bit * half, half)
    add_tail((keep_out, send_out), half, keep, recv, count)


def quarter_kernel(count, keep, recv, keep_out, *send_outs):
    _, _, z = position()
    part = count // 4
    for k, out in enumerate((keep_out,) + send_outs):
        add_rows(out, 0, keep, recv, lax.rem(z + k, 4) * part, part)
    add_tail((keep_out,) + send_outs, part, keep, recv, count)


def total_kernel(count, keep, a, b, c, total_out, sums_out, tails):
    _, _, z = position()

    def step(i, carry):
        here = pl.ds(pl.multiple_of(i * CHUNK, 16), CHUNK)
        total = keep[here, :].astype(F32) + a[here, :].astype(F32)
        total = total + b[here, :].astype(F32) + c[here, :].astype(F32)
        total_out[here, :] = total.astype(BF16)
        return carry

    lax.fori_loop(0, count // CHUNK, step, 0)
    for k, ref in enumerate((keep, a, b, c)):
        tails[lax.rem(z + 4 - k, 4)] = ref[count : count + VECS, :].astype(F32)
    sums_out[...] = tails[0] + tails[1] + tails[2] + tails[3]


def join_kernel(which, count, *refs):
    parts, out = refs[:-1], refs[-1]
    if which == "z":
        _, _, first = position()
    else:
        first = bit_of(which)
    size = len(parts)
    for k, ref in enumerate(parts):
        place = lax.rem(first + size - k, size) * count
        out[pl.ds(pl.multiple_of(place, 16), count), :] = ref[...]


def flat_pairs(move):
    pairs = []
    for core in range(2):
        for dp in range(16):
            x, y, z = dp % 2, dp // 2 % 2, dp // 4
            to_core, to_x, to_y, to_z = move(core, x, y, z)
            pairs.append((core * 16 + dp, to_core * 16 + to_z * 4 + to_y * 2 + to_x))
    return pairs


def exchange(values_in, step):
    def move(core, x, y, z):
        return (core, 1 - x, y, z) if core == step else (core, x, 1 - y, z)

    return lax.ppermute(values_in, ("section", "dp"), flat_pairs(move))


def forward_z(values_in, by):
    return lax.ppermute(
        values_in,
        ("section", "dp"),
        flat_pairs(lambda core, x, y, z: (core, x, y, (z + by) % 4)),
    )


def reduce_everywhere(keep, recv, count):
    tail = VECS
    for step in range(2):
        half = count // 2
        keep, send = call(
            functools.partial(halve_kernel, step, count),
            [shape(half + tail, WIDTH)] * 2,
            [VMEM] * 2,
            [VMEM] * 2,
            moved=6 * count * WIDTH,
        )(keep, recv)
        recv = exchange(send, step)
        count = half
    part = count // 4
    keep, *sends = call(
        functools.partial(quarter_kernel, count),
        [shape(part + tail, WIDTH)] * 4,
        [VMEM] * 2,
        [VMEM] * 4,
        moved=6 * count * WIDTH,
    )(keep, recv)
    recvs = [forward_z(send, k + 1) for k, send in enumerate(sends)]
    total, sums = call(
        functools.partial(total_kernel, part),
        [shape(part, WIDTH), shape(tail, WIDTH, dtype=F32)],
        [VMEM] * 4,
        [VMEM] * 2,
        [pltpu.VMEM((4, tail, WIDTH), F32)],
        moved=6 * count * WIDTH,
    )(keep, *recvs)
    parts = [total] + [forward_z(total, k) for k in range(1, 4)]
    whole = None
    for which in ("z", 1, 0):
        rows = parts[0].shape[0]
        whole = call(
            functools.partial(join_kernel, which, rows),
            shape(rows * len(parts), WIDTH),
            [VMEM] * len(parts),
            VMEM,
            moved=4 * rows * len(parts) * WIDTH,
        )(*parts)
        if which != "z" and which == 0:
            break
        parts = [whole, exchange(whole, 1 if which == "z" else 0)]
    return whole, sums


def plain_reduce(keep, recv, count):
    total = lax.psum(keep.astype(F32) + recv.astype(F32), "dp")
    return total[:count].astype(BF16), total[count:]


def swap(values_in):
    return lax.ppermute(values_in, "section", [(0, 1), (1, 0)])


def on_device(dp_size, global_ends, local_ends, global_live, local_live, *weights):
    (
        ln1_gain, ln1_bias, qkv_weight, query_bias, value_bias, proj_weight, proj_bias,
        ln2_gain, ln2_bias, fc1_weight, fc1_bias, fc2_weight, fc2_bias,
    ) = weights
    matrices = tuple(w[0] for w in (qkv_weight, proj_weight, fc1_weight, fc2_weight))
    got = tuple(swap(w) for w in matrices)
    vectors = (
        ln1_gain, ln1_bias, query_bias, value_bias, proj_bias, ln2_gain, ln2_bias, fc2_bias,
        fc1_bias,
    )
    keep, send = call(
        pack_kernel,
        [shape(ROWS + VECS, WIDTH)] * 2,
        [SMEM] * 2 + [VMEM] * 11,
        [VMEM] * 2,
        [pltpu.VMEM((ROWS, WIDTH), F32), pltpu.VMEM((VECS, WIDTH), F32)],
        moved=2000000,
    )(global_live, local_live, global_ends[0], local_ends[0], *vectors)
    recv = swap(send)
    grad_rows = HALF_ROWS + VECS
    saved_shapes = [
        shape(ROWS, WIDTH),
        shape(ROWS, 3 * WIDTH),
        shape(12, SEQ, SEQ),
        shape(ROWS, WIDTH),
        shape(ROWS, WIDTH, dtype=F32),
        shape(ROWS, WIDTH),
        shape(ROWS, FF),
        shape(ROWS, FF),
    ]
    weight_shapes = [(WIDTH, 3 * WIDTH), (WIDTH, WIDTH), (WIDTH, FF), (FF, WIDTH)]
    work = [
        pltpu.VMEM((ROWS, FF), BF16),
        pltpu.VMEM((ROWS, WIDTH), F32),
        pltpu.VMEM((ROWS, WIDTH), BF16),
        pltpu.VMEM((ROWS, 3 * WIDTH), BF16),
        pltpu.VMEM((ROWS, WIDTH), BF16),
        pltpu.VMEM((VECS, WIDTH), F32),
        pltpu.VMEM((2, grad_rows, WIDTH), BF16),
    ]
    *saved, result, dx, keep_b, send_b = call(
        forward_kernel,
        saved_shapes + [shape(ROWS, WIDTH)] * 2 + [shape(grad_rows, WIDTH)] * 2,
        [ANY] * 10,
        [ANY] * 12,
        [pltpu.VMEM((2, ROWS + VECS, WIDTH), BF16)]
        + [pltpu.VMEM((2,) + dims, BF16) for dims in weight_shapes]
        + [
            pltpu.VMEM((2, VECS, WIDTH), F32),
            pltpu.VMEM((2, SEQ, SEQ), F32),
            pltpu.VMEM((ROWS, WIDTH), BF16),
        ]
        + [pltpu.VMEM((2,) + s.shape, s.dtype) for s in saved_shapes]
        + [pltpu.VMEM((ROWS, WIDTH), BF16)]
        + work
        + [pltpu.SemaphoreType.DMA((2, 5)), pltpu.SemaphoreType.DMA((12,))],
        flops=6000000000,
        moved=20000000,
    )(keep, recv, *matrices, *got)
    recv_b = swap(send_b)
    rows_keep, rows_send, keep_a, send_a = call(
        backward_kernel,
        [shape(ROWS, WIDTH)] * 2 + [shape(grad_rows, WIDTH)] * 2,
        [ANY] * 20,
        [ANY] * 4,
        [pltpu.VMEM((ROWS + VECS, WIDTH), BF16)]
        + [pltpu.VMEM(dims, BF16) for dims in weight_shapes]
        + [pltpu.VMEM((VECS, WIDTH), F32)]
        + [pltpu.VMEM(s.shape, s.dtype) for s in saved_shapes]
        + [pltpu.VMEM((ROWS, WIDTH), BF16)]
        + work
        + [pltpu.SemaphoreType.DMA((14,)), pltpu.SemaphoreType.DMA((4,))],
        flops=3000000000,
        moved=15000000,
    )(keep, recv, *matrices, *got, *saved, dx, result)
    recv_a = swap(send_a)
    rows_recv = swap(rows_send)
    reduce = reduce_everywhere if dp_size == 16 else plain_reduce
    half_b, sums_b = reduce(keep_b, recv_b, HALF_ROWS)
    got_b = lax.ppermute(half_b, "section", [(0, 1)])
    half_a, sums_a = reduce(keep_a, recv_a, HALF_ROWS)
    got_a = lax.ppermute(half_a, "section", [(1, 0)])
    global_out, local_out = call(
        rows_kernel,
        [shape(*global_ends.shape[1:]), shape(*local_ends.shape[1:])],
        [SMEM] * 2 + [VMEM] * 2,
        [VMEM] * 2,
        [pltpu.VMEM((ROWS, WIDTH), F32)],
        moved=2000000,
    )(global_live, local_live, rows_keep, rows_recv)
    gradients = call(
        grads_kernel,
        [shape(*w.shape, dtype=F32) for w in weights],
        [ANY] * 6,
        [VMEM] * 13,
        [
            pltpu.VMEM((2, HALF_ROWS, WIDTH), BF16),
            pltpu.VMEM((VECS, WIDTH), F32),
            pltpu.SemaphoreType.DMA((3,)),
        ],
        moved=12000000,
    )(half_a, half_b, got_a, got_b, sums_a, sums_b)
    return (global_out[None], local_out[None]) + tuple(gradients)


def solution(mesh):
    matrix, vector = P("section", None, None), P("section", None)
    weights = (
        vector, vector, matrix, vector, vector, matrix, vector,
        vector, vector, matrix, vector, matrix, vector,
    )
    rows = P("section", "dp", None, None)
    return jax.shard_map(
        functools.partial(on_device, mesh.shape["dp"]),
        mesh=mesh,
        in_specs=(rows, rows, P("dp"), P("dp")) + weights,
        out_specs=(rows, rows) + weights,
        check_vma=False,
    )
```

time: 621 us -> 196 us (0.32); the launches traced: 609 us -> 195 us
  matrix products: 204 us -> 0 us
  local copies, waits for them, and re-layouts: 158 us -> 21.1 us
  Pallas kernels: 0 us -> 86.2 us
  blocking collectives: 79.9 us -> 0 us
  waiting for transfers between devices: 109 us -> 42.6 us
  starting transfers between devices: 7.6 us -> 44 us
  other arithmetic: 32.6 us -> 0 us
  between operations: 17.7 us -> 1 us
    dot_general x81 -> x0, matrix products: 182 us -> none  [the longest x18 59.4 us: product(): return jnp.dot(left, right, preferred_element_type=jnp.float32)]
    psum x1 -> x0, waiting for transfers between devices: 109 us -> none  [on_device(): lax.psum((pending[0], pending[1], pending[2], pending[3], pending[4], pen...]
    pallas_call x0 -> x19, Pallas kernels: none -> 86.2 us  [the longest x1 26.9 us: on_device(): call(forward_kernel, saved_shapes + [shape(ROWS, WIDTH)] * 2 + [shape(gra...]
    psum x1 -> x0, blocking collectives: 79.9 us -> none  [on_device(): lax.psum((pending[0], pending[1], pending[2], pending[3], pending[4], pen...]
    reshape x59 -> x0, local copies, waits for them, and re-layouts: 68.7 us -> none  [the longest x12 14 us: attend(): mixed.reshape(crop_count * crop_length, features)]
    slice x72 -> x0, local copies, waits for them, and re-layouts: 53.7 us -> none  [the longest x12 12.3 us: layer_parts(): value_rows[:boundary]]
    ppermute x4 -> x30, waiting for transfers between devices: 0.01 us -> 42.6 us  [the longest x8 27.7 us: exchange(): return lax.ppermute(values_in, ('section', 'dp'), flat_pairs(move))]
    ppermute x4 -> x30, starting transfers between devices: 7.57 us -> 44 us  [the longest x12 25.4 us: forward_z(): lax.ppermute(values_in, ('section', 'dp'), flat_pairs(lambda core, x, y,...]
  transfers between devices with their start and end apart: 5 -> 30, of which waited for: 1 -> 12; matrix products, arithmetic and copies ran while one was open for 20% -> 2% of each run, Pallas kernels for 0% -> 20%
where the time goes in v1:
time: 196 us; the launch traced here: 195 us
  Pallas kernels  86.2 us (44%)
  starting transfers between devices  44 us (22%)
  waiting for transfers between devices  42.6 us (22%)
  local copies, waits for them, and re-layouts  21.1 us (11%)
    ppermute x8, waiting for transfers between devices, exchange(): return lax.ppermute(values_in, ('section', 'dp'), flat_pairs(move))  27.7 us
    pallas_call x1, Pallas kernels, on_device(): call(forward_kernel, saved_shapes + [shape(ROWS, WIDTH)] * 2 + [shape(gra...  26.9 us
    ppermute x12, starting transfers between devices, forward_z(): lax.ppermute(values_in, ('section', 'dp'), flat_pairs(lambda core, x, y,...  25.4 us
    unnamed x66, local copies, waits for them, and re-layouts  21.1 us
    pallas_call x1, Pallas kernels, on_device(): call(backward_kernel, [shape(ROWS, WIDTH)] * 2 + [shape(grad_rows, WIDTH)...  15.3 us
    pallas_call x6, Pallas kernels, reduce_everywhere(): call(functools.partial(join_kernel, which, rows), shape(rows * len(parts)...  13.8 us
    pallas_call x4, Pallas kernels, reduce_everywhere(): call(functools.partial(halve_kernel, step, count), [shape(half + tail, WI...  13.2 us
    ppermute x8, starting transfers between devices, exchange(): return lax.ppermute(values_in, ('section', 'dp'), flat_pairs(move))  12.6 us
  transfers between devices with their start and end apart: 30, of which 12 were waited for; matrix products, arithmetic and copies ran while one was open for 2% of the time, Pallas kernels for 20%

profile of v1, /device:TPU:0, one launch (start us, length us, event | category | flops | bytes accessed | tf_op | source)
XLA Modules:
  0.0 194.9 jit_solution(1103940032154731044)
XLA Ops:
  3.4 2.1 %shard_map.280 = (bf16[432,384]{1,0:T(8,128)(2,1)}, bf16[432,384]{1,0:T(8,128)(2,1)}) custom-call(s32[2]{0:T(128)} %glive.3, s32[10]{0:T(128)} %llive.3, bf16[2,197,384]{2,1,0:T(8,128)(2,1)} %bitcast.10, bf16[10,37,384]{2,1,0:T(8,128)(2,1)} %bitcast.20, bf16[1,384]{1,0:T(2,128)(2,1)} %refs_0_.1, bf16[1,384]{1,0:T(2,128)(2,1)} %refs_1_.1, ...), custom_call_target="tpu_custom_call" | custom-call | bytes 2000000 | tf_op jit(solution)/shard_map/pallas_call | solution.py:658
  9.7 26.9 %shard_map.281 = (bf16[416,384]{1,0:T(8,128)(2,1)}, bf16[416,1152]{1,0:T(8,128)(2,1)}, bf16[12,208,208]{2,1,0:T(8,128)(2,1)}, bf16[416,384]{1,0:T(8,128)(2,1)}, ...) custom-call(bf16[432,384]{1,0:T(8,128)(2,1)} %get-tuple-element.68.r, ...), custom_call_target="tpu_custom_call" | custom-call | flops 6000000000 | bytes 20000000 | tf_op jit(solution)/shard_map/pallas_call | solution.py:688
  36.7 15.3 %shard_map.282 = (bf16[416,384]{1,0:T(8,128)(2,1)}, bf16[416,384]{1,0:T(8,128)(2,1)}, bf16[2320,384]{1,0:T(8,128)(2,1)}, bf16[2320,384]{1,0:T(8,128)(2,1)}) custom-call(bf16[432,384]{1,0:T(8,128)(2,1)} %get-tuple-element.68.refs_0_, bf16[432,384]{1,0:T(8,128)(2,1)} %copy-done.15, bf16[384,1152]{1,0:T(8,128)(2,1)} %bitcast.19, bf16[384,384]{1,0:T(8,128)(2,1)} %bitcast.24, ...), custom_call_target="tpu_custom_call" | custom-call | flops 3000000000 | bytes 15000000 | tf_op jit(solution)/shard_map/pallas_call | solution.py:708
  53.6 5.1 %collective-permute-done.6.recv = bf16[2320,384]{1,0:T(8,128)(2,1)S(1)} collective-permute-done((bf16[2320,384]{1,0:T(8,128)(2,1)}, bf16[2320,384]{1,0:T(8,128)(2,1)S(1)}, u32[]{:S(2)}, u32[]{:S(2)}) %collective-permute-start.6) | collective-permute-done | bytes 1781792 | tf_op jit(solution)/shard_map/ppermute | solution.py:644
  59.9 3.9 %shard_map.284 = (bf16[1168,384]{1,0:T(8,128)(2,1)}, bf16[1168,384]{1,0:T(8,128)(2,1)}) custom-call(bf16[2320,384]{1,0:T(8,128)(2,1)} %get-tuple-element.84.keep, bf16[2320,384]{1,0:T(8,128)(2,1)} %copy-done.1), custom_call_target="tpu_custom_call" | custom-call | bytes 5308416 | tf_op jit(solution)/shard_map/pallas_call | solution.py:595
  63.8 2.6 %collective-permute-start.7 = (bf16[1168,384]{1,0:T(8,128)(2,1)}, bf16[1168,384]{1,0:T(8,128)(2,1)S(1)}, u32[]{:S(2)}, u32[]{:S(2)}) collective-permute-start(bf16[1168,384]{1,0:T(8,128)(2,1)} %get-tuple-element.87), channel_id=1, source_target_pairs={{0,1},{1,0},{2,3},{3,2},{4,5},{5,4},{6,7},{7,6},{8,9},{9,8},{10,11... | collective-permute-start | bytes 2691080 | tf_op jit(solution)/shard_map/ppermute | solution.py:580
  67.7 4.0 %shard_map.291 = (bf16[1168,384]{1,0:T(8,128)(2,1)}, bf16[1168,384]{1,0:T(8,128)(2,1)}) custom-call(bf16[2320,384]{1,0:T(8,128)(2,1)} %get-tuple-element.95.keep, bf16[2320,384]{1,0:T(8,128)(2,1)} %copy-done), custom_call_target="tpu_custom_call" | custom-call | bytes 5308416 | tf_op jit(solution)/shard_map/pallas_call | solution.py:595
  71.6 6.2 %collective-permute-done.7.recv = bf16[1168,384]{1,0:T(8,128)(2,1)S(1)} collective-permute-done((bf16[1168,384]{1,0:T(8,128)(2,1)}, bf16[1168,384]{1,0:T(8,128)(2,1)S(1)}, u32[]{:S(2)}, u32[]{:S(2)}) %collective-permute-start.7) | collective-permute-done | bytes 897056 | tf_op jit(solution)/shard_map/ppermute | solution.py:580
  78.7 2.7 %shard_map.285 = (bf16[592,384]{1,0:T(8,128)(2,1)}, bf16[592,384]{1,0:T(8,128)(2,1)}) custom-call(bf16[1168,384]{1,0:T(8,128)(2,1)} %get-tuple-element.86.keep, bf16[1168,384]{1,0:T(8,128)(2,1)} %copy-done.6), custom_call_target="tpu_custom_call" | custom-call | bytes 2654208 | tf_op jit(solution)/shard_map/pallas_call | solution.py:595
  81.4 2.1 %collective-permute-start.8 = (bf16[592,384]{1,0:T(8,128)(2,1)}, bf16[592,384]{1,0:T(8,128)(2,1)S(1)}, u32[]{:S(2)}, u32[]{:S(2)}) collective-permute-start(bf16[592,384]{1,0:T(8,128)(2,1)} %get-tuple-element.89), channel_id=1, source_target_pairs={{0,2},{1,3},{2,0},{3,1},{4,6},{5,7},{6,4},{7,5},{8,10},{9,11},{10,... | collective-permute-start | bytes 1363976 | tf_op jit(solution)/shard_map/ppermute | solution.py:580
  83.5 7.3 %collective-permute-done.18.recv = bf16[1168,384]{1,0:T(8,128)(2,1)S(1)} collective-permute-done((bf16[1168,384]{1,0:T(8,128)(2,1)}, bf16[1168,384]{1,0:T(8,128)(2,1)S(1)}, u32[]{:S(2)}, u32[]{:S(2)}) %collective-permute-start.18) | collective-permute-done | bytes 897056 | tf_op jit(solution)/shard_map/ppermute | solution.py:580
  91.7 2.7 %shard_map.292 = (bf16[592,384]{1,0:T(8,128)(2,1)}, bf16[592,384]{1,0:T(8,128)(2,1)}) custom-call(bf16[1168,384]{1,0:T(8,128)(2,1)} %get-tuple-element.97.keep, bf16[1168,384]{1,0:T(8,128)(2,1)} %copy-done.7), custom_call_target="tpu_custom_call" | custom-call | bytes 2654208 | tf_op jit(solution)/shard_map/pallas_call | solution.py:595
  94.3 2.4 %collective-permute-start.19 = (bf16[592,384]{1,0:T(8,128)(2,1)}, bf16[592,384]{1,0:T(8,128)(2,1)S(1)}, u32[]{:S(2)}, u32[]{:S(2)}) collective-permute-start(bf16[592,384]{1,0:T(8,128)(2,1)} %get-tuple-element.100), channel_id=1, source_target_pairs={{0,2},{1,3},{2,0},{3,1},{4,6},{5,7},{6,4},{7,5},{8,10},{9,11},{10,... | collective-permute-start | bytes 1363976 | tf_op jit(solution)/shard_map/ppermute | solution.py:580
  97.5 2.0 %shard_map.286 = (bf16[160,384]{1,0:T(8,128)(2,1)}, bf16[160,384]{1,0:T(8,128)(2,1)}, bf16[160,384]{1,0:T(8,128)(2,1)}, bf16[160,384]{1,0:T(8,128)(2,1)}) custom-call(bf16[592,384]{1,0:T(8,128)(2,1)} %get-tuple-element.88.keep, bf16[592,384]{1,0:T(8,128)(2,1)} %copy-done.12), custom_call_target="tpu_custom_call" | custom-call | bytes 1327104 | tf_op jit(solution)/shard_map/pallas_call | solution.py:605
  101.0 2.6 %collective-permute-start.10 = (bf16[160,384]{1,0:T(8,128)(2,1)}, bf16[160,384]{1,0:T(8,128)(2,1)S(1)}, u32[]{:S(2)}, u32[]{:S(2)}) collective-permute-start(bf16[160,384]{1,0:T(8,128)(2,1)} %get-tuple-element.92), channel_id=1, source_target_pairs={{0,8},{1,9},{2,10},{3,11},{4,12},{5,13},{6,14},{7,15},{8,0},{9,1},... | collective-permute-start | bytes 368648 | tf_op jit(solution)/shard_map/ppermute | solution.py:584
  105.7 2.0 %shard_map.293 = (bf16[160,384]{1,0:T(8,128)(2,1)}, bf16[160,384]{1,0:T(8,128)(2,1)}, bf16[160,384]{1,0:T(8,128)(2,1)}, bf16[160,384]{1,0:T(8,128)(2,1)}) custom-call(bf16[592,384]{1,0:T(8,128)(2,1)} %get-tuple-element.99.keep, bf16[592,384]{1,0:T(8,128)(2,1)} %copy-done.11), custom_call_target="tpu_custom_call" | custom-call | bytes 1327104 | tf_op jit(solution)/shard_map/pallas_call | solution.py:605
  108.4 2.3 %collective-permute-start.21 = (bf16[160,384]{1,0:T(8,128)(2,1)}, bf16[160,384]{1,0:T(8,128)(2,1)S(1)}, u32[]{:S(2)}, u32[]{:S(2)}) collective-permute-start(bf16[160,384]{1,0:T(8,128)(2,1)} %get-tuple-element.103), channel_id=1, source_target_pairs={{0,8},{1,9},{2,10},{3,11},{4,12},{5,13},{6,14},{7,15},{8,0},{9,1},... | collective-permute-start | bytes 368648 | tf_op jit(solution)/shard_map/ppermute | solution.py:584
  115.8 8.1 %collective-permute-start.14 = (bf16[144,384]{1,0:T(8,128)(2,1)}, bf16[144,384]{1,0:T(8,128)(2,1)S(1)}, u32[]{:S(2)}, u32[]{:S(2)}) collective-permute-start(bf16[144,384]{1,0:T(8,128)(2,1)} %get-tuple-element.94.refs_0_), channel_id=1, source_target_pairs={{0,12},{1,13},{2,14},{3,15},{4,0},{5,1},{6,2},{7,3},{8,4},{9,5},{1... | collective-permute-start | bytes 331784 | tf_op jit(solution)/shard_map/ppermute | solution.py:584
  127.0 3.4 %collective-permute-start.25 = (bf16[144,384]{1,0:T(8,128)(2,1)}, bf16[144,384]{1,0:T(8,128)(2,1)S(1)}, u32[]{:S(2)}, u32[]{:S(2)}) collective-permute-start(bf16[144,384]{1,0:T(8,128)(2,1)} %get-tuple-element.105.refs_0_), channel_id=1, source_target_pairs={{0,12},{1,13},{2,14},{3,15},{4,0},{5,1},{6,2},{7,3},{8,4},{9,5},{1... | collective-permute-start | bytes 331784 | tf_op jit(solution)/shard_map/ppermute | solution.py:584
  131.4 2.5 %collective-permute-start.23 = (bf16[144,384]{1,0:T(8,128)(2,1)}, bf16[144,384]{1,0:T(8,128)(2,1)S(1)}, u32[]{:S(2)}, u32[]{:S(2)}) collective-permute-start(bf16[144,384]{1,0:T(8,128)(2,1)} %get-tuple-element.105.refs_0_), channel_id=1, source_target_pairs={{0,4},{1,5},{2,6},{3,7},{4,8},{5,9},{6,10},{7,11},{8,12},{9,13},{1... | collective-permute-start | bytes 331784 | tf_op jit(solution)/shard_map/ppermute | solution.py:584
  133.9 3.0 %collective-permute-done.13.refs_2_ = bf16[144,384]{1,0:T(8,128)(2,1)S(1)} collective-permute-done((bf16[144,384]{1,0:T(8,128)(2,1)}, bf16[144,384]{1,0:T(8,128)(2,1)S(1)}, u32[]{:S(2)}, u32[]{:S(2)}) %collective-permute-start.13) | collective-permute-done | bytes 110624 | tf_op jit(solution)/shard_map/ppermute | solution.py:584
  146.1 2.5 %collective-permute-done.15.refs_1_ = bf16[576,384]{1,0:T(8,128)(2,1)S(1)} collective-permute-done((bf16[576,384]{1,0:T(8,128)(2,1)}, bf16[576,384]{1,0:T(8,128)(2,1)S(1)}, u32[]{:S(2)}, u32[]{:S(2)}) %collective-permute-start.15) | collective-permute-done | bytes 442400 | tf_op jit(solution)/shard_map/ppermute | solution.py:580
  149.3 2.2 %shard_map.289.refs_0_ = bf16[1152,384]{1,0:T(8,128)(2,1)} custom-call(bf16[576,384]{1,0:T(8,128)(2,1)} %shard_map.288.refs_0_, bf16[576,384]{1,0:T(8,128)(2,1)} %copy-done.13), custom_call_target="tpu_custom_call" | custom-call | bytes 1769472 | tf_op jit(solution)/shard_map/pallas_call | solution.py:625
  152.8 4.0 %collective-permute-done.26.refs_1_ = bf16[576,384]{1,0:T(8,128)(2,1)S(1)} collective-permute-done((bf16[576,384]{1,0:T(8,128)(2,1)}, bf16[576,384]{1,0:T(8,128)(2,1)S(1)}, u32[]{:S(2)}, u32[]{:S(2)}) %collective-permute-start.26) | collective-permute-done | bytes 442400 | tf_op jit(solution)/shard_map/ppermute | solution.py:580
  157.6 2.2 %shard_map.296.refs_0_ = bf16[1152,384]{1,0:T(8,128)(2,1)} custom-call(bf16[576,384]{1,0:T(8,128)(2,1)} %shard_map.295.refs_0_, bf16[576,384]{1,0:T(8,128)(2,1)} %copy-done.14), custom_call_target="tpu_custom_call" | custom-call | bytes 1769472 | tf_op jit(solution)/shard_map/pallas_call | solution.py:625
  161.3 3.5 %collective-permute-done.16.refs_1_ = bf16[1152,384]{1,0:T(8,128)(2,1)S(1)} collective-permute-done((bf16[1152,384]{1,0:T(8,128)(2,1)}, bf16[1152,384]{1,0:T(8,128)(2,1)S(1)}, u32[]{:S(2)}, u32[]{:S(2)}) %collective-permute-start.16) | collective-permute-done | bytes 884768 | tf_op jit(solution)/shard_map/ppermute | solution.py:580
  165.7 2.9 %shard_map.290.refs_0_ = bf16[2304,384]{1,0:T(8,128)(2,1)} custom-call(bf16[1152,384]{1,0:T(8,128)(2,1)} %shard_map.289.refs_0_, bf16[1152,384]{1,0:T(8,128)(2,1)} %copy-done.8), custom_call_target="tpu_custom_call" | custom-call | bytes 3538944 | tf_op jit(solution)/shard_map/pallas_call | solution.py:625
  170.0 4.3 %collective-permute-done.27.refs_1_ = bf16[1152,384]{1,0:T(8,128)(2,1)S(1)} collective-permute-done((bf16[1152,384]{1,0:T(8,128)(2,1)}, bf16[1152,384]{1,0:T(8,128)(2,1)S(1)}, u32[]{:S(2)}, u32[]{:S(2)}) %collective-permute-start.27) | collective-permute-done | bytes 884768 | tf_op jit(solution)/shard_map/ppermute | solution.py:580
  175.2 2.9 %shard_map.297.refs_1_ = bf16[2304,384]{1,0:T(8,128)(2,1)} custom-call(bf16[1152,384]{1,0:T(8,128)(2,1)} %shard_map.296.refs_0_, bf16[1152,384]{1,0:T(8,128)(2,1)} %copy-done.9), custom_call_target="tpu_custom_call" | custom-call | bytes 3538944 | tf_op jit(solution)/shard_map/pallas_call | solution.py:625
  179.5 3.6 %collective-permute-done.5.recv = bf16[416,384]{1,0:T(8,128)(2,1)S(1)} collective-permute-done((bf16[416,384]{1,0:T(8,128)(2,1)S(1)}, bf16[416,384]{1,0:T(8,128)(2,1)S(1)}, u32[]{:S(2)}, u32[]{:S(2)}) %collective-permute-start.5) | collective-permute-done | bytes 319520 | tf_op jit(solution)/shard_map/ppermute | solution.py:644
  183.8 2.0 %shard_map.283 = (bf16[2,197,384]{2,1,0:T(8,128)(2,1)}, bf16[10,37,384]{2,1,0:T(8,128)(2,1)}) custom-call(s32[2]{0:T(128)} %glive.3, s32[10]{0:T(128)} %llive.3, bf16[416,384]{1,0:T(8,128)(2,1)} %get-tuple-element.80.keep, bf16[416,384]{1,0:T(8,128)(2,1)} %copy-done.16), custom_call_target="tpu_custom_call" | custom-call | bytes 2000000 | tf_op jit(solution)/shard_map/pallas_call | solution.py:730
  189.5 5.3 %shard_map.298 = (f32[1,384]{1,0:T(1,128)}, f32[1,384]{1,0:T(1,128)}, f32[1,384,1152]{2,1,0:T(8,128)}, f32[1,384]{1,0:T(1,128)}, f32[1,384]{1,0:T(1,128)}, /*ind...) custom-call(bf16[2304,384]{1,0:T(8,128)(2,1)} %shard_map.290.refs_0_, ...), custom_call_target="tpu_custom_call" | custom-call | bytes 12000000 | tf_op jit(solution)/shard_map/pallas_call | solution.py:738
  (113 shorter events, 49.7 us)
Async XLA Ops:
  0.6 7.1 %collective-permute-start.3 = (bf16[384,1536]{1,0:T(8,128)(2,1)}, bf16[384,1536]{1,0:T(8,128)(2,1)S(1)}, u32[]{:S(2)}, u32[]{:S(2)}) collective-permute-start(bf16[384,1536]{1,0:T(8,128)(2,1)} %bitcast.11), channel_id=1, source_target_pairs={{0,16},{16,0},{1,17},{17,1},{2,18},{18,2},{3,19},{19,3},{4,20},{20... | collective-permute-start | bytes 3538952 | tf_op jit(solution)/shard_map/ppermute | solution.py:644
  1.2 6.6 %collective-permute-start.4 = (bf16[1536,384]{1,0:T(8,128)(2,1)}, bf16[1536,384]{1,0:T(8,128)(2,1)S(1)}, u32[]{:S(2)}, u32[]{:S(2)}) collective-permute-start(bf16[1536,384]{1,0:T(8,128)(2,1)} %bitcast.14), channel_id=1, source_target_pairs={{0,16},{16,0},{1,17},{17,1},{2,18},{18,2},{3,19},{19,3},{4,20},{20... | collective-permute-start | bytes 3538952 | tf_op jit(solution)/shard_map/ppermute | solution.py:644
  1.2 6.5 %collective-permute-start.1 = (bf16[384,1152]{1,0:T(8,128)(2,1)}, bf16[384,1152]{1,0:T(8,128)(2,1)S(1)}, u32[]{:S(2)}, u32[]{:S(2)}) collective-permute-start(bf16[384,1152]{1,0:T(8,128)(2,1)} %bitcast.17), channel_id=1, source_target_pairs={{0,16},{16,0},{1,17},{17,1},{2,18},{18,2},{3,19},{19,3},{4,20},{20... | collective-permute-start | bytes 2654216 | tf_op jit(solution)/shard_map/ppermute | solution.py:644
  5.5 2.3 %collective-permute-start = (bf16[432,384]{1,0:T(8,128)(2,1)}, bf16[432,384]{1,0:T(8,128)(2,1)S(1)}, u32[]{:S(2)}, u32[]{:S(2)}) collective-permute-start(bf16[432,384]{1,0:T(8,128)(2,1)} %get-tuple-element.69), channel_id=1, source_target_pairs={{0,16},{16,0},{1,17},{17,1},{2,18},{18,2},{3,19},{19,3},{4,20},{20... | collective-permute-start | bytes 995336 | tf_op jit(solution)/shard_map/ppermute | solution.py:644
  5.5 2.2 %collective-permute-start.2 = (bf16[384,384]{1,0:T(8,128)(2,1)}, bf16[384,384]{1,0:T(8,128)(2,1)S(1)}, u32[]{:S(2)}, u32[]{:S(2)}) collective-permute-start(bf16[384,384]{1,0:T(8,128)(2,1)} %bitcast.22), channel_id=1, source_target_pairs={{0,16},{16,0},{1,17},{17,1},{2,18},{18,2},{3,19},{19,3},{4,20},{20... | collective-permute-start | bytes 884744 | tf_op jit(solution)/shard_map/ppermute | solution.py:644
  36.6 16.9 %copy-start.30 = (bf16[2320,384]{1,0:T(8,128)(2,1)S(1)}, bf16[2320,384]{1,0:T(8,128)(2,1)}, u32[]{:S(2)}) copy-start(bf16[2320,384]{1,0:T(8,128)(2,1)} %get-tuple-element.96) | copy-start | bytes 5345284
  52.0 6.7 %collective-permute-start.6 = (bf16[2320,384]{1,0:T(8,128)(2,1)}, bf16[2320,384]{1,0:T(8,128)(2,1)S(1)}, u32[]{:S(2)}, u32[]{:S(2)}) collective-permute-start(bf16[2320,384]{1,0:T(8,128)(2,1)} %get-tuple-element.85), channel_id=1, source_target_pairs={{0,16},{16,0},{1,17},{17,1},{2,18},{18,2},{3,19},{19,3},{4,20},{20... | collective-permute-start | bytes 5345288 | tf_op jit(solution)/shard_map/ppermute | solution.py:644
  53.5 12.9 %collective-permute-start.17 = (bf16[2320,384]{1,0:T(8,128)(2,1)S(1)}, bf16[2320,384]{1,0:T(8,128)(2,1)S(1)}, u32[]{:S(2)}, u32[]{:S(2)}) collective-permute-start(bf16[2320,384]{1,0:T(8,128)(2,1)S(1)} %copy-done.30), channel_id=1, source_target_pairs={{0,16},{16,0},{1,17},{17,1},{2,18},{18,2},{3,19},{19,3},{4,20},{20... | collective-permute-start | bytes 5345288 | tf_op jit(solution)/shard_map/ppermute | solution.py:644
  63.8 14.0 %collective-permute-start.7 = (bf16[1168,384]{1,0:T(8,128)(2,1)}, bf16[1168,384]{1,0:T(8,128)(2,1)S(1)}, u32[]{:S(2)}, u32[]{:S(2)}) collective-permute-start(bf16[1168,384]{1,0:T(8,128)(2,1)} %get-tuple-element.87), channel_id=1, source_target_pairs={{0,1},{1,0},{2,3},{3,2},{4,5},{5,4},{6,7},{7,6},{8,9},{9,8},{10,11... | collective-permute-start | bytes 2691080 | tf_op jit(solution)/shard_map/ppermute | solution.py:580
  71.6 19.1 %collective-permute-start.18 = (bf16[1168,384]{1,0:T(8,128)(2,1)}, bf16[1168,384]{1,0:T(8,128)(2,1)S(1)}, u32[]{:S(2)}, u32[]{:S(2)}) collective-permute-start(bf16[1168,384]{1,0:T(8,128)(2,1)} %get-tuple-element.98), channel_id=1, source_target_pairs={{0,1},{1,0},{2,3},{3,2},{4,5},{5,4},{6,7},{7,6},{8,9},{9,8},{10,11... | collective-permute-start | bytes 2691080 | tf_op jit(solution)/shard_map/ppermute | solution.py:580
  81.4 15.3 %collective-permute-start.8 = (bf16[592,384]{1,0:T(8,128)(2,1)}, bf16[592,384]{1,0:T(8,128)(2,1)S(1)}, u32[]{:S(2)}, u32[]{:S(2)}) collective-permute-start(bf16[592,384]{1,0:T(8,128)(2,1)} %get-tuple-element.89), channel_id=1, source_target_pairs={{0,2},{1,3},{2,0},{3,1},{4,6},{5,7},{6,4},{7,5},{8,10},{9,11},{10,... | collective-permute-start | bytes 1363976 | tf_op jit(solution)/shard_map/ppermute | solution.py:580
  94.3 10.6 %collective-permute-start.19 = (bf16[592,384]{1,0:T(8,128)(2,1)}, bf16[592,384]{1,0:T(8,128)(2,1)S(1)}, u32[]{:S(2)}, u32[]{:S(2)}) collective-permute-start(bf16[592,384]{1,0:T(8,128)(2,1)} %get-tuple-element.100), channel_id=1, source_target_pairs={{0,2},{1,3},{2,0},{3,1},{4,6},{5,7},{6,4},{7,5},{8,10},{9,11},{10,... | collective-permute-start | bytes 1363976 | tf_op jit(solution)/shard_map/ppermute | solution.py:580
  99.5 11.3 %collective-permute-start.9 = (bf16[160,384]{1,0:T(8,128)(2,1)}, bf16[160,384]{1,0:T(8,128)(2,1)S(1)}, u32[]{:S(2)}, u32[]{:S(2)}) collective-permute-start(bf16[160,384]{1,0:T(8,128)(2,1)} %get-tuple-element.91), channel_id=1, source_target_pairs={{0,4},{1,5},{2,6},{3,7},{4,8},{5,9},{6,10},{7,11},{8,12},{9,13},{1... | collective-permute-start | bytes 368648 | tf_op jit(solution)/shard_map/ppermute | solution.py:584
  101.0 12.3 %collective-permute-start.10 = (bf16[160,384]{1,0:T(8,128)(2,1)}, bf16[160,384]{1,0:T(8,128)(2,1)S(1)}, u32[]{:S(2)}, u32[]{:S(2)}) collective-permute-start(bf16[160,384]{1,0:T(8,128)(2,1)} %get-tuple-element.92), channel_id=1, source_target_pairs={{0,8},{1,9},{2,10},{3,11},{4,12},{5,13},{6,14},{7,15},{8,0},{9,1},... | collective-permute-start | bytes 368648 | tf_op jit(solution)/shard_map/ppermute | solution.py:584
  103.6 9.7 %collective-permute-start.11 = (bf16[160,384]{1,0:T(8,128)(2,1)}, bf16[160,384]{1,0:T(8,128)(2,1)S(1)}, u32[]{:S(2)}, u32[]{:S(2)}) collective-permute-start(bf16[160,384]{1,0:T(8,128)(2,1)} %get-tuple-element.93), channel_id=1, source_target_pairs={{0,12},{1,13},{2,14},{3,15},{4,0},{5,1},{6,2},{7,3},{8,4},{9,5},{1... | collective-permute-start | bytes 368648 | tf_op jit(solution)/shard_map/ppermute | solution.py:584
  107.7 16.2 %collective-permute-start.20 = (bf16[160,384]{1,0:T(8,128)(2,1)}, bf16[160,384]{1,0:T(8,128)(2,1)S(1)}, u32[]{:S(2)}, u32[]{:S(2)}) collective-permute-start(bf16[160,384]{1,0:T(8,128)(2,1)} %get-tuple-element.102), channel_id=1, source_target_pairs={{0,4},{1,5},{2,6},{3,7},{4,8},{5,9},{6,10},{7,11},{8,12},{9,13},{1... | collective-permute-start | bytes 368648 | tf_op jit(solution)/shard_map/ppermute | solution.py:584
  108.4 16.1 %collective-permute-start.21 = (bf16[160,384]{1,0:T(8,128)(2,1)}, bf16[160,384]{1,0:T(8,128)(2,1)S(1)}, u32[]{:S(2)}, u32[]{:S(2)}) collective-permute-start(bf16[160,384]{1,0:T(8,128)(2,1)} %get-tuple-element.103), channel_id=1, source_target_pairs={{0,8},{1,9},{2,10},{3,11},{4,12},{5,13},{6,14},{7,15},{8,0},{9,1},... | collective-permute-start | bytes 368648 | tf_op jit(solution)/shard_map/ppermute | solution.py:584
  110.7 13.7 %collective-permute-start.22 = (bf16[160,384]{1,0:T(8,128)(2,1)}, bf16[160,384]{1,0:T(8,128)(2,1)S(1)}, u32[]{:S(2)}, u32[]{:S(2)}) collective-permute-start(bf16[160,384]{1,0:T(8,128)(2,1)} %get-tuple-element.104), channel_id=1, source_target_pairs={{0,12},{1,13},{2,14},{3,15},{4,0},{5,1},{6,2},{7,3},{8,4},{9,5},{1... | collective-permute-start | bytes 368648 | tf_op jit(solution)/shard_map/ppermute | solution.py:584
  115.8 15.5 %collective-permute-start.14 = (bf16[144,384]{1,0:T(8,128)(2,1)}, bf16[144,384]{1,0:T(8,128)(2,1)S(1)}, u32[]{:S(2)}, u32[]{:S(2)}) collective-permute-start(bf16[144,384]{1,0:T(8,128)(2,1)} %get-tuple-element.94.refs_0_), channel_id=1, source_target_pairs={{0,12},{1,13},{2,14},{3,15},{4,0},{5,1},{6,2},{7,3},{8,4},{9,5},{1... | collective-permute-start | bytes 331784 | tf_op jit(solution)/shard_map/ppermute | solution.py:584
  123.9 13.0 %collective-permute-start.13 = (bf16[144,384]{1,0:T(8,128)(2,1)}, bf16[144,384]{1,0:T(8,128)(2,1)S(1)}, u32[]{:S(2)}, u32[]{:S(2)}) collective-permute-start(bf16[144,384]{1,0:T(8,128)(2,1)} %get-tuple-element.94.refs_0_), channel_id=1, source_target_pairs={{0,8},{1,9},{2,10},{3,11},{4,12},{5,13},{6,14},{7,15},{8,0},{9,1},... | collective-permute-start | bytes 331784 | tf_op jit(solution)/shard_map/ppermute | solution.py:584
  123.9 13.0 %collective-permute-start.12 = (bf16[144,384]{1,0:T(8,128)(2,1)}, bf16[144,384]{1,0:T(8,128)(2,1)S(1)}, u32[]{:S(2)}, u32[]{:S(2)}) collective-permute-start(bf16[144,384]{1,0:T(8,128)(2,1)} %get-tuple-element.94.refs_0_), channel_id=1, source_target_pairs={{0,4},{1,5},{2,6},{3,7},{4,8},{5,9},{6,10},{7,11},{8,12},{9,13},{1... | collective-permute-start | bytes 331784 | tf_op jit(solution)/shard_map/ppermute | solution.py:584
  127.0 14.2 %collective-permute-start.25 = (bf16[144,384]{1,0:T(8,128)(2,1)}, bf16[144,384]{1,0:T(8,128)(2,1)S(1)}, u32[]{:S(2)}, u32[]{:S(2)}) collective-permute-start(bf16[144,384]{1,0:T(8,128)(2,1)} %get-tuple-element.105.refs_0_), channel_id=1, source_target_pairs={{0,12},{1,13},{2,14},{3,15},{4,0},{5,1},{6,2},{7,3},{8,4},{9,5},{1... | collective-permute-start | bytes 331784 | tf_op jit(solution)/shard_map/ppermute | solution.py:584
  130.4 11.0 %collective-permute-start.24 = (bf16[144,384]{1,0:T(8,128)(2,1)}, bf16[144,384]{1,0:T(8,128)(2,1)S(1)}, u32[]{:S(2)}, u32[]{:S(2)}) collective-permute-start(bf16[144,384]{1,0:T(8,128)(2,1)} %get-tuple-element.105.refs_0_), channel_id=1, source_target_pairs={{0,8},{1,9},{2,10},{3,11},{4,12},{5,13},{6,14},{7,15},{8,0},{9,1},... | collective-permute-start | bytes 331784 | tf_op jit(solution)/shard_map/ppermute | solution.py:584
  131.4 10.0 %collective-permute-start.23 = (bf16[144,384]{1,0:T(8,128)(2,1)}, bf16[144,384]{1,0:T(8,128)(2,1)S(1)}, u32[]{:S(2)}, u32[]{:S(2)}) collective-permute-start(bf16[144,384]{1,0:T(8,128)(2,1)} %get-tuple-element.105.refs_0_), channel_id=1, source_target_pairs={{0,4},{1,5},{2,6},{3,7},{4,8},{5,9},{6,10},{7,11},{8,12},{9,13},{1... | collective-permute-start | bytes 331784 | tf_op jit(solution)/shard_map/ppermute | solution.py:584
  140.1 8.5 %collective-permute-start.15 = (bf16[576,384]{1,0:T(8,128)(2,1)}, bf16[576,384]{1,0:T(8,128)(2,1)S(1)}, u32[]{:S(2)}, u32[]{:S(2)}) collective-permute-start(bf16[576,384]{1,0:T(8,128)(2,1)} %shard_map.288.refs_0_), channel_id=1, source_target_pairs={{0,2},{1,3},{2,0},{3,1},{4,6},{5,7},{6,4},{7,5},{8,10},{9,11},{10,... | collective-permute-start | bytes 1327112 | tf_op jit(solution)/shard_map/ppermute | solution.py:580
  144.5 12.3 %collective-permute-start.26 = (bf16[576,384]{1,0:T(8,128)(2,1)}, bf16[576,384]{1,0:T(8,128)(2,1)S(1)}, u32[]{:S(2)}, u32[]{:S(2)}) collective-permute-start(bf16[576,384]{1,0:T(8,128)(2,1)} %shard_map.295.refs_0_), channel_id=1, source_target_pairs={{0,2},{1,3},{2,0},{3,1},{4,6},{5,7},{6,4},{7,5},{8,10},{9,11},{10,... | collective-permute-start | bytes 1327112 | tf_op jit(solution)/shard_map/ppermute | solution.py:580
  151.5 13.3 %collective-permute-start.16 = (bf16[1152,384]{1,0:T(8,128)(2,1)}, bf16[1152,384]{1,0:T(8,128)(2,1)S(1)}, u32[]{:S(2)}, u32[]{:S(2)}) collective-permute-start(bf16[1152,384]{1,0:T(8,128)(2,1)} %shard_map.289.refs_0_), channel_id=1, source_target_pairs={{0,1},{1,0},{2,3},{3,2},{4,5},{5,4},{6,7},{7,6},{8,9},{9,8},{10,11... | collective-permute-start | bytes 2654216 | tf_op jit(solution)/shard_map/ppermute | solution.py:580
  159.8 14.4 %collective-permute-start.27 = (bf16[1152,384]{1,0:T(8,128)(2,1)}, bf16[1152,384]{1,0:T(8,128)(2,1)S(1)}, u32[]{:S(2)}, u32[]{:S(2)}) collective-permute-start(bf16[1152,384]{1,0:T(8,128)(2,1)} %shard_map.296.refs_0_), channel_id=1, source_target_pairs={{0,1},{1,0},{2,3},{3,2},{4,5},{5,4},{6,7},{7,6},{8,9},{9,8},{10,11... | collective-permute-start | bytes 2654216 | tf_op jit(solution)/shard_map/ppermute | solution.py:580
  168.5 10.9 %copy-start.31 = (bf16[416,384]{1,0:T(8,128)(2,1)S(1)}, bf16[416,384]{1,0:T(8,128)(2,1)}, u32[]{:S(2)}) copy-start(bf16[416,384]{1,0:T(8,128)(2,1)} %get-tuple-element.81) | copy-start | bytes 958468
  168.5 19.2 %collective-permute-start.28 = (bf16[2304,384]{1,0:T(8,128)(2,1)}, bf16[2304,384]{1,0:T(8,128)(2,1)S(1)}, u32[]{:S(2)}, u32[]{:S(2)}) collective-permute-start(bf16[2304,384]{1,0:T(8,128)(2,1)} %shard_map.290.refs_0_), channel_id=1, source_target_pairs={{16,0},{17,1},{18,2},{19,3},{20,4},{21,5},{22,6},{23,7},{24,8},{25... | collective-permute-start | bytes 5308424 | tf_op jit(solution)/shard_map/ppermute | solution.py:729
  178.0 9.7 %collective-permute-start.29 = (bf16[2304,384]{1,0:T(8,128)(2,1)}, bf16[2304,384]{1,0:T(8,128)(2,1)S(1)}, u32[]{:S(2)}, u32[]{:S(2)}) collective-permute-start(bf16[2304,384]{1,0:T(8,128)(2,1)} %shard_map.297.refs_1_), channel_id=1, source_target_pairs={{0,16},{1,17},{2,18},{3,19},{4,20},{5,21},{6,22},{7,23},{8,24},{9,... | collective-permute-start | bytes 5308424 | tf_op jit(solution)/shard_map/ppermute | solution.py:727
  179.4 3.6 %collective-permute-start.5 = (bf16[416,384]{1,0:T(8,128)(2,1)S(1)}, bf16[416,384]{1,0:T(8,128)(2,1)S(1)}, u32[]{:S(2)}, u32[]{:S(2)}) collective-permute-start(bf16[416,384]{1,0:T(8,128)(2,1)S(1)} %copy-done.31), channel_id=1, source_target_pairs={{0,16},{16,0},{1,17},{17,1},{2,18},{18,2},{3,19},{19,3},{4,20},{20... | collective-permute-start | bytes 958472 | tf_op jit(solution)/shard_map/ppermute | solution.py:644
  (30 other events, 33.6 us)

commit v2 on v1

v2 whole, which is shorter than its diff:
```python
import functools

import jax
import jax.numpy as jnp
from jax import lax
from jax.experimental import pallas as pl
from jax.experimental.pallas import tpu as pltpu
from jax.sharding import PartitionSpec as P

HEAD = 64
GT = 197
LT = 37
WIDTH = 384
FF = 1536
SEQ = 208
ROWS = 2 * SEQ
SLOT = 40
LOCALS = 5
VECS = 16
EPSILON = 1e-06
MASKED = -1e30
ORDER = "b1c2d3j4jJjJjJjrJjJ5J76p8q"
DIMS_B = ((0, 1, 2, 3), (1, 0, 2, 3))
DIMS_A = ((0, 1, 2, 3), (1, 0, 2, 3))
PART_ROWS = {"m": 4 * WIDTH, "a": 2 * WIDTH}
COST = 10000000000
PACK_COST = 10
KA_VMEM = 12
KB_VMEM = 12
LN1G, LN1B, QB, VB, PB, LN2G, LN2B, F2B, F1B = range(9)
LIVE = 12
BF16 = jnp.bfloat16
F32 = jnp.float32
ANY = pl.BlockSpec(memory_space=pl.ANY)
VMEM = pl.BlockSpec(memory_space=pltpu.VMEM)
HBM = pl.BlockSpec(memory_space=pltpu.HBM)


def mm(left, right):
    return jnp.dot(left, right, preferred_element_type=F32)


def mm_right_t(left, right):
    return lax.dot_general(left, right, (((1,), (1,)), ((), ())), preferred_element_type=F32)


def mm_left_t(left, right):
    return lax.dot_general(left, right, (((0,), (0,)), ((), ())), preferred_element_type=F32)


def normalise(values_in):
    centred = values_in - jnp.mean(values_in, axis=-1, keepdims=True)
    scale = lax.rsqrt(jnp.mean(centred * centred, axis=-1, keepdims=True) + EPSILON)
    return centred * scale, scale


def normalise_back(unit, scale, grad_rows, gain):
    e = grad_rows * gain
    return scale * (
        e
        - jnp.mean(e, axis=-1, keepdims=True)
        - unit * jnp.mean(e * unit, axis=-1, keepdims=True)
    )


def seq_rows(seq):
    return pl.ds(pl.multiple_of(seq * SEQ, 16), SEQ)


def column(block):
    return slice(block * WIDTH, (block + 1) * WIDTH)


def row_sum(values_in):
    return jnp.sum(values_in, axis=0, keepdims=True)


def live_flag(tail, index):
    lane = lax.broadcasted_iota(jnp.int32, (1, WIDTH), 1)
    flags = tail[LIVE : LIVE + 1, :]
    return jnp.sum(jnp.where(lane == index, flags, 0.0), axis=1, keepdims=True)


def pack_kernel(g, l, tail, keep, send, rows):
    core = lax.axis_index("section")
    rows[...] = jnp.zeros_like(rows)
    tail_low = tail[...].astype(BF16)
    for out, half in ((keep, core), (send, 1 - core)):
        live = jnp.where(core == 1, live_flag(tail, half), 1.0)
        rows[:GT, :] = g[half].astype(F32) * live
        for j in range(LOCALS):
            crop = half * LOCALS + j
            live = jnp.where(core == 1, live_flag(tail, 2 + crop), 1.0)
            rows[SEQ + j * SLOT : SEQ + j * SLOT + LT, :] = l[crop].astype(F32) * live
        out[:ROWS, :] = rows[...].astype(BF16)
        out[ROWS:, :] = tail_low


def fill_masks(masks):
    row = lax.broadcasted_iota(jnp.int32, (SEQ, SEQ), 0)
    col = lax.broadcasted_iota(jnp.int32, (SEQ, SEQ), 1)
    masks[0] = jnp.where(col < GT, 0.0, MASKED)
    inside = jnp.zeros((SEQ, SEQ), jnp.bool_)
    for j in range(LOCALS):
        inside = inside | (
            (row >= j * SLOT)
            & (row < (j + 1) * SLOT)
            & (col >= j * SLOT)
            & (col < j * SLOT + LT)
        )
    masks[1] = jnp.where(inside, 0.0, MASKED)


def head_lanes():
    lane = lax.broadcasted_iota(jnp.int32, (SEQ, 2 * HEAD), 1)
    return (lane < HEAD, lane >= HEAD)


def only(mask, values_in):
    return jnp.where(mask, values_in, jnp.zeros_like(values_in))


def attention_forward(x, vec, masks, qkv_w, proj_w, n1, qkv, probs, mixed, middle):
    def body(seq, carry):
        rows = seq_rows(seq)
        x_rows = x[rows, :].astype(F32)
        unit, _ = normalise(x_rows)
        normed = (unit * vec[LN1G : LN1G + 1, :] + vec[LN1B : LN1B + 1, :]).astype(BF16)
        n1[rows, :] = normed
        for part in range(3):
            value = mm(normed, qkv_w[:, column(part)])
            if part == 0:
                value = (value + vec[QB : QB + 1, :]).astype(BF16) * BF16(HEAD**-0.5)
            if part == 2:
                value = value + vec[VB : VB + 1, :]
            qkv[rows, column(part)] = value.astype(BF16)
        lanes = head_lanes()
        mask = masks[seq]
        for pair in range(3):
            q = qkv[rows, pair * 128 : pair * 128 + 128]
            k = qkv[rows, WIDTH + pair * 128 : WIDTH + pair * 128 + 128]
            v = qkv[rows, 2 * WIDTH + pair * 128 : 2 * WIDTH + pair * 128 + 128]
            total = None
            for a in range(2):
                s = mm_right_t(only(lanes[a], q), k) + mask
                e = jnp.exp(s - jnp.max(s, axis=-1, keepdims=True))
                p = (e * (1.0 / jnp.sum(e, axis=-1, keepdims=True))).astype(BF16)
                probs[seq * 6 + pair * 2 + a] = p
                part = mm(p, only(lanes[a], v))
                total = part if total is None else total + part
            mixed[rows, pair * 128 : pair * 128 + 128] = total.astype(BF16)
        middle[rows, :] = x_rows + (mm(mixed[rows, :], proj_w[...]) + vec[PB : PB + 1, :])
        return carry

    lax.fori_loop(0, 2, body, 0)


def mlp_forward(vec, fc1_w, fc2_w, middle, n2, slope, active, result):
    def body(seq, carry):
        rows = seq_rows(seq)
        unit, _ = normalise(middle[rows, :])
        normed = (unit * vec[LN2G : LN2G + 1, :] + vec[LN2B : LN2B + 1, :]).astype(BF16)
        n2[rows, :] = normed
        for part in range(FF // WIDTH):
            hidden = mm(normed, fc1_w[:, column(part)]) + vec[F1B + part : F1B + part + 1, :]
            cdf = 0.5 + 0.5 * lax.erf(hidden * (0.5**0.5))
            active[rows, column(part)] = (hidden * cdf).astype(BF16)
            density = jnp.exp(hidden * hidden * -0.5) * 0.3989422804014327
            slope[rows, column(part)] = (cdf + hidden * density).astype(BF16)
        y = middle[rows, :] + (mm(active[rows, :], fc2_w[...]) + vec[F2B : F2B + 1, :])
        result[rows, :] = y.astype(BF16)
        return carry

    lax.fori_loop(0, 2, body, 0)


def mlp_backward(vec, fc1_w, fc2_w, middle, n2, slope, active, dy, dh, dmid, da, sums, emit):
    def body(seq, carry):
        rows = seq_rows(seq)
        dy_rows = dy[rows, :]
        for part in range(FF // WIDTH):
            dactive = mm_right_t(dy_rows, fc2_w[column(part), :])
            low = (slope[rows, column(part)].astype(F32) * dactive).astype(BF16)
            dh[rows, column(part)] = low
            sums[F1B + part : F1B + part + 1, :] += row_sum(low.astype(F32))
        dn2 = mm_right_t(dh[rows, :], fc1_w[...])
        unit, scale = normalise(middle[rows, :])
        dy_wide = dy_rows.astype(F32)
        grad = dy_wide + normalise_back(unit, scale, dn2, vec[LN2G : LN2G + 1, :])
        dmid[rows, :] = grad
        low = grad.astype(BF16)
        da[rows, :] = low
        sums[LN2G : LN2G + 1, :] += row_sum(dn2 * unit)
        sums[LN2B : LN2B + 1, :] += row_sum(dn2)
        sums[F2B : F2B + 1, :] += row_sum(dy_wide)
        sums[PB : PB + 1, :] += row_sum(low.astype(F32))
        return carry

    lax.fori_loop(0, 2, body, 0)
    for part in range(FF // WIDTH):
        emit(part, mm_left_t(active[:, column(part)], dy[:ROWS, :]))
    for part in range(FF // WIDTH):
        emit(4 + part, mm_left_t(n2[...], dh[:, column(part)]))


def attention_backward(
    x, vec, qkv_w, proj_w, n1, qkv, probs, mixed, dmid, da, dt, sums, emit, result
):
    def body(seq, carry):
        rows = seq_rows(seq)
        dmixed = mm_right_t(da[rows, :], proj_w[...]).astype(BF16)
        lanes = head_lanes()
        for pair in range(3):
            q = qkv[rows, pair * 128 : pair * 128 + 128]
            k = qkv[rows, WIDTH + pair * 128 : WIDTH + pair * 128 + 128]
            v = qkv[rows, 2 * WIDTH + pair * 128 : 2 * WIDTH + pair * 128 + 128]
            dm = dmixed[:, pair * 128 : pair * 128 + 128]
            dq = dk = dv = None
            for a in range(2):
                dm_a = only(lanes[a], dm)
                p = probs[seq * 6 + pair * 2 + a]
                dp = mm_right_t(dm_a, v)
                p_wide = p.astype(F32)
                ds = p_wide * (dp - jnp.sum(dp * p_wide, axis=-1, keepdims=True))
                ds = ds.astype(BF16)
                parts = (
                    mm(ds, only(lanes[a], k)),
                    mm_left_t(ds, only(lanes[a], q)),
                    mm_left_t(p, dm_a),
                )
                if a == 0:
                    dq, dk, dv = parts
                else:
                    dq, dk, dv = dq + parts[0], dk + parts[1], dv + parts[2]
            dq = (dq * HEAD**-0.5).astype(BF16)
            dv = dv.astype(BF16)
            here = slice(pair * 128, pair * 128 + 128)
            dt[rows, pair * 128 : pair * 128 + 128] = dq
            dt[rows, WIDTH + pair * 128 : WIDTH + pair * 128 + 128] = dk.astype(BF16)
            dt[rows, 2 * WIDTH + pair * 128 : 2 * WIDTH + pair * 128 + 128] = dv
            sums[QB : QB + 1, here] += row_sum(dq.astype(F32))
            sums[VB : VB + 1, here] += row_sum(dv.astype(F32))
        dn1 = mm_right_t(dt[rows, :], qkv_w[...])
        unit, scale = normalise(x[rows, :].astype(F32))
        grad = dmid[rows, :] + normalise_back(unit, scale, dn1, vec[LN1G : LN1G + 1, :])
        result[rows, :] = grad.astype(BF16)
        sums[LN1G : LN1G + 1, :] += row_sum(dn1 * unit)
        sums[LN1B : LN1B + 1, :] += row_sum(dn1)
        return carry

    lax.fori_loop(0, 2, body, 0)
    emit(8, mm_left_t(mixed[...], da[...]))
    for part in range(3):
        emit(9 + part, mm_left_t(n1[...], dt[:, column(part)]))


def make_emit(keep, send, core, first, blocks):
    def emit(block, value):
        half, place = block % 2, (block - first) // 2
        rows = slice(place * WIDTH, (place + 1) * WIDTH)
        low = value.astype(BF16)

        @pl.when(core == half)
        def _():
            keep[rows, :] = low

        @pl.when(core != half)
        def _():
            send[rows, :] = low

    return emit


def start_all(copies):
    for copy in copies:
        copy.start()


def wait_all(copies):
    for copy in copies:
        copy.wait()


def forward_kernel(*refs):
    own, got = refs[:1] + refs[2:6], refs[1:2] + refs[6:10]
    (
        pack, qkv_w, proj_w, fc1_w, fc2_w, vec, between,
        n1, qkv, probs, mixed, middle, n2, slope, active, result,
        dmid, da, sums, keep_out, send_out,
        masks, dh, in_sem,
    ) = refs[10:]
    core = lax.axis_index("section")
    other = 1 - core
    held = (pack, qkv_w, proj_w, fc1_w, fc2_w)

    def load(sources, layer, i):
        return pltpu.make_async_copy(sources[i], held[i].at[layer], in_sem.at[layer, i])

    for i in range(5):
        load(own, core, i).start()
        load(got, other, i).start()
    fill_masks(masks)
    sums[...] = jnp.zeros_like(sums)
    for layer in range(2):
        load(own, layer, 0).wait()
        vec[layer] = pack[layer, ROWS:, :].astype(F32)
    for layer in range(2):
        for i in (1, 2):
            load(own, layer, i).wait()
        x = pack.at[0] if layer == 0 else between
        attention_forward(
            x, vec.at[layer], masks, qkv_w.at[layer], proj_w.at[layer],
            n1.at[layer], qkv.at[layer], probs.at[layer], mixed.at[layer], middle.at[layer],
        )
        for i in (3, 4):
            load(own, layer, i).wait()
        mlp_forward(
            vec.at[layer], fc1_w.at[layer], fc2_w.at[layer], middle.at[layer], n2.at[layer],
            slope.at[layer], active.at[layer], between if layer == 0 else result,
        )
    mlp_backward(
        vec.at[1], fc1_w.at[1], fc2_w.at[1], middle.at[1], n2.at[1], slope.at[1], active.at[1],
        pack.at[1], dh, dmid, da, sums, make_emit(keep_out, send_out, core, 0, 8),
    )


def attention_backward_kernel(layer, *refs):
    (
        x, vec, qkv_w, proj_w, n1, qkv, probs, mixed, dmid, da, sums_in,
        dx, keep_out, send_out, dt, sums,
    ) = refs
    core = lax.axis_index("section")
    sums[...] = sums_in[...]
    attention_backward(
        x, vec.at[layer], qkv_w.at[layer], proj_w.at[layer], n1.at[layer], qkv.at[layer],
        probs.at[layer], mixed.at[layer], dmid, da, dt, sums,
        make_emit(keep_out, send_out, core, 8, 4), dx,
    )
    keep_out[2 * WIDTH :, :] = sums[...].astype(BF16)
    send_out[2 * WIDTH :, :] = sums[...].astype(BF16)


def last_backward_kernel(*refs):
    pack, result, rows_keep, rows_send, dx = refs[0], refs[11], refs[12], refs[13], refs[-1]
    attention_backward_kernel(
        0, pack.at[0], *refs[1:11], dx, refs[14], refs[15], refs[16], refs[17]
    )
    core = lax.axis_index("section")

    @pl.when(core == 0)
    def _():
        rows_keep[...] = dx[...]
        rows_send[...] = result[...]

    @pl.when(core == 1)
    def _():
        rows_keep[...] = result[...]
        rows_send[...] = dx[...]


def mlp_backward_kernel(*refs):
    (
        vec, fc1_w, fc2_w, middle, n2, slope, active, dy, dmid, da, sums, keep_out, send_out, dh,
    ) = refs
    core = lax.axis_index("section")
    sums[...] = jnp.zeros_like(sums)
    mlp_backward(
        vec.at[0], fc1_w.at[0], fc2_w.at[0], middle.at[0], n2.at[0], slope.at[0], active.at[0],
        dy, dh, dmid, da, sums, make_emit(keep_out, send_out, core, 0, 8),
    )


def rows_kernel(tails, keep, recv, g_out, l_out, wide):
    core = lax.axis_index("section")
    tail = tails.at[0]
    for source, half in ((keep, core), (recv, 1 - core)):
        wide[...] = source[...].astype(F32)
        live = jnp.where(core == 1, live_flag(tail, half), 1.0)
        g_out[half] = (wide[:GT, :] * live).astype(BF16)
        for j in range(LOCALS):
            crop = half * LOCALS + j
            live = jnp.where(core == 1, live_flag(tail, 2 + crop), 1.0)
            piece = wide[SEQ + j * SLOT : SEQ + j * SLOT + LT, :]
            l_out[crop] = (piece * live).astype(BF16)


def out_block(own, got, index):
    core = lax.axis_index("section")
    place = index // 2
    rows = slice(place * WIDTH, (place + 1) * WIDTH)
    return jnp.where(core == index % 2, own[rows, :], got[rows, :]).astype(F32)


def write_blocks(own, got, places, held, sem):
    copies = []
    for i, place in enumerate(places):
        held[i] = out_block(own, got, i)
        copies.append(pltpu.make_async_copy(held.at[i], place, sem.at[i]))
        copies[-1].start()
    return copies


def mlp_out_kernel(own, got, fc1, fc2, held, sem):
    places = [fc2.at[0, column(part), :] for part in range(4)]
    places += [fc1.at[0, :, column(part)] for part in range(4)]
    wait_all(write_blocks(own, got, places, held, sem))


def attention_out_kernel(*refs):
    (
        own, got, sums_a, sums_b,
        ln1g, ln1b, qkv, qb, vb, proj, pb, ln2g, ln2b, fc1b, fc2b, held, sem,
    ) = refs
    places = [proj.at[0]] + [qkv.at[0, :, column(part)] for part in range(3)]
    copies = write_blocks(own, got, places, held, sem)
    core = lax.axis_index("section")
    sums = jnp.where(core == 0, sums_a[...], sums_b[...])
    for out, row in (
        (ln1g, LN1G), (ln1b, LN1B), (qb, QB), (vb, VB), (pb, PB), (ln2g, LN2G), (ln2b, LN2B),
        (fc2b, F2B),
    ):
        out[...] = sums[row : row + 1, :]
    for part in range(4):
        fc1b[:, column(part)] = sums[F1B + part : F1B + part + 1, :]
    wait_all(copies)


def shape(*dims, dtype=BF16):
    return jax.ShapeDtypeStruct(dims, dtype)


class Ordered:
    def __init__(self):
        self.last = None

    def __call__(
        self, name, kernel, outs, in_specs, out_specs, scratch=(), vmem=8, cost=1
    ):
        before = [] if self.last is None else [self.last]
        count = len(in_specs)

        def body(*refs):
            kernel(*refs[:count], *refs[count + len(before) :])

        def run(*args):
            results = pl.pallas_call(
                body,
                out_shape=outs,
                name=name,
                in_specs=list(in_specs) + [ANY] * len(before),
                out_specs=out_specs,
                scratch_shapes=list(scratch),
                compiler_params=pltpu.CompilerParams(vmem_limit_bytes=vmem * 1024 * 1024),
                cost_estimate=pl.CostEstimate(
                    flops=cost * COST, bytes_accessed=0, transcendentals=0
                ),
            )(*args, *before)
            self.last = results[-1]
            return results

        return run


CHUNK = 48


def add_rows(out, start_out, left, right, start, count):
    def step(i, carry):
        here = pl.ds(pl.multiple_of(start + i * CHUNK, 16), CHUNK)
        there = pl.ds(pl.multiple_of(start_out + i * CHUNK, 16), CHUNK)
        out[there, :] = (left[here, :].astype(F32) + right[here, :].astype(F32)).astype(BF16)
        return carry

    lax.fori_loop(0, count // CHUNK, step, 0, unroll=2)


def add_tail(outs, start_out, left, right, start):
    if left.shape[0] == start:
        return
    here = slice(start, start + VECS)
    tail = (left[here, :].astype(F32) + right[here, :].astype(F32)).astype(BF16)
    for out in outs:
        out[start_out : start_out + VECS, :] = tail


def bit_of(dims, step):
    dp = lax.axis_index("dp")
    core = lax.axis_index("section")
    return jnp.where(core == 0, dp >> dims[0][step] & 1, dp >> dims[1][step] & 1)


def halve_kernel(dims, step, counts, *refs):
    sources, (keep_out, send_out) = refs[:-2], refs[-2:]
    bit = bit_of(dims, step)
    place = 0
    for count, keep, recv in zip(counts, sources[::2], sources[1::2]):
        half = count // 2
        add_rows(send_out, place, keep, recv, (1 - bit) * half, half)
        add_rows(keep_out, place, keep, recv, bit * half, half)
        place += half
    for count, keep, recv in zip(counts, sources[::2], sources[1::2]):
        add_tail((keep_out, send_out), place, keep, recv, count)


def sum_kernel(count, keep, recv, out):
    add_rows(out, 0, keep, recv, 0, count)
    add_tail((out,), count, keep, recv, count)


def total_kernel(count, own, recv, total_out, sums_out):
    add_rows(total_out, 0, own, recv, 0, count)
    sums_out[...] = own[count:, :].astype(F32) + recv[count:, :].astype(F32)


def join_rows(out, own, recv, bit, start, count):
    for ref, half in ((own, bit), (recv, 1 - bit)):
        out[pl.ds(pl.multiple_of(half * count, 16), count), :] = ref[start : start + count, :]


def join_kernel(dims, step, counts, own, recv, *outs):
    bit = bit_of(dims, step)
    start = 0
    for count, out in zip(counts, outs):
        join_rows(out, own, recv, bit, start, count)
        start += count


def last_join_kernel(dims, own, recv, other, mine, send, whole):
    join_rows(whole, own, recv, bit_of(dims, 0), 0, own.shape[0])
    core = lax.axis_index("section")

    @pl.when(core == 0)
    def _():
        mine[...] = whole[...]
        send[...] = other[...]

    @pl.when(core == 1)
    def _():
        mine[...] = other[...]
        send[...] = whole[...]


def exchange(values_in, dims, step):
    pairs = [
        (core * 16 + dp, core * 16 + (dp ^ 1 << dims[core][step]))
        for core in range(2)
        for dp in range(16)
    ]
    return lax.ppermute(values_in, ("section", "dp"), pairs)


class Reduction:
    def __init__(self, name, call, dims):
        self.name, self.call, self.dims = name, call, dims
        self.sources, self.wholes = {}, {}
        self.joint = self.run_joint()

    def add(self, part, keep, send):
        self.sources[part] = (keep, swap(send))

    def halve(self, step, label, counts, tail, sources):
        rows = sum(counts) // 2 + tail
        keep, send = self.call(
            f"{self.name}_halve{label}",
            functools.partial(halve_kernel, self.dims, step, counts),
            [shape(rows, WIDTH)] * 2,
            [VMEM] * len(sources),
            [VMEM] * 2,
        )(*sources)
        return keep, exchange(send, self.dims, step)

    def first(self, part):
        keep, recv = self.sources[part]
        count = PART_ROWS[part]
        tail = keep.shape[0] - count
        self.sources[part] = self.halve(0, f"0{part}", [count], tail, [keep, recv])

    def run_joint(self):
        counts = [PART_ROWS[part] // 2 for part in "ma"]
        sources = self.sources["m"] + self.sources["a"]
        keep, recv = self.halve(1, "1", counts, VECS, sources)
        yield
        count = sum(counts) // 2
        keep, recv = self.halve(2, "2", [count], VECS, [keep, recv])
        yield
        count //= 2
        (own,) = self.call(
            f"{self.name}_sum",
            functools.partial(sum_kernel, count),
            [shape(count + VECS, WIDTH)],
            [VMEM] * 2,
            [VMEM],
        )(keep, recv)
        recv = exchange(own, self.dims, 3)
        yield
        whole, self.sums = self.call(
            f"{self.name}_total",
            functools.partial(total_kernel, count),
            [shape(count, WIDTH), shape(VECS, WIDTH, dtype=F32)],
            [VMEM] * 2,
            [VMEM] * 2,
        )(own, recv)
        recv = exchange(whole, self.dims, 2)
        yield
        (whole,) = self.join(2, [count], whole, recv)
        recv = exchange(whole, self.dims, 1)
        yield
        wholes = self.join(1, [n // 2 for n in counts], whole, recv)
        for part, whole in zip("ma", wholes):
            self.wholes[part] = (whole, exchange(whole, self.dims, 0))
        yield

    def join(self, step, counts, own, recv):
        return self.call(
            f"{self.name}_join{step}",
            functools.partial(join_kernel, self.dims, step, counts),
            [shape(2 * count, WIDTH) for count in counts],
            [VMEM] * 2,
            [VMEM] * len(counts),
        )(own, recv)

    def last(self, part):
        own, recv = self.wholes[part]
        (self.wholes[part],) = self.join(0, [own.shape[0]], own, recv)

    def last_sorted(self, part, other):
        own, recv = self.wholes[part]
        mine, send = self.call(
            f"{self.name}_last_{part}",
            functools.partial(last_join_kernel, self.dims),
            [shape(PART_ROWS[part], WIDTH)] * 2,
            [VMEM] * 3,
            [VMEM] * 2,
            [pltpu.VMEM((PART_ROWS[part], WIDTH), BF16)],
        )(own, recv, other.wholes[part])
        return mine, swap(send)


class PlainReduction(Reduction):
    def first(self, part):
        keep, recv = self.sources[part]
        total = lax.psum(keep.astype(F32) + recv.astype(F32), "dp")
        self.wholes[part] = total[: PART_ROWS[part]].astype(BF16)
        self.sums = total[PART_ROWS[part] :]

    def run_joint(self):
        yield from [None] * 6

    def last(self, part):
        pass

    def last_sorted(self, part, other):
        leading = lax.axis_index("section") == 0
        pair = (self.wholes[part], other.wholes[part])
        return jnp.where(leading, *pair), swap(jnp.where(leading, *pair[::-1]))


def swap(values_in):
    return lax.ppermute(values_in, "section", [(0, 1), (1, 0)])


def on_device(dp_size, global_ends, local_ends, global_live, local_live, *weights):
    (
        ln1_gain, ln1_bias, qkv_weight, query_bias, value_bias, proj_weight, proj_bias,
        ln2_gain, ln2_bias, fc1_weight, fc1_bias, fc2_weight, fc2_bias,
    ) = weights
    matrices = tuple(w[0] for w in (qkv_weight, proj_weight, fc1_weight, fc2_weight))
    got = tuple(swap(w) for w in matrices)
    vectors = (
        ln1_gain, ln1_bias, query_bias, value_bias, proj_bias, ln2_gain, ln2_bias, fc2_bias,
        fc1_bias,
    )
    flags = jnp.concatenate([global_live, local_live]).astype(F32)
    tail = jnp.concatenate(
        [vector.reshape(-1, WIDTH).astype(F32) for vector in vectors]
        + [jnp.pad(flags, (0, WIDTH - flags.shape[0]))[None]]
    )
    tail = jnp.pad(tail, ((0, VECS - tail.shape[0]), (0, 0)))
    call = Ordered()
    keep, send = call(
        "pack",
        pack_kernel,
        [shape(ROWS + VECS, WIDTH)] * 2,
        [VMEM] * 3,
        [VMEM] * 2,
        [pltpu.VMEM((ROWS, WIDTH), F32)],
        cost=PACK_COST,
    )(global_ends[0], local_ends[0], tail)
    recv = swap(send)
    weight_shapes = [(WIDTH, 3 * WIDTH), (WIDTH, WIDTH), (WIDTH, FF), (FF, WIDTH)]
    rows_low, rows_wide = shape(ROWS, WIDTH), shape(ROWS, WIDTH, dtype=F32)
    sums_shape = shape(VECS, WIDTH, dtype=F32)
    mlp_pair = [shape(4 * WIDTH, WIDTH)] * 2
    attention_pair = [shape(2 * WIDTH + VECS, WIDTH)] * 2
    outs = (
        [shape(2, ROWS + VECS, WIDTH)]
        + [shape(2, *dims) for dims in weight_shapes]
        + [
            shape(2, VECS, WIDTH, dtype=F32),
            rows_low,
            shape(2, ROWS, WIDTH),
            shape(2, ROWS, 3 * WIDTH),
            shape(2, 12, SEQ, SEQ),
            shape(2, ROWS, WIDTH),
            shape(2, ROWS, WIDTH, dtype=F32),
            shape(2, ROWS, WIDTH),
            shape(2, ROWS, FF),
            shape(2, ROWS, FF),
            rows_low,
            rows_wide,
            rows_low,
            sums_shape,
        ]
        + mlp_pair
    )
    (
        pack, qkv_w, proj_w, fc1_w, fc2_w, vec, between,
        n1, qkv, probs, mixed, middle, n2, slope, active, result,
        dmid, da, sums, keep_1, send_1,
    ) = call(
        "forward",
        forward_kernel,
        outs,
        [HBM] * 10,
        [VMEM] * len(outs),
        [
            pltpu.VMEM((2, SEQ, SEQ), F32),
            pltpu.VMEM((ROWS, FF), BF16),
            pltpu.SemaphoreType.DMA((2, 5)),
        ],
        vmem=KA_VMEM,
    )(keep, recv, *matrices, *got)
    reduction = Reduction if dp_size == 16 else PlainReduction
    layer_a = reduction("a", call, DIMS_A)
    layer_b = reduction("b", call, DIMS_B)
    layer_b.add("m", keep_1, send_1)
    wide_work = [pltpu.VMEM((ROWS, 3 * WIDTH), BF16), pltpu.VMEM((VECS, WIDTH), F32)]
    held = {}

    def back_b_attention():
        held["dx"], keep, send = call(
            "back_b_attention",
            functools.partial(attention_backward_kernel, 1),
            [rows_low] + attention_pair,
            [VMEM] * 11,
            [VMEM] * 3,
            wide_work,
            vmem=KB_VMEM,
        )(between, vec, qkv_w, proj_w, n1, qkv, probs, mixed, dmid, da, sums)
        layer_b.add("a", keep, send)

    def back_a_mlp():
        *held["mlp"], keep, send = call(
            "back_a_mlp",
            mlp_backward_kernel,
            [rows_wide, rows_low, sums_shape] + mlp_pair,
            [VMEM] * 8,
            [VMEM] * 5,
            [pltpu.VMEM((ROWS, FF), BF16)],
            vmem=KB_VMEM,
        )(vec, fc1_w, fc2_w, middle, n2, slope, active, held["dx"])
        layer_a.add("m", keep, send)

    def back_a_attention():
        held["rows"], rows_send, keep, send = call(
            "back_a_attention",
            last_backward_kernel,
            [rows_low] * 2 + attention_pair,
            [VMEM] * 12,
            [VMEM] * 4,
            wide_work + [pltpu.VMEM((ROWS, WIDTH), BF16)],
            vmem=KB_VMEM,
        )(pack, vec, qkv_w, proj_w, n1, qkv, probs, mixed, *held["mlp"], result)
        layer_a.add("a", keep, send)
        held["rows_got"] = swap(rows_send)

    def rows_out():
        held["rows_out"] = call(
            "rows_out",
            rows_kernel,
            [shape(*global_ends.shape[1:]), shape(*local_ends.shape[1:])],
            [VMEM] * 3,
            [VMEM] * 2,
            [pltpu.VMEM((ROWS, WIDTH), F32)],
        )(vec, held["rows"], held["rows_got"])

    def grad(w):
        return shape(*w.shape, dtype=F32)

    def last_sorted(part):
        held[part] = layer_a.last_sorted(part, layer_b)

    def mlp_out():
        held["mlp_out"] = call(
            "mlp_out",
            mlp_out_kernel,
            [grad(fc1_weight), grad(fc2_weight)],
            [VMEM] * 2,
            [ANY] * 2,
            [pltpu.VMEM((8, WIDTH, WIDTH), F32), pltpu.SemaphoreType.DMA((8,))],
            vmem=16,
        )(*held["m"])

    def attention_out():
        wanted = (
            ln1_gain, ln1_bias, qkv_weight, query_bias, value_bias, proj_weight,
            proj_bias, ln2_gain, ln2_bias, fc1_bias, fc2_bias,
        )
        held["attention_out"] = call(
            "attention_out",
            attention_out_kernel,
            [grad(w) for w in wanted],
            [VMEM] * 4,
            [ANY if w.ndim == 3 else VMEM for w in wanted],
            [pltpu.VMEM((4, WIDTH, WIDTH), F32), pltpu.SemaphoreType.DMA((4,))],
        )(*held["a"], layer_a.sums, layer_b.sums)

    actions = {
        "b": back_b_attention, "c": back_a_mlp, "d": back_a_attention,
        "r": rows_out, "p": mlp_out, "q": attention_out,
        "1": lambda: layer_b.first("m"), "2": lambda: layer_b.first("a"),
        "3": lambda: layer_a.first("m"), "4": lambda: layer_a.first("a"),
        "j": lambda: next(layer_b.joint), "J": lambda: next(layer_a.joint),
        "5": lambda: layer_b.last("m"), "6": lambda: layer_b.last("a"),
        "7": lambda: last_sorted("m"), "8": lambda: last_sorted("a"),
    }
    for name in ORDER:
        actions[name]()
    global_out, local_out = held["rows_out"]
    grad_fc1, grad_fc2 = held["mlp_out"]
    (
        grad_ln1_gain, grad_ln1_bias, grad_qkv, grad_query_bias, grad_value_bias, grad_proj,
        grad_proj_bias, grad_ln2_gain, grad_ln2_bias, grad_fc1_bias, grad_fc2_bias,
    ) = held["attention_out"]
    return (
        global_out[None], local_out[None],
        grad_ln1_gain, grad_ln1_bias, grad_qkv, grad_query_bias, grad_value_bias, grad_proj,
        grad_proj_bias, grad_ln2_gain, grad_ln2_bias, grad_fc1, grad_fc1_bias, grad_fc2,
        grad_fc2_bias,
    )


def solution(mesh):
    matrix, vector = P("section", None, None), P("section", None)
    weights = (
        vector, vector, matrix, vector, vector, matrix, vector,
        vector, vector, matrix, vector, matrix, vector,
    )
    rows = P("section", "dp", None, None)
    return jax.shard_map(
        functools.partial(on_device, mesh.shape["dp"]),
        mesh=mesh,
        in_specs=(rows, rows, P("dp"), P("dp")) + weights,
        out_specs=(rows, rows) + weights,
        check_vma=False,
    )
```

time: 196 us -> 144 us (0.73)
  Pallas kernels: 86.2 us -> 48.6 us
  starting transfers between devices: 44 us -> 27.5 us
  waiting for transfers between devices: 42.6 us -> 58.6 us
  local copies, waits for them, and re-layouts: 21.1 us -> 6.99 us
    pallas_call x19 -> x28, Pallas kernels: 86.2 us -> 48.6 us  [run(): pl.pallas_call(body, out_shape=outs, name=name, in_specs=list(in_specs) +...]
    ppermute x22 -> x18, waiting for transfers between devices: 32.2 us -> 56.2 us  [exchange(): return lax.ppermute(values_in, ('section', 'dp'), pairs)]
    ppermute x22 -> x18, starting transfers between devices: 40.8 us -> 24.3 us  [exchange(): return lax.ppermute(values_in, ('section', 'dp'), pairs)]
    unnamed x66 -> x16, local copies, waits for them, and re-layouts: 21.1 us -> 6.12 us
    ppermute x8 -> x12, waiting for transfers between devices: 10.4 us -> 2.35 us  [swap(): return lax.ppermute(values_in, 'section', [(0, 1), (1, 0)])]
  transfers between devices with their start and end apart: 30 -> 30, of which waited for: 12 -> 16; matrix products, arithmetic and copies ran while one was open for 2% -> 3% of each run, Pallas kernels for 20% -> 18%
where the time goes in v2:
time: 144 us
  waiting for transfers between devices  58.6 us (41%)
  Pallas kernels  48.6 us (34%)
  starting transfers between devices  27.5 us (19%)
  local copies, waits for them, and re-layouts  6.99 us (5%)
  other arithmetic  1.46 us (1%)
    ppermute x18, waiting for transfers between devices, exchange(): return lax.ppermute(values_in, ('section', 'dp'), pairs)  56.2 us
    pallas_call x28, Pallas kernels, run(): pl.pallas_call(body, out_shape=outs, name=name, in_specs=list(in_specs) +...  48.6 us
    ppermute x18, starting transfers between devices, exchange(): return lax.ppermute(values_in, ('section', 'dp'), pairs)  24.3 us
    unnamed x16, local copies, waits for them, and re-layouts  6.12 us
    ppermute x12, starting transfers between devices, swap(): return lax.ppermute(values_in, 'section', [(0, 1), (1, 0)])  3.13 us
  transfers between devices with their start and end apart: 30, of which 16 were waited for; matrix products, arithmetic and copies ran while one was open for 3% of the time, Pallas kernels for 18%

profile of v2, /device:TPU:0, one launch (start us, length us, event | category | flops | bytes accessed | tf_op | source)
XLA Modules:
  0.0 144.1 jit_solution(284529106239397692)
XLA Ops:
  7.0 1.5 %collective-permute-done.2.refs_7_ = bf16[384,384]{1,0:T(8,128)(2,1)S(1)} collective-permute-done((bf16[384,384]{1,0:T(8,128)(2,1)S(1)}, bf16[384,384]{1,0:T(8,128)(2,1)S(1)}, u32[]{:S(2)}, u32[]{:S(2)}) %collective-permute-start.2) | collective-permute-done | bytes 294944 | tf_op jit(solution)/shard_map/ppermute | solution.py:659
  8.6 20.7 %forward.1 = (bf16[2,432,384]{2,1,0:T(8,128)(2,1)S(1)}, bf16[2,384,1152]{2,1,0:T(8,128)(2,1)S(1)}, bf16[2,384,384]{2,1,0:T(8,128)(2,1)S(1)}, bf16[2,384,1536]{2,...) custom-call(bf16[432,384]{1,0:T(8,128)(2,1)S(1)} %get-tuple-element., ...), custom_call_target="tpu_custom_call" | custom-call | flops 10000000000 | tf_op jit(solution)/shard_map/forward/pallas_call | solution.py:446
  29.5 6.5 %back_b_attention.1 = (bf16[416,384]{1,0:T(8,128)(2,1)S(1)}, bf16[784,384]{1,0:T(8,128)(2,1)S(1)}, bf16[784,384]{1,0:T(8,128)(2,1)S(1)}) custom-call(bf16[416,384]{1,0:T(8,128)(2,1)S(1)} %get-tuple-element.109.refs_0_, f32[2,16,384]{2,1,0:T(8,128)S(1)} %get-tuple-element.95.refs_1_.refs_0_, bf16[2,384,1152]{2,1,0:T(8,128)(2,1)S(1)} %get-tuple-element.97.refs_2_, ...), custom_call_target="tpu_custom_call" | custom-call | flops 10000000000 | tf_op jit(solution)/shard_map/back_b_attention/pallas_call | solution.py:446
  36.9 2.7 %collective-permute-start.8 = (bf16[768,384]{1,0:T(8,128)(2,1)S(1)}, bf16[768,384]{1,0:T(8,128)(2,1)S(1)}, u32[]{:S(2)}, u32[]{:S(2)}) collective-permute-start(bf16[768,384]{1,0:T(8,128)(2,1)S(1)} %get-tuple-element.117.refs_8_), channel_id=1, source_target_pairs={{0,1},{1,0},{2,3},{3,2},{4,5},{5,4},{6,7},{7,6},{8,9},{9,8},{10,11... | collective-permute-start | bytes 1769480 | tf_op jit(solution)/shard_map/ppermute | solution.py:549
  39.6 5.9 %back_a_mlp.1 = (f32[416,384]{1,0:T(8,128)S(1)}, bf16[416,384]{1,0:T(8,128)(2,1)S(1)}, f32[16,384]{1,0:T(8,128)S(1)}, bf16[1536,384]{1,0:T(8,128)(2,1)S(1)}, bf16[1536,384]{1,0:T(8,128)(2,1)S(1)}) custom-call(f32[2,16,384]{2,1,0:T(8,128)S(1)} %get-tuple-element.95.refs_1_.refs_0_, bf16[2,384,1536]{2,1,0:T(8,128)(2,1)S(1)} %get-tuple-element.103.refs_1_, ...), custom_call_target="tpu_custom_call" | custom-call | flops 10000000000 | tf_op jit(solution)/shard_map/back_a_mlp/pallas_call | solution.py:446
  45.9 1.6 %collective-permute-start.9 = (bf16[400,384]{1,0:T(8,128)(2,1)S(1)}, bf16[400,384]{1,0:T(8,128)(2,1)S(1)}, u32[]{:S(2)}, u32[]{:S(2)}) collective-permute-start(bf16[400,384]{1,0:T(8,128)(2,1)S(1)} %get-tuple-element.124.refs_12_), channel_id=1, source_target_pairs={{0,1},{1,0},{2,3},{3,2},{4,5},{5,4},{6,7},{7,6},{8,9},{9,8},{10,11... | collective-permute-start | bytes 921608 | tf_op jit(solution)/shard_map/ppermute | solution.py:549
  47.5 6.4 %back_a_attention.1 = (bf16[416,384]{1,0:T(8,128)(2,1)S(1)}, bf16[416,384]{1,0:T(8,128)(2,1)S(1)}, bf16[784,384]{1,0:T(8,128)(2,1)S(1)}, bf16[784,384]{1,0:T(8,128)(2,1)S(1)}) custom-call(bf16[2,432,384]{2,1,0:T(8,128)(2,1)S(1)} %get-tuple-element.96.refs_0_, f32[2,16,384]{2,1,0:T(8,128)S(1)} %get-tuple-element.95.refs_1_.refs_0_, ...), custom_call_target="tpu_custom_call" | custom-call | flops 10000000000 | tf_op jit(solution)/shard_map/back_a_attention/pallas_call | solution.py:446
  55.8 1.5 %collective-permute-start.11 = (bf16[592,384]{1,0:T(8,128)(2,1)S(1)}, bf16[592,384]{1,0:T(8,128)(2,1)S(1)}, u32[]{:S(2)}, u32[]{:S(2)}) collective-permute-start(bf16[592,384]{1,0:T(8,128)(2,1)S(1)} %get-tuple-element.133.refs_2_), channel_id=1, source_target_pairs={{0,2},{1,3},{2,0},{3,1},{4,6},{5,7},{6,4},{7,5},{8,10},{9,11},{10,... | collective-permute-start | bytes 1363976 | tf_op jit(solution)/shard_map/ppermute | solution.py:549
  58.1 11.1 %collective-permute-done.11.refs_1_ = bf16[592,384]{1,0:T(8,128)(2,1)S(1)} collective-permute-done((bf16[592,384]{1,0:T(8,128)(2,1)S(1)}, bf16[592,384]{1,0:T(8,128)(2,1)S(1)}, u32[]{:S(2)}, u32[]{:S(2)}) %collective-permute-start.11) | collective-permute-done | bytes 454688 | tf_op jit(solution)/shard_map/ppermute | solution.py:549
  69.4 1.6 %collective-permute-start.13 = (bf16[304,384]{1,0:T(8,128)(2,1)S(1)}, bf16[304,384]{1,0:T(8,128)(2,1)S(1)}, u32[]{:S(2)}, u32[]{:S(2)}) collective-permute-start(bf16[304,384]{1,0:T(8,128)(2,1)S(1)} %get-tuple-element.137.refs_4_), channel_id=1, source_target_pairs={{0,4},{1,5},{2,6},{3,7},{4,0},{5,1},{6,2},{7,3},{8,12},{9,13},{10,... | collective-permute-start | bytes 700424 | tf_op jit(solution)/shard_map/ppermute | solution.py:549
  71.0 1.7 %collective-permute-done.15.refs_3_ = bf16[400,384]{1,0:T(8,128)(2,1)S(1)} collective-permute-done((bf16[400,384]{1,0:T(8,128)(2,1)S(1)}, bf16[400,384]{1,0:T(8,128)(2,1)S(1)}, u32[]{:S(2)}, u32[]{:S(2)}) %collective-permute-start.15) | collective-permute-done | bytes 307232 | tf_op jit(solution)/shard_map/ppermute | solution.py:549
  73.9 1.9 %collective-permute-done.13.refs_1_ = bf16[304,384]{1,0:T(8,128)(2,1)S(1)} collective-permute-done((bf16[304,384]{1,0:T(8,128)(2,1)S(1)}, bf16[304,384]{1,0:T(8,128)(2,1)S(1)}, u32[]{:S(2)}, u32[]{:S(2)}) %collective-permute-start.13) | collective-permute-done | bytes 233504 | tf_op jit(solution)/shard_map/ppermute | solution.py:549
  75.9 2.6 %collective-permute-start.16 = (bf16[304,384]{1,0:T(8,128)(2,1)S(1)}, bf16[304,384]{1,0:T(8,128)(2,1)S(1)}, u32[]{:S(2)}, u32[]{:S(2)}) collective-permute-start(bf16[304,384]{1,0:T(8,128)(2,1)S(1)} %b_sum.1.refs_2_.refs_0_), channel_id=1, source_target_pairs={{0,8},{1,9},{2,10},{3,11},{4,12},{5,13},{6,14},{7,15},{8,0},{9,1},... | collective-permute-start | bytes 700424 | tf_op jit(solution)/shard_map/ppermute | solution.py:549
  78.5 3.1 %collective-permute-done.17.refs_1_ = bf16[592,384]{1,0:T(8,128)(2,1)S(1)} collective-permute-done((bf16[592,384]{1,0:T(8,128)(2,1)S(1)}, bf16[592,384]{1,0:T(8,128)(2,1)S(1)}, u32[]{:S(2)}, u32[]{:S(2)}) %collective-permute-start.17) | collective-permute-done | bytes 454688 | tf_op jit(solution)/shard_map/ppermute | solution.py:549
  81.8 1.6 %collective-permute-start.19 = (bf16[304,384]{1,0:T(8,128)(2,1)S(1)}, bf16[304,384]{1,0:T(8,128)(2,1)S(1)}, u32[]{:S(2)}, u32[]{:S(2)}) collective-permute-start(bf16[304,384]{1,0:T(8,128)(2,1)S(1)} %get-tuple-element.142.refs_2_), channel_id=1, source_target_pairs={{0,4},{1,5},{2,6},{3,7},{4,0},{5,1},{6,2},{7,3},{8,12},{9,13},{10,... | collective-permute-start | bytes 700424 | tf_op jit(solution)/shard_map/ppermute | solution.py:549
  83.4 3.9 %collective-permute-done.16.refs_1_ = bf16[304,384]{1,0:T(8,128)(2,1)S(1)} collective-permute-done((bf16[304,384]{1,0:T(8,128)(2,1)S(1)}, bf16[304,384]{1,0:T(8,128)(2,1)S(1)}, u32[]{:S(2)}, u32[]{:S(2)}) %collective-permute-start.16) | collective-permute-done | bytes 233504 | tf_op jit(solution)/shard_map/ppermute | solution.py:549
  88.1 4.3 %collective-permute-done.19.refs_1_ = bf16[304,384]{1,0:T(8,128)(2,1)S(1)} collective-permute-done((bf16[304,384]{1,0:T(8,128)(2,1)S(1)}, bf16[304,384]{1,0:T(8,128)(2,1)S(1)}, u32[]{:S(2)}, u32[]{:S(2)}) %collective-permute-start.19) | collective-permute-done | bytes 233504 | tf_op jit(solution)/shard_map/ppermute | solution.py:549
  92.5 1.5 %collective-permute-start.20 = (bf16[304,384]{1,0:T(8,128)(2,1)S(1)}, bf16[304,384]{1,0:T(8,128)(2,1)S(1)}, u32[]{:S(2)}, u32[]{:S(2)}) collective-permute-start(bf16[304,384]{1,0:T(8,128)(2,1)S(1)} %a_sum.1.refs_2_.refs_0_), channel_id=1, source_target_pairs={{0,8},{1,9},{2,10},{3,11},{4,12},{5,13},{6,14},{7,15},{8,0},{9,1},... | collective-permute-start | bytes 700424 | tf_op jit(solution)/shard_map/ppermute | solution.py:549
  94.0 4.0 %collective-permute-done.18.refs_1_ = bf16[288,384]{1,0:T(8,128)(2,1)S(1)} collective-permute-done((bf16[288,384]{1,0:T(8,128)(2,1)S(1)}, bf16[288,384]{1,0:T(8,128)(2,1)S(1)}, u32[]{:S(2)}, u32[]{:S(2)}) %collective-permute-start.18) | collective-permute-done | bytes 221216 | tf_op jit(solution)/shard_map/ppermute | solution.py:549
  98.1 2.2 %collective-permute-start.22 = (bf16[576,384]{1,0:T(8,128)(2,1)S(1)}, bf16[576,384]{1,0:T(8,128)(2,1)S(1)}, u32[]{:S(2)}, u32[]{:S(2)}) collective-permute-start(bf16[576,384]{1,0:T(8,128)(2,1)S(1)} %b_join2.1.refs_3_.refs_0_), channel_id=1, source_target_pairs={{0,2},{1,3},{2,0},{3,1},{4,6},{5,7},{6,4},{7,5},{8,10},{9,11},{10,... | collective-permute-start | bytes 1327112 | tf_op jit(solution)/shard_map/ppermute | solution.py:549
  101.2 3.7 %collective-permute-done.20.refs_1_ = bf16[304,384]{1,0:T(8,128)(2,1)S(1)} collective-permute-done((bf16[304,384]{1,0:T(8,128)(2,1)S(1)}, bf16[304,384]{1,0:T(8,128)(2,1)S(1)}, u32[]{:S(2)}, u32[]{:S(2)}) %collective-permute-start.20) | collective-permute-done | bytes 233504 | tf_op jit(solution)/shard_map/ppermute | solution.py:549
  106.7 1.4 collective-permute-start.24
  108.1 4.2 %collective-permute-done.21.refs_1_ = bf16[288,384]{1,0:T(8,128)(2,1)S(1)} collective-permute-done((bf16[288,384]{1,0:T(8,128)(2,1)S(1)}, bf16[288,384]{1,0:T(8,128)(2,1)S(1)}, u32[]{:S(2)}, u32[]{:S(2)}) %collective-permute-start.21) | collective-permute-done | bytes 221216 | tf_op jit(solution)/shard_map/ppermute | solution.py:549
  112.8 7.1 %collective-permute-done.24.refs_1_ = bf16[768,384]{1,0:T(8,128)(2,1)S(1)} collective-permute-done((bf16[768,384]{1,0:T(8,128)(2,1)S(1)}, bf16[768,384]{1,0:T(8,128)(2,1)S(1)}, u32[]{:S(2)}, u32[]{:S(2)}) %collective-permute-start.24) | collective-permute-done | bytes 589856 | tf_op jit(solution)/shard_map/ppermute | solution.py:549
  120.8 1.7 %collective-permute-start.27 = (bf16[768,384]{1,0:T(8,128)(2,1)S(1)}, bf16[768,384]{1,0:T(8,128)(2,1)S(1)}, u32[]{:S(2)}, u32[]{:S(2)}) collective-permute-start(bf16[768,384]{1,0:T(8,128)(2,1)S(1)} %get-tuple-element.153.refs_0_), channel_id=1, source_target_pairs={{0,1},{1,0},{2,3},{3,2},{4,5},{5,4},{6,7},{7,6},{8,9},{9,8},{10,11... | collective-permute-start | bytes 1769480 | tf_op jit(solution)/shard_map/ppermute | solution.py:549
  122.9 7.9 %collective-permute-done.27.refs_1_ = bf16[768,384]{1,0:T(8,128)(2,1)S(1)} collective-permute-done((bf16[768,384]{1,0:T(8,128)(2,1)S(1)}, bf16[768,384]{1,0:T(8,128)(2,1)S(1)}, u32[]{:S(2)}, u32[]{:S(2)}) %collective-permute-start.27) | collective-permute-done | bytes 589856 | tf_op jit(solution)/shard_map/ppermute | solution.py:549
  131.2 1.6 %collective-permute-start.25 = (bf16[384,384]{1,0:T(8,128)(2,1)S(1)}, bf16[384,384]{1,0:T(8,128)(2,1)S(1)}, u32[]{:S(2)}, u32[]{:S(2)}) collective-permute-start(bf16[384,384]{1,0:T(8,128)(2,1)S(1)} %get-tuple-element.152.refs_3_.refs_0_), channel_id=1, source_target_pairs={{0,1},{1,0},{2,3},{3,2},{4,5},{5,4},{6,7},{7,6},{8,9},{9,8},{10,11... | collective-permute-start | bytes 884744 | tf_op jit(solution)/shard_map/ppermute | solution.py:549
  132.9 1.0 collective-permute-done.26.refs_1_
  134.0 2.3 %mlp_out.1 = (f32[1,384,1536]{2,1,0:T(8,128)}, f32[1,1536,384]{2,1,0:T(8,128)}) custom-call(bf16[1536,384]{1,0:T(8,128)(2,1)S(1)} %get-tuple-element.155.refs_0_, bf16[1536,384]{1,0:T(8,128)(2,1)S(1)} %collective-permute-done.28.refs_1_, bf16[768,384]{1,0:T(8,128)(2,1)S(1)} %b_join0.3.refs_2_), custom_call_target="tpu_custom_call" | custom-call | flops 10000000000 | tf_op jit(solution)/shard_map/mlp_out/pallas_call | solution.py:446
  136.3 1.7 %collective-permute-done.25.refs_1_ = bf16[384,384]{1,0:T(8,128)(2,1)S(1)} collective-permute-done((bf16[384,384]{1,0:T(8,128)(2,1)S(1)}, bf16[384,384]{1,0:T(8,128)(2,1)S(1)}, u32[]{:S(2)}, u32[]{:S(2)}) %collective-permute-start.25) | collective-permute-done | bytes 294944 | tf_op jit(solution)/shard_map/ppermute | solution.py:549
  138.0 1.7 %copy-done.5 = f32[1,1536,384]{2,1,0:T(8,128)S(1)} copy-done((f32[1,1536,384]{2,1,0:T(8,128)S(1)}, f32[1,1536,384]{2,1,0:T(8,128)}, u32[]{:S(2)}) %copy-start.5) | copy-done | bytes 2359320
  141.9 2.1 %attention_out.1 = (f32[1,384]{1,0:T(1,128)}, f32[1,384]{1,0:T(1,128)}, f32[1,384,1152]{2,1,0:T(8,128)}, f32[1,384]{1,0:T(1,128)}, f32[1,384]{1,0:T(1,128)}, /*i...) custom-call(bf16[768,384]{1,0:T(8,128)(2,1)S(1)} %get-tuple-element., ...), custom_call_target="tpu_custom_call" | custom-call | flops 10000000000 | tf_op jit(solution)/shard_map/attention_out/pallas_call | solution.py:446
  (79 shorter events, 20.2 us)
Async XLA Ops:
  0.6 7.9 %collective-permute-start.1 = (bf16[384,1152]{1,0:T(8,128)(2,1)}, bf16[384,1152]{1,0:T(8,128)(2,1)S(1)}, u32[]{:S(2)}, u32[]{:S(2)}) collective-permute-start(bf16[384,1152]{1,0:T(8,128)(2,1)} %bitcast.16), channel_id=1, source_target_pairs={{0,16},{16,0},{1,17},{17,1},{2,18},{18,2},{3,19},{19,3},{4,20},{20... | collective-permute-start | bytes 2654216 | tf_op jit(solution)/shard_map/ppermute | solution.py:659
  1.2 7.4 %collective-permute-start.3 = (bf16[384,1536]{1,0:T(8,128)(2,1)}, bf16[384,1536]{1,0:T(8,128)(2,1)S(1)}, u32[]{:S(2)}, u32[]{:S(2)}) collective-permute-start(bf16[384,1536]{1,0:T(8,128)(2,1)} %bitcast.12), channel_id=1, source_target_pairs={{0,16},{16,0},{1,17},{17,1},{2,18},{18,2},{3,19},{19,3},{4,20},{20... | collective-permute-start | bytes 3538952 | tf_op jit(solution)/shard_map/ppermute | solution.py:659
  1.2 7.3 %collective-permute-start.4 = (bf16[1536,384]{1,0:T(8,128)(2,1)}, bf16[1536,384]{1,0:T(8,128)(2,1)S(1)}, u32[]{:S(2)}, u32[]{:S(2)}) collective-permute-start(bf16[1536,384]{1,0:T(8,128)(2,1)} %bitcast.14), channel_id=1, source_target_pairs={{0,16},{16,0},{1,17},{17,1},{2,18},{18,2},{3,19},{19,3},{4,20},{20... | collective-permute-start | bytes 3538952 | tf_op jit(solution)/shard_map/ppermute | solution.py:659
  6.0 2.6 %copy-start.1 = (bf16[1,1536,384]{2,1,0:T(8,128)(2,1)S(1)}, bf16[1,1536,384]{2,1,0:T(8,128)(2,1)}, u32[]{:S(2)}) copy-start(bf16[1,1536,384]{2,1,0:T(8,128)(2,1)} %param.32) | copy-start | bytes 3538948
  6.0 2.6 %copy-start.2 = (bf16[1,384,1152]{2,1,0:T(8,128)(2,1)S(1)}, bf16[1,384,1152]{2,1,0:T(8,128)(2,1)}, u32[]{:S(2)}) copy-start(bf16[1,384,1152]{2,1,0:T(8,128)(2,1)} %param.23) | copy-start | bytes 2654212
  6.2 2.3 %collective-permute-start = (bf16[432,384]{1,0:T(8,128)(2,1)S(1)}, bf16[432,384]{1,0:T(8,128)(2,1)S(1)}, u32[]{:S(2)}, u32[]{:S(2)}) collective-permute-start(bf16[432,384]{1,0:T(8,128)(2,1)S(1)} %get-tuple-element.94.refs_10_), channel_id=1, source_target_pairs={{0,16},{16,0},{1,17},{17,1},{2,18},{18,2},{3,19},{19,3},{4,20},{20... | collective-permute-start | bytes 995336 | tf_op jit(solution)/shard_map/ppermute | solution.py:659
  7.0 1.6 %collective-permute-start.2 = (bf16[384,384]{1,0:T(8,128)(2,1)S(1)}, bf16[384,384]{1,0:T(8,128)(2,1)S(1)}, u32[]{:S(2)}, u32[]{:S(2)}) collective-permute-start(bf16[384,384]{1,0:T(8,128)(2,1)S(1)} %bitcast.19), channel_id=1, source_target_pairs={{0,16},{16,0},{1,17},{17,1},{2,18},{18,2},{3,19},{19,3},{4,20},{20... | collective-permute-start | bytes 884744 | tf_op jit(solution)/shard_map/ppermute | solution.py:659
  29.3 7.2 %collective-permute-start.5 = (bf16[1536,384]{1,0:T(8,128)(2,1)S(1)}, bf16[1536,384]{1,0:T(8,128)(2,1)S(1)}, u32[]{:S(2)}, u32[]{:S(2)}) collective-permute-start(bf16[1536,384]{1,0:T(8,128)(2,1)S(1)} %get-tuple-element.113.refs_11_), channel_id=1, source_target_pairs={{0,16},{16,0},{1,17},{17,1},{2,18},{18,2},{3,19},{19,3},{4,20},{20... | collective-permute-start | bytes 3538952 | tf_op jit(solution)/shard_map/ppermute | solution.py:659
  36.0 9.7 %collective-permute-start.6 = (bf16[784,384]{1,0:T(8,128)(2,1)S(1)}, bf16[784,384]{1,0:T(8,128)(2,1)S(1)}, u32[]{:S(2)}, u32[]{:S(2)}) collective-permute-start(bf16[784,384]{1,0:T(8,128)(2,1)S(1)} %get-tuple-element.116.refs_2_), channel_id=1, source_target_pairs={{0,16},{16,0},{1,17},{17,1},{2,18},{18,2},{3,19},{19,3},{4,20},{20... | collective-permute-start | bytes 1806344 | tf_op jit(solution)/shard_map/ppermute | solution.py:659
  36.9 18.6 %collective-permute-start.8 = (bf16[768,384]{1,0:T(8,128)(2,1)S(1)}, bf16[768,384]{1,0:T(8,128)(2,1)S(1)}, u32[]{:S(2)}, u32[]{:S(2)}) collective-permute-start(bf16[768,384]{1,0:T(8,128)(2,1)S(1)} %get-tuple-element.117.refs_8_), channel_id=1, source_target_pairs={{0,1},{1,0},{2,3},{3,2},{4,5},{5,4},{6,7},{7,6},{8,9},{9,8},{10,11... | collective-permute-start | bytes 1769480 | tf_op jit(solution)/shard_map/ppermute | solution.py:549
  45.5 8.9 %collective-permute-start.10 = (bf16[1536,384]{1,0:T(8,128)(2,1)S(1)}, bf16[1536,384]{1,0:T(8,128)(2,1)S(1)}, u32[]{:S(2)}, u32[]{:S(2)}) collective-permute-start(bf16[1536,384]{1,0:T(8,128)(2,1)S(1)} %get-tuple-element.123.refs_2_), channel_id=1, source_target_pairs={{0,16},{16,0},{1,17},{17,1},{2,18},{18,2},{3,19},{19,3},{4,20},{20... | collective-permute-start | bytes 3538952 | tf_op jit(solution)/shard_map/ppermute | solution.py:659
  45.9 9.6 %collective-permute-start.9 = (bf16[400,384]{1,0:T(8,128)(2,1)S(1)}, bf16[400,384]{1,0:T(8,128)(2,1)S(1)}, u32[]{:S(2)}, u32[]{:S(2)}) collective-permute-start(bf16[400,384]{1,0:T(8,128)(2,1)S(1)} %get-tuple-element.124.refs_12_), channel_id=1, source_target_pairs={{0,1},{1,0},{2,3},{3,2},{4,5},{5,4},{6,7},{7,6},{8,9},{9,8},{10,11... | collective-permute-start | bytes 921608 | tf_op jit(solution)/shard_map/ppermute | solution.py:549
  53.9 46.4 %collective-permute-start.7 = (bf16[416,384]{1,0:T(8,128)(2,1)S(1)}, bf16[416,384]{1,0:T(8,128)(2,1)S(1)}, u32[]{:S(2)}, u32[]{:S(2)}) collective-permute-start(bf16[416,384]{1,0:T(8,128)(2,1)S(1)} %get-tuple-element.126), channel_id=1, source_target_pairs={{0,16},{16,0},{1,17},{17,1},{2,18},{18,2},{3,19},{19,3},{4,20},{20... | collective-permute-start | bytes 958472 | tf_op jit(solution)/shard_map/ppermute | solution.py:659
  54.1 3.3 %collective-permute-start.12 = (bf16[784,384]{1,0:T(8,128)(2,1)S(1)}, bf16[784,384]{1,0:T(8,128)(2,1)S(1)}, u32[]{:S(2)}, u32[]{:S(2)}) collective-permute-start(bf16[784,384]{1,0:T(8,128)(2,1)S(1)} %get-tuple-element.130.refs_2_), channel_id=1, source_target_pairs={{0,16},{16,0},{1,17},{17,1},{2,18},{18,2},{3,19},{19,3},{4,20},{20... | collective-permute-start | bytes 1806344 | tf_op jit(solution)/shard_map/ppermute | solution.py:659
  54.9 17.9 %collective-permute-start.14 = (bf16[768,384]{1,0:T(8,128)(2,1)S(1)}, bf16[768,384]{1,0:T(8,128)(2,1)S(1)}, u32[]{:S(2)}, u32[]{:S(2)}) collective-permute-start(bf16[768,384]{1,0:T(8,128)(2,1)S(1)} %get-tuple-element.131.refs_4_), channel_id=1, source_target_pairs={{0,1},{1,0},{2,3},{3,2},{4,5},{5,4},{6,7},{7,6},{8,9},{9,8},{10,11... | collective-permute-start | bytes 1769480 | tf_op jit(solution)/shard_map/ppermute | solution.py:549
  55.8 13.4 %collective-permute-start.11 = (bf16[592,384]{1,0:T(8,128)(2,1)S(1)}, bf16[592,384]{1,0:T(8,128)(2,1)S(1)}, u32[]{:S(2)}, u32[]{:S(2)}) collective-permute-start(bf16[592,384]{1,0:T(8,128)(2,1)S(1)} %get-tuple-element.133.refs_2_), channel_id=1, source_target_pairs={{0,2},{1,3},{2,0},{3,1},{4,6},{5,7},{6,4},{7,5},{8,10},{9,11},{10,... | collective-permute-start | bytes 1363976 | tf_op jit(solution)/shard_map/ppermute | solution.py:549
  57.5 15.2 %collective-permute-start.15 = (bf16[400,384]{1,0:T(8,128)(2,1)S(1)}, bf16[400,384]{1,0:T(8,128)(2,1)S(1)}, u32[]{:S(2)}, u32[]{:S(2)}) collective-permute-start(bf16[400,384]{1,0:T(8,128)(2,1)S(1)} %get-tuple-element.135.refs_2_), channel_id=1, source_target_pairs={{0,1},{1,0},{2,3},{3,2},{4,5},{5,4},{6,7},{7,6},{8,9},{9,8},{10,11... | collective-permute-start | bytes 921608 | tf_op jit(solution)/shard_map/ppermute | solution.py:549
  69.4 6.4 %collective-permute-start.13 = (bf16[304,384]{1,0:T(8,128)(2,1)S(1)}, bf16[304,384]{1,0:T(8,128)(2,1)S(1)}, u32[]{:S(2)}, u32[]{:S(2)}) collective-permute-start(bf16[304,384]{1,0:T(8,128)(2,1)S(1)} %get-tuple-element.137.refs_4_), channel_id=1, source_target_pairs={{0,4},{1,5},{2,6},{3,7},{4,0},{5,1},{6,2},{7,3},{8,12},{9,13},{10,... | collective-permute-start | bytes 700424 | tf_op jit(solution)/shard_map/ppermute | solution.py:549
  73.1 8.5 %collective-permute-start.17 = (bf16[592,384]{1,0:T(8,128)(2,1)S(1)}, bf16[592,384]{1,0:T(8,128)(2,1)S(1)}, u32[]{:S(2)}, u32[]{:S(2)}) collective-permute-start(bf16[592,384]{1,0:T(8,128)(2,1)S(1)} %get-tuple-element.140.refs_2_), channel_id=1, source_target_pairs={{0,2},{1,3},{2,0},{3,1},{4,6},{5,7},{6,4},{7,5},{8,10},{9,11},{10,... | collective-permute-start | bytes 1363976 | tf_op jit(solution)/shard_map/ppermute | solution.py:549
  75.9 11.5 %collective-permute-start.16 = (bf16[304,384]{1,0:T(8,128)(2,1)S(1)}, bf16[304,384]{1,0:T(8,128)(2,1)S(1)}, u32[]{:S(2)}, u32[]{:S(2)}) collective-permute-start(bf16[304,384]{1,0:T(8,128)(2,1)S(1)} %b_sum.1.refs_2_.refs_0_), channel_id=1, source_target_pairs={{0,8},{1,9},{2,10},{3,11},{4,12},{5,13},{6,14},{7,15},{8,0},{9,1},... | collective-permute-start | bytes 700424 | tf_op jit(solution)/shard_map/ppermute | solution.py:549
  81.8 10.6 %collective-permute-start.19 = (bf16[304,384]{1,0:T(8,128)(2,1)S(1)}, bf16[304,384]{1,0:T(8,128)(2,1)S(1)}, u32[]{:S(2)}, u32[]{:S(2)}) collective-permute-start(bf16[304,384]{1,0:T(8,128)(2,1)S(1)} %get-tuple-element.142.refs_2_), channel_id=1, source_target_pairs={{0,4},{1,5},{2,6},{3,7},{4,0},{5,1},{6,2},{7,3},{8,12},{9,13},{10,... | collective-permute-start | bytes 700424 | tf_op jit(solution)/shard_map/ppermute | solution.py:549
  87.4 10.6 %collective-permute-start.18 = (bf16[288,384]{1,0:T(8,128)(2,1)S(1)}, bf16[288,384]{1,0:T(8,128)(2,1)S(1)}, u32[]{:S(2)}, u32[]{:S(2)}) collective-permute-start(bf16[288,384]{1,0:T(8,128)(2,1)S(1)} %get-tuple-element.143.refs_0_), channel_id=1, source_target_pairs={{0,4},{1,5},{2,6},{3,7},{4,0},{5,1},{6,2},{7,3},{8,12},{9,13},{10,... | collective-permute-start | bytes 663560 | tf_op jit(solution)/shard_map/ppermute | solution.py:549
  92.5 12.4 %collective-permute-start.20 = (bf16[304,384]{1,0:T(8,128)(2,1)S(1)}, bf16[304,384]{1,0:T(8,128)(2,1)S(1)}, u32[]{:S(2)}, u32[]{:S(2)}) collective-permute-start(bf16[304,384]{1,0:T(8,128)(2,1)S(1)} %a_sum.1.refs_2_.refs_0_), channel_id=1, source_target_pairs={{0,8},{1,9},{2,10},{3,11},{4,12},{5,13},{6,14},{7,15},{8,0},{9,1},... | collective-permute-start | bytes 700424 | tf_op jit(solution)/shard_map/ppermute | solution.py:549
  98.1 8.6 %collective-permute-start.22 = (bf16[576,384]{1,0:T(8,128)(2,1)S(1)}, bf16[576,384]{1,0:T(8,128)(2,1)S(1)}, u32[]{:S(2)}, u32[]{:S(2)}) collective-permute-start(bf16[576,384]{1,0:T(8,128)(2,1)S(1)} %b_join2.1.refs_3_.refs_0_), channel_id=1, source_target_pairs={{0,2},{1,3},{2,0},{3,1},{4,6},{5,7},{6,4},{7,5},{8,10},{9,11},{10,... | collective-permute-start | bytes 1327112 | tf_op jit(solution)/shard_map/ppermute | solution.py:549
  105.9 6.4 %collective-permute-start.21 = (bf16[288,384]{1,0:T(8,128)(2,1)S(1)}, bf16[288,384]{1,0:T(8,128)(2,1)S(1)}, u32[]{:S(2)}, u32[]{:S(2)}) collective-permute-start(bf16[288,384]{1,0:T(8,128)(2,1)S(1)} %get-tuple-element.148.refs_0_), channel_id=1, source_target_pairs={{0,4},{1,5},{2,6},{3,7},{4,0},{5,1},{6,2},{7,3},{8,12},{9,13},{10,... | collective-permute-start | bytes 663560 | tf_op jit(solution)/shard_map/ppermute | solution.py:549
  106.7 13.2 %collective-permute-start.24 = (bf16[768,384]{1,0:T(8,128)(2,1)S(1)}, bf16[768,384]{1,0:T(8,128)(2,1)S(1)}, u32[]{:S(2)}, u32[]{:S(2)}) collective-permute-start(bf16[768,384]{1,0:T(8,128)(2,1)S(1)} %get-tuple-element.151.refs_0_), channel_id=1, source_target_pairs={{0,1},{1,0},{2,3},{3,2},{4,5},{5,4},{6,7},{7,6},{8,9},{9,8},{10,11... | collective-permute-start | bytes 1769480 | tf_op jit(solution)/shard_map/ppermute | solution.py:549
  112.3 8.4 %collective-permute-start.23 = (bf16[576,384]{1,0:T(8,128)(2,1)S(1)}, bf16[576,384]{1,0:T(8,128)(2,1)S(1)}, u32[]{:S(2)}, u32[]{:S(2)}) collective-permute-start(bf16[576,384]{1,0:T(8,128)(2,1)S(1)} %a_join2.1.refs_2_.refs_0_), channel_id=1, source_target_pairs={{0,2},{1,3},{2,0},{3,1},{4,6},{5,7},{6,4},{7,5},{8,10},{9,11},{10,... | collective-permute-start | bytes 1327112 | tf_op jit(solution)/shard_map/ppermute | solution.py:549
  120.8 9.9 %collective-permute-start.27 = (bf16[768,384]{1,0:T(8,128)(2,1)S(1)}, bf16[768,384]{1,0:T(8,128)(2,1)S(1)}, u32[]{:S(2)}, u32[]{:S(2)}) collective-permute-start(bf16[768,384]{1,0:T(8,128)(2,1)S(1)} %get-tuple-element.153.refs_0_), channel_id=1, source_target_pairs={{0,1},{1,0},{2,3},{3,2},{4,5},{5,4},{6,7},{7,6},{8,9},{9,8},{10,11... | collective-permute-start | bytes 1769480 | tf_op jit(solution)/shard_map/ppermute | solution.py:549
  122.5 11.4 %collective-permute-start.26 = (bf16[384,384]{1,0:T(8,128)(2,1)S(1)}, bf16[384,384]{1,0:T(8,128)(2,1)S(1)}, u32[]{:S(2)}, u32[]{:S(2)}) collective-permute-start(bf16[384,384]{1,0:T(8,128)(2,1)S(1)} %get-tuple-element.150.refs_2_.refs_0_), channel_id=1, source_target_pairs={{0,1},{1,0},{2,3},{3,2},{4,5},{5,4},{6,7},{7,6},{8,9},{9,8},{10,11... | collective-permute-start | bytes 884744 | tf_op jit(solution)/shard_map/ppermute | solution.py:549
  131.1 2.9 %collective-permute-start.28 = (bf16[1536,384]{1,0:T(8,128)(2,1)S(1)}, bf16[1536,384]{1,0:T(8,128)(2,1)S(1)}, u32[]{:S(2)}, u32[]{:S(2)}) collective-permute-start(bf16[1536,384]{1,0:T(8,128)(2,1)S(1)} %get-tuple-element.154.refs_2_), channel_id=1, source_target_pairs={{0,16},{16,0},{1,17},{17,1},{2,18},{18,2},{3,19},{19,3},{4,20},{20... | collective-permute-start | bytes 3538952 | tf_op jit(solution)/shard_map/ppermute | solution.py:659
  131.2 6.7 %collective-permute-start.25 = (bf16[384,384]{1,0:T(8,128)(2,1)S(1)}, bf16[384,384]{1,0:T(8,128)(2,1)S(1)}, u32[]{:S(2)}, u32[]{:S(2)}) collective-permute-start(bf16[384,384]{1,0:T(8,128)(2,1)S(1)} %get-tuple-element.152.refs_3_.refs_0_), channel_id=1, source_target_pairs={{0,1},{1,0},{2,3},{3,2},{4,5},{5,4},{6,7},{7,6},{8,9},{9,8},{10,11... | collective-permute-start | bytes 884744 | tf_op jit(solution)/shard_map/ppermute | solution.py:549
  139.8 2.1 %collective-permute-start.29 = (bf16[768,384]{1,0:T(8,128)(2,1)S(1)}, bf16[768,384]{1,0:T(8,128)(2,1)S(1)}, u32[]{:S(2)}, u32[]{:S(2)}) collective-permute-start(bf16[768,384]{1,0:T(8,128)(2,1)S(1)} %get-tuple-element.158.refs_4_), channel_id=1, source_target_pairs={{0,16},{16,0},{1,17},{17,1},{2,18},{18,2},{3,19},{19,3},{4,20},{20... | collective-permute-start | bytes 1769480 | tf_op jit(solution)/shard_map/ppermute | solution.py:659
  (5 other events, 7.1 us)

commit v3 on v2

--- a/solution.py
+++ b/solution.py
@@ -19,11 +19,16 @@
 VECS = 16
 EPSILON = 1e-06
 MASKED = -1e30
-ORDER = "b1c2d3j4jJjJjJjrJjJ5J76p8q"
-DIMS_B = ((0, 1, 2, 3), (1, 0, 2, 3))
-DIMS_A = ((0, 1, 2, 3), (1, 0, 2, 3))
+CHUNK_FF = 768
+ORDER = "bwcxywdywzywzyxzwxzwyxzwyxzrxyxzWYXZpq"
+DIMS = {
+    "bm": ((0, 1, 2, 3), (2, 0, 1, 3)),
+    "ba": ((2, 0, 1, 3), (2, 1, 0, 3)),
+    "am": ((0, 1, 2, 3), (1, 2, 0, 3)),
+    "aa": ((0, 1, 2, 3), (1, 0, 2, 3)),
+}
 PART_ROWS = {"m": 4 * WIDTH, "a": 2 * WIDTH}
-COST = 10000000000
+COST = 30000000000
 PACK_COST = 10
 KA_VMEM = 12
 KB_VMEM = 12
@@ -69,6 +74,10 @@
 
 def column(block):
     return slice(block * WIDTH, (block + 1) * WIDTH)
+
+
+def wide(part):
+    return slice(part * CHUNK_FF, (part + 1) * CHUNK_FF)
 
 
 def row_sum(values_in):
@@ -97,16 +106,16 @@
 
 
 def fill_masks(masks):
-    row = lax.broadcasted_iota(jnp.int32, (SEQ, SEQ), 0)
-    col = lax.broadcasted_iota(jnp.int32, (SEQ, SEQ), 1)
-    masks[0] = jnp.where(col < GT, 0.0, MASKED)
+    key = lax.broadcasted_iota(jnp.int32, (SEQ, SEQ), 0)
+    query = lax.broadcasted_iota(jnp.int32, (SEQ, SEQ), 1)
+    masks[0] = jnp.where(key < GT, 0.0, MASKED)
     inside = jnp.zeros((SEQ, SEQ), jnp.bool_)
     for j in range(LOCALS):
         inside = inside | (
-            (row >= j * SLOT)
-            & (row < (j + 1) * SLOT)
-            & (col >= j * SLOT)
-            & (col < j * SLOT + LT)
+            (query >= j * SLOT)
+            & (query < (j + 1) * SLOT)
+            & (key >= j * SLOT)
+            & (key < j * SLOT + LT)
         )
     masks[1] = jnp.where(inside, 0.0, MASKED)
 
@@ -127,13 +136,11 @@
         unit, _ = normalise(x_rows)
         normed = (unit * vec[LN1G : LN1G + 1, :] + vec[LN1B : LN1B + 1, :]).astype(BF16)
         n1[rows, :] = normed
-        for part in range(3):
-            value = mm(normed, qkv_w[:, column(part)])
-            if part == 0:
-                value = (value + vec[QB : QB + 1, :]).astype(BF16) * BF16(HEAD**-0.5)
-            if part == 2:
-                value = value + vec[VB : VB + 1, :]
-            qkv[rows, column(part)] = value.astype(BF16)
+        triple = mm(normed, qkv_w[...])
+        query = (triple[:, :WIDTH] + vec[QB : QB + 1, :]).astype(BF16) * BF16(HEAD**-0.5)
+        qkv[rows, :WIDTH] = query
+        qkv[rows, column(1)] = triple[:, column(1)].astype(BF16)
+        qkv[rows, column(2)] = (triple[:, column(2)] + vec[VB : VB + 1, :]).astype(BF16)
         lanes = head_lanes()
         mask = masks[seq]
         for pair in range(3):
@@ -142,17 +149,26 @@
             v = qkv[rows, 2 * WIDTH + pair * 128 : 2 * WIDTH + pair * 128 + 128]
             total = None
             for a in range(2):
-                s = mm_right_t(only(lanes[a], q), k) + mask
-                e = jnp.exp(s - jnp.max(s, axis=-1, keepdims=True))
-                p = (e * (1.0 / jnp.sum(e, axis=-1, keepdims=True))).astype(BF16)
+                s = mm_right_t(only(lanes[a], k), q) + mask
+                e = jnp.exp(s - jnp.max(s, axis=0, keepdims=True))
+                p = (e * (1.0 / jnp.sum(e, axis=0, keepdims=True))).astype(BF16)
                 probs[seq * 6 + pair * 2 + a] = p
-                part = mm(p, only(lanes[a], v))
+                part = mm_left_t(p, only(lanes[a], v))
                 total = part if total is None else total + part
             mixed[rows, pair * 128 : pair * 128 + 128] = total.astype(BF16)
         middle[rows, :] = x_rows + (mm(mixed[rows, :], proj_w[...]) + vec[PB : PB + 1, :])
         return carry
 
-    lax.fori_loop(0, 2, body, 0)
+    lax.fori_loop(0, 2, body, 0, unroll=True)
+
+
+def wide_bias(vec, part):
+    rows = CHUNK_FF // 128
+    pieces = []
+    for i in range(part * rows, (part + 1) * rows):
+        row, lane = F1B + i * 128 // WIDTH, i * 128 % WIDTH
+        pieces.append(vec[row : row + 1, lane : lane + 128])
+    return jnp.concatenate(pieces, axis=1)
 
 
 def mlp_forward(vec, fc1_w, fc2_w, middle, n2, slope, active, result):
@@ -161,17 +177,17 @@
         unit, _ = normalise(middle[rows, :])
         normed = (unit * vec[LN2G : LN2G + 1, :] + vec[LN2B : LN2B + 1, :]).astype(BF16)
         n2[rows, :] = normed
-        for part in range(FF // WIDTH):
-            hidden = mm(normed, fc1_w[:, column(part)]) + vec[F1B + part : F1B + part + 1, :]
+        for part in range(FF // CHUNK_FF):
+            hidden = mm(normed, fc1_w[:, wide(part)]) + wide_bias(vec, part)
             cdf = 0.5 + 0.5 * lax.erf(hidden * (0.5**0.5))
-            active[rows, column(part)] = (hidden * cdf).astype(BF16)
+            active[rows, wide(part)] = (hidden * cdf).astype(BF16)
             density = jnp.exp(hidden * hidden * -0.5) * 0.3989422804014327
-            slope[rows, column(part)] = (cdf + hidden * density).astype(BF16)
+            slope[rows, wide(part)] = (cdf + hidden * density).astype(BF16)
         y = middle[rows, :] + (mm(active[rows, :], fc2_w[...]) + vec[F2B : F2B + 1, :])
         result[rows, :] = y.astype(BF16)
         return carry
 
-    lax.fori_loop(0, 2, body, 0)
+    lax.fori_loop(0, 2, body, 0, unroll=True)
 
 
 def mlp_backward(vec, fc1_w, fc2_w, middle, n2, slope, active, dy, dh, dmid, da, sums, emit):
@@ -196,11 +212,13 @@
         sums[PB : PB + 1, :] += row_sum(low.astype(F32))
         return carry
 
-    lax.fori_loop(0, 2, body, 0)
+    lax.fori_loop(0, 2, body, 0, unroll=True)
     for part in range(FF // WIDTH):
         emit(part, mm_left_t(active[:, column(part)], dy[:ROWS, :]))
-    for part in range(FF // WIDTH):
-        emit(4 + part, mm_left_t(n2[...], dh[:, column(part)]))
+    for part in range(2):
+        value = mm_left_t(n2[...], dh[:, part * 2 * WIDTH : (part + 1) * 2 * WIDTH])
+        emit(4 + 2 * part, value[:, :WIDTH])
+        emit(5 + 2 * part, value[:, WIDTH:])
 
 
 def attention_backward(
@@ -219,14 +237,14 @@
             for a in range(2):
                 dm_a = only(lanes[a], dm)
                 p = probs[seq * 6 + pair * 2 + a]
-                dp = mm_right_t(dm_a, v)
+                dp = mm_right_t(only(lanes[a], v), dm)
                 p_wide = p.astype(F32)
-                ds = p_wide * (dp - jnp.sum(dp * p_wide, axis=-1, keepdims=True))
+                ds = p_wide * (dp - jnp.sum(dp * p_wide, axis=0, keepdims=True))
                 ds = ds.astype(BF16)
                 parts = (
-                    mm(ds, only(lanes[a], k)),
-                    mm_left_t(ds, only(lanes[a], q)),
-                    mm_left_t(p, dm_a),
+                    mm_left_t(ds, only(lanes[a], k)),
+                    mm(ds, only(lanes[a], q)),
+                    mm(p, dm_a),
                 )
                 if a == 0:
                     dq, dk, dv = parts
@@ -248,10 +266,11 @@
         sums[LN1B : LN1B + 1, :] += row_sum(dn1)
         return carry
 
-    lax.fori_loop(0, 2, body, 0)
+    lax.fori_loop(0, 2, body, 0, unroll=True)
     emit(8, mm_left_t(mixed[...], da[...]))
+    value = mm_left_t(n1[...], dt[...])
     for part in range(3):
-        emit(9 + part, mm_left_t(n1[...], dt[:, column(part)]))
+        emit(9 + part, value[:, column(part)])
 
 
 def make_emit(keep, send, core, first, blocks):
@@ -489,17 +508,12 @@
     return jnp.where(core == 0, dp >> dims[0][step] & 1, dp >> dims[1][step] & 1)
 
 
-def halve_kernel(dims, step, counts, *refs):
-    sources, (keep_out, send_out) = refs[:-2], refs[-2:]
+def halve_kernel(dims, step, count, keep, recv, keep_out, send_out):
     bit = bit_of(dims, step)
-    place = 0
-    for count, keep, recv in zip(counts, sources[::2], sources[1::2]):
-        half = count // 2
-        add_rows(send_out, place, keep, recv, (1 - bit) * half, half)
-        add_rows(keep_out, place, keep, recv, bit * half, half)
-        place += half
-    for count, keep, recv in zip(counts, sources[::2], sources[1::2]):
-        add_tail((keep_out, send_out), place, keep, recv, count)
+    half = count // 2
+    add_rows(send_out, 0, keep, recv, (1 - bit) * half, half)
+    add_rows(keep_out, 0, keep, recv, bit * half, half)
+    add_tail((keep_out, send_out), half, keep, recv, count)
 
 
 def sum_kernel(count, keep, recv, out):
@@ -507,26 +521,24 @@
     add_tail((out,), count, keep, recv, count)
 
 
-def total_kernel(count, own, recv, total_out, sums_out):
+def total_kernel(count, own, recv, total_out, *sums_out):
     add_rows(total_out, 0, own, recv, 0, count)
-    sums_out[...] = own[count:, :].astype(F32) + recv[count:, :].astype(F32)
-
-
-def join_rows(out, own, recv, bit, start, count):
+    for out in sums_out:
+        out[...] = own[count:, :].astype(F32) + recv[count:, :].astype(F32)
+
+
+def join_rows(out, own, recv, bit):
+    count = own.shape[0]
     for ref, half in ((own, bit), (recv, 1 - bit)):
-        out[pl.ds(pl.multiple_of(half * count, 16), count), :] = ref[start : start + count, :]
-
-
-def join_kernel(dims, step, counts, own, recv, *outs):
-    bit = bit_of(dims, step)
-    start = 0
-    for count, out in zip(counts, outs):
-        join_rows(out, own, recv, bit, start, count)
-        start += count
+        out[pl.ds(pl.multiple_of(half * count, 16), count), :] = ref[...]
+
+
+def join_kernel(dims, step, own, recv, out):
+    join_rows(out, own, recv, bit_of(dims, step))
 
 
 def last_join_kernel(dims, own, recv, other, mine, send, whole):
-    join_rows(whole, own, recv, bit_of(dims, 0), 0, own.shape[0])
+    join_rows(whole, own, recv, bit_of(dims, 0))
     core = lax.axis_index("section")
 
     @pl.when(core == 0)
@@ -550,108 +562,77 @@
 
 
 class Reduction:
-    def __init__(self, name, call, dims):
+    def __init__(self, name, call, dims, keep, send, count):
         self.name, self.call, self.dims = name, call, dims
-        self.sources, self.wholes = {}, {}
-        self.joint = self.run_joint()
-
-    def add(self, part, keep, send):
-        self.sources[part] = (keep, swap(send))
-
-    def halve(self, step, label, counts, tail, sources):
-        rows = sum(counts) // 2 + tail
-        keep, send = self.call(
-            f"{self.name}_halve{label}",
-            functools.partial(halve_kernel, self.dims, step, counts),
-            [shape(rows, WIDTH)] * 2,
-            [VMEM] * len(sources),
-            [VMEM] * 2,
-        )(*sources)
-        return keep, exchange(send, self.dims, step)
-
-    def first(self, part):
-        keep, recv = self.sources[part]
-        count = PART_ROWS[part]
-        tail = keep.shape[0] - count
-        self.sources[part] = self.halve(0, f"0{part}", [count], tail, [keep, recv])
-
-    def run_joint(self):
-        counts = [PART_ROWS[part] // 2 for part in "ma"]
-        sources = self.sources["m"] + self.sources["a"]
-        keep, recv = self.halve(1, "1", counts, VECS, sources)
-        yield
-        count = sum(counts) // 2
-        keep, recv = self.halve(2, "2", [count], VECS, [keep, recv])
-        yield
-        count //= 2
-        (own,) = self.call(
-            f"{self.name}_sum",
-            functools.partial(sum_kernel, count),
-            [shape(count + VECS, WIDTH)],
-            [VMEM] * 2,
-            [VMEM],
-        )(keep, recv)
+        self.keep, self.recv, self.count = keep, swap(send), count
+        self.steps = self.run(count, keep.shape[0] - count)
+
+    def kernel(self, label, body, rows, *args):
+        outs = [shape(n, WIDTH) for n in rows]
+        return self.call(
+            f"{self.name}_{label}", body, outs, [VMEM] * len(args), [VMEM] * len(outs)
+        )(*args)
+
+    def run(self, count, tail):
+        keep, recv = self.keep, self.recv
+        for step in range(3):
+            body = functools.partial(halve_kernel, self.dims, step, count)
+            count //= 2
+            keep, send = self.kernel(f"halve{step}", body, [count + tail] * 2, keep, recv)
+            recv = exchange(send, self.dims, step)
+            yield
+        body = functools.partial(sum_kernel, count)
+        (own,) = self.kernel("sum", body, [count + tail], keep, recv)
         recv = exchange(own, self.dims, 3)
         yield
-        whole, self.sums = self.call(
+        whole, *sums = self.call(
             f"{self.name}_total",
             functools.partial(total_kernel, count),
-            [shape(count, WIDTH), shape(VECS, WIDTH, dtype=F32)],
+            [shape(count, WIDTH)] + [shape(tail, WIDTH, dtype=F32)] * bool(tail),
             [VMEM] * 2,
-            [VMEM] * 2,
+            [VMEM] * (1 + bool(tail)),
         )(own, recv)
-        recv = exchange(whole, self.dims, 2)
-        yield
-        (whole,) = self.join(2, [count], whole, recv)
-        recv = exchange(whole, self.dims, 1)
-        yield
-        wholes = self.join(1, [n // 2 for n in counts], whole, recv)
-        for part, whole in zip("ma", wholes):
-            self.wholes[part] = (whole, exchange(whole, self.dims, 0))
-        yield
-
-    def join(self, step, counts, own, recv):
-        return self.call(
-            f"{self.name}_join{step}",
-            functools.partial(join_kernel, self.dims, step, counts),
-            [shape(2 * count, WIDTH) for count in counts],
-            [VMEM] * 2,
-            [VMEM] * len(counts),
-        )(own, recv)
-
-    def last(self, part):
-        own, recv = self.wholes[part]
-        (self.wholes[part],) = self.join(0, [own.shape[0]], own, recv)
-
-    def last_sorted(self, part, other):
-        own, recv = self.wholes[part]
+        self.sums = sums
+        for step in (2, 1, 0):
+            recv = exchange(whole, self.dims, step)
+            self.pair = (whole, recv)
+            yield
+            if step:
+                body = functools.partial(join_kernel, self.dims, step)
+                (whole,) = self.kernel(f"join{step}", body, [2 * whole.shape[0]], whole, recv)
+
+    def advance(self):
+        next(self.steps)
+
+    def last(self):
+        body = functools.partial(join_kernel, self.dims, 0)
+        (self.whole,) = self.kernel("join0", body, [self.count], *self.pair)
+
+    def last_sorted(self, other):
         mine, send = self.call(
-            f"{self.name}_last_{part}",
+            f"{self.name}_last",
             functools.partial(last_join_kernel, self.dims),
-            [shape(PART_ROWS[part], WIDTH)] * 2,
+            [shape(self.count, WIDTH)] * 2,
             [VMEM] * 3,
             [VMEM] * 2,
-            [pltpu.VMEM((PART_ROWS[part], WIDTH), BF16)],
-        )(own, recv, other.wholes[part])
+            [pltpu.VMEM((self.count, WIDTH), BF16)],
+        )(*self.pair, other.whole)
         return mine, swap(send)
 
 
 class PlainReduction(Reduction):
-    def first(self, part):
-        keep, recv = self.sources[part]
-        total = lax.psum(keep.astype(F32) + recv.astype(F32), "dp")
-        self.wholes[part] = total[: PART_ROWS[part]].astype(BF16)
-        self.sums = total[PART_ROWS[part] :]
-
-    def run_joint(self):
-        yield from [None] * 6
-
-    def last(self, part):
+    def advance(self):
         pass
 
-    def last_sorted(self, part, other):
+    def last(self):
+        total = lax.psum(self.keep.astype(F32) + self.recv.astype(F32), "dp")
+        self.whole = total[: self.count].astype(BF16)
+        self.sums = [total[self.count :]] * (total.shape[0] > self.count)
+
+    def last_sorted(self, other):
+        self.last()
         leading = lax.axis_index("section") == 0
-        pair = (self.wholes[part], other.wholes[part])
+        pair = (self.whole, other.whole)
         return jnp.where(leading, *pair), swap(jnp.where(leading, *pair[::-1]))
 
 
@@ -731,12 +712,14 @@
         vmem=KA_VMEM,
     )(keep, recv, *matrices, *got)
     reduction = Reduction if dp_size == 16 else PlainReduction
-    layer_a = reduction("a", call, DIMS_A)
-    layer_b = reduction("b", call, DIMS_B)
-    layer_b.add("m", keep_1, send_1)
+    chains, held = {}, {}
+
+    def begin(name, keep, send):
+        count = PART_ROWS[name[1]]
+        chains[name] = reduction(name, call, DIMS[name], keep, send, count)
+
+    begin("bm", keep_1, send_1)
     wide_work = [pltpu.VMEM((ROWS, 3 * WIDTH), BF16), pltpu.VMEM((VECS, WIDTH), F32)]
-    held = {}
-
     def back_b_attention():
         held["dx"], keep, send = call(
             "back_b_attention",
@@ -747,7 +730,7 @@
             wide_work,
             vmem=KB_VMEM,
         )(between, vec, qkv_w, proj_w, n1, qkv, probs, mixed, dmid, da, sums)
-        layer_b.add("a", keep, send)
+        begin("ba", keep, send)
 
     def back_a_mlp():
         *held["mlp"], keep, send = call(
@@ -759,7 +742,7 @@
             [pltpu.VMEM((ROWS, FF), BF16)],
             vmem=KB_VMEM,
         )(vec, fc1_w, fc2_w, middle, n2, slope, active, held["dx"])
-        layer_a.add("m", keep, send)
+        begin("am", keep, send)
 
     def back_a_attention():
         held["rows"], rows_send, keep, send = call(
@@ -771,7 +754,7 @@
             wide_work + [pltpu.VMEM((ROWS, WIDTH), BF16)],
             vmem=KB_VMEM,
         )(pack, vec, qkv_w, proj_w, n1, qkv, probs, mixed, *held["mlp"], result)
-        layer_a.add("a", keep, send)
+        begin("aa", keep, send)
         held["rows_got"] = swap(rows_send)
 
     def rows_out():
@@ -788,7 +771,7 @@
         return shape(*w.shape, dtype=F32)
 
     def last_sorted(part):
-        held[part] = layer_a.last_sorted(part, layer_b)
+        held[part] = chains["a" + part].last_sorted(chains["b" + part])
 
     def mlp_out():
         held["mlp_out"] = call(
@@ -813,16 +796,15 @@
             [VMEM] * 4,
             [ANY if w.ndim == 3 else VMEM for w in wanted],
             [pltpu.VMEM((4, WIDTH, WIDTH), F32), pltpu.SemaphoreType.DMA((4,))],
-        )(*held["a"], layer_a.sums, layer_b.sums)
+        )(*held["a"], *chains["aa"].sums, *chains["ba"].sums)
 
     actions = {
         "b": back_b_attention, "c": back_a_mlp, "d": back_a_attention,
         "r": rows_out, "p": mlp_out, "q": attention_out,
-        "1": lambda: layer_b.first("m"), "2": lambda: layer_b.first("a"),
-        "3": lambda: layer_a.first("m"), "4": lambda: layer_a.first("a"),
-        "j": lambda: next(layer_b.joint), "J": lambda: next(layer_a.joint),
-        "5": lambda: layer_b.last("m"), "6": lambda: layer_b.last("a"),
-        "7": lambda: last_sorted("m"), "8": lambda: last_sorted("a"),
+        "w": lambda: chains["bm"].advance(), "x": lambda: chains["ba"].advance(),
+        "y": lambda: chains["am"].advance(), "z": lambda: chains["aa"].advance(),
+        "W": lambda: chains["bm"].last(), "X": lambda: chains["ba"].last(),
+        "Y": lambda: last_sorted("m"), "Z": lambda: last_sorted("a"),
     }
     for name in ORDER:
         actions[name]()

time: 144 us -> 127 us (0.88)
  waiting for transfers between devices: 58.6 us -> 28.6 us
  starting transfers between devices: 27.5 us -> 38.8 us
    ppermute x18 -> x28, waiting for transfers between devices: 56.2 us -> 26.8 us  [exchange(): return lax.ppermute(values_in, ('section', 'dp'), pairs)]
    ppermute x18 -> x28, starting transfers between devices: 24.3 us -> 35.8 us  [exchange(): return lax.ppermute(values_in, ('section', 'dp'), pairs)]
    unnamed x16 -> x36, local copies, waits for them, and re-layouts: 6.12 us -> 7.09 us
    pallas_call x28 -> x40, Pallas kernels: 48.6 us -> 48.3 us  [run(): pl.pallas_call(body, out_shape=outs, name=name, in_specs=list(in_specs) +...]
  transfers between devices with their start and end apart: 30 -> 40, of which waited for: 16 -> 13; matrix products, arithmetic and copies ran while one was open for 3% -> 3% of each run, Pallas kernels for 18% -> 23%
where the time goes in v3:
time: 127 us; the launch traced here: 126 us
  Pallas kernels  48.3 us (38%)
  starting transfers between devices  38.8 us (31%)
  waiting for transfers between devices  28.6 us (23%)
  local copies, waits for them, and re-layouts  7.96 us (6%)
  other arithmetic  1.46 us (1%)
  between operations  1.3 us (1%)
    pallas_call x40, Pallas kernels, run(): pl.pallas_call(body, out_shape=outs, name=name, in_specs=list(in_specs) +...  48.3 us
    ppermute x28, starting transfers between devices, exchange(): return lax.ppermute(values_in, ('section', 'dp'), pairs)  35.8 us
    ppermute x28, waiting for transfers between devices, exchange(): return lax.ppermute(values_in, ('section', 'dp'), pairs)  26.8 us
    unnamed x36, local copies, waits for them, and re-layouts  7.09 us
    ppermute x12, starting transfers between devices, swap(): return lax.ppermute(values_in, 'section', [(0, 1), (1, 0)])  3.06 us
  transfers between devices with their start and end apart: 40, of which 13 were waited for; matrix products, arithmetic and copies ran while one was open for 3% of the time, Pallas kernels for 23%

profile of v3, /device:TPU:0, one launch (start us, length us, event | category | flops | bytes accessed | tf_op | source)
XLA Modules:
  0.0 126.5 jit_solution(18247293778161994224)
XLA Ops:
  7.0 1.5 %collective-permute-done.2.refs_7_ = bf16[384,384]{1,0:T(8,128)(2,1)S(1)} collective-permute-done((bf16[384,384]{1,0:T(8,128)(2,1)S(1)}, bf16[384,384]{1,0:T(8,128)(2,1)S(1)}, u32[]{:S(2)}, u32[]{:S(2)}) %collective-permute-start.2) | collective-permute-done | bytes 294944 | tf_op jit(solution)/shard_map/ppermute | solution.py:640
  8.6 16.8 %forward.1 = (bf16[2,432,384]{2,1,0:T(8,128)(2,1)S(1)}, bf16[2,384,1152]{2,1,0:T(8,128)(2,1)S(1)}, bf16[2,384,384]{2,1,0:T(8,128)(2,1)S(1)}, bf16[2,384,1536]{2,...) custom-call(bf16[432,384]{1,0:T(8,128)(2,1)S(1)} %get-tuple-element., ...), custom_call_target="tpu_custom_call" | custom-call | flops 30000001024 | tf_op jit(solution)/shard_map/forward/pallas_call | solution.py:465
  26.1 5.1 %back_b_attention.1 = (bf16[416,384]{1,0:T(8,128)(2,1)S(1)}, bf16[784,384]{1,0:T(8,128)(2,1)S(1)}, bf16[784,384]{1,0:T(8,128)(2,1)S(1)}) custom-call(bf16[416,384]{1,0:T(8,128)(2,1)S(1)} %get-tuple-element.113.refs_0_, f32[2,16,384]{2,1,0:T(8,128)S(1)} %get-tuple-element.99.refs_1_.refs_0_, bf16[2,384,1152]{2,1,0:T(8,128)(2,1)S(1)} %get-tuple-element.101.refs_2_, ...), custom_call_target="tpu_custom_call" | custom-call | flops 30000001024 | tf_op jit(solution)/shard_map/back_b_attention/pallas_call | solution.py:465
  31.8 2.9 %collective-permute-start.6 = (bf16[768,384]{1,0:T(8,128)(2,1)S(1)}, bf16[768,384]{1,0:T(8,128)(2,1)S(1)}, u32[]{:S(2)}, u32[]{:S(2)}) collective-permute-start(bf16[768,384]{1,0:T(8,128)(2,1)S(1)} %get-tuple-element.121.refs_8_), channel_id=1, source_target_pairs={{0,1},{1,0},{2,3},{3,2},{4,5},{5,4},{6,7},{7,6},{8,9},{9,8},{10,11... | collective-permute-start | bytes 1769480 | tf_op jit(solution)/shard_map/ppermute | solution.py:561
  34.7 5.1 %back_a_mlp.1 = (f32[416,384]{1,0:T(8,128)S(1)}, bf16[416,384]{1,0:T(8,128)(2,1)S(1)}, f32[16,384]{1,0:T(8,128)S(1)}, bf16[1536,384]{1,0:T(8,128)(2,1)S(1)}, bf16[1536,384]{1,0:T(8,128)(2,1)S(1)}) custom-call(f32[2,16,384]{2,1,0:T(8,128)S(1)} %get-tuple-element.99.refs_1_.refs_0_, bf16[2,384,1536]{2,1,0:T(8,128)(2,1)S(1)} %get-tuple-element.107.refs_1_, ...), custom_call_target="tpu_custom_call" | custom-call | flops 30000001024 | tf_op jit(solution)/shard_map/back_a_mlp/pallas_call | solution.py:465
  41.2 1.3 %collective-permute-start.17 = (bf16[400,384]{1,0:T(8,128)(2,1)}, bf16[400,384]{1,0:T(8,128)(2,1)}, u32[]{:S(2)}, u32[]{:S(2)}) collective-permute-start(bf16[400,384]{1,0:T(8,128)(2,1)} %get-tuple-element.130.refs_2_), channel_id=1, source_target_pairs={{0,4},{1,5},{2,6},{3,7},{4,0},{5,1},{6,2},{7,3},{8,12},{9,13},{10,... | collective-permute-start | bytes 921608 | tf_op jit(solution)/shard_map/ppermute | solution.py:561
  43.2 1.5 %collective-permute-start.12 = (bf16[768,384]{1,0:T(8,128)(2,1)S(1)}, bf16[768,384]{1,0:T(8,128)(2,1)S(1)}, u32[]{:S(2)}, u32[]{:S(2)}) collective-permute-start(bf16[768,384]{1,0:T(8,128)(2,1)S(1)} %get-tuple-element.131.refs_2_), channel_id=1, source_target_pairs={{0,1},{1,0},{2,3},{3,2},{4,5},{5,4},{6,7},{7,6},{8,9},{9,8},{10,11... | collective-permute-start | bytes 1769480 | tf_op jit(solution)/shard_map/ppermute | solution.py:561
  44.9 1.6 %collective-permute-start.11 = (bf16[384,384]{1,0:T(8,128)(2,1)S(1)}, bf16[384,384]{1,0:T(8,128)(2,1)S(1)}, u32[]{:S(2)}, u32[]{:S(2)}) collective-permute-start(bf16[384,384]{1,0:T(8,128)(2,1)S(1)} %get-tuple-element.132.refs_12_), channel_id=1, source_target_pairs={{0,2},{1,3},{2,0},{3,1},{4,6},{5,7},{6,4},{7,5},{8,10},{9,11},{10,... | collective-permute-start | bytes 884744 | tf_op jit(solution)/shard_map/ppermute | solution.py:561
  46.9 5.8 %back_a_attention.1 = (bf16[416,384]{1,0:T(8,128)(2,1)S(1)}, bf16[416,384]{1,0:T(8,128)(2,1)}, bf16[784,384]{1,0:T(8,128)(2,1)S(1)}, bf16[784,384]{1,0:T(8,128)(2,1)S(1)}) custom-call(bf16[2,432,384]{2,1,0:T(8,128)(2,1)S(1)} %get-tuple-element.100.refs_0_, f32[2,16,384]{2,1,0:T(8,128)S(1)} %get-tuple-element.99.refs_1_.refs_0_, ...), custom_call_target="tpu_custom_call" | custom-call | flops 30000001024 | tf_op jit(solution)/shard_map/back_a_attention/pallas_call | solution.py:465
  53.2 3.1 %collective-permute-done.12.refs_1_ = bf16[768,384]{1,0:T(8,128)(2,1)S(1)} collective-permute-done((bf16[768,384]{1,0:T(8,128)(2,1)S(1)}, bf16[768,384]{1,0:T(8,128)(2,1)S(1)}, u32[]{:S(2)}, u32[]{:S(2)}) %collective-permute-start.12) | collective-permute-done | bytes 589856 | tf_op jit(solution)/shard_map/ppermute | solution.py:561
  56.5 1.4 %collective-permute-start.15 = (bf16[384,384]{1,0:T(8,128)(2,1)S(1)}, bf16[384,384]{1,0:T(8,128)(2,1)S(1)}, u32[]{:S(2)}, u32[]{:S(2)}) collective-permute-start(bf16[384,384]{1,0:T(8,128)(2,1)S(1)} %get-tuple-element.139.refs_2_), channel_id=1, source_target_pairs={{0,2},{1,3},{2,0},{3,1},{4,6},{5,7},{6,4},{7,5},{8,10},{9,11},{10,... | collective-permute-start | bytes 884744 | tf_op jit(solution)/shard_map/ppermute | solution.py:561
  58.1 1.5 %collective-permute-start.14 = (bf16[192,384]{1,0:T(8,128)(2,1)S(1)}, bf16[192,384]{1,0:T(8,128)(2,1)S(1)}, u32[]{:S(2)}, u32[]{:S(2)}) collective-permute-start(bf16[192,384]{1,0:T(8,128)(2,1)S(1)} %get-tuple-element.140.refs_2_), channel_id=1, source_target_pairs={{0,4},{1,5},{2,6},{3,7},{4,0},{5,1},{6,2},{7,3},{8,12},{9,13},{10,... | collective-permute-start | bytes 442376 | tf_op jit(solution)/shard_map/ppermute | solution.py:561
  60.4 6.1 %collective-permute-done.15.refs_1_ = bf16[384,384]{1,0:T(8,128)(2,1)S(1)} collective-permute-done((bf16[384,384]{1,0:T(8,128)(2,1)S(1)}, bf16[384,384]{1,0:T(8,128)(2,1)S(1)}, u32[]{:S(2)}, u32[]{:S(2)}) %collective-permute-start.15) | collective-permute-done | bytes 294944 | tf_op jit(solution)/shard_map/ppermute | solution.py:561
  66.6 1.7 %collective-permute-start.18 = (bf16[192,384]{1,0:T(8,128)(2,1)S(1)}, bf16[192,384]{1,0:T(8,128)(2,1)S(1)}, u32[]{:S(2)}, u32[]{:S(2)}) collective-permute-start(bf16[192,384]{1,0:T(8,128)(2,1)S(1)} %get-tuple-element.145.refs_2_), channel_id=1, source_target_pairs={{0,4},{1,5},{2,6},{3,7},{4,0},{5,1},{6,2},{7,3},{8,12},{9,13},{10,... | collective-permute-start | bytes 442376 | tf_op jit(solution)/shard_map/ppermute | solution.py:561
  68.3 2.7 %collective-permute-start.21 = (bf16[192,384]{1,0:T(8,128)(2,1)S(1)}, bf16[192,384]{1,0:T(8,128)(2,1)S(1)}, u32[]{:S(2)}, u32[]{:S(2)}) collective-permute-start(bf16[192,384]{1,0:T(8,128)(2,1)S(1)} %bm_sum.1.refs_2_.refs_0_), channel_id=1, source_target_pairs={{0,8},{1,9},{2,10},{3,11},{4,12},{5,13},{6,14},{7,15},{8,0},{9,1},... | collective-permute-start | bytes 442376 | tf_op jit(solution)/shard_map/ppermute | solution.py:561
  73.1 2.0 %collective-permute-start.24 = (bf16[192,384]{1,0:T(8,128)(2,1)}, bf16[192,384]{1,0:T(8,128)(2,1)}, u32[]{:S(2)}, u32[]{:S(2)}) collective-permute-start(bf16[192,384]{1,0:T(8,128)(2,1)} %am_sum.1.refs_2_.refs_0_), channel_id=1, source_target_pairs={{0,8},{1,9},{2,10},{3,11},{4,12},{5,13},{6,14},{7,15},{8,0},{9,1},... | collective-permute-start | bytes 442376 | tf_op jit(solution)/shard_map/ppermute | solution.py:561
  76.2 2.4 %collective-permute-start.20 = (bf16[208,384]{1,0:T(8,128)(2,1)S(1)}, bf16[208,384]{1,0:T(8,128)(2,1)S(1)}, u32[]{:S(2)}, u32[]{:S(2)}) collective-permute-start(bf16[208,384]{1,0:T(8,128)(2,1)S(1)} %get-tuple-element.150.refs_2_), channel_id=1, source_target_pairs={{0,1},{1,0},{2,3},{3,2},{4,5},{5,4},{6,7},{7,6},{8,9},{9,8},{10,11... | collective-permute-start | bytes 479240 | tf_op jit(solution)/shard_map/ppermute | solution.py:561
  79.0 1.6 %collective-permute-done.21.refs_1_ = bf16[192,384]{1,0:T(8,128)(2,1)S(1)} collective-permute-done((bf16[192,384]{1,0:T(8,128)(2,1)S(1)}, bf16[192,384]{1,0:T(8,128)(2,1)S(1)}, u32[]{:S(2)}, u32[]{:S(2)}) %collective-permute-start.21) | collective-permute-done | bytes 147488 | tf_op jit(solution)/shard_map/ppermute | solution.py:561
  80.8 1.8 %collective-permute-done.20.refs_1_ = bf16[208,384]{1,0:T(8,128)(2,1)S(1)} collective-permute-done((bf16[208,384]{1,0:T(8,128)(2,1)S(1)}, bf16[208,384]{1,0:T(8,128)(2,1)S(1)}, u32[]{:S(2)}, u32[]{:S(2)}) %collective-permute-start.20) | collective-permute-done | bytes 159776 | tf_op jit(solution)/shard_map/ppermute | solution.py:561
  82.7 2.1 %collective-permute-start.23 = (bf16[112,384]{1,0:T(8,128)(2,1)S(1)}, bf16[112,384]{1,0:T(8,128)(2,1)S(1)}, u32[]{:S(2)}, u32[]{:S(2)}) collective-permute-start(bf16[112,384]{1,0:T(8,128)(2,1)S(1)} %get-tuple-element.154.refs_2_), channel_id=1, source_target_pairs={{0,2},{1,3},{2,0},{3,1},{4,6},{5,7},{6,4},{7,5},{8,10},{9,11},{10,... | collective-permute-start | bytes 258056 | tf_op jit(solution)/shard_map/ppermute | solution.py:561
  88.9 2.6 %collective-permute-start.27 = (bf16[112,384]{1,0:T(8,128)(2,1)S(1)}, bf16[112,384]{1,0:T(8,128)(2,1)S(1)}, u32[]{:S(2)}, u32[]{:S(2)}) collective-permute-start(bf16[112,384]{1,0:T(8,128)(2,1)S(1)} %ba_sum.1.refs_2_.refs_0_), channel_id=1, source_target_pairs={{0,8},{1,9},{2,10},{3,11},{4,12},{5,13},{6,14},{7,15},{8,0},{9,1},... | collective-permute-start | bytes 258056 | tf_op jit(solution)/shard_map/ppermute | solution.py:561
  94.0 1.9 %collective-permute-done.28.refs_1_ = bf16[192,384]{1,0:T(8,128)(2,1)S(1)} collective-permute-done((bf16[192,384]{1,0:T(8,128)(2,1)S(1)}, bf16[192,384]{1,0:T(8,128)(2,1)S(1)}, u32[]{:S(2)}, u32[]{:S(2)}) %collective-permute-start.28) | collective-permute-done | bytes 147488 | tf_op jit(solution)/shard_map/ppermute | solution.py:561
  99.8 1.9 %rows_out.1 = (bf16[2,197,384]{2,1,0:T(8,128)(2,1)S(1)}, bf16[10,37,384]{2,1,0:T(8,128)(2,1)}) custom-call(f32[2,16,384]{2,1,0:T(8,128)S(1)} %get-tuple-element.99.refs_1_.refs_0_, bf16[416,384]{1,0:T(8,128)(2,1)S(1)} %get-tuple-element.133.refs_1_, bf16[416,384]{1,0:T(8,128)(2,1)} %collective-permute-done.9.refs_2_, ...), custom_call_target="tpu_custom_call" | custom-call | flops 30000001024 | tf_op jit(solution)/shard_map/rows_out/pallas_call | solution.py:465
  102.6 1.3 %collective-permute-done.31.refs_1_ = bf16[96,384]{1,0:T(8,128)(2,1)S(1)} collective-permute-done((bf16[96,384]{1,0:T(8,128)(2,1)S(1)}, bf16[96,384]{1,0:T(8,128)(2,1)S(1)}, u32[]{:S(2)}, u32[]{:S(2)}) %collective-permute-start.31) | collective-permute-done | bytes 73760 | tf_op jit(solution)/shard_map/ppermute | solution.py:561
  104.9 1.8 %collective-permute-start.32 = (bf16[192,384]{1,0:T(8,128)(2,1)S(1)}, bf16[192,384]{1,0:T(8,128)(2,1)S(1)}, u32[]{:S(2)}, u32[]{:S(2)}) collective-permute-start(bf16[192,384]{1,0:T(8,128)(2,1)S(1)} %ba_join2.1.refs_2_.refs_0_), channel_id=1, source_target_pairs={{0,1},{1,0},{2,3},{3,2},{4,5},{5,4},{6,7},{7,6},{8,9},{9,8},{10,11... | collective-permute-start | bytes 442376 | tf_op jit(solution)/shard_map/ppermute | solution.py:561
  107.2 3.0 %collective-permute-done.32.refs_1_ = bf16[192,384]{1,0:T(8,128)(2,1)S(1)} collective-permute-done((bf16[192,384]{1,0:T(8,128)(2,1)S(1)}, bf16[192,384]{1,0:T(8,128)(2,1)S(1)}, u32[]{:S(2)}, u32[]{:S(2)}) %collective-permute-start.32) | collective-permute-done | bytes 147488 | tf_op jit(solution)/shard_map/ppermute | solution.py:561
  112.2 1.4 %bm_join0.1.refs_2_.refs_3_ = bf16[1536,384]{1,0:T(8,128)(2,1)S(1)} custom-call(bf16[768,384]{1,0:T(8,128)(2,1)} %bm_join1.1.refs_2_.refs_0_, bf16[768,384]{1,0:T(8,128)(2,1)} %collective-permute-done.37.refs_1_, bf16[384,384]{1,0:T(8,128)(2,1)S(1)} %aa_join1.1.refs_2_.refs_0_), custom_call_target="tpu_custom_call" | custom-call | flops 30000001024 | tf_op jit(solution)/shard_map/bm_join0/pallas_call | solution.py:465
  113.5 3.2 %collective-permute-done.36.refs_1_ = bf16[768,384]{1,0:T(8,128)(2,1)S(1)} collective-permute-done((bf16[768,384]{1,0:T(8,128)(2,1)S(1)}, bf16[768,384]{1,0:T(8,128)(2,1)S(1)}, u32[]{:S(2)}, u32[]{:S(2)}) %collective-permute-start.36) | collective-permute-done | bytes 589856 | tf_op jit(solution)/shard_map/ppermute | solution.py:561
  117.2 2.7 %collective-permute-done.34.refs_1_ = bf16[384,384]{1,0:T(8,128)(2,1)S(1)} collective-permute-done((bf16[384,384]{1,0:T(8,128)(2,1)S(1)}, bf16[384,384]{1,0:T(8,128)(2,1)S(1)}, u32[]{:S(2)}, u32[]{:S(2)}) %collective-permute-start.34) | collective-permute-done | bytes 294944 | tf_op jit(solution)/shard_map/ppermute | solution.py:561
  120.2 2.3 %mlp_out.1 = (f32[1,384,1536]{2,1,0:T(8,128)}, f32[1,1536,384]{2,1,0:T(8,128)}) custom-call(bf16[1536,384]{1,0:T(8,128)(2,1)S(1)} %get-tuple-element.165.refs_0_, bf16[1536,384]{1,0:T(8,128)(2,1)S(1)} %collective-permute-done.39.refs_1_, bf16[768,384]{1,0:T(8,128)(2,1)S(1)} %get-tuple-element.164.refs_2_), custom_call_target="tpu_custom_call" | custom-call | flops 30000001024 | tf_op jit(solution)/shard_map/mlp_out/pallas_call | solution.py:465
  122.5 1.7 %copy-done.5 = f32[1,1536,384]{2,1,0:T(8,128)S(1)} copy-done((f32[1,1536,384]{2,1,0:T(8,128)S(1)}, f32[1,1536,384]{2,1,0:T(8,128)}, u32[]{:S(2)}) %copy-start.5) | copy-done | bytes 2359320
  124.2 2.1 %attention_out.1 = (f32[1,384]{1,0:T(1,128)}, f32[1,384]{1,0:T(1,128)}, f32[1,384,1152]{2,1,0:T(8,128)}, f32[1,384]{1,0:T(1,128)}, f32[1,384]{1,0:T(1,128)}, /*i...) custom-call(bf16[768,384]{1,0:T(8,128)(2,1)S(1)} %get-tuple-element., ...), custom_call_target="tpu_custom_call" | custom-call | flops 30000001024 | tf_op jit(solution)/shard_map/attention_out/pallas_call | solution.py:465
  (131 shorter events, 31.3 us)
Async XLA Ops:
  0.6 7.9 %collective-permute-start.1 = (bf16[384,1152]{1,0:T(8,128)(2,1)}, bf16[384,1152]{1,0:T(8,128)(2,1)}, u32[]{:S(2)}, u32[]{:S(2)}) collective-permute-start(bf16[384,1152]{1,0:T(8,128)(2,1)} %bitcast.16), channel_id=1, source_target_pairs={{0,16},{16,0},{1,17},{17,1},{2,18},{18,2},{3,19},{19,3},{4,20},{20... | collective-permute-start | bytes 2654216 | tf_op jit(solution)/shard_map/ppermute | solution.py:640
  1.2 7.4 %collective-permute-start.3 = (bf16[384,1536]{1,0:T(8,128)(2,1)}, bf16[384,1536]{1,0:T(8,128)(2,1)}, u32[]{:S(2)}, u32[]{:S(2)}) collective-permute-start(bf16[384,1536]{1,0:T(8,128)(2,1)} %bitcast.12), channel_id=1, source_target_pairs={{0,16},{16,0},{1,17},{17,1},{2,18},{18,2},{3,19},{19,3},{4,20},{20... | collective-permute-start | bytes 3538952 | tf_op jit(solution)/shard_map/ppermute | solution.py:640
  1.2 7.3 %collective-permute-start.4 = (bf16[1536,384]{1,0:T(8,128)(2,1)}, bf16[1536,384]{1,0:T(8,128)(2,1)}, u32[]{:S(2)}, u32[]{:S(2)}) collective-permute-start(bf16[1536,384]{1,0:T(8,128)(2,1)} %bitcast.14), channel_id=1, source_target_pairs={{0,16},{16,0},{1,17},{17,1},{2,18},{18,2},{3,19},{19,3},{4,20},{20... | collective-permute-start | bytes 3538952 | tf_op jit(solution)/shard_map/ppermute | solution.py:640
  25.4 5.9 %collective-permute-start.5 = (bf16[1536,384]{1,0:T(8,128)(2,1)S(1)}, bf16[1536,384]{1,0:T(8,128)(2,1)S(1)}, u32[]{:S(2)}, u32[]{:S(2)}) collective-permute-start(bf16[1536,384]{1,0:T(8,128)(2,1)S(1)} %get-tuple-element.117.refs_11_), channel_id=1, source_target_pairs={{0,16},{16,0},{1,17},{17,1},{2,18},{18,2},{3,19},{19,3},{4,20},{20... | collective-permute-start | bytes 3538952 | tf_op jit(solution)/shard_map/ppermute | solution.py:640
  31.2 9.0 %collective-permute-start.8 = (bf16[784,384]{1,0:T(8,128)(2,1)S(1)}, bf16[784,384]{1,0:T(8,128)(2,1)S(1)}, u32[]{:S(2)}, u32[]{:S(2)}) collective-permute-start(bf16[784,384]{1,0:T(8,128)(2,1)S(1)} %get-tuple-element.120.refs_2_), channel_id=1, source_target_pairs={{0,16},{16,0},{1,17},{17,1},{2,18},{18,2},{3,19},{19,3},{4,20},{20... | collective-permute-start | bytes 1806344 | tf_op jit(solution)/shard_map/ppermute | solution.py:640
  31.8 12.9 %collective-permute-start.6 = (bf16[768,384]{1,0:T(8,128)(2,1)S(1)}, bf16[768,384]{1,0:T(8,128)(2,1)S(1)}, u32[]{:S(2)}, u32[]{:S(2)}) collective-permute-start(bf16[768,384]{1,0:T(8,128)(2,1)S(1)} %get-tuple-element.121.refs_8_), channel_id=1, source_target_pairs={{0,1},{1,0},{2,3},{3,2},{4,5},{5,4},{6,7},{7,6},{8,9},{9,8},{10,11... | collective-permute-start | bytes 1769480 | tf_op jit(solution)/shard_map/ppermute | solution.py:561
  41.2 33.9 %collective-permute-start.17 = (bf16[400,384]{1,0:T(8,128)(2,1)}, bf16[400,384]{1,0:T(8,128)(2,1)}, u32[]{:S(2)}, u32[]{:S(2)}) collective-permute-start(bf16[400,384]{1,0:T(8,128)(2,1)} %get-tuple-element.130.refs_2_), channel_id=1, source_target_pairs={{0,4},{1,5},{2,6},{3,7},{4,0},{5,1},{6,2},{7,3},{8,12},{9,13},{10,... | collective-permute-start | bytes 921608 | tf_op jit(solution)/shard_map/ppermute | solution.py:561
  43.2 13.1 %collective-permute-start.12 = (bf16[768,384]{1,0:T(8,128)(2,1)S(1)}, bf16[768,384]{1,0:T(8,128)(2,1)S(1)}, u32[]{:S(2)}, u32[]{:S(2)}) collective-permute-start(bf16[768,384]{1,0:T(8,128)(2,1)S(1)} %get-tuple-element.131.refs_2_), channel_id=1, source_target_pairs={{0,1},{1,0},{2,3},{3,2},{4,5},{5,4},{6,7},{7,6},{8,9},{9,8},{10,11... | collective-permute-start | bytes 1769480 | tf_op jit(solution)/shard_map/ppermute | solution.py:561
  44.9 13.1 %collective-permute-start.11 = (bf16[384,384]{1,0:T(8,128)(2,1)S(1)}, bf16[384,384]{1,0:T(8,128)(2,1)S(1)}, u32[]{:S(2)}, u32[]{:S(2)}) collective-permute-start(bf16[384,384]{1,0:T(8,128)(2,1)S(1)} %get-tuple-element.132.refs_12_), channel_id=1, source_target_pairs={{0,2},{1,3},{2,0},{3,1},{4,6},{5,7},{6,4},{7,5},{8,10},{9,11},{10,... | collective-permute-start | bytes 884744 | tf_op jit(solution)/shard_map/ppermute | solution.py:561
  52.7 47.1 %collective-permute-start.9 = (bf16[416,384]{1,0:T(8,128)(2,1)}, bf16[416,384]{1,0:T(8,128)(2,1)}, u32[]{:S(2)}, u32[]{:S(2)}) collective-permute-start(bf16[416,384]{1,0:T(8,128)(2,1)} %get-tuple-element.134), channel_id=1, source_target_pairs={{0,16},{16,0},{1,17},{17,1},{2,18},{18,2},{3,19},{19,3},{4,20},{20... | collective-permute-start | bytes 958472 | tf_op jit(solution)/shard_map/ppermute | solution.py:640
  52.8 6.8 %collective-permute-start.10 = (bf16[784,384]{1,0:T(8,128)(2,1)S(1)}, bf16[784,384]{1,0:T(8,128)(2,1)S(1)}, u32[]{:S(2)}, u32[]{:S(2)}) collective-permute-start(bf16[784,384]{1,0:T(8,128)(2,1)S(1)} %get-tuple-element.136.refs_2_), channel_id=1, source_target_pairs={{0,16},{16,0},{1,17},{17,1},{2,18},{18,2},{3,19},{19,3},{4,20},{20... | collective-permute-start | bytes 1806344 | tf_op jit(solution)/shard_map/ppermute | solution.py:640
  56.5 9.9 %collective-permute-start.15 = (bf16[384,384]{1,0:T(8,128)(2,1)S(1)}, bf16[384,384]{1,0:T(8,128)(2,1)S(1)}, u32[]{:S(2)}, u32[]{:S(2)}) collective-permute-start(bf16[384,384]{1,0:T(8,128)(2,1)S(1)} %get-tuple-element.139.refs_2_), channel_id=1, source_target_pairs={{0,2},{1,3},{2,0},{3,1},{4,6},{5,7},{6,4},{7,5},{8,10},{9,11},{10,... | collective-permute-start | bytes 884744 | tf_op jit(solution)/shard_map/ppermute | solution.py:561
  58.1 10.2 %collective-permute-start.14 = (bf16[192,384]{1,0:T(8,128)(2,1)S(1)}, bf16[192,384]{1,0:T(8,128)(2,1)S(1)}, u32[]{:S(2)}, u32[]{:S(2)}) collective-permute-start(bf16[192,384]{1,0:T(8,128)(2,1)S(1)} %get-tuple-element.140.refs_2_), channel_id=1, source_target_pairs={{0,4},{1,5},{2,6},{3,7},{4,0},{5,1},{6,2},{7,3},{8,12},{9,13},{10,... | collective-permute-start | bytes 442376 | tf_op jit(solution)/shard_map/ppermute | solution.py:561
  59.8 11.2 %collective-permute-start.13 = (bf16[400,384]{1,0:T(8,128)(2,1)S(1)}, bf16[400,384]{1,0:T(8,128)(2,1)S(1)}, u32[]{:S(2)}, u32[]{:S(2)}) collective-permute-start(bf16[400,384]{1,0:T(8,128)(2,1)S(1)} %get-tuple-element.142.refs_2_), channel_id=1, source_target_pairs={{0,1},{1,0},{2,3},{3,2},{4,5},{5,4},{6,7},{7,6},{8,9},{9,8},{10,11... | collective-permute-start | bytes 921608 | tf_op jit(solution)/shard_map/ppermute | solution.py:561
  68.3 12.4 %collective-permute-start.21 = (bf16[192,384]{1,0:T(8,128)(2,1)S(1)}, bf16[192,384]{1,0:T(8,128)(2,1)S(1)}, u32[]{:S(2)}, u32[]{:S(2)}) collective-permute-start(bf16[192,384]{1,0:T(8,128)(2,1)S(1)} %bm_sum.1.refs_2_.refs_0_), channel_id=1, source_target_pairs={{0,8},{1,9},{2,10},{3,11},{4,12},{5,13},{6,14},{7,15},{8,0},{9,1},... | collective-permute-start | bytes 442376 | tf_op jit(solution)/shard_map/ppermute | solution.py:561
  71.1 7.5 %collective-permute-start.16 = (bf16[208,384]{1,0:T(8,128)(2,1)S(1)}, bf16[208,384]{1,0:T(8,128)(2,1)S(1)}, u32[]{:S(2)}, u32[]{:S(2)}) collective-permute-start(bf16[208,384]{1,0:T(8,128)(2,1)S(1)} %get-tuple-element.147.refs_2_), channel_id=1, source_target_pairs={{0,2},{1,3},{2,0},{3,1},{4,6},{5,7},{6,4},{7,5},{8,10},{9,11},{10,... | collective-permute-start | bytes 479240 | tf_op jit(solution)/shard_map/ppermute | solution.py:561
  73.1 14.1 %collective-permute-start.24 = (bf16[192,384]{1,0:T(8,128)(2,1)}, bf16[192,384]{1,0:T(8,128)(2,1)}, u32[]{:S(2)}, u32[]{:S(2)}) collective-permute-start(bf16[192,384]{1,0:T(8,128)(2,1)} %am_sum.1.refs_2_.refs_0_), channel_id=1, source_target_pairs={{0,8},{1,9},{2,10},{3,11},{4,12},{5,13},{6,14},{7,15},{8,0},{9,1},... | collective-permute-start | bytes 442376 | tf_op jit(solution)/shard_map/ppermute | solution.py:561
  76.2 6.5 %collective-permute-start.20 = (bf16[208,384]{1,0:T(8,128)(2,1)S(1)}, bf16[208,384]{1,0:T(8,128)(2,1)S(1)}, u32[]{:S(2)}, u32[]{:S(2)}) collective-permute-start(bf16[208,384]{1,0:T(8,128)(2,1)S(1)} %get-tuple-element.150.refs_2_), channel_id=1, source_target_pairs={{0,1},{1,0},{2,3},{3,2},{4,5},{5,4},{6,7},{7,6},{8,9},{9,8},{10,11... | collective-permute-start | bytes 479240 | tf_op jit(solution)/shard_map/ppermute | solution.py:561
  78.6 6.2 %collective-permute-start.19 = (bf16[112,384]{1,0:T(8,128)(2,1)S(1)}, bf16[112,384]{1,0:T(8,128)(2,1)S(1)}, u32[]{:S(2)}, u32[]{:S(2)}) collective-permute-start(bf16[112,384]{1,0:T(8,128)(2,1)S(1)} %get-tuple-element.152.refs_2_), channel_id=1, source_target_pairs={{0,4},{1,5},{2,6},{3,7},{4,0},{5,1},{6,2},{7,3},{8,12},{9,13},{10,... | collective-permute-start | bytes 258056 | tf_op jit(solution)/shard_map/ppermute | solution.py:561
  82.7 6.1 %collective-permute-start.23 = (bf16[112,384]{1,0:T(8,128)(2,1)S(1)}, bf16[112,384]{1,0:T(8,128)(2,1)S(1)}, u32[]{:S(2)}, u32[]{:S(2)}) collective-permute-start(bf16[112,384]{1,0:T(8,128)(2,1)S(1)} %get-tuple-element.154.refs_2_), channel_id=1, source_target_pairs={{0,2},{1,3},{2,0},{3,1},{4,6},{5,7},{6,4},{7,5},{8,10},{9,11},{10,... | collective-permute-start | bytes 258056 | tf_op jit(solution)/shard_map/ppermute | solution.py:561
  84.8 6.6 %collective-permute-start.22 = (bf16[112,384]{1,0:T(8,128)(2,1)S(1)}, bf16[112,384]{1,0:T(8,128)(2,1)S(1)}, u32[]{:S(2)}, u32[]{:S(2)}) collective-permute-start(bf16[112,384]{1,0:T(8,128)(2,1)S(1)} %aa_sum.1.refs_2_.refs_0_), channel_id=1, source_target_pairs={{0,8},{1,9},{2,10},{3,11},{4,12},{5,13},{6,14},{7,15},{8,0},{9,1},... | collective-permute-start | bytes 258056 | tf_op jit(solution)/shard_map/ppermute | solution.py:561
  86.1 6.8 %collective-permute-start.29 = (bf16[384,384]{1,0:T(8,128)(2,1)S(1)}, bf16[384,384]{1,0:T(8,128)(2,1)S(1)}, u32[]{:S(2)}, u32[]{:S(2)}) collective-permute-start(bf16[384,384]{1,0:T(8,128)(2,1)S(1)} %bm_join2.1.refs_2_.refs_0_), channel_id=1, source_target_pairs={{0,2},{1,3},{2,0},{3,1},{4,6},{5,7},{6,4},{7,5},{8,10},{9,11},{10,... | collective-permute-start | bytes 884744 | tf_op jit(solution)/shard_map/ppermute | solution.py:561
  88.2 7.8 %collective-permute-start.28 = (bf16[192,384]{1,0:T(8,128)(2,1)S(1)}, bf16[192,384]{1,0:T(8,128)(2,1)S(1)}, u32[]{:S(2)}, u32[]{:S(2)}) collective-permute-start(bf16[192,384]{1,0:T(8,128)(2,1)S(1)} %am_total.1.refs_2_.refs_0_), channel_id=1, source_target_pairs={{0,4},{1,5},{2,6},{3,7},{4,0},{5,1},{6,2},{7,3},{8,12},{9,13},{10,... | collective-permute-start | bytes 442376 | tf_op jit(solution)/shard_map/ppermute | solution.py:561
  88.9 8.1 %collective-permute-start.27 = (bf16[112,384]{1,0:T(8,128)(2,1)S(1)}, bf16[112,384]{1,0:T(8,128)(2,1)S(1)}, u32[]{:S(2)}, u32[]{:S(2)}) collective-permute-start(bf16[112,384]{1,0:T(8,128)(2,1)S(1)} %ba_sum.1.refs_2_.refs_0_), channel_id=1, source_target_pairs={{0,8},{1,9},{2,10},{3,11},{4,12},{5,13},{6,14},{7,15},{8,0},{9,1},... | collective-permute-start | bytes 258056 | tf_op jit(solution)/shard_map/ppermute | solution.py:561
  91.5 6.7 %collective-permute-start.26 = (bf16[96,384]{1,0:T(8,128)(2,1)S(1)}, bf16[96,384]{1,0:T(8,128)(2,1)S(1)}, u32[]{:S(2)}, u32[]{:S(2)}) collective-permute-start(bf16[96,384]{1,0:T(8,128)(2,1)S(1)} %get-tuple-element.156.refs_0_), channel_id=1, source_target_pairs={{0,4},{1,5},{2,6},{3,7},{4,0},{5,1},{6,2},{7,3},{8,12},{9,13},{10,... | collective-permute-start | bytes 221192 | tf_op jit(solution)/shard_map/ppermute | solution.py:561
  93.7 18.4 %collective-permute-start.37 = (bf16[768,384]{1,0:T(8,128)(2,1)}, bf16[768,384]{1,0:T(8,128)(2,1)}, u32[]{:S(2)}, u32[]{:S(2)}) collective-permute-start(bf16[768,384]{1,0:T(8,128)(2,1)} %bm_join1.1.refs_2_.refs_0_), channel_id=1, source_target_pairs={{0,1},{1,0},{2,3},{3,2},{4,5},{5,4},{6,7},{7,6},{8,9},{9,8},{10,11... | collective-permute-start | bytes 1769480 | tf_op jit(solution)/shard_map/ppermute | solution.py:561
  96.0 10.7 %collective-permute-start.33 = (bf16[384,384]{1,0:T(8,128)(2,1)S(1)}, bf16[384,384]{1,0:T(8,128)(2,1)S(1)}, u32[]{:S(2)}, u32[]{:S(2)}) collective-permute-start(bf16[384,384]{1,0:T(8,128)(2,1)S(1)} %am_join2.1.refs_2_.refs_0_), channel_id=1, source_target_pairs={{0,2},{1,3},{2,0},{3,1},{4,6},{5,7},{6,4},{7,5},{8,10},{9,11},{10,... | collective-permute-start | bytes 884744 | tf_op jit(solution)/shard_map/ppermute | solution.py:561
  97.0 6.9 %collective-permute-start.31 = (bf16[96,384]{1,0:T(8,128)(2,1)S(1)}, bf16[96,384]{1,0:T(8,128)(2,1)S(1)}, u32[]{:S(2)}, u32[]{:S(2)}) collective-permute-start(bf16[96,384]{1,0:T(8,128)(2,1)S(1)} %get-tuple-element.161.refs_0_), channel_id=1, source_target_pairs={{0,2},{1,3},{2,0},{3,1},{4,6},{5,7},{6,4},{7,5},{8,10},{9,11},{10,... | collective-permute-start | bytes 221192 | tf_op jit(solution)/shard_map/ppermute | solution.py:561
  98.8 12.3 %collective-permute-start.30 = (bf16[192,384]{1,0:T(8,128)(2,1)S(1)}, bf16[192,384]{1,0:T(8,128)(2,1)S(1)}, u32[]{:S(2)}, u32[]{:S(2)}) collective-permute-start(bf16[192,384]{1,0:T(8,128)(2,1)S(1)} %aa_join2.1.refs_3_.refs_0_), channel_id=1, source_target_pairs={{0,2},{1,3},{2,0},{3,1},{4,6},{5,7},{6,4},{7,5},{8,10},{9,11},{10,... | collective-permute-start | bytes 442376 | tf_op jit(solution)/shard_map/ppermute | solution.py:561
  106.8 9.9 %collective-permute-start.36 = (bf16[768,384]{1,0:T(8,128)(2,1)S(1)}, bf16[768,384]{1,0:T(8,128)(2,1)S(1)}, u32[]{:S(2)}, u32[]{:S(2)}) collective-permute-start(bf16[768,384]{1,0:T(8,128)(2,1)S(1)} %am_join1.1.refs_2_.refs_0_), channel_id=1, source_target_pairs={{0,1},{1,0},{2,3},{3,2},{4,5},{5,4},{6,7},{7,6},{8,9},{9,8},{10,11... | collective-permute-start | bytes 1769480 | tf_op jit(solution)/shard_map/ppermute | solution.py:561
  110.2 7.0 %collective-permute-start.35 = (bf16[384,384]{1,0:T(8,128)(2,1)S(1)}, bf16[384,384]{1,0:T(8,128)(2,1)S(1)}, u32[]{:S(2)}, u32[]{:S(2)}) collective-permute-start(bf16[384,384]{1,0:T(8,128)(2,1)S(1)} %ba_join1.1.refs_2_.refs_0_), channel_id=1, source_target_pairs={{0,4},{1,5},{2,6},{3,7},{4,0},{5,1},{6,2},{7,3},{8,12},{9,13},{10,... | collective-permute-start | bytes 884744 | tf_op jit(solution)/shard_map/ppermute | solution.py:561
  111.2 8.7 %collective-permute-start.34 = (bf16[384,384]{1,0:T(8,128)(2,1)S(1)}, bf16[384,384]{1,0:T(8,128)(2,1)S(1)}, u32[]{:S(2)}, u32[]{:S(2)}) collective-permute-start(bf16[384,384]{1,0:T(8,128)(2,1)S(1)} %aa_join1.1.refs_2_.refs_0_), channel_id=1, source_target_pairs={{0,1},{1,0},{2,3},{3,2},{4,5},{5,4},{6,7},{7,6},{8,9},{9,8},{10,11... | collective-permute-start | bytes 884744 | tf_op jit(solution)/shard_map/ppermute | solution.py:561
  (25 other events, 71.9 us)

commit v4 on v3

--- a/solution.py
+++ b/solution.py
@@ -20,25 +20,32 @@
 EPSILON = 1e-06
 MASKED = -1e30
 CHUNK_FF = 768
-ORDER = "bwcxywdywzywzyxzwxzwyxzwyxzrxyxzWYXZpq"
+ORDER = "bcwxydwzxwywxzywyzwyxwzxyzWxzyxzrYXZpq"
 DIMS = {
-    "bm": ((0, 1, 2, 3), (2, 0, 1, 3)),
-    "ba": ((2, 0, 1, 3), (2, 1, 0, 3)),
-    "am": ((0, 1, 2, 3), (1, 2, 0, 3)),
-    "aa": ((0, 1, 2, 3), (1, 0, 2, 3)),
+    "bm": ((0, 1, 2, 3), (1, 2, 0, 3)),
+    "ba": ((1, 2, 0, 3), (2, 1, 0, 3)),
+    "am": ((0, 2, 1, 3), (2, 1, 0, 3)),
+    "aa": ((0, 1, 2, 3), (1, 2, 0, 3)),
 }
 PART_ROWS = {"m": 4 * WIDTH, "a": 2 * WIDTH}
-COST = 30000000000
+COST = 10000000000
 PACK_COST = 10
-KA_VMEM = 12
+PACK_VMEM = 55
+FIRST_VMEM = 8
+KA_VMEM = 16
+OUT_VMEM = 8
+ROWS_VMEM = 8
+LAST_VMEM = 8
 KB_VMEM = 12
 LN1G, LN1B, QB, VB, PB, LN2G, LN2B, F2B, F1B = range(9)
 LIVE = 12
+PROJ = ROWS + VECS
+PACKED = PROJ + WIDTH
 BF16 = jnp.bfloat16
 F32 = jnp.float32
 ANY = pl.BlockSpec(memory_space=pl.ANY)
 VMEM = pl.BlockSpec(memory_space=pltpu.VMEM)
-HBM = pl.BlockSpec(memory_space=pltpu.HBM)
+SMEM = pl.BlockSpec(memory_space=pltpu.SMEM)
 
 
 def mm(left, right):
@@ -84,40 +91,46 @@
     return jnp.sum(values_in, axis=0, keepdims=True)
 
 
-def live_flag(tail, index):
+def live_flag(vec, index):
     lane = lax.broadcasted_iota(jnp.int32, (1, WIDTH), 1)
-    flags = tail[LIVE : LIVE + 1, :]
+    flags = vec[LIVE : LIVE + 1, :]
     return jnp.sum(jnp.where(lane == index, flags, 0.0), axis=1, keepdims=True)
 
 
-def pack_kernel(g, l, tail, keep, send, rows):
+def pack_kernel(*refs):
+    sources, (keep, send), held = refs[:12], refs[12:14], refs[14:26]
+    rows, tail, sem = refs[26:]
+    g, l, proj, vecs = held[0], held[1], held[2], held[3:]
+    copies = [
+        pltpu.make_async_copy(source, place, sem.at[i])
+        for i, (source, place) in enumerate(zip(sources, held))
+    ]
+    start_all(copies)
     core = lax.axis_index("section")
     rows[...] = jnp.zeros_like(rows)
-    tail_low = tail[...].astype(BF16)
+    tail[...] = jnp.zeros_like(tail)
+    wait_all(copies)
+    for i, vec in enumerate(vecs[:8]):
+        tail[i : i + 1, :] = vec[...].astype(F32)
+    for i in range(FF // WIDTH):
+        tail[F1B + i : F1B + i + 1, :] = vecs[8][:, column(i)].astype(F32)
+    crops = g[...].astype(F32)
     for out, half in ((keep, core), (send, 1 - core)):
-        live = jnp.where(core == 1, live_flag(tail, half), 1.0)
-        rows[:GT, :] = g[half].astype(F32) * live
+        rows[:GT, :] = jnp.where(half == 0, crops[:, 0, :], crops[:, 1, :])
         for j in range(LOCALS):
-            crop = half * LOCALS + j
-            live = jnp.where(core == 1, live_flag(tail, 2 + crop), 1.0)
-            rows[SEQ + j * SLOT : SEQ + j * SLOT + LT, :] = l[crop].astype(F32) * live
+            rows[SEQ + j * SLOT : SEQ + j * SLOT + LT, :] = l[half * LOCALS + j].astype(F32)
         out[:ROWS, :] = rows[...].astype(BF16)
-        out[ROWS:, :] = tail_low
-
-
-def fill_masks(masks):
-    key = lax.broadcasted_iota(jnp.int32, (SEQ, SEQ), 0)
-    query = lax.broadcasted_iota(jnp.int32, (SEQ, SEQ), 1)
-    masks[0] = jnp.where(key < GT, 0.0, MASKED)
-    inside = jnp.zeros((SEQ, SEQ), jnp.bool_)
-    for j in range(LOCALS):
-        inside = inside | (
-            (query >= j * SLOT)
-            & (query < (j + 1) * SLOT)
-            & (key >= j * SLOT)
-            & (key < j * SLOT + LT)
-        )
-    masks[1] = jnp.where(inside, 0.0, MASKED)
+        out[ROWS:PROJ, :] = tail[...].astype(BF16)
+        out[PROJ:, :] = proj[...]
+
+
+def crop_of(axis):
+    dims = (SEQ, 1) if axis == 0 else (1, SEQ)
+    row = lax.broadcasted_iota(jnp.int32, dims, axis)
+    crop = jnp.zeros(dims, jnp.int32)
+    for j in range(1, LOCALS + 1):
+        crop += (row >= j * SLOT).astype(jnp.int32)
+    return crop, (crop < LOCALS) & (row - crop * SLOT < LT)
 
 
 def head_lanes():
@@ -213,12 +226,12 @@
         return carry
 
     lax.fori_loop(0, 2, body, 0, unroll=True)
-    for part in range(FF // WIDTH):
-        emit(part, mm_left_t(active[:, column(part)], dy[:ROWS, :]))
+    for pair in range(2):
+        parts = (column(2 * pair), column(2 * pair + 1))
+        emit(pair, *(mm_left_t(active[:, part], dy[:ROWS, :]) for part in parts))
     for part in range(2):
         value = mm_left_t(n2[...], dh[:, part * 2 * WIDTH : (part + 1) * 2 * WIDTH])
-        emit(4 + 2 * part, value[:, :WIDTH])
-        emit(5 + 2 * part, value[:, WIDTH:])
+        emit(2 + part, value[:, :WIDTH], value[:, WIDTH:])
 
 
 def attention_backward(
@@ -267,25 +280,17 @@
         return carry
 
     lax.fori_loop(0, 2, body, 0, unroll=True)
-    emit(8, mm_left_t(mixed[...], da[...]))
     value = mm_left_t(n1[...], dt[...])
-    for part in range(3):
-        emit(9 + part, value[:, column(part)])
-
-
-def make_emit(keep, send, core, first, blocks):
-    def emit(block, value):
-        half, place = block % 2, (block - first) // 2
-        rows = slice(place * WIDTH, (place + 1) * WIDTH)
-        low = value.astype(BF16)
-
-        @pl.when(core == half)
-        def _():
-            keep[rows, :] = low
-
-        @pl.when(core != half)
-        def _():
-            send[rows, :] = low
+    emit(0, mm_left_t(mixed[...], da[...]), value[:, column(0)])
+    emit(1, value[:, column(1)], value[:, column(2)])
+
+
+def make_emit(keep, send, core):
+    def emit(pair, first, second):
+        rows = slice(pair * WIDTH, (pair + 1) * WIDTH)
+        first, second = first.astype(BF16), second.astype(BF16)
+        keep[rows, :] = jnp.where(core == 0, first, second)
+        send[rows, :] = jnp.where(core == 0, second, first)
 
     return emit
 
@@ -300,107 +305,133 @@
         copy.wait()
 
 
+def hold_flags(glive, llive, vec, dy):
+    core = lax.axis_index("section")
+    lane = lax.broadcasted_iota(jnp.int32, (1, WIDTH), 1)
+    flags = jnp.zeros((1, WIDTH), F32)
+    for i in range(2):
+        flags = jnp.where(lane == i, glive[i].astype(F32), flags)
+    for i in range(2 * LOCALS):
+        flags = jnp.where(lane == 2 + i, llive[i].astype(F32), flags)
+    vec[LIVE : LIVE + 1, :] = flags
+    crop, _ = crop_of(0)
+    live = jnp.zeros((SEQ, 1), F32)
+    for j in range(LOCALS):
+        live = jnp.where(crop == j, llive[core * LOCALS + j].astype(F32), live)
+    dy[:SEQ, :] = (dy[:SEQ, :].astype(F32) * glive[core].astype(F32)).astype(BF16)
+    dy[SEQ:ROWS, :] = (dy[SEQ:ROWS, :].astype(F32) * live).astype(BF16)
+
+
+def sort_by_core(own, got, first, second):
+    core = lax.axis_index("section")
+    first[...] = jnp.where(core == 0, own[...], got[...])
+    second[...] = jnp.where(core == 0, got[...], own[...])
+
+
+def settle_kernel(_, own, got, masks, qkv_w):
+    key = lax.broadcasted_iota(jnp.int32, (SEQ, SEQ), 0)
+    masks[0] = jnp.where(key < GT, 0.0, MASKED)
+    key_crop, true_key = crop_of(0)
+    query_crop, _ = crop_of(1)
+    masks[1] = jnp.where(jnp.where(true_key, key_crop, -1) == query_crop, 0.0, MASKED)
+    sort_by_core(own, got, qkv_w.at[0], qkv_w.at[1])
+
+
+def first_attention_kernel(*refs):
+    (
+        glive, llive, keep, recv, qkv_w, masks,
+        pack, vec, n1, qkv, probs, mixed, middle,
+    ) = refs
+    sort_by_core(keep, recv, pack.at[0], pack.at[1])
+    for layer in range(2):
+        vec[layer] = pack[layer, ROWS:PROJ, :].astype(F32)
+    hold_flags(glive, llive, vec.at[0], pack.at[1])
+    attention_forward(
+        pack.at[0], vec.at[0], masks, qkv_w.at[0], pack.at[0, pl.ds(PROJ, WIDTH)],
+        n1, qkv, probs, mixed, middle,
+    )
+
+
 def forward_kernel(*refs):
-    own, got = refs[:1] + refs[2:6], refs[1:2] + refs[6:10]
     (
-        pack, qkv_w, proj_w, fc1_w, fc2_w, vec, between,
-        n1, qkv, probs, mixed, middle, n2, slope, active, result,
-        dmid, da, sums, keep_out, send_out,
-        masks, dh, in_sem,
-    ) = refs[10:]
-    core = lax.axis_index("section")
-    other = 1 - core
-    held = (pack, qkv_w, proj_w, fc1_w, fc2_w)
-
-    def load(sources, layer, i):
-        return pltpu.make_async_copy(sources[i], held[i].at[layer], in_sem.at[layer, i])
-
-    for i in range(5):
-        load(own, core, i).start()
-        load(got, other, i).start()
-    fill_masks(masks)
+        fc1_own, fc2_own, fc1_got, fc2_got, pack, qkv_w, vec, masks, middle_a,
+        fc1_a, fc2_a, between, result, n2_a, slope_a, active_a,
+        n1_b, qkv_b, probs_b, mixed_b, dmid, da, sums, keep_out, send_out,
+        fc1_b, fc2_b, middle_b, n2_b, slope_b, active_b, dh,
+    ) = refs
+    core = lax.axis_index("section")
+    sort_by_core(fc1_own, fc1_got, fc1_a, fc1_b)
+    sort_by_core(fc2_own, fc2_got, fc2_a, fc2_b)
     sums[...] = jnp.zeros_like(sums)
-    for layer in range(2):
-        load(own, layer, 0).wait()
-        vec[layer] = pack[layer, ROWS:, :].astype(F32)
-    for layer in range(2):
-        for i in (1, 2):
-            load(own, layer, i).wait()
-        x = pack.at[0] if layer == 0 else between
-        attention_forward(
-            x, vec.at[layer], masks, qkv_w.at[layer], proj_w.at[layer],
-            n1.at[layer], qkv.at[layer], probs.at[layer], mixed.at[layer], middle.at[layer],
-        )
-        for i in (3, 4):
-            load(own, layer, i).wait()
-        mlp_forward(
-            vec.at[layer], fc1_w.at[layer], fc2_w.at[layer], middle.at[layer], n2.at[layer],
-            slope.at[layer], active.at[layer], between if layer == 0 else result,
-        )
+    mlp_forward(vec.at[0], fc1_a, fc2_a, middle_a, n2_a, slope_a, active_a, between)
+    attention_forward(
+        between, vec.at[1], masks, qkv_w.at[1], pack.at[1, pl.ds(PROJ, WIDTH)],
+        n1_b, qkv_b, probs_b, mixed_b, middle_b,
+    )
+    mlp_forward(vec.at[1], fc1_b, fc2_b, middle_b, n2_b, slope_b, active_b, result)
     mlp_backward(
-        vec.at[1], fc1_w.at[1], fc2_w.at[1], middle.at[1], n2.at[1], slope.at[1], active.at[1],
-        pack.at[1], dh, dmid, da, sums, make_emit(keep_out, send_out, core, 0, 8),
+        vec.at[1], fc1_b, fc2_b, middle_b, n2_b, slope_b, active_b, pack.at[1], dh, dmid, da,
+        sums, make_emit(keep_out, send_out, core),
     )
 
 
 def attention_backward_kernel(layer, *refs):
     (
-        x, vec, qkv_w, proj_w, n1, qkv, probs, mixed, dmid, da, sums_in,
+        x, pack, vec, qkv_w, n1, qkv, probs, mixed, dmid, da, sums_in,
         dx, keep_out, send_out, dt, sums,
     ) = refs
     core = lax.axis_index("section")
     sums[...] = sums_in[...]
     attention_backward(
-        x, vec.at[layer], qkv_w.at[layer], proj_w.at[layer], n1.at[layer], qkv.at[layer],
-        probs.at[layer], mixed.at[layer], dmid, da, dt, sums,
-        make_emit(keep_out, send_out, core, 8, 4), dx,
+        x, vec.at[layer], qkv_w.at[layer], pack.at[layer, pl.ds(PROJ, WIDTH)], n1, qkv, probs,
+        mixed, dmid, da, dt, sums, make_emit(keep_out, send_out, core), dx,
     )
     keep_out[2 * WIDTH :, :] = sums[...].astype(BF16)
     send_out[2 * WIDTH :, :] = sums[...].astype(BF16)
 
 
 def last_backward_kernel(*refs):
-    pack, result, rows_keep, rows_send, dx = refs[0], refs[11], refs[12], refs[13], refs[-1]
-    attention_backward_kernel(
-        0, pack.at[0], *refs[1:11], dx, refs[14], refs[15], refs[16], refs[17]
-    )
-    core = lax.axis_index("section")
-
-    @pl.when(core == 0)
-    def _():
-        rows_keep[...] = dx[...]
-        rows_send[...] = result[...]
-
-    @pl.when(core == 1)
-    def _():
-        rows_keep[...] = result[...]
-        rows_send[...] = dx[...]
+    pack, result, rows_keep, rows_send, dx = refs[0], refs[10], refs[11], refs[12], refs[-1]
+    attention_backward_kernel(0, pack.at[0], *refs[:10], dx, *refs[13:17])
+    core = lax.axis_index("section")
+
+    rows_keep[...] = jnp.where(core == 0, dx[...], result[...])
+    rows_send[...] = jnp.where(core == 0, result[...], dx[...])
 
 
 def mlp_backward_kernel(*refs):
     (
-        vec, fc1_w, fc2_w, middle, n2, slope, active, dy, dmid, da, sums, keep_out, send_out, dh,
+        _, vec, fc1_w, fc2_w, middle, n2, slope, active, dy,
+        dmid, da, sums, keep_out, send_out, dh,
     ) = refs
     core = lax.axis_index("section")
     sums[...] = jnp.zeros_like(sums)
     mlp_backward(
-        vec.at[0], fc1_w.at[0], fc2_w.at[0], middle.at[0], n2.at[0], slope.at[0], active.at[0],
-        dy, dh, dmid, da, sums, make_emit(keep_out, send_out, core, 0, 8),
-    )
-
-
-def rows_kernel(tails, keep, recv, g_out, l_out, wide):
-    core = lax.axis_index("section")
-    tail = tails.at[0]
+        vec.at[0], fc1_w, fc2_w, middle, n2, slope, active, dy, dh, dmid, da, sums, make_emit(keep_out, send_out, core),
+    )
+
+
+def rows_kernel(vec, keep, recv, g_out, l_out, mark, wide, g, l, sem):
+    mark[...] = jnp.zeros_like(mark)
+    core = lax.axis_index("section")
+    globals_live = []
     for source, half in ((keep, core), (recv, 1 - core)):
         wide[...] = source[...].astype(F32)
-        live = jnp.where(core == 1, live_flag(tail, half), 1.0)
-        g_out[half] = (wide[:GT, :] * live).astype(BF16)
+        live = jnp.where(core == 1, live_flag(vec.at[0], half), 1.0)
+        globals_live.append(wide[:GT, :] * live)
         for j in range(LOCALS):
             crop = half * LOCALS + j
-            live = jnp.where(core == 1, live_flag(tail, 2 + crop), 1.0)
+            live = jnp.where(core == 1, live_flag(vec.at[0], 2 + crop), 1.0)
             piece = wide[SEQ + j * SLOT : SEQ + j * SLOT + LT, :]
-            l_out[crop] = (piece * live).astype(BF16)
+            l[crop] = (piece * live).astype(BF16)
+    g[:, 0, :] = jnp.where(core == 0, *globals_live).astype(BF16)
+    g[:, 1, :] = jnp.where(core == 1, *globals_live).astype(BF16)
+    copies = [
+        pltpu.make_async_copy(g, g_out, sem.at[0]),
+        pltpu.make_async_copy(l, l_out, sem.at[1]),
+    ]
+    start_all(copies)
+    wait_all(copies)
 
 
 def out_block(own, got, index):
@@ -419,7 +450,8 @@
     return copies
 
 
-def mlp_out_kernel(own, got, fc1, fc2, held, sem):
+def mlp_out_kernel(own, got, fc1, fc2, mark, held, sem):
+    mark[...] = jnp.zeros_like(mark)
     places = [fc2.at[0, column(part), :] for part in range(4)]
     places += [fc1.at[0, :, column(part)] for part in range(4)]
     wait_all(write_blocks(own, got, places, held, sem))
@@ -448,12 +480,15 @@
     return jax.ShapeDtypeStruct(dims, dtype)
 
 
+MARK = shape(8, 128, dtype=F32)
+
+
 class Ordered:
     def __init__(self):
         self.last = None
 
     def __call__(
-        self, name, kernel, outs, in_specs, out_specs, scratch=(), vmem=8, cost=1
+        self, name, kernel, outs, in_specs, out_specs, scratch=(), vmem=8, cost=1, mark=0
     ):
         before = [] if self.last is None else [self.last]
         count = len(in_specs)
@@ -469,12 +504,12 @@
                 in_specs=list(in_specs) + [ANY] * len(before),
                 out_specs=out_specs,
                 scratch_shapes=list(scratch),
-                compiler_params=pltpu.CompilerParams(vmem_limit_bytes=vmem * 1024 * 1024),
+                compiler_params=pltpu.CompilerParams(vmem_limit_bytes=int(vmem * 1024 * 1024)),
                 cost_estimate=pl.CostEstimate(
                     flops=cost * COST, bytes_accessed=0, transcendentals=0
                 ),
             )(*args, *before)
-            self.last = results[-1]
+            self.last = results[mark]
             return results
 
         return run
@@ -605,10 +640,12 @@
         next(self.steps)
 
     def last(self):
+        assert 2 * self.pair[0].shape[0] == self.count
         body = functools.partial(join_kernel, self.dims, 0)
         (self.whole,) = self.kernel("join0", body, [self.count], *self.pair)
 
     def last_sorted(self, other):
+        assert 2 * self.pair[0].shape[0] == self.count
         mine, send = self.call(
             f"{self.name}_last",
             functools.partial(last_join_kernel, self.dims),
@@ -645,72 +682,76 @@
         ln1_gain, ln1_bias, qkv_weight, query_bias, value_bias, proj_weight, proj_bias,
         ln2_gain, ln2_bias, fc1_weight, fc1_bias, fc2_weight, fc2_bias,
     ) = weights
-    matrices = tuple(w[0] for w in (qkv_weight, proj_weight, fc1_weight, fc2_weight))
-    got = tuple(swap(w) for w in matrices)
+    qkv_own, fc1_own, fc2_own = (w[0] for w in (qkv_weight, fc1_weight, fc2_weight))
+    qkv_got = swap(qkv_own)
     vectors = (
         ln1_gain, ln1_bias, query_bias, value_bias, proj_bias, ln2_gain, ln2_bias, fc2_bias,
         fc1_bias,
     )
-    flags = jnp.concatenate([global_live, local_live]).astype(F32)
-    tail = jnp.concatenate(
-        [vector.reshape(-1, WIDTH).astype(F32) for vector in vectors]
-        + [jnp.pad(flags, (0, WIDTH - flags.shape[0]))[None]]
-    )
-    tail = jnp.pad(tail, ((0, VECS - tail.shape[0]), (0, 0)))
     call = Ordered()
+    packed = [global_ends[0].transpose(1, 0, 2), local_ends[0], proj_weight[0], *vectors]
     keep, send = call(
         "pack",
         pack_kernel,
-        [shape(ROWS + VECS, WIDTH)] * 2,
-        [VMEM] * 3,
+        [shape(PACKED, WIDTH)] * 2,
+        [ANY] * len(packed),
         [VMEM] * 2,
-        [pltpu.VMEM((ROWS, WIDTH), F32)],
+        [pltpu.VMEM(v.shape, BF16) for v in packed]
+        + [
+            pltpu.VMEM((ROWS, WIDTH), F32),
+            pltpu.VMEM((VECS, WIDTH), F32),
+            pltpu.SemaphoreType.DMA((len(packed),)),
+        ],
+        vmem=PACK_VMEM,
         cost=PACK_COST,
-    )(global_ends[0], local_ends[0], tail)
+    )(*packed)
     recv = swap(send)
-    weight_shapes = [(WIDTH, 3 * WIDTH), (WIDTH, WIDTH), (WIDTH, FF), (FF, WIDTH)]
+    fc1_own, fc2_own, _ = lax.optimization_barrier((fc1_own, fc2_own, send))
+    fc1_got, fc2_got = swap(fc1_own), swap(fc2_own)
     rows_low, rows_wide = shape(ROWS, WIDTH), shape(ROWS, WIDTH, dtype=F32)
+    hidden_low = shape(ROWS, FF)
+    triple_low = shape(ROWS, 3 * WIDTH)
+    weights_low = [shape(WIDTH, FF), shape(FF, WIDTH)]
     sums_shape = shape(VECS, WIDTH, dtype=F32)
     mlp_pair = [shape(4 * WIDTH, WIDTH)] * 2
     attention_pair = [shape(2 * WIDTH + VECS, WIDTH)] * 2
-    outs = (
-        [shape(2, ROWS + VECS, WIDTH)]
-        + [shape(2, *dims) for dims in weight_shapes]
-        + [
-            shape(2, VECS, WIDTH, dtype=F32),
-            rows_low,
-            shape(2, ROWS, WIDTH),
-            shape(2, ROWS, 3 * WIDTH),
-            shape(2, 12, SEQ, SEQ),
-            shape(2, ROWS, WIDTH),
-            shape(2, ROWS, WIDTH, dtype=F32),
-            shape(2, ROWS, WIDTH),
-            shape(2, ROWS, FF),
-            shape(2, ROWS, FF),
-            rows_low,
-            rows_wide,
-            rows_low,
-            sums_shape,
-        ]
-        + mlp_pair
-    )
+    attention_saved = [rows_low, triple_low, shape(12, SEQ, SEQ), rows_low]
+    mlp_saved = [rows_wide, rows_low, hidden_low, hidden_low]
+    masks_shape = shape(2, SEQ, SEQ, dtype=F32)
+    masks, qkv_w = call(
+        "settle",
+        settle_kernel,
+        [masks_shape, shape(2, WIDTH, 3 * WIDTH)],
+        [VMEM] * 3,
+        [VMEM] * 2,
+    )(keep, qkv_own, qkv_got)
+    outs = [shape(2, PACKED, WIDTH), shape(2, VECS, WIDTH, dtype=F32)]
+    outs += attention_saved + [rows_wide]
+    pack, vec, n1_a, qkv_a, probs_a, mixed_a, middle_a = call(
+        "first_attention",
+        first_attention_kernel,
+        outs,
+        [SMEM] * 2 + [VMEM] * 4,
+        [VMEM] * len(outs),
+        vmem=FIRST_VMEM,
+        mark=1,
+    )(global_live, local_live, keep, recv, qkv_w, masks)
+    outs = weights_low + [rows_low] * 2 + mlp_saved[1:] + attention_saved
+    outs += [rows_wide, rows_low, sums_shape] + mlp_pair
     (
-        pack, qkv_w, proj_w, fc1_w, fc2_w, vec, between,
-        n1, qkv, probs, mixed, middle, n2, slope, active, result,
-        dmid, da, sums, keep_1, send_1,
+        fc1_a, fc2_a, between, result, n2_a, slope_a, active_a,
+        n1_b, qkv_b, probs_b, mixed_b, dmid, da, sums, keep_1, send_1,
     ) = call(
         "forward",
         forward_kernel,
         outs,
-        [HBM] * 10,
+        [VMEM] * 9,
         [VMEM] * len(outs),
-        [
-            pltpu.VMEM((2, SEQ, SEQ), F32),
-            pltpu.VMEM((ROWS, FF), BF16),
-            pltpu.SemaphoreType.DMA((2, 5)),
-        ],
+        [pltpu.VMEM(held.shape, held.dtype) for held in weights_low + mlp_saved]
+        + [pltpu.VMEM((ROWS, FF), BF16)],
         vmem=KA_VMEM,
-    )(keep, recv, *matrices, *got)
+        mark=13,
+    )(fc1_own, fc2_own, fc1_got, fc2_got, pack, qkv_w, vec, masks, middle_a)
     reduction = Reduction if dp_size == 16 else PlainReduction
     chains, held = {}, {}
 
@@ -729,7 +770,7 @@
             [VMEM] * 3,
             wide_work,
             vmem=KB_VMEM,
-        )(between, vec, qkv_w, proj_w, n1, qkv, probs, mixed, dmid, da, sums)
+        )(between, pack, vec, qkv_w, n1_b, qkv_b, probs_b, mixed_b, dmid, da, sums)
         begin("ba", keep, send)
 
     def back_a_mlp():
@@ -737,11 +778,11 @@
             "back_a_mlp",
             mlp_backward_kernel,
             [rows_wide, rows_low, sums_shape] + mlp_pair,
-            [VMEM] * 8,
+            [VMEM] * 9,
             [VMEM] * 5,
             [pltpu.VMEM((ROWS, FF), BF16)],
             vmem=KB_VMEM,
-        )(vec, fc1_w, fc2_w, middle, n2, slope, active, held["dx"])
+        )(pack, vec, fc1_a, fc2_a, middle_a, n2_a, slope_a, active_a, held["dx"])
         begin("am", keep, send)
 
     def back_a_attention():
@@ -749,22 +790,27 @@
             "back_a_attention",
             last_backward_kernel,
             [rows_low] * 2 + attention_pair,
-            [VMEM] * 12,
+            [VMEM] * 11,
             [VMEM] * 4,
             wide_work + [pltpu.VMEM((ROWS, WIDTH), BF16)],
             vmem=KB_VMEM,
-        )(pack, vec, qkv_w, proj_w, n1, qkv, probs, mixed, *held["mlp"], result)
+        )(pack, vec, qkv_w, n1_a, qkv_a, probs_a, mixed_a, *held["mlp"], result)
         begin("aa", keep, send)
         held["rows_got"] = swap(rows_send)
 
     def rows_out():
+        ends = [shape(GT, global_ends.shape[1], WIDTH), shape(*local_ends.shape[1:])]
         held["rows_out"] = call(
             "rows_out",
             rows_kernel,
-            [shape(*global_ends.shape[1:]), shape(*local_ends.shape[1:])],
+            ends + [MARK],
             [VMEM] * 3,
-            [VMEM] * 2,
-            [pltpu.VMEM((ROWS, WIDTH), F32)],
+            [ANY] * 2 + [VMEM],
+            [pltpu.VMEM((ROWS, WIDTH), F32)]
+            + [pltpu.VMEM(end.shape, BF16) for end in ends]
+            + [pltpu.SemaphoreType.DMA((2,))],
+            vmem=ROWS_VMEM,
+            mark=2,
         )(vec, held["rows"], held["rows_got"])
 
     def grad(w):
@@ -777,11 +823,12 @@
         held["mlp_out"] = call(
             "mlp_out",
             mlp_out_kernel,
-            [grad(fc1_weight), grad(fc2_weight)],
+            [grad(fc1_weight), grad(fc2_weight), MARK],
             [VMEM] * 2,
-            [ANY] * 2,
+            [ANY] * 2 + [VMEM],
             [pltpu.VMEM((8, WIDTH, WIDTH), F32), pltpu.SemaphoreType.DMA((8,))],
-            vmem=16,
+            vmem=OUT_VMEM,
+            mark=2,
         )(*held["m"])
 
     def attention_out():
@@ -796,6 +843,7 @@
             [VMEM] * 4,
             [ANY if w.ndim == 3 else VMEM for w in wanted],
             [pltpu.VMEM((4, WIDTH, WIDTH), F32), pltpu.SemaphoreType.DMA((4,))],
+            vmem=LAST_VMEM,
         )(*held["a"], *chains["aa"].sums, *chains["ba"].sums)
 
     actions = {
@@ -808,14 +856,14 @@
     }
     for name in ORDER:
         actions[name]()
-    global_out, local_out = held["rows_out"]
-    grad_fc1, grad_fc2 = held["mlp_out"]
+    global_out, local_out, _ = held["rows_out"]
+    grad_fc1, grad_fc2, _ = held["mlp_out"]
     (
         grad_ln1_gain, grad_ln1_bias, grad_qkv, grad_query_bias, grad_value_bias, grad_proj,
         grad_proj_bias, grad_ln2_gain, grad_ln2_bias, grad_fc1_bias, grad_fc2_bias,
     ) = held["attention_out"]
     return (
-        global_out[None], local_out[None],
+        global_out.transpose(1, 0, 2)[None], local_out[None],
         grad_ln1_gain, grad_ln1_bias, grad_qkv, grad_query_bias, grad_value_bias, grad_proj,
         grad_proj_bias, grad_ln2_gain, grad_ln2_bias, grad_fc1, grad_fc1_bias, grad_fc2,
         grad_fc2_bias,

time: 127 us -> 116 us (0.913)
  Pallas kernels: 48.3 us -> 40.9 us
  local copies, waits for them, and re-layouts: 7.96 us -> 1.17 us
  waiting for transfers between devices: 28.6 us -> 34.1 us
  other arithmetic: 1.46 us -> 0 us
    pallas_call x40 -> x42, Pallas kernels: 48.3 us -> 40.9 us  [run(): pl.pallas_call(body, out_shape=outs, name=name, in_specs=list(in_specs) +...]
    ppermute x28, waiting for transfers between devices: 26.8 us -> 33.1 us  [exchange(): return lax.ppermute(values_in, ('section', 'dp'), pairs)]
    unnamed x36 -> x12, local copies, waits for them, and re-layouts: 7.09 us -> 1.17 us
    convert_element_type x2 -> x0, other arithmetic: 1.46 us -> none  [the longest x1 0.75 us: on_device(): flags = jnp.concatenate([global_live, local_live]).astype(F32)]
    ppermute x12 -> x11, starting transfers between devices: 3.06 us -> 3 us  [swap(): return lax.ppermute(values_in, 'section', [(0, 1), (1, 0)])]
  transfers between devices with their start and end apart: 40 -> 39, of which waited for: 13 -> 16; matrix products, arithmetic and copies ran while one was open for 3% -> 0% of each run, Pallas kernels for 23% -> 24%
where the time goes in v4:
time: 116 us
  Pallas kernels  40.9 us (35%)
  starting transfers between devices  38.8 us (33%)
  waiting for transfers between devices  34.1 us (29%)
  between operations  1.22 us (1%)
  local copies, waits for them, and re-layouts  1.17 us (1%)
    pallas_call x42, Pallas kernels, run(): pl.pallas_call(body, out_shape=outs, name=name, in_specs=list(in_specs) +...  40.9 us
    ppermute x28, starting transfers between devices, exchange(): return lax.ppermute(values_in, ('section', 'dp'), pairs)  35.8 us
    ppermute x28, waiting for transfers between devices, exchange(): return lax.ppermute(values_in, ('section', 'dp'), pairs)  33.1 us
    ppermute x11, starting transfers between devices, swap(): return lax.ppermute(values_in, 'section', [(0, 1), (1, 0)])  3 us
  transfers between devices with their start and end apart: 39, of which 16 were waited for; matrix products, arithmetic and copies ran while one was open for 0% of the time, Pallas kernels for 24%

profile of v4, /device:TPU:0, one launch (start us, length us, event | category | flops | bytes accessed | tf_op | source)
XLA Modules:
  0.0 116.2 jit_solution(6645617085453861246)
XLA Ops:
  1.2 2.8 %pack.1 = (bf16[816,384]{1,0:T(8,128)(2,1)}, bf16[816,384]{1,0:T(8,128)(2,1)}) custom-call(bf16[197,2,384]{2,1,0:T(2,128)(2,1)} %bitcast.19, bf16[10,37,384]{2,1,0:T(8,128)(2,1)} %bitcast.18, bf16[384,384]{1,0:T(8,128)(2,1)} %bitcast.20, bf16[1,384]{1,0:T(2,128)(2,1)} %refs_3_.1, bf16[1,384]{1,0:T(2,128)(2,1)} %refs_4_.1, bf16[1,384]{1,0:T(2,128)(2,1)} %refs_5_.1, ...), custom_call_target="tpu_custom_call" | custom-call | flops 99999997952 | tf_op jit(solution)/shard_map/pack/pallas_call | solution.py:500
  6.4 3.6 %first_attention.1 = (bf16[2,816,384]{2,1,0:T(8,128)(2,1)S(1)}, f32[2,16,384]{2,1,0:T(8,128)S(1)}, bf16[416,384]{1,0:T(8,128)(2,1)S(1)}, bf16[416,1152]{1,0:T(8,...) custom-call(s32[2]{0:T(128)S(1)} %copy-done.3, ...), custom_call_target="tpu_custom_call" | custom-call | flops 10000000000 | tf_op jit(solution)/shard_map/first_attention/pallas_call | solution.py:500
  10.0 10.8 %forward.1 = (bf16[384,1536]{1,0:T(8,128)(2,1)S(1)}, bf16[1536,384]{1,0:T(8,128)(2,1)S(1)}, bf16[416,384]{1,0:T(8,128)(2,1)S(1)}, bf16[416,384]{1,0:T(8,128)(2,1...) custom-call(bf16[384,1536]{1,0:T(8,128)(2,1)S(1)} %bitcast.13, ...), custom_call_target="tpu_custom_call" | custom-call | flops 10000000000 | tf_op jit(solution)/shard_map/forward/pallas_call | solution.py:500
  21.3 4.6 %back_b_attention.1 = (bf16[416,384]{1,0:T(8,128)(2,1)S(1)}, bf16[784,384]{1,0:T(8,128)(2,1)S(1)}, bf16[784,384]{1,0:T(8,128)(2,1)S(1)}) custom-call(bf16[416,384]{1,0:T(8,128)(2,1)S(1)} %get-tuple-element.123.refs_0_, bf16[2,816,384]{2,1,0:T(8,128)(2,1)S(1)} %get-tuple-element.110.refs_4_.refs_1_.refs_0_, ...), custom_call_target="tpu_custom_call" | custom-call | flops 10000000000 | tf_op jit(solution)/shard_map/back_b_attention/pallas_call | solution.py:500
  26.1 3.5 %back_a_mlp.1 = (f32[416,384]{1,0:T(8,128)S(1)}, bf16[416,384]{1,0:T(8,128)(2,1)S(1)}, f32[16,384]{1,0:T(8,128)S(1)}, bf16[1536,384]{1,0:T(8,128)(2,1)S(1)}, bf16[1536,384]{1,0:T(8,128)(2,1)S(1)}) custom-call(bf16[2,816,384]{2,1,0:T(8,128)(2,1)S(1)} %get-tuple-element.110.refs_4_.refs_1_.refs_0_, ...), custom_call_target="tpu_custom_call" | custom-call | flops 10000000000 | tf_op jit(solution)/shard_map/back_a_mlp/pallas_call | solution.py:500
  30.4 2.8 %collective-permute-start.9 = (bf16[768,384]{1,0:T(8,128)(2,1)S(1)}, bf16[768,384]{1,0:T(8,128)(2,1)S(1)}, u32[]{:S(2)}, u32[]{:S(2)}) collective-permute-start(bf16[768,384]{1,0:T(8,128)(2,1)S(1)} %get-tuple-element.149), channel_id=1, source_target_pairs={{0,1},{1,0},{2,3},{3,2},{4,5},{5,4},{6,7},{7,6},{8,9},{9,8},{10,11... | collective-permute-start | bytes 1769480 | tf_op jit(solution)/shard_map/ppermute | solution.py:596
  33.5 1.6 %collective-permute-start.11 = (bf16[400,384]{1,0:T(8,128)(2,1)S(1)}, bf16[400,384]{1,0:T(8,128)(2,1)S(1)}, u32[]{:S(2)}, u32[]{:S(2)}) collective-permute-start(bf16[400,384]{1,0:T(8,128)(2,1)S(1)} %get-tuple-element.153), channel_id=1, source_target_pairs={{0,2},{1,3},{2,0},{3,1},{4,6},{5,7},{6,4},{7,5},{8,10},{9,11},{10,... | collective-permute-start | bytes 921608 | tf_op jit(solution)/shard_map/ppermute | solution.py:596
  35.5 5.1 %back_a_attention.1 = (bf16[416,384]{1,0:T(8,128)(2,1)S(1)}, bf16[416,384]{1,0:T(8,128)(2,1)}, bf16[784,384]{1,0:T(8,128)(2,1)S(1)}, bf16[784,384]{1,0:T(8,128)(2,1)S(1)}) custom-call(bf16[2,816,384]{2,1,0:T(8,128)(2,1)S(1)} %get-tuple-element.110.refs_4_.refs_1_.refs_0_, f32[2,16,384]{2,1,0:T(8,128)S(1)} %get-tuple-element.109.refs_6_.refs_9_.refs_2_.refs_1_.refs_0_, ...), custom_call_target="tpu_custom_call" | custom-call | flops 10000000000 | tf_op jit(solution)/shard_map/back_a_attention/pallas_call | solution.py:500
  45.5 1.4 %collective-permute-start.10 = (bf16[400,384]{1,0:T(8,128)(2,1)S(1)}, bf16[400,384]{1,0:T(8,128)(2,1)S(1)}, u32[]{:S(2)}, u32[]{:S(2)}) collective-permute-start(bf16[400,384]{1,0:T(8,128)(2,1)S(1)} %get-tuple-element.152), channel_id=1, source_target_pairs={{0,1},{1,0},{2,3},{3,2},{4,5},{5,4},{6,7},{7,6},{8,9},{9,8},{10,11... | collective-permute-start | bytes 921608 | tf_op jit(solution)/shard_map/ppermute | solution.py:596
  47.0 2.8 %collective-permute-done.13.refs_1_ = bf16[384,384]{1,0:T(8,128)(2,1)S(1)} collective-permute-done((bf16[384,384]{1,0:T(8,128)(2,1)S(1)}, bf16[384,384]{1,0:T(8,128)(2,1)S(1)}, u32[]{:S(2)}, u32[]{:S(2)}) %collective-permute-start.13) | collective-permute-done | bytes 294944 | tf_op jit(solution)/shard_map/ppermute | solution.py:596
  49.9 1.4 %collective-permute-start.14 = (bf16[192,384]{1,0:T(8,128)(2,1)S(1)}, bf16[192,384]{1,0:T(8,128)(2,1)S(1)}, u32[]{:S(2)}, u32[]{:S(2)}) collective-permute-start(bf16[192,384]{1,0:T(8,128)(2,1)S(1)} %get-tuple-element.158), channel_id=1, source_target_pairs={{0,4},{1,5},{2,6},{3,7},{4,0},{5,1},{6,2},{7,3},{8,12},{9,13},{10,... | collective-permute-start | bytes 442376 | tf_op jit(solution)/shard_map/ppermute | solution.py:596
  52.3 4.1 %collective-permute-done.14.refs_1_ = bf16[192,384]{1,0:T(8,128)(2,1)S(1)} collective-permute-done((bf16[192,384]{1,0:T(8,128)(2,1)S(1)}, bf16[192,384]{1,0:T(8,128)(2,1)S(1)}, u32[]{:S(2)}, u32[]{:S(2)}) %collective-permute-start.14) | collective-permute-done | bytes 147488 | tf_op jit(solution)/shard_map/ppermute | solution.py:596
  56.5 2.7 %collective-permute-start.19 = (bf16[192,384]{1,0:T(8,128)(2,1)S(1)}, bf16[192,384]{1,0:T(8,128)(2,1)S(1)}, u32[]{:S(2)}, u32[]{:S(2)}) collective-permute-start(bf16[192,384]{1,0:T(8,128)(2,1)S(1)} %bm_sum.1.refs_2_.refs_0_), channel_id=1, source_target_pairs={{0,8},{1,9},{2,10},{3,11},{4,12},{5,13},{6,14},{7,15},{8,0},{9,1},... | collective-permute-start | bytes 442376 | tf_op jit(solution)/shard_map/ppermute | solution.py:596
  62.4 1.8 %collective-permute-done.19.refs_1_ = bf16[192,384]{1,0:T(8,128)(2,1)S(1)} collective-permute-done((bf16[192,384]{1,0:T(8,128)(2,1)S(1)}, bf16[192,384]{1,0:T(8,128)(2,1)S(1)}, u32[]{:S(2)}, u32[]{:S(2)}) %collective-permute-start.19) | collective-permute-done | bytes 147488 | tf_op jit(solution)/shard_map/ppermute | solution.py:596
  65.1 2.0 %collective-permute-done.18.refs_1_ = bf16[192,384]{1,0:T(8,128)(2,1)S(1)} collective-permute-done((bf16[192,384]{1,0:T(8,128)(2,1)S(1)}, bf16[192,384]{1,0:T(8,128)(2,1)S(1)}, u32[]{:S(2)}, u32[]{:S(2)}) %collective-permute-start.18) | collective-permute-done | bytes 147488 | tf_op jit(solution)/shard_map/ppermute | solution.py:596
  67.1 3.0 %collective-permute-start.24 = (bf16[192,384]{1,0:T(8,128)(2,1)S(1)}, bf16[192,384]{1,0:T(8,128)(2,1)S(1)}, u32[]{:S(2)}, u32[]{:S(2)}) collective-permute-start(bf16[192,384]{1,0:T(8,128)(2,1)S(1)} %am_sum.1.refs_2_.refs_0_), channel_id=1, source_target_pairs={{0,8},{1,9},{2,10},{3,11},{4,12},{5,13},{6,14},{7,15},{8,0},{9,1},... | collective-permute-start | bytes 442376 | tf_op jit(solution)/shard_map/ppermute | solution.py:596
  71.6 5.5 %collective-permute-done.24.refs_1_ = bf16[192,384]{1,0:T(8,128)(2,1)S(1)} collective-permute-done((bf16[192,384]{1,0:T(8,128)(2,1)S(1)}, bf16[192,384]{1,0:T(8,128)(2,1)S(1)}, u32[]{:S(2)}, u32[]{:S(2)}) %collective-permute-start.24) | collective-permute-done | bytes 147488 | tf_op jit(solution)/shard_map/ppermute | solution.py:596
  77.2 1.8 %collective-permute-start.26 = (bf16[192,384]{1,0:T(8,128)(2,1)S(1)}, bf16[192,384]{1,0:T(8,128)(2,1)S(1)}, u32[]{:S(2)}, u32[]{:S(2)}) collective-permute-start(bf16[192,384]{1,0:T(8,128)(2,1)S(1)} %am_total.1.refs_2_.refs_0_), channel_id=1, source_target_pairs={{0,2},{1,3},{2,0},{3,1},{4,6},{5,7},{6,4},{7,5},{8,10},{9,11},{10,... | collective-permute-start | bytes 442376 | tf_op jit(solution)/shard_map/ppermute | solution.py:596
  79.1 1.5 %collective-permute-start.30 = (bf16[768,384]{1,0:T(8,128)(2,1)S(1)}, bf16[768,384]{1,0:T(8,128)(2,1)S(1)}, u32[]{:S(2)}, u32[]{:S(2)}) collective-permute-start(bf16[768,384]{1,0:T(8,128)(2,1)S(1)} %bm_join1.1.refs_2_.refs_0_), channel_id=1, source_target_pairs={{0,1},{1,0},{2,3},{3,2},{4,5},{5,4},{6,7},{7,6},{8,9},{9,8},{10,11... | collective-permute-start | bytes 1769480 | tf_op jit(solution)/shard_map/ppermute | solution.py:596
  80.7 3.0 %collective-permute-start.25 = (bf16[112,384]{1,0:T(8,128)(2,1)S(1)}, bf16[112,384]{1,0:T(8,128)(2,1)S(1)}, u32[]{:S(2)}, u32[]{:S(2)}) collective-permute-start(bf16[112,384]{1,0:T(8,128)(2,1)S(1)} %aa_sum.1.refs_2_.refs_0_), channel_id=1, source_target_pairs={{0,8},{1,9},{2,10},{3,11},{4,12},{5,13},{6,14},{7,15},{8,0},{9,1},... | collective-permute-start | bytes 258056 | tf_op jit(solution)/shard_map/ppermute | solution.py:596
  83.7 3.6 %collective-permute-done.27.refs_1_ = bf16[112,384]{1,0:T(8,128)(2,1)S(1)} collective-permute-done((bf16[112,384]{1,0:T(8,128)(2,1)S(1)}, bf16[112,384]{1,0:T(8,128)(2,1)S(1)}, u32[]{:S(2)}, u32[]{:S(2)}) %collective-permute-start.27) | collective-permute-done | bytes 86048 | tf_op jit(solution)/shard_map/ppermute | solution.py:596
  87.3 1.9 %collective-permute-start.29 = (bf16[96,384]{1,0:T(8,128)(2,1)S(1)}, bf16[96,384]{1,0:T(8,128)(2,1)S(1)}, u32[]{:S(2)}, u32[]{:S(2)}) collective-permute-start(bf16[96,384]{1,0:T(8,128)(2,1)S(1)} %get-tuple-element.170.refs_2_.refs_0_), channel_id=1, source_target_pairs={{0,1},{1,0},{2,3},{3,2},{4,5},{5,4},{6,7},{7,6},{8,9},{9,8},{10,11... | collective-permute-start | bytes 221192 | tf_op jit(solution)/shard_map/ppermute | solution.py:596
  90.0 1.4 %collective-permute-start.28 = (bf16[96,384]{1,0:T(8,128)(2,1)S(1)}, bf16[96,384]{1,0:T(8,128)(2,1)S(1)}, u32[]{:S(2)}, u32[]{:S(2)}) collective-permute-start(bf16[96,384]{1,0:T(8,128)(2,1)S(1)} %get-tuple-element.171.refs_2_.refs_0_), channel_id=1, source_target_pairs={{0,4},{1,5},{2,6},{3,7},{4,0},{5,1},{6,2},{7,3},{8,12},{9,13},{10,... | collective-permute-start | bytes 221192 | tf_op jit(solution)/shard_map/ppermute | solution.py:596
  91.8 2.3 %collective-permute-start.32 = (bf16[192,384]{1,0:T(8,128)(2,1)S(1)}, bf16[192,384]{1,0:T(8,128)(2,1)S(1)}, u32[]{:S(2)}, u32[]{:S(2)}) collective-permute-start(bf16[192,384]{1,0:T(8,128)(2,1)S(1)} %ba_join2.1.refs_2_.refs_0_), channel_id=1, source_target_pairs={{0,4},{1,5},{2,6},{3,7},{4,0},{5,1},{6,2},{7,3},{8,12},{9,13},{10,... | collective-permute-start | bytes 442376 | tf_op jit(solution)/shard_map/ppermute | solution.py:596
  94.1 3.2 %collective-permute-done.28.refs_1_ = bf16[96,384]{1,0:T(8,128)(2,1)S(1)} collective-permute-done((bf16[96,384]{1,0:T(8,128)(2,1)S(1)}, bf16[96,384]{1,0:T(8,128)(2,1)S(1)}, u32[]{:S(2)}, u32[]{:S(2)}) %collective-permute-start.28) | collective-permute-done | bytes 73760 | tf_op jit(solution)/shard_map/ppermute | solution.py:596
  98.3 2.1 %collective-permute-done.32.refs_1_ = bf16[192,384]{1,0:T(8,128)(2,1)S(1)} collective-permute-done((bf16[192,384]{1,0:T(8,128)(2,1)S(1)}, bf16[192,384]{1,0:T(8,128)(2,1)S(1)}, u32[]{:S(2)}, u32[]{:S(2)}) %collective-permute-start.32) | collective-permute-done | bytes 147488 | tf_op jit(solution)/shard_map/ppermute | solution.py:596
  101.3 1.4 %collective-permute-done.31.refs_1_ = bf16[192,384]{1,0:T(8,128)(2,1)S(1)} collective-permute-done((bf16[192,384]{1,0:T(8,128)(2,1)S(1)}, bf16[192,384]{1,0:T(8,128)(2,1)S(1)}, u32[]{:S(2)}, u32[]{:S(2)}) %collective-permute-start.31) | collective-permute-done | bytes 147488 | tf_op jit(solution)/shard_map/ppermute | solution.py:596
  102.8 2.4 %rows_out.1 = (bf16[197,2,384]{2,1,0:T(2,128)(2,1)}, bf16[10,37,384]{2,1,0:T(8,128)(2,1)}, f32[8,128]{1,0:T(8,128)S(1)}) custom-call(f32[2,16,384]{2,1,0:T(8,128)S(1)} %get-tuple-element.109.refs_6_.refs_9_.refs_2_.refs_1_.refs_0_, bf16[416,384]{1,0:T(8,128)(2,1)S(1)} %get-tuple-element.145.refs_2_.refs_1_, bf16[416,384]{1,0:T(8,128)(2,1)} %collective-permute-done.7.refs_2_, ...), custom_call_target="tpu_custom_call" | custom-call | flops 10000000000 | tf_op jit(solution)/shard_map/rows_out/pallas_call | solution.py:500
  105.2 2.9 %collective-permute-done.36.refs_1_ = bf16[768,384]{1,0:T(8,128)(2,1)S(1)} collective-permute-done((bf16[768,384]{1,0:T(8,128)(2,1)S(1)}, bf16[768,384]{1,0:T(8,128)(2,1)S(1)}, u32[]{:S(2)}, u32[]{:S(2)}) %collective-permute-start.36) | collective-permute-done | bytes 589856 | tf_op jit(solution)/shard_map/ppermute | solution.py:596
  108.9 2.4 %collective-permute-done.34.refs_1_ = bf16[384,384]{1,0:T(8,128)(2,1)S(1)} collective-permute-done((bf16[384,384]{1,0:T(8,128)(2,1)S(1)}, bf16[384,384]{1,0:T(8,128)(2,1)S(1)}, u32[]{:S(2)}, u32[]{:S(2)}) %collective-permute-start.34) | collective-permute-done | bytes 294944 | tf_op jit(solution)/shard_map/ppermute | solution.py:596
  111.6 2.3 %mlp_out.1 = (f32[1,384,1536]{2,1,0:T(8,128)}, f32[1,1536,384]{2,1,0:T(8,128)}, f32[8,128]{1,0:T(8,128)S(1)}) custom-call(bf16[1536,384]{1,0:T(8,128)(2,1)S(1)} %get-tuple-element.175.refs_2_.refs_0_, bf16[1536,384]{1,0:T(8,128)(2,1)S(1)} %collective-permute-done.38.refs_1_, bf16[768,384]{1,0:T(8,128)(2,1)S(1)} %get-tuple-element.176.refs_2_.refs_0_), custom_call_target="tpu_custom_call" | custom-call | flops 10000000000 | tf_op jit(solution)/shard_map/mlp_out/pallas_call | solution.py:500
  113.9 2.1 %attention_out.1 = (f32[1,384]{1,0:T(1,128)}, f32[1,384]{1,0:T(1,128)}, f32[1,384,1152]{2,1,0:T(8,128)}, f32[1,384]{1,0:T(1,128)}, f32[1,384]{1,0:T(1,128)}, /*i...) custom-call(bf16[768,384]{1,0:T(8,128)(2,1)S(1)} %get-tuple-element., ...), custom_call_target="tpu_custom_call" | custom-call | flops 10000000000 | tf_op jit(solution)/shard_map/attention_out/pallas_call | solution.py:500
  (100 shorter events, 21.0 us)
Async XLA Ops:
  4.1 5.9 %collective-permute-start.2 = (bf16[384,1536]{1,0:T(8,128)(2,1)S(1)}, bf16[384,1536]{1,0:T(8,128)(2,1)S(1)}, u32[]{:S(2)}, u32[]{:S(2)}) collective-permute-start(bf16[384,1536]{1,0:T(8,128)(2,1)S(1)} %bitcast.12), channel_id=1, source_target_pairs={{0,16},{16,0},{1,17},{17,1},{2,18},{18,2},{3,19},{19,3},{4,20},{20... | collective-permute-start | bytes 3538952 | tf_op jit(solution)/shard_map/ppermute | solution.py:677
  4.5 5.5 %collective-permute-start.3 = (bf16[1536,384]{1,0:T(8,128)(2,1)S(1)}, bf16[1536,384]{1,0:T(8,128)(2,1)S(1)}, u32[]{:S(2)}, u32[]{:S(2)}) collective-permute-start(bf16[1536,384]{1,0:T(8,128)(2,1)S(1)} %bitcast.14), channel_id=1, source_target_pairs={{0,16},{16,0},{1,17},{17,1},{2,18},{18,2},{3,19},{19,3},{4,20},{20... | collective-permute-start | bytes 3538952 | tf_op jit(solution)/shard_map/ppermute | solution.py:677
  20.8 9.2 %collective-permute-start.6 = (bf16[1536,384]{1,0:T(8,128)(2,1)S(1)}, bf16[1536,384]{1,0:T(8,128)(2,1)S(1)}, u32[]{:S(2)}, u32[]{:S(2)}) collective-permute-start(bf16[1536,384]{1,0:T(8,128)(2,1)S(1)} %get-tuple-element.141), channel_id=1, source_target_pairs={{0,16},{16,0},{1,17},{17,1},{2,18},{18,2},{3,19},{19,3},{4,20},{20... | collective-permute-start | bytes 3538952 | tf_op jit(solution)/shard_map/ppermute | solution.py:677
  25.9 7.4 %collective-permute-start.5 = (bf16[784,384]{1,0:T(8,128)(2,1)S(1)}, bf16[784,384]{1,0:T(8,128)(2,1)S(1)}, u32[]{:S(2)}, u32[]{:S(2)}) collective-permute-start(bf16[784,384]{1,0:T(8,128)(2,1)S(1)} %get-tuple-element.139), channel_id=1, source_target_pairs={{0,16},{16,0},{1,17},{17,1},{2,18},{18,2},{3,19},{19,3},{4,20},{20... | collective-permute-start | bytes 1806344 | tf_op jit(solution)/shard_map/ppermute | solution.py:677
  29.5 5.6 %collective-permute-start.4 = (bf16[1536,384]{1,0:T(8,128)(2,1)S(1)}, bf16[1536,384]{1,0:T(8,128)(2,1)S(1)}, u32[]{:S(2)}, u32[]{:S(2)}) collective-permute-start(bf16[1536,384]{1,0:T(8,128)(2,1)S(1)} %get-tuple-element.137), channel_id=1, source_target_pairs={{0,16},{16,0},{1,17},{17,1},{2,18},{18,2},{3,19},{19,3},{4,20},{20... | collective-permute-start | bytes 3538952 | tf_op jit(solution)/shard_map/ppermute | solution.py:677
  30.4 11.9 %collective-permute-start.9 = (bf16[768,384]{1,0:T(8,128)(2,1)S(1)}, bf16[768,384]{1,0:T(8,128)(2,1)S(1)}, u32[]{:S(2)}, u32[]{:S(2)}) collective-permute-start(bf16[768,384]{1,0:T(8,128)(2,1)S(1)} %get-tuple-element.149), channel_id=1, source_target_pairs={{0,1},{1,0},{2,3},{3,2},{4,5},{5,4},{6,7},{7,6},{8,9},{9,8},{10,11... | collective-permute-start | bytes 1769480 | tf_op jit(solution)/shard_map/ppermute | solution.py:596
  33.5 10.8 %collective-permute-start.11 = (bf16[400,384]{1,0:T(8,128)(2,1)S(1)}, bf16[400,384]{1,0:T(8,128)(2,1)S(1)}, u32[]{:S(2)}, u32[]{:S(2)}) collective-permute-start(bf16[400,384]{1,0:T(8,128)(2,1)S(1)} %get-tuple-element.153), channel_id=1, source_target_pairs={{0,2},{1,3},{2,0},{3,1},{4,6},{5,7},{6,4},{7,5},{8,10},{9,11},{10,... | collective-permute-start | bytes 921608 | tf_op jit(solution)/shard_map/ppermute | solution.py:596
  40.6 62.2 %collective-permute-start.7 = (bf16[416,384]{1,0:T(8,128)(2,1)}, bf16[416,384]{1,0:T(8,128)(2,1)}, u32[]{:S(2)}, u32[]{:S(2)}) collective-permute-start(bf16[416,384]{1,0:T(8,128)(2,1)} %get-tuple-element.146), channel_id=1, source_target_pairs={{0,16},{16,0},{1,17},{17,1},{2,18},{18,2},{3,19},{19,3},{4,20},{20... | collective-permute-start | bytes 958472 | tf_op jit(solution)/shard_map/ppermute | solution.py:677
  40.6 10.7 %collective-permute-start.15 = (bf16[768,384]{1,0:T(8,128)(2,1)S(1)}, bf16[768,384]{1,0:T(8,128)(2,1)S(1)}, u32[]{:S(2)}, u32[]{:S(2)}) collective-permute-start(bf16[768,384]{1,0:T(8,128)(2,1)S(1)} %get-tuple-element.159), channel_id=1, source_target_pairs={{0,1},{1,0},{2,3},{3,2},{4,5},{5,4},{6,7},{7,6},{8,9},{9,8},{10,11... | collective-permute-start | bytes 1769480 | tf_op jit(solution)/shard_map/ppermute | solution.py:596
  42.6 7.2 %collective-permute-start.13 = (bf16[384,384]{1,0:T(8,128)(2,1)S(1)}, bf16[384,384]{1,0:T(8,128)(2,1)S(1)}, u32[]{:S(2)}, u32[]{:S(2)}) collective-permute-start(bf16[384,384]{1,0:T(8,128)(2,1)S(1)} %get-tuple-element.156), channel_id=1, source_target_pairs={{0,2},{1,3},{2,0},{3,1},{4,6},{5,7},{6,4},{7,5},{8,10},{9,11},{10,... | collective-permute-start | bytes 884744 | tf_op jit(solution)/shard_map/ppermute | solution.py:596
  44.4 14.8 %collective-permute-start.12 = (bf16[208,384]{1,0:T(8,128)(2,1)S(1)}, bf16[208,384]{1,0:T(8,128)(2,1)S(1)}, u32[]{:S(2)}, u32[]{:S(2)}) collective-permute-start(bf16[208,384]{1,0:T(8,128)(2,1)S(1)} %get-tuple-element.155), channel_id=1, source_target_pairs={{0,4},{1,5},{2,6},{3,7},{4,0},{5,1},{6,2},{7,3},{8,12},{9,13},{10,... | collective-permute-start | bytes 479240 | tf_op jit(solution)/shard_map/ppermute | solution.py:596
  45.5 14.5 %collective-permute-start.10 = (bf16[400,384]{1,0:T(8,128)(2,1)S(1)}, bf16[400,384]{1,0:T(8,128)(2,1)S(1)}, u32[]{:S(2)}, u32[]{:S(2)}) collective-permute-start(bf16[400,384]{1,0:T(8,128)(2,1)S(1)} %get-tuple-element.152), channel_id=1, source_target_pairs={{0,1},{1,0},{2,3},{3,2},{4,5},{5,4},{6,7},{7,6},{8,9},{9,8},{10,11... | collective-permute-start | bytes 921608 | tf_op jit(solution)/shard_map/ppermute | solution.py:596
  49.9 6.6 %collective-permute-start.14 = (bf16[192,384]{1,0:T(8,128)(2,1)S(1)}, bf16[192,384]{1,0:T(8,128)(2,1)S(1)}, u32[]{:S(2)}, u32[]{:S(2)}) collective-permute-start(bf16[192,384]{1,0:T(8,128)(2,1)S(1)} %get-tuple-element.158), channel_id=1, source_target_pairs={{0,4},{1,5},{2,6},{3,7},{4,0},{5,1},{6,2},{7,3},{8,12},{9,13},{10,... | collective-permute-start | bytes 442376 | tf_op jit(solution)/shard_map/ppermute | solution.py:596
  51.5 9.7 %collective-permute-start.17 = (bf16[384,384]{1,0:T(8,128)(2,1)S(1)}, bf16[384,384]{1,0:T(8,128)(2,1)S(1)}, u32[]{:S(2)}, u32[]{:S(2)}) collective-permute-start(bf16[384,384]{1,0:T(8,128)(2,1)S(1)} %get-tuple-element.164), channel_id=1, source_target_pairs={{0,4},{1,5},{2,6},{3,7},{4,0},{5,1},{6,2},{7,3},{8,12},{9,13},{10,... | collective-permute-start | bytes 884744 | tf_op jit(solution)/shard_map/ppermute | solution.py:596
  56.5 7.8 %collective-permute-start.19 = (bf16[192,384]{1,0:T(8,128)(2,1)S(1)}, bf16[192,384]{1,0:T(8,128)(2,1)S(1)}, u32[]{:S(2)}, u32[]{:S(2)}) collective-permute-start(bf16[192,384]{1,0:T(8,128)(2,1)S(1)} %bm_sum.1.refs_2_.refs_0_), channel_id=1, source_target_pairs={{0,8},{1,9},{2,10},{3,11},{4,12},{5,13},{6,14},{7,15},{8,0},{9,1},... | collective-permute-start | bytes 442376 | tf_op jit(solution)/shard_map/ppermute | solution.py:596
  59.2 19.7 %collective-permute-start.23 = (bf16[112,384]{1,0:T(8,128)(2,1)S(1)}, bf16[112,384]{1,0:T(8,128)(2,1)S(1)}, u32[]{:S(2)}, u32[]{:S(2)}) collective-permute-start(bf16[112,384]{1,0:T(8,128)(2,1)S(1)} %get-tuple-element.169), channel_id=1, source_target_pairs={{0,1},{1,0},{2,3},{3,2},{4,5},{5,4},{6,7},{7,6},{8,9},{9,8},{10,11... | collective-permute-start | bytes 258056 | tf_op jit(solution)/shard_map/ppermute | solution.py:596
  60.2 10.0 %collective-permute-start.16 = (bf16[208,384]{1,0:T(8,128)(2,1)S(1)}, bf16[208,384]{1,0:T(8,128)(2,1)S(1)}, u32[]{:S(2)}, u32[]{:S(2)}) collective-permute-start(bf16[208,384]{1,0:T(8,128)(2,1)S(1)} %get-tuple-element.163), channel_id=1, source_target_pairs={{0,2},{1,3},{2,0},{3,1},{4,6},{5,7},{6,4},{7,5},{8,10},{9,11},{10,... | collective-permute-start | bytes 479240 | tf_op jit(solution)/shard_map/ppermute | solution.py:596
  61.4 5.7 %collective-permute-start.18 = (bf16[192,384]{1,0:T(8,128)(2,1)S(1)}, bf16[192,384]{1,0:T(8,128)(2,1)S(1)}, u32[]{:S(2)}, u32[]{:S(2)}) collective-permute-start(bf16[192,384]{1,0:T(8,128)(2,1)S(1)} %get-tuple-element.166), channel_id=1, source_target_pairs={{0,2},{1,3},{2,0},{3,1},{4,6},{5,7},{6,4},{7,5},{8,10},{9,11},{10,... | collective-permute-start | bytes 442376 | tf_op jit(solution)/shard_map/ppermute | solution.py:596
  64.3 6.3 %collective-permute-start.21 = (bf16[192,384]{1,0:T(8,128)(2,1)S(1)}, bf16[192,384]{1,0:T(8,128)(2,1)S(1)}, u32[]{:S(2)}, u32[]{:S(2)}) collective-permute-start(bf16[192,384]{1,0:T(8,128)(2,1)S(1)} %bm_total.1.refs_2_.refs_0_), channel_id=1, source_target_pairs={{0,4},{1,5},{2,6},{3,7},{4,0},{5,1},{6,2},{7,3},{8,12},{9,13},{10,... | collective-permute-start | bytes 442376 | tf_op jit(solution)/shard_map/ppermute | solution.py:596
  67.1 10.0 %collective-permute-start.24 = (bf16[192,384]{1,0:T(8,128)(2,1)S(1)}, bf16[192,384]{1,0:T(8,128)(2,1)S(1)}, u32[]{:S(2)}, u32[]{:S(2)}) collective-permute-start(bf16[192,384]{1,0:T(8,128)(2,1)S(1)} %am_sum.1.refs_2_.refs_0_), channel_id=1, source_target_pairs={{0,8},{1,9},{2,10},{3,11},{4,12},{5,13},{6,14},{7,15},{8,0},{9,1},... | collective-permute-start | bytes 442376 | tf_op jit(solution)/shard_map/ppermute | solution.py:596
  70.3 10.4 %collective-permute-start.20 = (bf16[112,384]{1,0:T(8,128)(2,1)S(1)}, bf16[112,384]{1,0:T(8,128)(2,1)S(1)}, u32[]{:S(2)}, u32[]{:S(2)}) collective-permute-start(bf16[112,384]{1,0:T(8,128)(2,1)S(1)} %get-tuple-element.168), channel_id=1, source_target_pairs={{0,4},{1,5},{2,6},{3,7},{4,0},{5,1},{6,2},{7,3},{8,12},{9,13},{10,... | collective-permute-start | bytes 258056 | tf_op jit(solution)/shard_map/ppermute | solution.py:596
  70.6 8.4 %collective-permute-start.22 = (bf16[384,384]{1,0:T(8,128)(2,1)S(1)}, bf16[384,384]{1,0:T(8,128)(2,1)S(1)}, u32[]{:S(2)}, u32[]{:S(2)}) collective-permute-start(bf16[384,384]{1,0:T(8,128)(2,1)S(1)} %bm_join2.1.refs_2_.refs_0_), channel_id=1, source_target_pairs={{0,2},{1,3},{2,0},{3,1},{4,6},{5,7},{6,4},{7,5},{8,10},{9,11},{10,... | collective-permute-start | bytes 884744 | tf_op jit(solution)/shard_map/ppermute | solution.py:596
  77.2 12.0 %collective-permute-start.26 = (bf16[192,384]{1,0:T(8,128)(2,1)S(1)}, bf16[192,384]{1,0:T(8,128)(2,1)S(1)}, u32[]{:S(2)}, u32[]{:S(2)}) collective-permute-start(bf16[192,384]{1,0:T(8,128)(2,1)S(1)} %am_total.1.refs_2_.refs_0_), channel_id=1, source_target_pairs={{0,2},{1,3},{2,0},{3,1},{4,6},{5,7},{6,4},{7,5},{8,10},{9,11},{10,... | collective-permute-start | bytes 442376 | tf_op jit(solution)/shard_map/ppermute | solution.py:596
  79.0 8.3 %collective-permute-start.27 = (bf16[112,384]{1,0:T(8,128)(2,1)S(1)}, bf16[112,384]{1,0:T(8,128)(2,1)S(1)}, u32[]{:S(2)}, u32[]{:S(2)}) collective-permute-start(bf16[112,384]{1,0:T(8,128)(2,1)S(1)} %ba_sum.1.refs_2_.refs_0_), channel_id=1, source_target_pairs={{0,8},{1,9},{2,10},{3,11},{4,12},{5,13},{6,14},{7,15},{8,0},{9,1},... | collective-permute-start | bytes 258056 | tf_op jit(solution)/shard_map/ppermute | solution.py:596
  79.1 12.3 %collective-permute-start.30 = (bf16[768,384]{1,0:T(8,128)(2,1)S(1)}, bf16[768,384]{1,0:T(8,128)(2,1)S(1)}, u32[]{:S(2)}, u32[]{:S(2)}) collective-permute-start(bf16[768,384]{1,0:T(8,128)(2,1)S(1)} %bm_join1.1.refs_2_.refs_0_), channel_id=1, source_target_pairs={{0,1},{1,0},{2,3},{3,2},{4,5},{5,4},{6,7},{7,6},{8,9},{9,8},{10,11... | collective-permute-start | bytes 1769480 | tf_op jit(solution)/shard_map/ppermute | solution.py:596
  80.7 9.2 %collective-permute-start.25 = (bf16[112,384]{1,0:T(8,128)(2,1)S(1)}, bf16[112,384]{1,0:T(8,128)(2,1)S(1)}, u32[]{:S(2)}, u32[]{:S(2)}) collective-permute-start(bf16[112,384]{1,0:T(8,128)(2,1)S(1)} %aa_sum.1.refs_2_.refs_0_), channel_id=1, source_target_pairs={{0,8},{1,9},{2,10},{3,11},{4,12},{5,13},{6,14},{7,15},{8,0},{9,1},... | collective-permute-start | bytes 258056 | tf_op jit(solution)/shard_map/ppermute | solution.py:596
  89.2 8.9 %collective-permute-start.33 = (bf16[384,384]{1,0:T(8,128)(2,1)S(1)}, bf16[384,384]{1,0:T(8,128)(2,1)S(1)}, u32[]{:S(2)}, u32[]{:S(2)}) collective-permute-start(bf16[384,384]{1,0:T(8,128)(2,1)S(1)} %am_join2.1.refs_2_.refs_0_), channel_id=1, source_target_pairs={{0,4},{1,5},{2,6},{3,7},{4,0},{5,1},{6,2},{7,3},{8,12},{9,13},{10,... | collective-permute-start | bytes 884744 | tf_op jit(solution)/shard_map/ppermute | solution.py:596
  90.0 7.3 %collective-permute-start.28 = (bf16[96,384]{1,0:T(8,128)(2,1)S(1)}, bf16[96,384]{1,0:T(8,128)(2,1)S(1)}, u32[]{:S(2)}, u32[]{:S(2)}) collective-permute-start(bf16[96,384]{1,0:T(8,128)(2,1)S(1)} %get-tuple-element.171.refs_2_.refs_0_), channel_id=1, source_target_pairs={{0,4},{1,5},{2,6},{3,7},{4,0},{5,1},{6,2},{7,3},{8,12},{9,13},{10,... | collective-permute-start | bytes 221192 | tf_op jit(solution)/shard_map/ppermute | solution.py:596
  91.8 8.7 %collective-permute-start.32 = (bf16[192,384]{1,0:T(8,128)(2,1)S(1)}, bf16[192,384]{1,0:T(8,128)(2,1)S(1)}, u32[]{:S(2)}, u32[]{:S(2)}) collective-permute-start(bf16[192,384]{1,0:T(8,128)(2,1)S(1)} %ba_join2.1.refs_2_.refs_0_), channel_id=1, source_target_pairs={{0,4},{1,5},{2,6},{3,7},{4,0},{5,1},{6,2},{7,3},{8,12},{9,13},{10,... | collective-permute-start | bytes 442376 | tf_op jit(solution)/shard_map/ppermute | solution.py:596
  98.2 9.9 %collective-permute-start.36 = (bf16[768,384]{1,0:T(8,128)(2,1)S(1)}, bf16[768,384]{1,0:T(8,128)(2,1)S(1)}, u32[]{:S(2)}, u32[]{:S(2)}) collective-permute-start(bf16[768,384]{1,0:T(8,128)(2,1)S(1)} %am_join1.1.refs_2_.refs_0_), channel_id=1, source_target_pairs={{0,1},{1,0},{2,3},{3,2},{4,5},{5,4},{6,7},{7,6},{8,9},{9,8},{10,11... | collective-permute-start | bytes 1769480 | tf_op jit(solution)/shard_map/ppermute | solution.py:596
  100.5 8.4 %collective-permute-start.35 = (bf16[384,384]{1,0:T(8,128)(2,1)S(1)}, bf16[384,384]{1,0:T(8,128)(2,1)S(1)}, u32[]{:S(2)}, u32[]{:S(2)}) collective-permute-start(bf16[384,384]{1,0:T(8,128)(2,1)S(1)} %ba_join1.1.refs_2_.refs_0_), channel_id=1, source_target_pairs={{0,2},{1,3},{2,0},{3,1},{4,6},{5,7},{6,4},{7,5},{8,10},{9,11},{10,... | collective-permute-start | bytes 884744 | tf_op jit(solution)/shard_map/ppermute | solution.py:596
  102.7 8.6 %collective-permute-start.34 = (bf16[384,384]{1,0:T(8,128)(2,1)S(1)}, bf16[384,384]{1,0:T(8,128)(2,1)S(1)}, u32[]{:S(2)}, u32[]{:S(2)}) collective-permute-start(bf16[384,384]{1,0:T(8,128)(2,1)S(1)} %aa_join1.1.refs_3_.refs_0_), channel_id=1, source_target_pairs={{0,1},{1,0},{2,3},{3,2},{4,5},{5,4},{6,7},{7,6},{8,9},{9,8},{10,11... | collective-permute-start | bytes 884744 | tf_op jit(solution)/shard_map/ppermute | solution.py:596
  (13 other events, 35.8 us)

commit v5 on v4

--- a/solution.py
+++ b/solution.py
@@ -20,7 +20,7 @@
 EPSILON = 1e-06
 MASKED = -1e30
 CHUNK_FF = 768
-ORDER = "bcwxydwzxwywxzywyzwyxwzxyzWxzyxzrYXZpq"
+ORDER = "bcwxydwzxywwxzywyzwyxwzxyzWxzyxzrYXZpq"
 DIMS = {
     "bm": ((0, 1, 2, 3), (1, 2, 0, 3)),
     "ba": ((1, 2, 0, 3), (2, 1, 0, 3)),
@@ -28,8 +28,9 @@
     "aa": ((0, 1, 2, 3), (1, 2, 0, 3)),
 }
 PART_ROWS = {"m": 4 * WIDTH, "a": 2 * WIDTH}
-COST = 10000000000
+COST = 26214400000
 PACK_COST = 10
+COSTS = {"bm_halve1": 0.5, "bm_sum": 0.001, "aa_halve0": 0.013, "ba_halve1": 0.002, "bm_halve2": 0.006, "back_a_attention": 0.5, "am_halve1": 0.005, "ba_halve2": 0.001, "aa_halve1": 0.5, "am_halve2": 0.025, "bm_total": 0.125, "am_sum": 0.5, "aa_halve2": 0.125, "bm_join2": 0.125, "am_total": 0.25, "ba_sum": 0.125, "bm_join1": 0.25, "aa_sum": 0.062, "ba_total": 0.02, "am_join2": 0.125, "aa_total": 0.1, "bm_join0": 0.125, "ba_join2": 0.125, "aa_join2": 0.125, "am_join1": 0.25, "ba_join1": 0.013, "aa_join1": 0.125, "back_b_attention": 0.5}
 PACK_VMEM = 55
 FIRST_VMEM = 8
 KA_VMEM = 16
@@ -506,7 +507,9 @@
                 scratch_shapes=list(scratch),
                 compiler_params=pltpu.CompilerParams(vmem_limit_bytes=int(vmem * 1024 * 1024)),
                 cost_estimate=pl.CostEstimate(
-                    flops=cost * COST, bytes_accessed=0, transcendentals=0
+                    flops=int(COSTS.get(name, cost) * COST),
+                    bytes_accessed=0,
+                    transcendentals=0,
                 ),
             )(*args, *before)
             self.last = results[mark]

time: 116 us -> 114 us (0.983)
  waiting for transfers between devices: 34.1 us -> 25 us
  starting transfers between devices: 38.8 us -> 46.3 us
    ppermute x28, waiting for transfers between devices: 33.1 us -> 25 us  [exchange(): return lax.ppermute(values_in, ('section', 'dp'), pairs)]
    ppermute x28, starting transfers between devices: 35.8 us -> 41.9 us  [exchange(): return lax.ppermute(values_in, ('section', 'dp'), pairs)]
    ppermute x11, starting transfers between devices: 3 us -> 4.36 us  [swap(): return lax.ppermute(values_in, 'section', [(0, 1), (1, 0)])]
  transfers between devices with their start and end apart: 39 -> 39, of which waited for: 16 -> 15; matrix products, arithmetic and copies ran while one was open for 0% -> 0% of each run, Pallas kernels for 24% -> 24%
where the time goes in v5:
time: 114 us
  starting transfers between devices  46.3 us (41%)
  Pallas kernels  40.6 us (36%)
  waiting for transfers between devices  25 us (22%)
  between operations  1.22 us (1%)
    ppermute x28, starting transfers between devices, exchange(): return lax.ppermute(values_in, ('section', 'dp'), pairs)  41.9 us
    pallas_call x42, Pallas kernels, run(): pl.pallas_call(body, out_shape=outs, name=name, in_specs=list(in_specs) +...  40.6 us
    ppermute x28, waiting for transfers between devices, exchange(): return lax.ppermute(values_in, ('section', 'dp'), pairs)  25 us
    ppermute x11, starting transfers between devices, swap(): return lax.ppermute(values_in, 'section', [(0, 1), (1, 0)])  4.36 us
  transfers between devices with their start and end apart: 39, of which 15 were waited for; matrix products, arithmetic and copies ran while one was open for 0% of the time, Pallas kernels for 24%

profile of v5, /device:TPU:0, one launch (start us, length us, event | category | flops | bytes accessed | tf_op | source)
XLA Modules:
  0.0 114.2 jit_solution(10681400416688884203)
XLA Ops:
  1.2 2.8 %pack.1 = (bf16[816,384]{1,0:T(8,128)(2,1)}, bf16[816,384]{1,0:T(8,128)(2,1)}) custom-call(bf16[197,2,384]{2,1,0:T(2,128)(2,1)} %bitcast.19, bf16[10,37,384]{2,1,0:T(8,128)(2,1)} %bitcast.18, bf16[384,384]{1,0:T(8,128)(2,1)} %bitcast.20, bf16[1,384]{1,0:T(2,128)(2,1)} %refs_3_.1, bf16[1,384]{1,0:T(2,128)(2,1)} %refs_4_.1, bf16[1,384]{1,0:T(2,128)(2,1)} %refs_5_.1, ...), custom_call_target="tpu_custom_call" | custom-call | flops 262144000000 | tf_op jit(solution)/shard_map/pack/pallas_call | solution.py:501
  7.1 3.6 %first_attention.1 = (bf16[2,816,384]{2,1,0:T(8,128)(2,1)S(1)}, f32[2,16,384]{2,1,0:T(8,128)S(1)}, bf16[416,384]{1,0:T(8,128)(2,1)S(1)}, bf16[416,1152]{1,0:T(8,...) custom-call(s32[2]{0:T(128)S(1)} %copy-done.3, ...), custom_call_target="tpu_custom_call" | custom-call | flops 26214400000 | tf_op jit(solution)/shard_map/first_attention/pallas_call | solution.py:501
  10.8 10.8 %forward.1 = (bf16[384,1536]{1,0:T(8,128)(2,1)S(1)}, bf16[1536,384]{1,0:T(8,128)(2,1)S(1)}, bf16[416,384]{1,0:T(8,128)(2,1)S(1)}, bf16[416,384]{1,0:T(8,128)(2,1...) custom-call(bf16[384,1536]{1,0:T(8,128)(2,1)S(1)} %bitcast.13, ...), custom_call_target="tpu_custom_call" | custom-call | flops 26214400000 | tf_op jit(solution)/shard_map/forward/pallas_call | solution.py:501
  22.1 4.6 %back_b_attention.1 = (bf16[416,384]{1,0:T(8,128)(2,1)S(1)}, bf16[784,384]{1,0:T(8,128)(2,1)S(1)}, bf16[784,384]{1,0:T(8,128)(2,1)S(1)}) custom-call(bf16[416,384]{1,0:T(8,128)(2,1)S(1)} %get-tuple-element.123.refs_0_, bf16[2,816,384]{2,1,0:T(8,128)(2,1)S(1)} %get-tuple-element.110.refs_4_.refs_1_.refs_0_, ...), custom_call_target="tpu_custom_call" | custom-call | flops 13107200000 | tf_op jit(solution)/shard_map/back_b_attention/pallas_call | solution.py:501
  26.8 3.5 %back_a_mlp.1 = (f32[416,384]{1,0:T(8,128)S(1)}, bf16[416,384]{1,0:T(8,128)(2,1)S(1)}, f32[16,384]{1,0:T(8,128)S(1)}, bf16[1536,384]{1,0:T(8,128)(2,1)S(1)}, bf16[1536,384]{1,0:T(8,128)(2,1)S(1)}) custom-call(bf16[2,816,384]{2,1,0:T(8,128)(2,1)S(1)} %get-tuple-element.110.refs_4_.refs_1_.refs_0_, ...), custom_call_target="tpu_custom_call" | custom-call | flops 26214400000 | tf_op jit(solution)/shard_map/back_a_mlp/pallas_call | solution.py:501
  31.2 2.8 %collective-permute-start.9 = (bf16[768,384]{1,0:T(8,128)(2,1)S(1)}, bf16[768,384]{1,0:T(8,128)(2,1)S(1)}, u32[]{:S(2)}, u32[]{:S(2)}) collective-permute-start(bf16[768,384]{1,0:T(8,128)(2,1)S(1)} %get-tuple-element.149), channel_id=1, source_target_pairs={{0,1},{1,0},{2,3},{3,2},{4,5},{5,4},{6,7},{7,6},{8,9},{9,8},{10,11... | collective-permute-start | bytes 1769480 | tf_op jit(solution)/shard_map/ppermute | solution.py:599
  34.2 1.6 %collective-permute-start.11 = (bf16[400,384]{1,0:T(8,128)(2,1)S(1)}, bf16[400,384]{1,0:T(8,128)(2,1)S(1)}, u32[]{:S(2)}, u32[]{:S(2)}) collective-permute-start(bf16[400,384]{1,0:T(8,128)(2,1)S(1)} %get-tuple-element.153), channel_id=1, source_target_pairs={{0,2},{1,3},{2,0},{3,1},{4,6},{5,7},{6,4},{7,5},{8,10},{9,11},{10,... | collective-permute-start | bytes 921608 | tf_op jit(solution)/shard_map/ppermute | solution.py:599
  36.9 4.6 %back_a_attention.1 = (bf16[416,384]{1,0:T(8,128)(2,1)S(1)}, bf16[416,384]{1,0:T(8,128)(2,1)S(1)}, bf16[784,384]{1,0:T(8,128)(2,1)S(1)}, bf16[784,384]{1,0:T(8,128)(2,1)S(1)}) custom-call(bf16[2,816,384]{2,1,0:T(8,128)(2,1)S(1)} %get-tuple-element.110.refs_4_.refs_1_.refs_0_, f32[2,16,384]{2,1,0:T(8,128)S(1)} %get-tuple-element.109.refs_6_.refs_9_.refs_2_.refs_1_.refs_0_, ...), custom_call_target="tpu_custom_call" | custom-call | flops 13107200000 | tf_op jit(solution)/shard_map/back_a_attention/pallas_call | solution.py:501
  42.1 2.1 %collective-permute-start.13 = (bf16[384,384]{1,0:T(8,128)(2,1)S(1)}, bf16[384,384]{1,0:T(8,128)(2,1)S(1)}, u32[]{:S(2)}, u32[]{:S(2)}) collective-permute-start(bf16[384,384]{1,0:T(8,128)(2,1)S(1)} %get-tuple-element.156), channel_id=1, source_target_pairs={{0,2},{1,3},{2,0},{3,1},{4,6},{5,7},{6,4},{7,5},{8,10},{9,11},{10,... | collective-permute-start | bytes 884744 | tf_op jit(solution)/shard_map/ppermute | solution.py:599
  44.4 1.6 %collective-permute-start.10 = (bf16[400,384]{1,0:T(8,128)(2,1)S(1)}, bf16[400,384]{1,0:T(8,128)(2,1)S(1)}, u32[]{:S(2)}, u32[]{:S(2)}) collective-permute-start(bf16[400,384]{1,0:T(8,128)(2,1)S(1)} %get-tuple-element.152), channel_id=1, source_target_pairs={{0,1},{1,0},{2,3},{3,2},{4,5},{5,4},{6,7},{7,6},{8,9},{9,8},{10,11... | collective-permute-start | bytes 921608 | tf_op jit(solution)/shard_map/ppermute | solution.py:599
  46.1 1.6 %collective-permute-start.12 = (bf16[208,384]{1,0:T(8,128)(2,1)S(1)}, bf16[208,384]{1,0:T(8,128)(2,1)S(1)}, u32[]{:S(2)}, u32[]{:S(2)}) collective-permute-start(bf16[208,384]{1,0:T(8,128)(2,1)S(1)} %get-tuple-element.155), channel_id=1, source_target_pairs={{0,4},{1,5},{2,6},{3,7},{4,0},{5,1},{6,2},{7,3},{8,12},{9,13},{10,... | collective-permute-start | bytes 479240 | tf_op jit(solution)/shard_map/ppermute | solution.py:599
  49.0 3.2 %collective-permute-start.15 = (bf16[192,384]{1,0:T(8,128)(2,1)S(1)}, bf16[192,384]{1,0:T(8,128)(2,1)S(1)}, u32[]{:S(2)}, u32[]{:S(2)}) collective-permute-start(bf16[192,384]{1,0:T(8,128)(2,1)S(1)} %get-tuple-element.160), channel_id=1, source_target_pairs={{0,4},{1,5},{2,6},{3,7},{4,0},{5,1},{6,2},{7,3},{8,12},{9,13},{10,... | collective-permute-start | bytes 442376 | tf_op jit(solution)/shard_map/ppermute | solution.py:599
  52.2 1.8 %collective-permute-start.7 = (bf16[416,384]{1,0:T(8,128)(2,1)S(1)}, bf16[416,384]{1,0:T(8,128)(2,1)S(1)}, u32[]{:S(2)}, u32[]{:S(2)}) collective-permute-start(bf16[416,384]{1,0:T(8,128)(2,1)S(1)} %get-tuple-element.146), channel_id=1, source_target_pairs={{0,16},{16,0},{1,17},{17,1},{2,18},{18,2},{3,19},{19,3},{4,20},{20... | collective-permute-start | bytes 958472 | tf_op jit(solution)/shard_map/ppermute | solution.py:680
  54.1 1.6 %collective-permute-start.17 = (bf16[384,384]{1,0:T(8,128)(2,1)S(1)}, bf16[384,384]{1,0:T(8,128)(2,1)S(1)}, u32[]{:S(2)}, u32[]{:S(2)}) collective-permute-start(bf16[384,384]{1,0:T(8,128)(2,1)S(1)} %get-tuple-element.164), channel_id=1, source_target_pairs={{0,4},{1,5},{2,6},{3,7},{4,0},{5,1},{6,2},{7,3},{8,12},{9,13},{10,... | collective-permute-start | bytes 884744 | tf_op jit(solution)/shard_map/ppermute | solution.py:599
  55.7 2.7 %collective-permute-start.19 = (bf16[192,384]{1,0:T(8,128)(2,1)S(1)}, bf16[192,384]{1,0:T(8,128)(2,1)S(1)}, u32[]{:S(2)}, u32[]{:S(2)}) collective-permute-start(bf16[192,384]{1,0:T(8,128)(2,1)S(1)} %bm_sum.1.refs_2_.refs_0_), channel_id=1, source_target_pairs={{0,8},{1,9},{2,10},{3,11},{4,12},{5,13},{6,14},{7,15},{8,0},{9,1},... | collective-permute-start | bytes 442376 | tf_op jit(solution)/shard_map/ppermute | solution.py:599
  59.6 2.8 %collective-permute-done.17.refs_1_ = bf16[384,384]{1,0:T(8,128)(2,1)S(1)} collective-permute-done((bf16[384,384]{1,0:T(8,128)(2,1)S(1)}, bf16[384,384]{1,0:T(8,128)(2,1)S(1)}, u32[]{:S(2)}, u32[]{:S(2)}) %collective-permute-start.17) | collective-permute-done | bytes 294944 | tf_op jit(solution)/shard_map/ppermute | solution.py:599
  62.6 1.7 %collective-permute-start.18 = (bf16[192,384]{1,0:T(8,128)(2,1)S(1)}, bf16[192,384]{1,0:T(8,128)(2,1)S(1)}, u32[]{:S(2)}, u32[]{:S(2)}) collective-permute-start(bf16[192,384]{1,0:T(8,128)(2,1)S(1)} %get-tuple-element.166), channel_id=1, source_target_pairs={{0,2},{1,3},{2,0},{3,1},{4,6},{5,7},{6,4},{7,5},{8,10},{9,11},{10,... | collective-permute-start | bytes 442376 | tf_op jit(solution)/shard_map/ppermute | solution.py:599
  66.0 1.6 %collective-permute-start.21 = (bf16[192,384]{1,0:T(8,128)(2,1)S(1)}, bf16[192,384]{1,0:T(8,128)(2,1)S(1)}, u32[]{:S(2)}, u32[]{:S(2)}) collective-permute-start(bf16[192,384]{1,0:T(8,128)(2,1)S(1)} %bm_total.1.refs_2_.refs_0_), channel_id=1, source_target_pairs={{0,4},{1,5},{2,6},{3,7},{4,0},{5,1},{6,2},{7,3},{8,12},{9,13},{10,... | collective-permute-start | bytes 442376 | tf_op jit(solution)/shard_map/ppermute | solution.py:599
  67.8 3.1 %collective-permute-start.24 = (bf16[192,384]{1,0:T(8,128)(2,1)S(1)}, bf16[192,384]{1,0:T(8,128)(2,1)S(1)}, u32[]{:S(2)}, u32[]{:S(2)}) collective-permute-start(bf16[192,384]{1,0:T(8,128)(2,1)S(1)} %am_sum.1.refs_2_.refs_0_), channel_id=1, source_target_pairs={{0,8},{1,9},{2,10},{3,11},{4,12},{5,13},{6,14},{7,15},{8,0},{9,1},... | collective-permute-start | bytes 442376 | tf_op jit(solution)/shard_map/ppermute | solution.py:599
  72.7 4.5 %collective-permute-done.24.refs_1_ = bf16[192,384]{1,0:T(8,128)(2,1)S(1)} collective-permute-done((bf16[192,384]{1,0:T(8,128)(2,1)S(1)}, bf16[192,384]{1,0:T(8,128)(2,1)S(1)}, u32[]{:S(2)}, u32[]{:S(2)}) %collective-permute-start.24) | collective-permute-done | bytes 147488 | tf_op jit(solution)/shard_map/ppermute | solution.py:599
  81.1 2.2 %collective-permute-start.25 = (bf16[112,384]{1,0:T(8,128)(2,1)S(1)}, bf16[112,384]{1,0:T(8,128)(2,1)S(1)}, u32[]{:S(2)}, u32[]{:S(2)}) collective-permute-start(bf16[112,384]{1,0:T(8,128)(2,1)S(1)} %aa_sum.1.refs_2_.refs_0_), channel_id=1, source_target_pairs={{0,8},{1,9},{2,10},{3,11},{4,12},{5,13},{6,14},{7,15},{8,0},{9,1},... | collective-permute-start | bytes 258056 | tf_op jit(solution)/shard_map/ppermute | solution.py:599
  83.3 3.4 %collective-permute-done.27.refs_1_ = bf16[112,384]{1,0:T(8,128)(2,1)S(1)} collective-permute-done((bf16[112,384]{1,0:T(8,128)(2,1)S(1)}, bf16[112,384]{1,0:T(8,128)(2,1)S(1)}, u32[]{:S(2)}, u32[]{:S(2)}) %collective-permute-start.27) | collective-permute-done | bytes 86048 | tf_op jit(solution)/shard_map/ppermute | solution.py:599
  87.3 1.6 %collective-permute-done.25.refs_1_ = bf16[112,384]{1,0:T(8,128)(2,1)S(1)} collective-permute-done((bf16[112,384]{1,0:T(8,128)(2,1)S(1)}, bf16[112,384]{1,0:T(8,128)(2,1)S(1)}, u32[]{:S(2)}, u32[]{:S(2)}) %collective-permute-start.25) | collective-permute-done | bytes 86048 | tf_op jit(solution)/shard_map/ppermute | solution.py:599
  89.0 1.6 %collective-permute-done.30.refs_1_ = bf16[768,384]{1,0:T(8,128)(2,1)S(1)} collective-permute-done((bf16[768,384]{1,0:T(8,128)(2,1)S(1)}, bf16[768,384]{1,0:T(8,128)(2,1)S(1)}, u32[]{:S(2)}, u32[]{:S(2)}) %collective-permute-start.30) | collective-permute-done | bytes 589856 | tf_op jit(solution)/shard_map/ppermute | solution.py:599
  91.6 2.8 %collective-permute-start.32 = (bf16[192,384]{1,0:T(8,128)(2,1)S(1)}, bf16[192,384]{1,0:T(8,128)(2,1)S(1)}, u32[]{:S(2)}, u32[]{:S(2)}) collective-permute-start(bf16[192,384]{1,0:T(8,128)(2,1)S(1)} %ba_join2.1.refs_2_.refs_0_), channel_id=1, source_target_pairs={{0,4},{1,5},{2,6},{3,7},{4,0},{5,1},{6,2},{7,3},{8,12},{9,13},{10,... | collective-permute-start | bytes 442376 | tf_op jit(solution)/shard_map/ppermute | solution.py:599
  94.4 1.7 %collective-permute-start.31 = (bf16[192,384]{1,0:T(8,128)(2,1)S(1)}, bf16[192,384]{1,0:T(8,128)(2,1)S(1)}, u32[]{:S(2)}, u32[]{:S(2)}) collective-permute-start(bf16[192,384]{1,0:T(8,128)(2,1)S(1)} %aa_join2.1.refs_2_.refs_0_), channel_id=1, source_target_pairs={{0,2},{1,3},{2,0},{3,1},{4,6},{5,7},{6,4},{7,5},{8,10},{9,11},{10,... | collective-permute-start | bytes 442376 | tf_op jit(solution)/shard_map/ppermute | solution.py:599
  96.2 1.7 %collective-permute-start.36 = (bf16[768,384]{1,0:T(8,128)(2,1)S(1)}, bf16[768,384]{1,0:T(8,128)(2,1)S(1)}, u32[]{:S(2)}, u32[]{:S(2)}) collective-permute-start(bf16[768,384]{1,0:T(8,128)(2,1)S(1)} %am_join1.1.refs_2_.refs_0_), channel_id=1, source_target_pairs={{0,1},{1,0},{2,3},{3,2},{4,5},{5,4},{6,7},{7,6},{8,9},{9,8},{10,11... | collective-permute-start | bytes 1769480 | tf_op jit(solution)/shard_map/ppermute | solution.py:599
  99.8 2.6 %collective-permute-start.34 = (bf16[384,384]{1,0:T(8,128)(2,1)S(1)}, bf16[384,384]{1,0:T(8,128)(2,1)S(1)}, u32[]{:S(2)}, u32[]{:S(2)}) collective-permute-start(bf16[384,384]{1,0:T(8,128)(2,1)S(1)} %aa_join1.1.refs_3_.refs_0_), channel_id=1, source_target_pairs={{0,1},{1,0},{2,3},{3,2},{4,5},{5,4},{6,7},{7,6},{8,9},{9,8},{10,11... | collective-permute-start | bytes 884744 | tf_op jit(solution)/shard_map/ppermute | solution.py:599
  103.9 2.3 %collective-permute-done.36.refs_1_ = bf16[768,384]{1,0:T(8,128)(2,1)S(1)} collective-permute-done((bf16[768,384]{1,0:T(8,128)(2,1)S(1)}, bf16[768,384]{1,0:T(8,128)(2,1)S(1)}, u32[]{:S(2)}, u32[]{:S(2)}) %collective-permute-start.36) | collective-permute-done | bytes 589856 | tf_op jit(solution)/shard_map/ppermute | solution.py:599
  106.7 2.7 %collective-permute-done.34.refs_1_ = bf16[384,384]{1,0:T(8,128)(2,1)S(1)} collective-permute-done((bf16[384,384]{1,0:T(8,128)(2,1)S(1)}, bf16[384,384]{1,0:T(8,128)(2,1)S(1)}, u32[]{:S(2)}, u32[]{:S(2)}) %collective-permute-start.34) | collective-permute-done | bytes 294944 | tf_op jit(solution)/shard_map/ppermute | solution.py:599
  109.6 2.3 %mlp_out.1 = (f32[1,384,1536]{2,1,0:T(8,128)}, f32[1,1536,384]{2,1,0:T(8,128)}, f32[8,128]{1,0:T(8,128)S(1)}) custom-call(bf16[1536,384]{1,0:T(8,128)(2,1)S(1)} %get-tuple-element.175.refs_2_.refs_0_, bf16[1536,384]{1,0:T(8,128)(2,1)S(1)} %collective-permute-done.38.refs_1_, bf16[768,384]{1,0:T(8,128)(2,1)S(1)} %get-tuple-element.176.refs_2_.refs_0_), custom_call_target="tpu_custom_call" | custom-call | flops 26214400000 | tf_op jit(solution)/shard_map/mlp_out/pallas_call | solution.py:501
  111.9 2.1 %attention_out.1 = (f32[1,384]{1,0:T(1,128)}, f32[1,384]{1,0:T(1,128)}, f32[1,384,1152]{2,1,0:T(8,128)}, f32[1,384]{1,0:T(1,128)}, f32[1,384]{1,0:T(1,128)}, /*i...) custom-call(bf16[768,384]{1,0:T(8,128)(2,1)S(1)} %get-tuple-element., ...), custom_call_target="tpu_custom_call" | custom-call | flops 26214400000 | tf_op jit(solution)/shard_map/attention_out/pallas_call | solution.py:501
  (100 shorter events, 23.4 us)
Async XLA Ops:
  4.1 6.7 %collective-permute-start.2 = (bf16[384,1536]{1,0:T(8,128)(2,1)S(1)}, bf16[384,1536]{1,0:T(8,128)(2,1)S(1)}, u32[]{:S(2)}, u32[]{:S(2)}) collective-permute-start(bf16[384,1536]{1,0:T(8,128)(2,1)S(1)} %bitcast.12), channel_id=1, source_target_pairs={{0,16},{16,0},{1,17},{17,1},{2,18},{18,2},{3,19},{19,3},{4,20},{20... | collective-permute-start | bytes 3538952 | tf_op jit(solution)/shard_map/ppermute | solution.py:680
  4.5 6.2 %collective-permute-start.3 = (bf16[1536,384]{1,0:T(8,128)(2,1)S(1)}, bf16[1536,384]{1,0:T(8,128)(2,1)S(1)}, u32[]{:S(2)}, u32[]{:S(2)}) collective-permute-start(bf16[1536,384]{1,0:T(8,128)(2,1)S(1)} %bitcast.14), channel_id=1, source_target_pairs={{0,16},{16,0},{1,17},{17,1},{2,18},{18,2},{3,19},{19,3},{4,20},{20... | collective-permute-start | bytes 3538952 | tf_op jit(solution)/shard_map/ppermute | solution.py:680
  21.6 9.2 %collective-permute-start.6 = (bf16[1536,384]{1,0:T(8,128)(2,1)S(1)}, bf16[1536,384]{1,0:T(8,128)(2,1)S(1)}, u32[]{:S(2)}, u32[]{:S(2)}) collective-permute-start(bf16[1536,384]{1,0:T(8,128)(2,1)S(1)} %get-tuple-element.141), channel_id=1, source_target_pairs={{0,16},{16,0},{1,17},{17,1},{2,18},{18,2},{3,19},{19,3},{4,20},{20... | collective-permute-start | bytes 3538952 | tf_op jit(solution)/shard_map/ppermute | solution.py:680
  26.6 7.4 %collective-permute-start.5 = (bf16[784,384]{1,0:T(8,128)(2,1)S(1)}, bf16[784,384]{1,0:T(8,128)(2,1)S(1)}, u32[]{:S(2)}, u32[]{:S(2)}) collective-permute-start(bf16[784,384]{1,0:T(8,128)(2,1)S(1)} %get-tuple-element.139), channel_id=1, source_target_pairs={{0,16},{16,0},{1,17},{17,1},{2,18},{18,2},{3,19},{19,3},{4,20},{20... | collective-permute-start | bytes 1806344 | tf_op jit(solution)/shard_map/ppermute | solution.py:680
  30.3 5.6 %collective-permute-start.4 = (bf16[1536,384]{1,0:T(8,128)(2,1)S(1)}, bf16[1536,384]{1,0:T(8,128)(2,1)S(1)}, u32[]{:S(2)}, u32[]{:S(2)}) collective-permute-start(bf16[1536,384]{1,0:T(8,128)(2,1)S(1)} %get-tuple-element.137), channel_id=1, source_target_pairs={{0,16},{16,0},{1,17},{17,1},{2,18},{18,2},{3,19},{19,3},{4,20},{20... | collective-permute-start | bytes 3538952 | tf_op jit(solution)/shard_map/ppermute | solution.py:680
  31.2 10.7 %collective-permute-start.9 = (bf16[768,384]{1,0:T(8,128)(2,1)S(1)}, bf16[768,384]{1,0:T(8,128)(2,1)S(1)}, u32[]{:S(2)}, u32[]{:S(2)}) collective-permute-start(bf16[768,384]{1,0:T(8,128)(2,1)S(1)} %get-tuple-element.149), channel_id=1, source_target_pairs={{0,1},{1,0},{2,3},{3,2},{4,5},{5,4},{6,7},{7,6},{8,9},{9,8},{10,11... | collective-permute-start | bytes 1769480 | tf_op jit(solution)/shard_map/ppermute | solution.py:599
  34.2 11.8 %collective-permute-start.11 = (bf16[400,384]{1,0:T(8,128)(2,1)S(1)}, bf16[400,384]{1,0:T(8,128)(2,1)S(1)}, u32[]{:S(2)}, u32[]{:S(2)}) collective-permute-start(bf16[400,384]{1,0:T(8,128)(2,1)S(1)} %get-tuple-element.153), channel_id=1, source_target_pairs={{0,2},{1,3},{2,0},{3,1},{4,6},{5,7},{6,4},{7,5},{8,10},{9,11},{10,... | collective-permute-start | bytes 921608 | tf_op jit(solution)/shard_map/ppermute | solution.py:599
  36.3 11.9 %collective-permute-start.14 = (bf16[768,384]{1,0:T(8,128)(2,1)S(1)}, bf16[768,384]{1,0:T(8,128)(2,1)S(1)}, u32[]{:S(2)}, u32[]{:S(2)}) collective-permute-start(bf16[768,384]{1,0:T(8,128)(2,1)S(1)} %get-tuple-element.157), channel_id=1, source_target_pairs={{0,1},{1,0},{2,3},{3,2},{4,5},{5,4},{6,7},{7,6},{8,9},{9,8},{10,11... | collective-permute-start | bytes 1769480 | tf_op jit(solution)/shard_map/ppermute | solution.py:599
  42.1 6.8 %collective-permute-start.13 = (bf16[384,384]{1,0:T(8,128)(2,1)S(1)}, bf16[384,384]{1,0:T(8,128)(2,1)S(1)}, u32[]{:S(2)}, u32[]{:S(2)}) collective-permute-start(bf16[384,384]{1,0:T(8,128)(2,1)S(1)} %get-tuple-element.156), channel_id=1, source_target_pairs={{0,2},{1,3},{2,0},{3,1},{4,6},{5,7},{6,4},{7,5},{8,10},{9,11},{10,... | collective-permute-start | bytes 884744 | tf_op jit(solution)/shard_map/ppermute | solution.py:599
  44.4 15.1 %collective-permute-start.10 = (bf16[400,384]{1,0:T(8,128)(2,1)S(1)}, bf16[400,384]{1,0:T(8,128)(2,1)S(1)}, u32[]{:S(2)}, u32[]{:S(2)}) collective-permute-start(bf16[400,384]{1,0:T(8,128)(2,1)S(1)} %get-tuple-element.152), channel_id=1, source_target_pairs={{0,1},{1,0},{2,3},{3,2},{4,5},{5,4},{6,7},{7,6},{8,9},{9,8},{10,11... | collective-permute-start | bytes 921608 | tf_op jit(solution)/shard_map/ppermute | solution.py:599
  46.1 12.2 %collective-permute-start.12 = (bf16[208,384]{1,0:T(8,128)(2,1)S(1)}, bf16[208,384]{1,0:T(8,128)(2,1)S(1)}, u32[]{:S(2)}, u32[]{:S(2)}) collective-permute-start(bf16[208,384]{1,0:T(8,128)(2,1)S(1)} %get-tuple-element.155), channel_id=1, source_target_pairs={{0,4},{1,5},{2,6},{3,7},{4,0},{5,1},{6,2},{7,3},{8,12},{9,13},{10,... | collective-permute-start | bytes 479240 | tf_op jit(solution)/shard_map/ppermute | solution.py:599
  49.0 6.6 %collective-permute-start.15 = (bf16[192,384]{1,0:T(8,128)(2,1)S(1)}, bf16[192,384]{1,0:T(8,128)(2,1)S(1)}, u32[]{:S(2)}, u32[]{:S(2)}) collective-permute-start(bf16[192,384]{1,0:T(8,128)(2,1)S(1)} %get-tuple-element.160), channel_id=1, source_target_pairs={{0,4},{1,5},{2,6},{3,7},{4,0},{5,1},{6,2},{7,3},{8,12},{9,13},{10,... | collective-permute-start | bytes 442376 | tf_op jit(solution)/shard_map/ppermute | solution.py:599
  52.2 50.2 %collective-permute-start.7 = (bf16[416,384]{1,0:T(8,128)(2,1)S(1)}, bf16[416,384]{1,0:T(8,128)(2,1)S(1)}, u32[]{:S(2)}, u32[]{:S(2)}) collective-permute-start(bf16[416,384]{1,0:T(8,128)(2,1)S(1)} %get-tuple-element.146), channel_id=1, source_target_pairs={{0,16},{16,0},{1,17},{17,1},{2,18},{18,2},{3,19},{19,3},{4,20},{20... | collective-permute-start | bytes 958472 | tf_op jit(solution)/shard_map/ppermute | solution.py:680
  54.1 8.4 %collective-permute-start.17 = (bf16[384,384]{1,0:T(8,128)(2,1)S(1)}, bf16[384,384]{1,0:T(8,128)(2,1)S(1)}, u32[]{:S(2)}, u32[]{:S(2)}) collective-permute-start(bf16[384,384]{1,0:T(8,128)(2,1)S(1)} %get-tuple-element.164), channel_id=1, source_target_pairs={{0,4},{1,5},{2,6},{3,7},{4,0},{5,1},{6,2},{7,3},{8,12},{9,13},{10,... | collective-permute-start | bytes 884744 | tf_op jit(solution)/shard_map/ppermute | solution.py:599
  55.7 10.3 %collective-permute-start.19 = (bf16[192,384]{1,0:T(8,128)(2,1)S(1)}, bf16[192,384]{1,0:T(8,128)(2,1)S(1)}, u32[]{:S(2)}, u32[]{:S(2)}) collective-permute-start(bf16[192,384]{1,0:T(8,128)(2,1)S(1)} %bm_sum.1.refs_2_.refs_0_), channel_id=1, source_target_pairs={{0,8},{1,9},{2,10},{3,11},{4,12},{5,13},{6,14},{7,15},{8,0},{9,1},... | collective-permute-start | bytes 442376 | tf_op jit(solution)/shard_map/ppermute | solution.py:599
  58.4 20.4 %collective-permute-start.23 = (bf16[112,384]{1,0:T(8,128)(2,1)S(1)}, bf16[112,384]{1,0:T(8,128)(2,1)S(1)}, u32[]{:S(2)}, u32[]{:S(2)}) collective-permute-start(bf16[112,384]{1,0:T(8,128)(2,1)S(1)} %get-tuple-element.169), channel_id=1, source_target_pairs={{0,1},{1,0},{2,3},{3,2},{4,5},{5,4},{6,7},{7,6},{8,9},{9,8},{10,11... | collective-permute-start | bytes 258056 | tf_op jit(solution)/shard_map/ppermute | solution.py:599
  64.3 6.7 %collective-permute-start.16 = (bf16[208,384]{1,0:T(8,128)(2,1)S(1)}, bf16[208,384]{1,0:T(8,128)(2,1)S(1)}, u32[]{:S(2)}, u32[]{:S(2)}) collective-permute-start(bf16[208,384]{1,0:T(8,128)(2,1)S(1)} %get-tuple-element.163), channel_id=1, source_target_pairs={{0,2},{1,3},{2,0},{3,1},{4,6},{5,7},{6,4},{7,5},{8,10},{9,11},{10,... | collective-permute-start | bytes 479240 | tf_op jit(solution)/shard_map/ppermute | solution.py:599
  66.0 6.4 %collective-permute-start.21 = (bf16[192,384]{1,0:T(8,128)(2,1)S(1)}, bf16[192,384]{1,0:T(8,128)(2,1)S(1)}, u32[]{:S(2)}, u32[]{:S(2)}) collective-permute-start(bf16[192,384]{1,0:T(8,128)(2,1)S(1)} %bm_total.1.refs_2_.refs_0_), channel_id=1, source_target_pairs={{0,4},{1,5},{2,6},{3,7},{4,0},{5,1},{6,2},{7,3},{8,12},{9,13},{10,... | collective-permute-start | bytes 442376 | tf_op jit(solution)/shard_map/ppermute | solution.py:599
  67.8 9.4 %collective-permute-start.24 = (bf16[192,384]{1,0:T(8,128)(2,1)S(1)}, bf16[192,384]{1,0:T(8,128)(2,1)S(1)}, u32[]{:S(2)}, u32[]{:S(2)}) collective-permute-start(bf16[192,384]{1,0:T(8,128)(2,1)S(1)} %am_sum.1.refs_2_.refs_0_), channel_id=1, source_target_pairs={{0,8},{1,9},{2,10},{3,11},{4,12},{5,13},{6,14},{7,15},{8,0},{9,1},... | collective-permute-start | bytes 442376 | tf_op jit(solution)/shard_map/ppermute | solution.py:599
  71.0 10.0 %collective-permute-start.20 = (bf16[112,384]{1,0:T(8,128)(2,1)S(1)}, bf16[112,384]{1,0:T(8,128)(2,1)S(1)}, u32[]{:S(2)}, u32[]{:S(2)}) collective-permute-start(bf16[112,384]{1,0:T(8,128)(2,1)S(1)} %get-tuple-element.168), channel_id=1, source_target_pairs={{0,4},{1,5},{2,6},{3,7},{4,0},{5,1},{6,2},{7,3},{8,12},{9,13},{10,... | collective-permute-start | bytes 258056 | tf_op jit(solution)/shard_map/ppermute | solution.py:599
  72.5 7.4 %collective-permute-start.22 = (bf16[384,384]{1,0:T(8,128)(2,1)S(1)}, bf16[384,384]{1,0:T(8,128)(2,1)S(1)}, u32[]{:S(2)}, u32[]{:S(2)}) collective-permute-start(bf16[384,384]{1,0:T(8,128)(2,1)S(1)} %bm_join2.1.refs_2_.refs_0_), channel_id=1, source_target_pairs={{0,2},{1,3},{2,0},{3,1},{4,6},{5,7},{6,4},{7,5},{8,10},{9,11},{10,... | collective-permute-start | bytes 884744 | tf_op jit(solution)/shard_map/ppermute | solution.py:599
  77.3 9.5 %collective-permute-start.26 = (bf16[192,384]{1,0:T(8,128)(2,1)S(1)}, bf16[192,384]{1,0:T(8,128)(2,1)S(1)}, u32[]{:S(2)}, u32[]{:S(2)}) collective-permute-start(bf16[192,384]{1,0:T(8,128)(2,1)S(1)} %am_total.1.refs_2_.refs_0_), channel_id=1, source_target_pairs={{0,2},{1,3},{2,0},{3,1},{4,6},{5,7},{6,4},{7,5},{8,10},{9,11},{10,... | collective-permute-start | bytes 442376 | tf_op jit(solution)/shard_map/ppermute | solution.py:599
  78.8 7.8 %collective-permute-start.27 = (bf16[112,384]{1,0:T(8,128)(2,1)S(1)}, bf16[112,384]{1,0:T(8,128)(2,1)S(1)}, u32[]{:S(2)}, u32[]{:S(2)}) collective-permute-start(bf16[112,384]{1,0:T(8,128)(2,1)S(1)} %ba_sum.1.refs_2_.refs_0_), channel_id=1, source_target_pairs={{0,8},{1,9},{2,10},{3,11},{4,12},{5,13},{6,14},{7,15},{8,0},{9,1},... | collective-permute-start | bytes 258056 | tf_op jit(solution)/shard_map/ppermute | solution.py:599
  79.9 10.7 %collective-permute-start.30 = (bf16[768,384]{1,0:T(8,128)(2,1)S(1)}, bf16[768,384]{1,0:T(8,128)(2,1)S(1)}, u32[]{:S(2)}, u32[]{:S(2)}) collective-permute-start(bf16[768,384]{1,0:T(8,128)(2,1)S(1)} %bm_join1.1.refs_2_.refs_0_), channel_id=1, source_target_pairs={{0,1},{1,0},{2,3},{3,2},{4,5},{5,4},{6,7},{7,6},{8,9},{9,8},{10,11... | collective-permute-start | bytes 1769480 | tf_op jit(solution)/shard_map/ppermute | solution.py:599
  81.1 7.8 %collective-permute-start.25 = (bf16[112,384]{1,0:T(8,128)(2,1)S(1)}, bf16[112,384]{1,0:T(8,128)(2,1)S(1)}, u32[]{:S(2)}, u32[]{:S(2)}) collective-permute-start(bf16[112,384]{1,0:T(8,128)(2,1)S(1)} %aa_sum.1.refs_2_.refs_0_), channel_id=1, source_target_pairs={{0,8},{1,9},{2,10},{3,11},{4,12},{5,13},{6,14},{7,15},{8,0},{9,1},... | collective-permute-start | bytes 258056 | tf_op jit(solution)/shard_map/ppermute | solution.py:599
  86.8 9.3 %collective-permute-start.33 = (bf16[384,384]{1,0:T(8,128)(2,1)S(1)}, bf16[384,384]{1,0:T(8,128)(2,1)S(1)}, u32[]{:S(2)}, u32[]{:S(2)}) collective-permute-start(bf16[384,384]{1,0:T(8,128)(2,1)S(1)} %am_join2.1.refs_2_.refs_0_), channel_id=1, source_target_pairs={{0,4},{1,5},{2,6},{3,7},{4,0},{5,1},{6,2},{7,3},{8,12},{9,13},{10,... | collective-permute-start | bytes 884744 | tf_op jit(solution)/shard_map/ppermute | solution.py:599
  88.9 5.5 %collective-permute-start.28 = (bf16[96,384]{1,0:T(8,128)(2,1)S(1)}, bf16[96,384]{1,0:T(8,128)(2,1)S(1)}, u32[]{:S(2)}, u32[]{:S(2)}) collective-permute-start(bf16[96,384]{1,0:T(8,128)(2,1)S(1)} %get-tuple-element.171.refs_2_.refs_0_), channel_id=1, source_target_pairs={{0,4},{1,5},{2,6},{3,7},{4,0},{5,1},{6,2},{7,3},{8,12},{9,13},{10,... | collective-permute-start | bytes 221192 | tf_op jit(solution)/shard_map/ppermute | solution.py:599
  91.6 7.5 %collective-permute-start.32 = (bf16[192,384]{1,0:T(8,128)(2,1)S(1)}, bf16[192,384]{1,0:T(8,128)(2,1)S(1)}, u32[]{:S(2)}, u32[]{:S(2)}) collective-permute-start(bf16[192,384]{1,0:T(8,128)(2,1)S(1)} %ba_join2.1.refs_2_.refs_0_), channel_id=1, source_target_pairs={{0,4},{1,5},{2,6},{3,7},{4,0},{5,1},{6,2},{7,3},{8,12},{9,13},{10,... | collective-permute-start | bytes 442376 | tf_op jit(solution)/shard_map/ppermute | solution.py:599
  94.4 5.3 %collective-permute-start.31 = (bf16[192,384]{1,0:T(8,128)(2,1)S(1)}, bf16[192,384]{1,0:T(8,128)(2,1)S(1)}, u32[]{:S(2)}, u32[]{:S(2)}) collective-permute-start(bf16[192,384]{1,0:T(8,128)(2,1)S(1)} %aa_join2.1.refs_2_.refs_0_), channel_id=1, source_target_pairs={{0,2},{1,3},{2,0},{3,1},{4,6},{5,7},{6,4},{7,5},{8,10},{9,11},{10,... | collective-permute-start | bytes 442376 | tf_op jit(solution)/shard_map/ppermute | solution.py:599
  96.2 9.9 %collective-permute-start.36 = (bf16[768,384]{1,0:T(8,128)(2,1)S(1)}, bf16[768,384]{1,0:T(8,128)(2,1)S(1)}, u32[]{:S(2)}, u32[]{:S(2)}) collective-permute-start(bf16[768,384]{1,0:T(8,128)(2,1)S(1)} %am_join1.1.refs_2_.refs_0_), channel_id=1, source_target_pairs={{0,1},{1,0},{2,3},{3,2},{4,5},{5,4},{6,7},{7,6},{8,9},{9,8},{10,11... | collective-permute-start | bytes 1769480 | tf_op jit(solution)/shard_map/ppermute | solution.py:599
  99.1 7.5 %collective-permute-start.35 = (bf16[384,384]{1,0:T(8,128)(2,1)S(1)}, bf16[384,384]{1,0:T(8,128)(2,1)S(1)}, u32[]{:S(2)}, u32[]{:S(2)}) collective-permute-start(bf16[384,384]{1,0:T(8,128)(2,1)S(1)} %ba_join1.1.refs_2_.refs_0_), channel_id=1, source_target_pairs={{0,2},{1,3},{2,0},{3,1},{4,6},{5,7},{6,4},{7,5},{8,10},{9,11},{10,... | collective-permute-start | bytes 884744 | tf_op jit(solution)/shard_map/ppermute | solution.py:599
  99.8 9.5 %collective-permute-start.34 = (bf16[384,384]{1,0:T(8,128)(2,1)S(1)}, bf16[384,384]{1,0:T(8,128)(2,1)S(1)}, u32[]{:S(2)}, u32[]{:S(2)}) collective-permute-start(bf16[384,384]{1,0:T(8,128)(2,1)S(1)} %aa_join1.1.refs_3_.refs_0_), channel_id=1, source_target_pairs={{0,1},{1,0},{2,3},{3,2},{4,5},{5,4},{6,7},{7,6},{8,9},{9,8},{10,11... | collective-permute-start | bytes 884744 | tf_op jit(solution)/shard_map/ppermute | solution.py:599
  (13 other events, 39.1 us)

commit v6 on v5

--- a/solution.py
+++ b/solution.py
@@ -575,19 +575,19 @@
     join_rows(out, own, recv, bit_of(dims, step))
 
 
-def last_join_kernel(dims, own, recv, other, mine, send, whole):
-    join_rows(whole, own, recv, bit_of(dims, 0))
+def last_join_kernel(dims, own, recv, other, mine, send):
+    bit = bit_of(dims, 0)
     core = lax.axis_index("section")
 
     @pl.when(core == 0)
     def _():
-        mine[...] = whole[...]
+        join_rows(mine, own, recv, bit)
         send[...] = other[...]
 
     @pl.when(core == 1)
     def _():
+        join_rows(send, own, recv, bit)
         mine[...] = other[...]
-        send[...] = whole[...]
 
 
 def exchange(values_in, dims, step):
@@ -655,7 +655,6 @@
             [shape(self.count, WIDTH)] * 2,
             [VMEM] * 3,
             [VMEM] * 2,
-            [pltpu.VMEM((self.count, WIDTH), BF16)],
         )(*self.pair, other.whole)
         return mine, swap(send)
 

time: 114 us -> 114 us (level)
  no operation moved by 1% of the time
where the time goes in v6:
time: 114 us
  starting transfers between devices  46.3 us (41%)
  Pallas kernels  40.4 us (35%)
  waiting for transfers between devices  25.1 us (22%)
  between operations  1.22 us (1%)
    ppermute x28, starting transfers between devices, exchange(): return lax.ppermute(values_in, ('section', 'dp'), pairs)  41.9 us
    pallas_call x42, Pallas kernels, run(): pl.pallas_call(body, out_shape=outs, name=name, in_specs=list(in_specs) +...  40.4 us
    ppermute x28, waiting for transfers between devices, exchange(): return lax.ppermute(values_in, ('section', 'dp'), pairs)  25.1 us
    ppermute x11, starting transfers between devices, swap(): return lax.ppermute(values_in, 'section', [(0, 1), (1, 0)])  4.36 us
  transfers between devices with their start and end apart: 39, of which 15 were waited for; matrix products, arithmetic and copies ran while one was open for 0% of the time, Pallas kernels for 24%

profile of v6, /device:TPU:0, one launch (start us, length us, event | category | flops | bytes accessed | tf_op | source)
XLA Modules:
  0.0 114.1 jit_solution(4123078095118293887)
XLA Ops:
  1.2 2.8 %pack.1 = (bf16[816,384]{1,0:T(8,128)(2,1)}, bf16[816,384]{1,0:T(8,128)(2,1)}) custom-call(bf16[197,2,384]{2,1,0:T(2,128)(2,1)} %bitcast.19, bf16[10,37,384]{2,1,0:T(8,128)(2,1)} %bitcast.18, bf16[384,384]{1,0:T(8,128)(2,1)} %bitcast.20, bf16[1,384]{1,0:T(2,128)(2,1)} %refs_3_.1, bf16[1,384]{1,0:T(2,128)(2,1)} %refs_4_.1, bf16[1,384]{1,0:T(2,128)(2,1)} %refs_5_.1, ...), custom_call_target="tpu_custom_call" | custom-call | flops 262144000000 | tf_op jit(solution)/shard_map/pack/pallas_call | solution.py:501
  7.1 3.6 %first_attention.1 = (bf16[2,816,384]{2,1,0:T(8,128)(2,1)S(1)}, f32[2,16,384]{2,1,0:T(8,128)S(1)}, bf16[416,384]{1,0:T(8,128)(2,1)S(1)}, bf16[416,1152]{1,0:T(8,...) custom-call(s32[2]{0:T(128)S(1)} %copy-done.3, ...), custom_call_target="tpu_custom_call" | custom-call | flops 26214400000 | tf_op jit(solution)/shard_map/first_attention/pallas_call | solution.py:501
  10.8 10.8 %forward.1 = (bf16[384,1536]{1,0:T(8,128)(2,1)S(1)}, bf16[1536,384]{1,0:T(8,128)(2,1)S(1)}, bf16[416,384]{1,0:T(8,128)(2,1)S(1)}, bf16[416,384]{1,0:T(8,128)(2,1...) custom-call(bf16[384,1536]{1,0:T(8,128)(2,1)S(1)} %bitcast.13, ...), custom_call_target="tpu_custom_call" | custom-call | flops 26214400000 | tf_op jit(solution)/shard_map/forward/pallas_call | solution.py:501
  22.1 4.6 %back_b_attention.1 = (bf16[416,384]{1,0:T(8,128)(2,1)S(1)}, bf16[784,384]{1,0:T(8,128)(2,1)S(1)}, bf16[784,384]{1,0:T(8,128)(2,1)S(1)}) custom-call(bf16[416,384]{1,0:T(8,128)(2,1)S(1)} %get-tuple-element.123.refs_0_, bf16[2,816,384]{2,1,0:T(8,128)(2,1)S(1)} %get-tuple-element.110.refs_4_.refs_1_.refs_0_, ...), custom_call_target="tpu_custom_call" | custom-call | flops 13107200000 | tf_op jit(solution)/shard_map/back_b_attention/pallas_call | solution.py:501
  26.8 3.5 %back_a_mlp.1 = (f32[416,384]{1,0:T(8,128)S(1)}, bf16[416,384]{1,0:T(8,128)(2,1)S(1)}, f32[16,384]{1,0:T(8,128)S(1)}, bf16[1536,384]{1,0:T(8,128)(2,1)S(1)}, bf16[1536,384]{1,0:T(8,128)(2,1)S(1)}) custom-call(bf16[2,816,384]{2,1,0:T(8,128)(2,1)S(1)} %get-tuple-element.110.refs_4_.refs_1_.refs_0_, ...), custom_call_target="tpu_custom_call" | custom-call | flops 26214400000 | tf_op jit(solution)/shard_map/back_a_mlp/pallas_call | solution.py:501
  31.2 2.8 %collective-permute-start.9 = (bf16[768,384]{1,0:T(8,128)(2,1)S(1)}, bf16[768,384]{1,0:T(8,128)(2,1)S(1)}, u32[]{:S(2)}, u32[]{:S(2)}) collective-permute-start(bf16[768,384]{1,0:T(8,128)(2,1)S(1)} %get-tuple-element.149), channel_id=1, source_target_pairs={{0,1},{1,0},{2,3},{3,2},{4,5},{5,4},{6,7},{7,6},{8,9},{9,8},{10,11... | collective-permute-start | bytes 1769480 | tf_op jit(solution)/shard_map/ppermute | solution.py:599
  34.2 1.6 %collective-permute-start.11 = (bf16[400,384]{1,0:T(8,128)(2,1)S(1)}, bf16[400,384]{1,0:T(8,128)(2,1)S(1)}, u32[]{:S(2)}, u32[]{:S(2)}) collective-permute-start(bf16[400,384]{1,0:T(8,128)(2,1)S(1)} %get-tuple-element.153), channel_id=1, source_target_pairs={{0,2},{1,3},{2,0},{3,1},{4,6},{5,7},{6,4},{7,5},{8,10},{9,11},{10,... | collective-permute-start | bytes 921608 | tf_op jit(solution)/shard_map/ppermute | solution.py:599
  36.9 4.6 %back_a_attention.1 = (bf16[416,384]{1,0:T(8,128)(2,1)S(1)}, bf16[416,384]{1,0:T(8,128)(2,1)S(1)}, bf16[784,384]{1,0:T(8,128)(2,1)S(1)}, bf16[784,384]{1,0:T(8,128)(2,1)S(1)}) custom-call(bf16[2,816,384]{2,1,0:T(8,128)(2,1)S(1)} %get-tuple-element.110.refs_4_.refs_1_.refs_0_, f32[2,16,384]{2,1,0:T(8,128)S(1)} %get-tuple-element.109.refs_6_.refs_9_.refs_2_.refs_1_.refs_0_, ...), custom_call_target="tpu_custom_call" | custom-call | flops 13107200000 | tf_op jit(solution)/shard_map/back_a_attention/pallas_call | solution.py:501
  42.1 2.1 %collective-permute-start.13 = (bf16[384,384]{1,0:T(8,128)(2,1)S(1)}, bf16[384,384]{1,0:T(8,128)(2,1)S(1)}, u32[]{:S(2)}, u32[]{:S(2)}) collective-permute-start(bf16[384,384]{1,0:T(8,128)(2,1)S(1)} %get-tuple-element.156), channel_id=1, source_target_pairs={{0,2},{1,3},{2,0},{3,1},{4,6},{5,7},{6,4},{7,5},{8,10},{9,11},{10,... | collective-permute-start | bytes 884744 | tf_op jit(solution)/shard_map/ppermute | solution.py:599
  44.4 1.6 %collective-permute-start.10 = (bf16[400,384]{1,0:T(8,128)(2,1)S(1)}, bf16[400,384]{1,0:T(8,128)(2,1)S(1)}, u32[]{:S(2)}, u32[]{:S(2)}) collective-permute-start(bf16[400,384]{1,0:T(8,128)(2,1)S(1)} %get-tuple-element.152), channel_id=1, source_target_pairs={{0,1},{1,0},{2,3},{3,2},{4,5},{5,4},{6,7},{7,6},{8,9},{9,8},{10,11... | collective-permute-start | bytes 921608 | tf_op jit(solution)/shard_map/ppermute | solution.py:599
  46.1 1.6 %collective-permute-start.12 = (bf16[208,384]{1,0:T(8,128)(2,1)S(1)}, bf16[208,384]{1,0:T(8,128)(2,1)S(1)}, u32[]{:S(2)}, u32[]{:S(2)}) collective-permute-start(bf16[208,384]{1,0:T(8,128)(2,1)S(1)} %get-tuple-element.155), channel_id=1, source_target_pairs={{0,4},{1,5},{2,6},{3,7},{4,0},{5,1},{6,2},{7,3},{8,12},{9,13},{10,... | collective-permute-start | bytes 479240 | tf_op jit(solution)/shard_map/ppermute | solution.py:599
  49.0 3.2 %collective-permute-start.15 = (bf16[192,384]{1,0:T(8,128)(2,1)S(1)}, bf16[192,384]{1,0:T(8,128)(2,1)S(1)}, u32[]{:S(2)}, u32[]{:S(2)}) collective-permute-start(bf16[192,384]{1,0:T(8,128)(2,1)S(1)} %get-tuple-element.160), channel_id=1, source_target_pairs={{0,4},{1,5},{2,6},{3,7},{4,0},{5,1},{6,2},{7,3},{8,12},{9,13},{10,... | collective-permute-start | bytes 442376 | tf_op jit(solution)/shard_map/ppermute | solution.py:599
  52.2 1.8 %collective-permute-start.7 = (bf16[416,384]{1,0:T(8,128)(2,1)S(1)}, bf16[416,384]{1,0:T(8,128)(2,1)S(1)}, u32[]{:S(2)}, u32[]{:S(2)}) collective-permute-start(bf16[416,384]{1,0:T(8,128)(2,1)S(1)} %get-tuple-element.146), channel_id=1, source_target_pairs={{0,16},{16,0},{1,17},{17,1},{2,18},{18,2},{3,19},{19,3},{4,20},{20... | collective-permute-start | bytes 958472 | tf_op jit(solution)/shard_map/ppermute | solution.py:679
  54.1 1.6 %collective-permute-start.17 = (bf16[384,384]{1,0:T(8,128)(2,1)S(1)}, bf16[384,384]{1,0:T(8,128)(2,1)S(1)}, u32[]{:S(2)}, u32[]{:S(2)}) collective-permute-start(bf16[384,384]{1,0:T(8,128)(2,1)S(1)} %get-tuple-element.164), channel_id=1, source_target_pairs={{0,4},{1,5},{2,6},{3,7},{4,0},{5,1},{6,2},{7,3},{8,12},{9,13},{10,... | collective-permute-start | bytes 884744 | tf_op jit(solution)/shard_map/ppermute | solution.py:599
  55.7 2.7 %collective-permute-start.19 = (bf16[192,384]{1,0:T(8,128)(2,1)S(1)}, bf16[192,384]{1,0:T(8,128)(2,1)S(1)}, u32[]{:S(2)}, u32[]{:S(2)}) collective-permute-start(bf16[192,384]{1,0:T(8,128)(2,1)S(1)} %bm_sum.1.refs_2_.refs_0_), channel_id=1, source_target_pairs={{0,8},{1,9},{2,10},{3,11},{4,12},{5,13},{6,14},{7,15},{8,0},{9,1},... | collective-permute-start | bytes 442376 | tf_op jit(solution)/shard_map/ppermute | solution.py:599
  59.6 2.8 %collective-permute-done.17.refs_1_ = bf16[384,384]{1,0:T(8,128)(2,1)S(1)} collective-permute-done((bf16[384,384]{1,0:T(8,128)(2,1)S(1)}, bf16[384,384]{1,0:T(8,128)(2,1)S(1)}, u32[]{:S(2)}, u32[]{:S(2)}) %collective-permute-start.17) | collective-permute-done | bytes 294944 | tf_op jit(solution)/shard_map/ppermute | solution.py:599
  62.6 1.7 %collective-permute-start.18 = (bf16[192,384]{1,0:T(8,128)(2,1)S(1)}, bf16[192,384]{1,0:T(8,128)(2,1)S(1)}, u32[]{:S(2)}, u32[]{:S(2)}) collective-permute-start(bf16[192,384]{1,0:T(8,128)(2,1)S(1)} %get-tuple-element.166), channel_id=1, source_target_pairs={{0,2},{1,3},{2,0},{3,1},{4,6},{5,7},{6,4},{7,5},{8,10},{9,11},{10,... | collective-permute-start | bytes 442376 | tf_op jit(solution)/shard_map/ppermute | solution.py:599
  66.0 1.6 %collective-permute-start.21 = (bf16[192,384]{1,0:T(8,128)(2,1)S(1)}, bf16[192,384]{1,0:T(8,128)(2,1)S(1)}, u32[]{:S(2)}, u32[]{:S(2)}) collective-permute-start(bf16[192,384]{1,0:T(8,128)(2,1)S(1)} %bm_total.1.refs_2_.refs_0_), channel_id=1, source_target_pairs={{0,4},{1,5},{2,6},{3,7},{4,0},{5,1},{6,2},{7,3},{8,12},{9,13},{10,... | collective-permute-start | bytes 442376 | tf_op jit(solution)/shard_map/ppermute | solution.py:599
  67.8 3.1 %collective-permute-start.24 = (bf16[192,384]{1,0:T(8,128)(2,1)S(1)}, bf16[192,384]{1,0:T(8,128)(2,1)S(1)}, u32[]{:S(2)}, u32[]{:S(2)}) collective-permute-start(bf16[192,384]{1,0:T(8,128)(2,1)S(1)} %am_sum.1.refs_2_.refs_0_), channel_id=1, source_target_pairs={{0,8},{1,9},{2,10},{3,11},{4,12},{5,13},{6,14},{7,15},{8,0},{9,1},... | collective-permute-start | bytes 442376 | tf_op jit(solution)/shard_map/ppermute | solution.py:599
  72.7 4.5 %collective-permute-done.24.refs_1_ = bf16[192,384]{1,0:T(8,128)(2,1)S(1)} collective-permute-done((bf16[192,384]{1,0:T(8,128)(2,1)S(1)}, bf16[192,384]{1,0:T(8,128)(2,1)S(1)}, u32[]{:S(2)}, u32[]{:S(2)}) %collective-permute-start.24) | collective-permute-done | bytes 147488 | tf_op jit(solution)/shard_map/ppermute | solution.py:599
  81.1 2.2 %collective-permute-start.25 = (bf16[112,384]{1,0:T(8,128)(2,1)S(1)}, bf16[112,384]{1,0:T(8,128)(2,1)S(1)}, u32[]{:S(2)}, u32[]{:S(2)}) collective-permute-start(bf16[112,384]{1,0:T(8,128)(2,1)S(1)} %aa_sum.1.refs_2_.refs_0_), channel_id=1, source_target_pairs={{0,8},{1,9},{2,10},{3,11},{4,12},{5,13},{6,14},{7,15},{8,0},{9,1},... | collective-permute-start | bytes 258056 | tf_op jit(solution)/shard_map/ppermute | solution.py:599
  83.3 3.4 %collective-permute-done.27.refs_1_ = bf16[112,384]{1,0:T(8,128)(2,1)S(1)} collective-permute-done((bf16[112,384]{1,0:T(8,128)(2,1)S(1)}, bf16[112,384]{1,0:T(8,128)(2,1)S(1)}, u32[]{:S(2)}, u32[]{:S(2)}) %collective-permute-start.27) | collective-permute-done | bytes 86048 | tf_op jit(solution)/shard_map/ppermute | solution.py:599
  87.3 1.6 %collective-permute-done.25.refs_1_ = bf16[112,384]{1,0:T(8,128)(2,1)S(1)} collective-permute-done((bf16[112,384]{1,0:T(8,128)(2,1)S(1)}, bf16[112,384]{1,0:T(8,128)(2,1)S(1)}, u32[]{:S(2)}, u32[]{:S(2)}) %collective-permute-start.25) | collective-permute-done | bytes 86048 | tf_op jit(solution)/shard_map/ppermute | solution.py:599
  89.0 1.6 %collective-permute-done.30.refs_1_ = bf16[768,384]{1,0:T(8,128)(2,1)S(1)} collective-permute-done((bf16[768,384]{1,0:T(8,128)(2,1)S(1)}, bf16[768,384]{1,0:T(8,128)(2,1)S(1)}, u32[]{:S(2)}, u32[]{:S(2)}) %collective-permute-start.30) | collective-permute-done | bytes 589856 | tf_op jit(solution)/shard_map/ppermute | solution.py:599
  91.6 2.8 %collective-permute-start.32 = (bf16[192,384]{1,0:T(8,128)(2,1)S(1)}, bf16[192,384]{1,0:T(8,128)(2,1)S(1)}, u32[]{:S(2)}, u32[]{:S(2)}) collective-permute-start(bf16[192,384]{1,0:T(8,128)(2,1)S(1)} %ba_join2.1.refs_2_.refs_0_), channel_id=1, source_target_pairs={{0,4},{1,5},{2,6},{3,7},{4,0},{5,1},{6,2},{7,3},{8,12},{9,13},{10,... | collective-permute-start | bytes 442376 | tf_op jit(solution)/shard_map/ppermute | solution.py:599
  94.4 1.7 %collective-permute-start.31 = (bf16[192,384]{1,0:T(8,128)(2,1)S(1)}, bf16[192,384]{1,0:T(8,128)(2,1)S(1)}, u32[]{:S(2)}, u32[]{:S(2)}) collective-permute-start(bf16[192,384]{1,0:T(8,128)(2,1)S(1)} %aa_join2.1.refs_2_.refs_0_), channel_id=1, source_target_pairs={{0,2},{1,3},{2,0},{3,1},{4,6},{5,7},{6,4},{7,5},{8,10},{9,11},{10,... | collective-permute-start | bytes 442376 | tf_op jit(solution)/shard_map/ppermute | solution.py:599
  96.2 1.7 %collective-permute-start.36 = (bf16[768,384]{1,0:T(8,128)(2,1)S(1)}, bf16[768,384]{1,0:T(8,128)(2,1)S(1)}, u32[]{:S(2)}, u32[]{:S(2)}) collective-permute-start(bf16[768,384]{1,0:T(8,128)(2,1)S(1)} %am_join1.1.refs_2_.refs_0_), channel_id=1, source_target_pairs={{0,1},{1,0},{2,3},{3,2},{4,5},{5,4},{6,7},{7,6},{8,9},{9,8},{10,11... | collective-permute-start | bytes 1769480 | tf_op jit(solution)/shard_map/ppermute | solution.py:599
  99.8 2.6 %collective-permute-start.34 = (bf16[384,384]{1,0:T(8,128)(2,1)S(1)}, bf16[384,384]{1,0:T(8,128)(2,1)S(1)}, u32[]{:S(2)}, u32[]{:S(2)}) collective-permute-start(bf16[384,384]{1,0:T(8,128)(2,1)S(1)} %aa_join1.1.refs_3_.refs_0_), channel_id=1, source_target_pairs={{0,1},{1,0},{2,3},{3,2},{4,5},{5,4},{6,7},{7,6},{8,9},{9,8},{10,11... | collective-permute-start | bytes 884744 | tf_op jit(solution)/shard_map/ppermute | solution.py:599
  103.9 2.3 %collective-permute-done.36.refs_1_ = bf16[768,384]{1,0:T(8,128)(2,1)S(1)} collective-permute-done((bf16[768,384]{1,0:T(8,128)(2,1)S(1)}, bf16[768,384]{1,0:T(8,128)(2,1)S(1)}, u32[]{:S(2)}, u32[]{:S(2)}) %collective-permute-start.36) | collective-permute-done | bytes 589856 | tf_op jit(solution)/shard_map/ppermute | solution.py:599
  106.6 2.8 %collective-permute-done.34.refs_1_ = bf16[384,384]{1,0:T(8,128)(2,1)S(1)} collective-permute-done((bf16[384,384]{1,0:T(8,128)(2,1)S(1)}, bf16[384,384]{1,0:T(8,128)(2,1)S(1)}, u32[]{:S(2)}, u32[]{:S(2)}) %collective-permute-start.34) | collective-permute-done | bytes 294944 | tf_op jit(solution)/shard_map/ppermute | solution.py:599
  109.6 2.3 %mlp_out.1 = (f32[1,384,1536]{2,1,0:T(8,128)}, f32[1,1536,384]{2,1,0:T(8,128)}, f32[8,128]{1,0:T(8,128)S(1)}) custom-call(bf16[1536,384]{1,0:T(8,128)(2,1)S(1)} %get-tuple-element.175.refs_2_.refs_0_, bf16[1536,384]{1,0:T(8,128)(2,1)S(1)} %collective-permute-done.38.refs_1_, bf16[768,384]{1,0:T(8,128)(2,1)S(1)} %get-tuple-element.176.refs_2_.refs_0_), custom_call_target="tpu_custom_call" | custom-call | flops 26214400000 | tf_op jit(solution)/shard_map/mlp_out/pallas_call | solution.py:501
  111.9 2.1 %attention_out.1 = (f32[1,384]{1,0:T(1,128)}, f32[1,384]{1,0:T(1,128)}, f32[1,384,1152]{2,1,0:T(8,128)}, f32[1,384]{1,0:T(1,128)}, f32[1,384]{1,0:T(1,128)}, /*i...) custom-call(bf16[768,384]{1,0:T(8,128)(2,1)S(1)} %get-tuple-element., ...), custom_call_target="tpu_custom_call" | custom-call | flops 26214400000 | tf_op jit(solution)/shard_map/attention_out/pallas_call | solution.py:501
  (100 shorter events, 23.2 us)
Async XLA Ops:
  4.1 6.7 %collective-permute-start.2 = (bf16[384,1536]{1,0:T(8,128)(2,1)S(1)}, bf16[384,1536]{1,0:T(8,128)(2,1)S(1)}, u32[]{:S(2)}, u32[]{:S(2)}) collective-permute-start(bf16[384,1536]{1,0:T(8,128)(2,1)S(1)} %bitcast.12), channel_id=1, source_target_pairs={{0,16},{16,0},{1,17},{17,1},{2,18},{18,2},{3,19},{19,3},{4,20},{20... | collective-permute-start | bytes 3538952 | tf_op jit(solution)/shard_map/ppermute | solution.py:679
  4.5 6.2 %collective-permute-start.3 = (bf16[1536,384]{1,0:T(8,128)(2,1)S(1)}, bf16[1536,384]{1,0:T(8,128)(2,1)S(1)}, u32[]{:S(2)}, u32[]{:S(2)}) collective-permute-start(bf16[1536,384]{1,0:T(8,128)(2,1)S(1)} %bitcast.14), channel_id=1, source_target_pairs={{0,16},{16,0},{1,17},{17,1},{2,18},{18,2},{3,19},{19,3},{4,20},{20... | collective-permute-start | bytes 3538952 | tf_op jit(solution)/shard_map/ppermute | solution.py:679
  21.6 9.2 %collective-permute-start.6 = (bf16[1536,384]{1,0:T(8,128)(2,1)S(1)}, bf16[1536,384]{1,0:T(8,128)(2,1)S(1)}, u32[]{:S(2)}, u32[]{:S(2)}) collective-permute-start(bf16[1536,384]{1,0:T(8,128)(2,1)S(1)} %get-tuple-element.141), channel_id=1, source_target_pairs={{0,16},{16,0},{1,17},{17,1},{2,18},{18,2},{3,19},{19,3},{4,20},{20... | collective-permute-start | bytes 3538952 | tf_op jit(solution)/shard_map/ppermute | solution.py:679
  26.6 7.4 %collective-permute-start.5 = (bf16[784,384]{1,0:T(8,128)(2,1)S(1)}, bf16[784,384]{1,0:T(8,128)(2,1)S(1)}, u32[]{:S(2)}, u32[]{:S(2)}) collective-permute-start(bf16[784,384]{1,0:T(8,128)(2,1)S(1)} %get-tuple-element.139), channel_id=1, source_target_pairs={{0,16},{16,0},{1,17},{17,1},{2,18},{18,2},{3,19},{19,3},{4,20},{20... | collective-permute-start | bytes 1806344 | tf_op jit(solution)/shard_map/ppermute | solution.py:679
  30.3 5.6 %collective-permute-start.4 = (bf16[1536,384]{1,0:T(8,128)(2,1)S(1)}, bf16[1536,384]{1,0:T(8,128)(2,1)S(1)}, u32[]{:S(2)}, u32[]{:S(2)}) collective-permute-start(bf16[1536,384]{1,0:T(8,128)(2,1)S(1)} %get-tuple-element.137), channel_id=1, source_target_pairs={{0,16},{16,0},{1,17},{17,1},{2,18},{18,2},{3,19},{19,3},{4,20},{20... | collective-permute-start | bytes 3538952 | tf_op jit(solution)/shard_map/ppermute | solution.py:679
  31.2 10.7 %collective-permute-start.9 = (bf16[768,384]{1,0:T(8,128)(2,1)S(1)}, bf16[768,384]{1,0:T(8,128)(2,1)S(1)}, u32[]{:S(2)}, u32[]{:S(2)}) collective-permute-start(bf16[768,384]{1,0:T(8,128)(2,1)S(1)} %get-tuple-element.149), channel_id=1, source_target_pairs={{0,1},{1,0},{2,3},{3,2},{4,5},{5,4},{6,7},{7,6},{8,9},{9,8},{10,11... | collective-permute-start | bytes 1769480 | tf_op jit(solution)/shard_map/ppermute | solution.py:599
  34.2 11.8 %collective-permute-start.11 = (bf16[400,384]{1,0:T(8,128)(2,1)S(1)}, bf16[400,384]{1,0:T(8,128)(2,1)S(1)}, u32[]{:S(2)}, u32[]{:S(2)}) collective-permute-start(bf16[400,384]{1,0:T(8,128)(2,1)S(1)} %get-tuple-element.153), channel_id=1, source_target_pairs={{0,2},{1,3},{2,0},{3,1},{4,6},{5,7},{6,4},{7,5},{8,10},{9,11},{10,... | collective-permute-start | bytes 921608 | tf_op jit(solution)/shard_map/ppermute | solution.py:599
  36.3 11.9 %collective-permute-start.14 = (bf16[768,384]{1,0:T(8,128)(2,1)S(1)}, bf16[768,384]{1,0:T(8,128)(2,1)S(1)}, u32[]{:S(2)}, u32[]{:S(2)}) collective-permute-start(bf16[768,384]{1,0:T(8,128)(2,1)S(1)} %get-tuple-element.157), channel_id=1, source_target_pairs={{0,1},{1,0},{2,3},{3,2},{4,5},{5,4},{6,7},{7,6},{8,9},{9,8},{10,11... | collective-permute-start | bytes 1769480 | tf_op jit(solution)/shard_map/ppermute | solution.py:599
  42.1 6.8 %collective-permute-start.13 = (bf16[384,384]{1,0:T(8,128)(2,1)S(1)}, bf16[384,384]{1,0:T(8,128)(2,1)S(1)}, u32[]{:S(2)}, u32[]{:S(2)}) collective-permute-start(bf16[384,384]{1,0:T(8,128)(2,1)S(1)} %get-tuple-element.156), channel_id=1, source_target_pairs={{0,2},{1,3},{2,0},{3,1},{4,6},{5,7},{6,4},{7,5},{8,10},{9,11},{10,... | collective-permute-start | bytes 884744 | tf_op jit(solution)/shard_map/ppermute | solution.py:599
  44.4 15.1 %collective-permute-start.10 = (bf16[400,384]{1,0:T(8,128)(2,1)S(1)}, bf16[400,384]{1,0:T(8,128)(2,1)S(1)}, u32[]{:S(2)}, u32[]{:S(2)}) collective-permute-start(bf16[400,384]{1,0:T(8,128)(2,1)S(1)} %get-tuple-element.152), channel_id=1, source_target_pairs={{0,1},{1,0},{2,3},{3,2},{4,5},{5,4},{6,7},{7,6},{8,9},{9,8},{10,11... | collective-permute-start | bytes 921608 | tf_op jit(solution)/shard_map/ppermute | solution.py:599
  46.1 12.2 %collective-permute-start.12 = (bf16[208,384]{1,0:T(8,128)(2,1)S(1)}, bf16[208,384]{1,0:T(8,128)(2,1)S(1)}, u32[]{:S(2)}, u32[]{:S(2)}) collective-permute-start(bf16[208,384]{1,0:T(8,128)(2,1)S(1)} %get-tuple-element.155), channel_id=1, source_target_pairs={{0,4},{1,5},{2,6},{3,7},{4,0},{5,1},{6,2},{7,3},{8,12},{9,13},{10,... | collective-permute-start | bytes 479240 | tf_op jit(solution)/shard_map/ppermute | solution.py:599
  49.0 6.6 %collective-permute-start.15 = (bf16[192,384]{1,0:T(8,128)(2,1)S(1)}, bf16[192,384]{1,0:T(8,128)(2,1)S(1)}, u32[]{:S(2)}, u32[]{:S(2)}) collective-permute-start(bf16[192,384]{1,0:T(8,128)(2,1)S(1)} %get-tuple-element.160), channel_id=1, source_target_pairs={{0,4},{1,5},{2,6},{3,7},{4,0},{5,1},{6,2},{7,3},{8,12},{9,13},{10,... | collective-permute-start | bytes 442376 | tf_op jit(solution)/shard_map/ppermute | solution.py:599
  52.2 50.2 %collective-permute-start.7 = (bf16[416,384]{1,0:T(8,128)(2,1)S(1)}, bf16[416,384]{1,0:T(8,128)(2,1)S(1)}, u32[]{:S(2)}, u32[]{:S(2)}) collective-permute-start(bf16[416,384]{1,0:T(8,128)(2,1)S(1)} %get-tuple-element.146), channel_id=1, source_target_pairs={{0,16},{16,0},{1,17},{17,1},{2,18},{18,2},{3,19},{19,3},{4,20},{20... | collective-permute-start | bytes 958472 | tf_op jit(solution)/shard_map/ppermute | solution.py:679
  54.1 8.4 %collective-permute-start.17 = (bf16[384,384]{1,0:T(8,128)(2,1)S(1)}, bf16[384,384]{1,0:T(8,128)(2,1)S(1)}, u32[]{:S(2)}, u32[]{:S(2)}) collective-permute-start(bf16[384,384]{1,0:T(8,128)(2,1)S(1)} %get-tuple-element.164), channel_id=1, source_target_pairs={{0,4},{1,5},{2,6},{3,7},{4,0},{5,1},{6,2},{7,3},{8,12},{9,13},{10,... | collective-permute-start | bytes 884744 | tf_op jit(solution)/shard_map/ppermute | solution.py:599
  55.7 10.3 %collective-permute-start.19 = (bf16[192,384]{1,0:T(8,128)(2,1)S(1)}, bf16[192,384]{1,0:T(8,128)(2,1)S(1)}, u32[]{:S(2)}, u32[]{:S(2)}) collective-permute-start(bf16[192,384]{1,0:T(8,128)(2,1)S(1)} %bm_sum.1.refs_2_.refs_0_), channel_id=1, source_target_pairs={{0,8},{1,9},{2,10},{3,11},{4,12},{5,13},{6,14},{7,15},{8,0},{9,1},... | collective-permute-start | bytes 442376 | tf_op jit(solution)/shard_map/ppermute | solution.py:599
  58.4 20.4 %collective-permute-start.23 = (bf16[112,384]{1,0:T(8,128)(2,1)S(1)}, bf16[112,384]{1,0:T(8,128)(2,1)S(1)}, u32[]{:S(2)}, u32[]{:S(2)}) collective-permute-start(bf16[112,384]{1,0:T(8,128)(2,1)S(1)} %get-tuple-element.169), channel_id=1, source_target_pairs={{0,1},{1,0},{2,3},{3,2},{4,5},{5,4},{6,7},{7,6},{8,9},{9,8},{10,11... | collective-permute-start | bytes 258056 | tf_op jit(solution)/shard_map/ppermute | solution.py:599
  64.3 6.7 %collective-permute-start.16 = (bf16[208,384]{1,0:T(8,128)(2,1)S(1)}, bf16[208,384]{1,0:T(8,128)(2,1)S(1)}, u32[]{:S(2)}, u32[]{:S(2)}) collective-permute-start(bf16[208,384]{1,0:T(8,128)(2,1)S(1)} %get-tuple-element.163), channel_id=1, source_target_pairs={{0,2},{1,3},{2,0},{3,1},{4,6},{5,7},{6,4},{7,5},{8,10},{9,11},{10,... | collective-permute-start | bytes 479240 | tf_op jit(solution)/shard_map/ppermute | solution.py:599
  66.0 6.4 %collective-permute-start.21 = (bf16[192,384]{1,0:T(8,128)(2,1)S(1)}, bf16[192,384]{1,0:T(8,128)(2,1)S(1)}, u32[]{:S(2)}, u32[]{:S(2)}) collective-permute-start(bf16[192,384]{1,0:T(8,128)(2,1)S(1)} %bm_total.1.refs_2_.refs_0_), channel_id=1, source_target_pairs={{0,4},{1,5},{2,6},{3,7},{4,0},{5,1},{6,2},{7,3},{8,12},{9,13},{10,... | collective-permute-start | bytes 442376 | tf_op jit(solution)/shard_map/ppermute | solution.py:599
  67.8 9.4 %collective-permute-start.24 = (bf16[192,384]{1,0:T(8,128)(2,1)S(1)}, bf16[192,384]{1,0:T(8,128)(2,1)S(1)}, u32[]{:S(2)}, u32[]{:S(2)}) collective-permute-start(bf16[192,384]{1,0:T(8,128)(2,1)S(1)} %am_sum.1.refs_2_.refs_0_), channel_id=1, source_target_pairs={{0,8},{1,9},{2,10},{3,11},{4,12},{5,13},{6,14},{7,15},{8,0},{9,1},... | collective-permute-start | bytes 442376 | tf_op jit(solution)/shard_map/ppermute | solution.py:599
  71.0 10.0 %collective-permute-start.20 = (bf16[112,384]{1,0:T(8,128)(2,1)S(1)}, bf16[112,384]{1,0:T(8,128)(2,1)S(1)}, u32[]{:S(2)}, u32[]{:S(2)}) collective-permute-start(bf16[112,384]{1,0:T(8,128)(2,1)S(1)} %get-tuple-element.168), channel_id=1, source_target_pairs={{0,4},{1,5},{2,6},{3,7},{4,0},{5,1},{6,2},{7,3},{8,12},{9,13},{10,... | collective-permute-start | bytes 258056 | tf_op jit(solution)/shard_map/ppermute | solution.py:599
  72.5 7.4 %collective-permute-start.22 = (bf16[384,384]{1,0:T(8,128)(2,1)S(1)}, bf16[384,384]{1,0:T(8,128)(2,1)S(1)}, u32[]{:S(2)}, u32[]{:S(2)}) collective-permute-start(bf16[384,384]{1,0:T(8,128)(2,1)S(1)} %bm_join2.1.refs_2_.refs_0_), channel_id=1, source_target_pairs={{0,2},{1,3},{2,0},{3,1},{4,6},{5,7},{6,4},{7,5},{8,10},{9,11},{10,... | collective-permute-start | bytes 884744 | tf_op jit(solution)/shard_map/ppermute | solution.py:599
  77.3 9.5 %collective-permute-start.26 = (bf16[192,384]{1,0:T(8,128)(2,1)S(1)}, bf16[192,384]{1,0:T(8,128)(2,1)S(1)}, u32[]{:S(2)}, u32[]{:S(2)}) collective-permute-start(bf16[192,384]{1,0:T(8,128)(2,1)S(1)} %am_total.1.refs_2_.refs_0_), channel_id=1, source_target_pairs={{0,2},{1,3},{2,0},{3,1},{4,6},{5,7},{6,4},{7,5},{8,10},{9,11},{10,... | collective-permute-start | bytes 442376 | tf_op jit(solution)/shard_map/ppermute | solution.py:599
  78.8 7.8 %collective-permute-start.27 = (bf16[112,384]{1,0:T(8,128)(2,1)S(1)}, bf16[112,384]{1,0:T(8,128)(2,1)S(1)}, u32[]{:S(2)}, u32[]{:S(2)}) collective-permute-start(bf16[112,384]{1,0:T(8,128)(2,1)S(1)} %ba_sum.1.refs_2_.refs_0_), channel_id=1, source_target_pairs={{0,8},{1,9},{2,10},{3,11},{4,12},{5,13},{6,14},{7,15},{8,0},{9,1},... | collective-permute-start | bytes 258056 | tf_op jit(solution)/shard_map/ppermute | solution.py:599
  79.9 10.7 %collective-permute-start.30 = (bf16[768,384]{1,0:T(8,128)(2,1)S(1)}, bf16[768,384]{1,0:T(8,128)(2,1)S(1)}, u32[]{:S(2)}, u32[]{:S(2)}) collective-permute-start(bf16[768,384]{1,0:T(8,128)(2,1)S(1)} %bm_join1.1.refs_2_.refs_0_), channel_id=1, source_target_pairs={{0,1},{1,0},{2,3},{3,2},{4,5},{5,4},{6,7},{7,6},{8,9},{9,8},{10,11... | collective-permute-start | bytes 1769480 | tf_op jit(solution)/shard_map/ppermute | solution.py:599
  81.1 7.8 %collective-permute-start.25 = (bf16[112,384]{1,0:T(8,128)(2,1)S(1)}, bf16[112,384]{1,0:T(8,128)(2,1)S(1)}, u32[]{:S(2)}, u32[]{:S(2)}) collective-permute-start(bf16[112,384]{1,0:T(8,128)(2,1)S(1)} %aa_sum.1.refs_2_.refs_0_), channel_id=1, source_target_pairs={{0,8},{1,9},{2,10},{3,11},{4,12},{5,13},{6,14},{7,15},{8,0},{9,1},... | collective-permute-start | bytes 258056 | tf_op jit(solution)/shard_map/ppermute | solution.py:599
  86.8 9.3 %collective-permute-start.33 = (bf16[384,384]{1,0:T(8,128)(2,1)S(1)}, bf16[384,384]{1,0:T(8,128)(2,1)S(1)}, u32[]{:S(2)}, u32[]{:S(2)}) collective-permute-start(bf16[384,384]{1,0:T(8,128)(2,1)S(1)} %am_join2.1.refs_2_.refs_0_), channel_id=1, source_target_pairs={{0,4},{1,5},{2,6},{3,7},{4,0},{5,1},{6,2},{7,3},{8,12},{9,13},{10,... | collective-permute-start | bytes 884744 | tf_op jit(solution)/shard_map/ppermute | solution.py:599
  88.9 5.5 %collective-permute-start.28 = (bf16[96,384]{1,0:T(8,128)(2,1)S(1)}, bf16[96,384]{1,0:T(8,128)(2,1)S(1)}, u32[]{:S(2)}, u32[]{:S(2)}) collective-permute-start(bf16[96,384]{1,0:T(8,128)(2,1)S(1)} %get-tuple-element.171.refs_2_.refs_0_), channel_id=1, source_target_pairs={{0,4},{1,5},{2,6},{3,7},{4,0},{5,1},{6,2},{7,3},{8,12},{9,13},{10,... | collective-permute-start | bytes 221192 | tf_op jit(solution)/shard_map/ppermute | solution.py:599
  91.6 7.5 %collective-permute-start.32 = (bf16[192,384]{1,0:T(8,128)(2,1)S(1)}, bf16[192,384]{1,0:T(8,128)(2,1)S(1)}, u32[]{:S(2)}, u32[]{:S(2)}) collective-permute-start(bf16[192,384]{1,0:T(8,128)(2,1)S(1)} %ba_join2.1.refs_2_.refs_0_), channel_id=1, source_target_pairs={{0,4},{1,5},{2,6},{3,7},{4,0},{5,1},{6,2},{7,3},{8,12},{9,13},{10,... | collective-permute-start | bytes 442376 | tf_op jit(solution)/shard_map/ppermute | solution.py:599
  94.4 5.3 %collective-permute-start.31 = (bf16[192,384]{1,0:T(8,128)(2,1)S(1)}, bf16[192,384]{1,0:T(8,128)(2,1)S(1)}, u32[]{:S(2)}, u32[]{:S(2)}) collective-permute-start(bf16[192,384]{1,0:T(8,128)(2,1)S(1)} %aa_join2.1.refs_2_.refs_0_), channel_id=1, source_target_pairs={{0,2},{1,3},{2,0},{3,1},{4,6},{5,7},{6,4},{7,5},{8,10},{9,11},{10,... | collective-permute-start | bytes 442376 | tf_op jit(solution)/shard_map/ppermute | solution.py:599
  96.2 9.9 %collective-permute-start.36 = (bf16[768,384]{1,0:T(8,128)(2,1)S(1)}, bf16[768,384]{1,0:T(8,128)(2,1)S(1)}, u32[]{:S(2)}, u32[]{:S(2)}) collective-permute-start(bf16[768,384]{1,0:T(8,128)(2,1)S(1)} %am_join1.1.refs_2_.refs_0_), channel_id=1, source_target_pairs={{0,1},{1,0},{2,3},{3,2},{4,5},{5,4},{6,7},{7,6},{8,9},{9,8},{10,11... | collective-permute-start | bytes 1769480 | tf_op jit(solution)/shard_map/ppermute | solution.py:599
  99.1 7.4 %collective-permute-start.35 = (bf16[384,384]{1,0:T(8,128)(2,1)S(1)}, bf16[384,384]{1,0:T(8,128)(2,1)S(1)}, u32[]{:S(2)}, u32[]{:S(2)}) collective-permute-start(bf16[384,384]{1,0:T(8,128)(2,1)S(1)} %ba_join1.1.refs_2_.refs_0_), channel_id=1, source_target_pairs={{0,2},{1,3},{2,0},{3,1},{4,6},{5,7},{6,4},{7,5},{8,10},{9,11},{10,... | collective-permute-start | bytes 884744 | tf_op jit(solution)/shard_map/ppermute | solution.py:599
  99.8 9.5 %collective-permute-start.34 = (bf16[384,384]{1,0:T(8,128)(2,1)S(1)}, bf16[384,384]{1,0:T(8,128)(2,1)S(1)}, u32[]{:S(2)}, u32[]{:S(2)}) collective-permute-start(bf16[384,384]{1,0:T(8,128)(2,1)S(1)} %aa_join1.1.refs_3_.refs_0_), channel_id=1, source_target_pairs={{0,1},{1,0},{2,3},{3,2},{4,5},{5,4},{6,7},{7,6},{8,9},{9,8},{10,11... | collective-permute-start | bytes 884744 | tf_op jit(solution)/shard_map/ppermute | solution.py:599
  (13 other events, 39.2 us)
